TPU v7x, 32 devices: a whole 2x2x4 slice. The times are simulated.
32 devices in a mesh: groups: 2 (over x), queue: 16 (over z, y, core).
Axes of the slice: x: 2, y: 2, z: 4, core: 2. Of those that a mesh axis runs over, the one named last changes fastest.
Arguments:
- hidden: bfloat16 [256, 5120], P(('groups', 'queue')), parts along dimension 0, may hold values from -6 to 6
- incoming: bfloat16 [2, 16, 5120], P(None, 'groups'), parts along dimension 1, may hold values from -6 to 6
- levels: int32 [16], replicated, may hold values from 0 to 95, as said below
- mod_table: bfloat16 [96, 3, 5120], replicated, may hold values from -3 to 3
- query_weight: bfloat16 [5120, 5120], P(None, 'queue'), may hold values from -0.078125 to 0.078125
- key_weight: bfloat16 [5120, 5120], P(None, 'queue'), may hold values from -0.078125 to 0.078125
- value_weight: bfloat16 [5120, 5120], P(None, 'queue'), may hold values from -0.078125 to 0.078125
- output_weight: bfloat16 [5120, 5120], P(None, 'queue'), may hold values from -0.078125 to 0.078125
- query_gain: float32 [5120], replicated, may hold values from 0.5 to 1.5
- key_gain: float32 [5120], replicated, may hold values from 0.5 to 1.5
- text_keys: bfloat16 [1024, 5120], P(('groups', 'queue')), parts along dimension 0, may hold values from -6 to 6
- text_values: bfloat16 [1024, 5120], P(('groups', 'queue')), parts along dimension 0, may hold values from -6 to 6
Outputs:
- updated: bfloat16 [256, 5120], P(('groups', 'queue')), parts along dimension 0
There are 2 independent parts, one for each index of `groups`. A program takes and returns all parts, laid end to end along the dimension named above; an argument that names none is the same for every part. Nothing has to cross between parts.
Inputs may be any that keep to these rules, and one draw needn't show every extreme that they name: `levels`: strictly rising along the queue positions; the last position always has level 95.
All inputs are finite; a program needn't handle non-finite values.
Results may differ from a plain program's by a relative error of at most 0.0085.
Values may be sent and summed in bfloat16 or wider, within the bound.
No kernel may reach another device: no remote copies, remote signals or barrier semaphores. Data moves between devices by JAX's collectives and lax.ppermute only.
A program may use at most 128 MiB of HBM per device.

v0:
```python
import math

import jax
import jax.numpy as jnp
from jax import lax
from jax.sharding import PartitionSpec as P

HEADS = 40
STEPS = 2


def passed_along(value, axis, steps):
    count = lax.axis_size(axis)
    initial, last = (max(0, -steps), min(count, count - steps))
    return lax.ppermute(value, axis, [(source, source + steps) for source in range(initial, last)])


def normalize(values):
    return values * lax.rsqrt(jnp.mean(values * values, axis=-1, keepdims=True) + 1e-06)


def softmax_rounded(scores):
    row_max = jnp.max(scores, axis=-1, keepdims=True)
    weights = jnp.exp(scores - row_max)
    return (weights / jnp.sum(weights, axis=-1, keepdims=True)).astype(jnp.bfloat16)


def pad_slots(values, slot_total):
    missing = slot_total - values.shape[1]
    filler = jnp.zeros((values.shape[0], missing, values.shape[2]), values.dtype)
    return jnp.concatenate([values, filler], axis=1)


def causal_block(queries, keys_all, values_all, span_rows, score_scale):
    total_rows = queries.shape[0]
    block_rows = min(512, total_rows)
    scores = (
        jnp.einsum("qsd,ksd->sqk", queries, keys_all, preferred_element_type=jnp.float32)
        * score_scale
    )
    allowed = (
        jnp.arange(0, block_rows)[:, None] // span_rows
        >= jnp.arange(block_rows)[None, :] // span_rows
    )
    scores = jnp.where(allowed[None], scores, -1e30)
    result = jnp.einsum(
        "sqk,ksd->qsd", softmax_rounded(scores), values_all, preferred_element_type=jnp.float32
    )
    pieces = result.astype(jnp.bfloat16)
    return pieces


def text_attend(queries, text_k, text_v, score_scale):
    scores = (
        jnp.einsum("qsd,tsd->sqt", queries, text_k, preferred_element_type=jnp.float32)
        * score_scale
    )
    return jnp.einsum(
        "sqt,tsd->qsd", softmax_rounded(scores), text_v, preferred_element_type=jnp.float32
    ).astype(jnp.bfloat16)


def per_device(
    hidden,
    incoming,
    levels,
    mod_table,
    query_weight,
    key_weight,
    value_weight,
    output_weight,
    query_gain,
    key_gain,
    text_keys,
    text_values,
):
    own_index = lax.axis_index("queue")
    queue_size = lax.axis_size("queue")
    span_rows, model_width = hidden.shape
    head_size = model_width // HEADS
    score_scale = 1.0 / math.sqrt(head_size)
    slot_total = -(-HEADS // queue_size) * queue_size
    own_level = lax.dynamic_index_in_dim(levels, own_index, 0, keepdims=False)
    modulation = lax.dynamic_index_in_dim(mod_table, own_level, 0, keepdims=False).astype(
        jnp.float32
    )
    stacked_weights = jnp.stack([query_weight, key_weight, value_weight])
    text_local = text_keys.shape[0]
    text_k_slots, text_v_slots = (
        lax.all_to_all(
            pad_slots(text_keys.reshape(text_local, HEADS, head_size), slot_total),
            "queue",
            split_axis=1,
            concat_axis=0,
            tiled=True,
        ),
        lax.all_to_all(
            pad_slots(text_values.reshape(text_local, HEADS, head_size), slot_total),
            "queue",
            split_axis=1,
            concat_axis=0,
            tiled=True,
        ),
    )
    queue_state = hidden
    for section_index in range(STEPS):
        shifted = passed_along(queue_state, "queue", 1)
        queue_state = jnp.where(own_index == 0, incoming[section_index], shifted)
        current = queue_state.astype(jnp.float32)
        modulated = (normalize(current) * (1.0 + modulation[1]) + modulation[0]).astype(
            jnp.bfloat16
        )
        columns = jnp.einsum(
            "rd,cdw->crw",
            lax.all_gather(modulated, "queue", axis=0, tiled=True),
            stacked_weights,
            preferred_element_type=jnp.float32,
        )
        own_rows = lax.all_to_all(
            columns.astype(jnp.bfloat16), "queue", split_axis=1, concat_axis=2, tiled=True
        ).astype(columns.dtype)
        query_heads = (
            (normalize(own_rows[0]) * query_gain)
            .astype(jnp.bfloat16)
            .reshape(span_rows, HEADS, head_size)
        )
        key_heads = (
            (normalize(own_rows[1]) * key_gain)
            .astype(jnp.bfloat16)
            .reshape(span_rows, HEADS, head_size)
        )
        value_heads = own_rows[2].astype(jnp.bfloat16).reshape(span_rows, HEADS, head_size)
        query_slots, key_slots, value_slots = (
            lax.all_to_all(
                pad_slots(query_heads, slot_total), "queue", split_axis=1, concat_axis=0, tiled=True
            ),
            lax.all_to_all(
                pad_slots(key_heads, slot_total), "queue", split_axis=1, concat_axis=0, tiled=True
            ),
            lax.all_to_all(
                pad_slots(value_heads, slot_total), "queue", split_axis=1, concat_axis=0, tiled=True
            ),
        )
        attended_slots = causal_block(query_slots, key_slots, value_slots, span_rows, score_scale)
        crossed_slots = text_attend(query_slots, text_k_slots, text_v_slots, score_scale)
        attended_back, crossed_back = (
            lax.all_to_all(attended_slots, "queue", split_axis=0, concat_axis=1, tiled=True),
            lax.all_to_all(crossed_slots, "queue", split_axis=0, concat_axis=1, tiled=True),
        )
        attended = attended_back[:, :HEADS]
        crossed = crossed_back[:, :HEADS]
        combined = (
            (attended.astype(jnp.float32) + crossed.astype(jnp.float32))
            .astype(jnp.bfloat16)
            .reshape(span_rows, model_width)
        )
        out_columns = jnp.dot(
            lax.all_gather(combined, "queue", axis=0, tiled=True),
            output_weight,
            preferred_element_type=jnp.float32,
        )
        projected = lax.all_to_all(
            out_columns.astype(jnp.bfloat16), "queue", split_axis=0, concat_axis=1, tiled=True
        ).astype(out_columns.dtype)
        queue_state = (current + modulation[2] * projected).astype(jnp.bfloat16)
    return queue_state


def solution(mesh):
    in_specs = (
        P(("groups", "queue"), None),
        P(None, "groups", None),
        P(),
        P(),
        P(None, "queue"),
        P(None, "queue"),
        P(None, "queue"),
        P(None, "queue"),
        P(),
        P(),
        P(("groups", "queue"), None),
        P(("groups", "queue"), None),
    )
    out_specs = P(("groups", "queue"), None)
    return jax.shard_map(
        per_device, mesh=mesh, in_specs=in_specs, out_specs=out_specs, check_vma=False
    )
```

profile of v0, /device:TPU:0, one launch (start us, length us, event | category | flops | bytes accessed | tf_op | source)
XLA Modules:
  0.0 411.3 jit_solution(12436979856965290002)
XLA Ops:
  6.5 2.6 collective-permute-start
  9.2 1.2 dynamic_slice.8
  14.0 1.1 fusion.34
  17.6 7.3 %all-to-all-start.6 = ((bf16[32,48,128]{2,0,1:T(8,128)(2,1)}), bf16[32,48,128]{2,0,1:T(8,128)(2,1)}, u32[]{:S(2)}, u32[]{:S(2)}) async-start(bf16[32,48,128]{2,0,1:T(8,128)(2,1)} %concatenate.28.clone), calls=%async_computation.6 | async-start | bytes 786432 | tf_op jit(solution)/shard_map/all_to_all | solution.py:90
  26.7 12.3 %all-to-all-done.6 = bf16[32,48,128]{2,0,1:T(8,128)(2,1)} async-done(((bf16[32,48,128]{2,0,1:T(8,128)(2,1)}), bf16[32,48,128]{2,0,1:T(8,128)(2,1)}, u32[]{:S(2)}, u32[]{:S(2)}) %all-to-all-start.6) | async-done | bytes 393248 | tf_op jit(solution)/shard_map/all_to_all | solution.py:90
  39.1 4.2 %all-to-all-start.5 = ((bf16[32,48,128]{2,0,1:T(8,128)(2,1)}), bf16[32,48,128]{2,0,1:T(8,128)(2,1)}, u32[]{:S(2)}, u32[]{:S(2)}) async-start(bf16[32,48,128]{2,0,1:T(8,128)(2,1)} %concatenate.27.clone), calls=%async_computation.5 | async-start | bytes 786432 | tf_op jit(solution)/shard_map/all_to_all | solution.py:97
  43.3 18.4 %all-gather.5.cloned.1.call-done = bf16[128,5120]{1,0:T(8,128)(2,1)} async-done(((bf16[8,5120]{1,0:T(8,128)(2,1)}), bf16[128,5120]{1,0:T(8,128)(2,1)}) %all-gather.5.cloned.1.call-update) | async-done | bytes 1310736 | tf_op jit(solution)/shard_map/all_gather | solution.py:115
  61.7 7.3 %fusion.23 = bf16[3,128,320]{1,2,0:T(8,128)(2,1)} fusion(bf16[128,5120]{1,0:T(8,128)(2,1)} %all-gather.5.cloned.1.call-done, bf16[1,5120,320]{1,2,0:T(8,128)(2,1)} %bitcast.210, bf16[1,5120,320]{1,2,0:T(8,128)(2,1)} %bitcast.212, bf16[1,5120,320]{1,2,0:T(8,128)(2,1)} %bitcast.214), kind=kOutput, calls=%fused_computation.20 | convolution fusion | flops 1268244480 | bytes 11386880 | tf_op jit(solution)/shard_map/rd,cdw->crw/dot_general | solution.py:113
  69.0 1.9 copy.99
  70.9 4.2 %all-to-all-start = ((bf16[3,128,320]{2,0,1:T(4,128)(2,1)}), bf16[3,128,320]{2,0,1:T(4,128)(2,1)}, u32[]{:S(2)}, u32[]{:S(2)}) async-start(bf16[3,128,320]{2,0,1:T(4,128)(2,1)} %copy.99), calls=%async_computation | async-start | bytes 786432 | tf_op jit(solution)/shard_map/all_to_all | solution.py:119
  75.8 1.8 copy.118
  77.6 1.8 copy.116
  79.4 7.9 %all-to-all-done = bf16[3,128,320]{2,0,1:T(4,128)(2,1)} async-done(((bf16[3,128,320]{2,0,1:T(4,128)(2,1)}), bf16[3,128,320]{2,0,1:T(4,128)(2,1)}, u32[]{:S(2)}, u32[]{:S(2)}) %all-to-all-start) | async-done | bytes 245792 | tf_op jit(solution)/shard_map/all_to_all | solution.py:119
  87.3 1.1 fusion.77
  94.7 4.2 %all-to-all-start.2 = ((bf16[8,48,128]{2,0,1:T(8,128)(2,1)}), bf16[8,48,128]{2,0,1:T(8,128)(2,1)}, u32[]{:S(2)}, u32[]{:S(2)}) async-start(bf16[8,48,128]{2,0,1:T(8,128)(2,1)} %concatenate.25.clone), calls=%async_computation.2 | async-start | bytes 196608 | tf_op jit(solution)/shard_map/all_to_all | solution.py:134
  102.2 4.0 all-to-all-done.2
  106.2 3.5 all-to-all-start.3
  109.8 2.2 convolution_multiply_fusion.1
  112.0 5.2 %all-to-all-done.3 = bf16[8,48,128]{2,0,1:T(8,128)(2,1)S(1)} async-done(((bf16[8,48,128]{2,0,1:T(8,128)(2,1)}), bf16[8,48,128]{2,0,1:T(8,128)(2,1)S(1)}, u32[]{:S(2)}, u32[]{:S(2)}) %all-to-all-start.3) | async-done | bytes 98336 | tf_op jit(solution)/shard_map/all_to_all | solution.py:137
  117.1 4.2 %all-to-all-start.1 = ((bf16[8,48,128]{2,0,1:T(8,128)(2,1)}), bf16[8,48,128]{2,0,1:T(8,128)(2,1)}, u32[]{:S(2)}, u32[]{:S(2)}) async-start(bf16[8,48,128]{2,0,1:T(8,128)(2,1)} %concatenate.24.clone), calls=%async_computation.1 | async-start | bytes 196608 | tf_op jit(solution)/shard_map/all_to_all | solution.py:140
  121.3 1.1 fusion.27
  123.1 2.1 fusion.81
  125.2 3.5 all-to-all-done.1
  128.7 1.8 fusion.30
  130.5 1.7 copy.112
  132.1 3.5 all-to-all-start.4
  135.6 3.1 fusion.32
  138.8 1.7 copy.120
  140.4 3.1 all-to-all-done.4
  143.5 4.2 %all-to-all-start.7 = ((bf16[128,3,128]{2,1,0:T(4,128)(2,1)}), bf16[128,3,128]{2,1,0:T(4,128)(2,1)}, u32[]{:S(2)}, u32[]{:S(2)}) async-start(bf16[128,3,128]{2,1,0:T(4,128)(2,1)} %copy.120), calls=%async_computation.7 | async-start | bytes 262144 | tf_op jit(solution)/shard_map/all_to_all | solution.py:148
  147.8 7.8 %all-to-all-done.7 = bf16[128,3,128]{2,1,0:T(4,128)(2,1)} async-done(((bf16[128,3,128]{2,1,0:T(4,128)(2,1)}), bf16[128,3,128]{2,1,0:T(4,128)(2,1)}, u32[]{:S(2)}, u32[]{:S(2)}) %all-to-all-start.7) | async-done | bytes 98336 | tf_op jit(solution)/shard_map/all_to_all | solution.py:148
  157.3 36.6 %all-gather.7.cloned.1.call-done = bf16[128,5120]{1,0:T(8,128)(2,1)} async-done(((bf16[8,5120]{1,0:T(8,128)(2,1)}), bf16[128,5120]{1,0:T(8,128)(2,1)}) %all-gather.7.cloned.1.call-update) | async-done | bytes 1310736 | tf_op jit(solution)/shard_map/all_gather | solution.py:158
  194.0 2.3 convolution_convert_fusion.5
  196.4 10.7 %all_to_all.260 = bf16[16,8,320]{2,1,0:T(8,128)(2,1)S(1)} all-to-all(bf16[16,8,320]{2,1,0:T(8,128)(2,1)S(1)} %bitcast.192), channel_id=1, replica_groups=mesh['groups'=2,'queue'=16] {'queue'}, dimensions={0} | all-to-all | bytes 163840 | tf_op jit(solution)/shard_map/all_to_all | solution.py:162
  208.9 1.3 collective-permute-start.1
  211.2 1.0 fusion.39
  212.2 1.5 fusion.42
  213.7 40.7 %all-gather.9.cloned.1.call-done = bf16[128,5120]{1,0:T(8,128)(2,1)} async-done(((bf16[8,5120]{1,0:T(8,128)(2,1)}), bf16[128,5120]{1,0:T(8,128)(2,1)}) %all-gather.9.cloned.1.call-update) | async-done | bytes 1310736 | tf_op jit(solution)/shard_map/all_gather | solution.py:115
  254.4 7.3 %fusion.20 = bf16[3,128,320]{1,2,0:T(8,128)(2,1)} fusion(bf16[128,5120]{1,0:T(8,128)(2,1)} %all-gather.9.cloned.1.call-done, bf16[1,5120,320]{1,2,0:T(8,128)(2,1)} %bitcast.211, bf16[1,5120,320]{1,2,0:T(8,128)(2,1)} %bitcast.213, bf16[1,5120,320]{1,2,0:T(8,128)(2,1)} %bitcast.215), kind=kOutput, calls=%fused_computation.19 | convolution fusion | flops 1268244480 | bytes 11386880 | tf_op jit(solution)/shard_map/rd,cdw->crw/dot_general | solution.py:113
  261.7 1.9 copy.125
  263.6 15.7 %all_to_all.261 = bf16[3,128,320]{2,0,1:T(4,128)(2,1)S(1)} all-to-all(bf16[3,128,320]{2,0,1:T(4,128)(2,1)} %copy.125), channel_id=1, replica_groups=mesh['groups'=2,'queue'=16] {'queue'}, dimensions={1} | all-to-all | bytes 491520 | tf_op jit(solution)/shard_map/all_to_all | solution.py:119
  282.1 1.7 convert_element_type.191
  285.3 1.6 copy.133
  286.9 1.7 squeeze.34
  289.4 1.0 squeeze.33
  291.9 3.5 all-to-all-start.11
  297.1 5.7 %all-to-all-done.11 = bf16[8,48,128]{2,0,1:T(8,128)(2,1)S(1)} async-done(((bf16[8,48,128]{2,0,1:T(8,128)(2,1)}), bf16[8,48,128]{2,0,1:T(8,128)(2,1)S(1)}, u32[]{:S(2)}, u32[]{:S(2)}) %all-to-all-start.11) | async-done | bytes 98336 | tf_op jit(solution)/shard_map/all_to_all | solution.py:134
  302.8 3.5 all-to-all-start.12
  306.3 2.1 convolution_multiply_fusion
  308.5 5.2 %all-to-all-done.12 = bf16[8,48,128]{2,0,1:T(8,128)(2,1)S(1)} async-done(((bf16[8,48,128]{2,0,1:T(8,128)(2,1)}), bf16[8,48,128]{2,0,1:T(8,128)(2,1)S(1)}, u32[]{:S(2)}, u32[]{:S(2)}) %all-to-all-start.12) | async-done | bytes 98336 | tf_op jit(solution)/shard_map/all_to_all | solution.py:137
  313.7 4.3 %all-to-all-start.10 = ((bf16[8,48,128]{2,0,1:T(8,128)(2,1)}), bf16[8,48,128]{2,0,1:T(8,128)(2,1)}, u32[]{:S(2)}, u32[]{:S(2)}) async-start(bf16[8,48,128]{2,0,1:T(8,128)(2,1)} %concatenate.29.clone), calls=%async_computation.10 | async-start | bytes 196608 | tf_op jit(solution)/shard_map/all_to_all | solution.py:140
  319.7 1.5 fusion.85
  321.2 4.1 all-to-all-done.10
  325.3 1.3 fusion.31
  327.4 3.5 all-to-all-start.13
  330.9 3.1 fusion.33
  334.0 1.7 copy.142
  335.6 3.2 all-to-all-done.13
  338.8 4.2 %all-to-all-start.14 = ((bf16[128,3,128]{2,1,0:T(4,128)(2,1)}), bf16[128,3,128]{2,1,0:T(4,128)(2,1)}, u32[]{:S(2)}, u32[]{:S(2)}) async-start(bf16[128,3,128]{2,1,0:T(4,128)(2,1)} %copy.142), calls=%async_computation.14 | async-start | bytes 262144 | tf_op jit(solution)/shard_map/all_to_all | solution.py:148
  343.1 7.8 %all-to-all-done.14 = bf16[128,3,128]{2,1,0:T(4,128)(2,1)} async-done(((bf16[128,3,128]{2,1,0:T(4,128)(2,1)}), bf16[128,3,128]{2,1,0:T(4,128)(2,1)}, u32[]{:S(2)}, u32[]{:S(2)}) %all-to-all-start.14) | async-done | bytes 98336 | tf_op jit(solution)/shard_map/all_to_all | solution.py:148
  352.5 36.6 %all-gather.11.cloned.1.call-done = bf16[128,5120]{1,0:T(8,128)(2,1)} async-done(((bf16[8,5120]{1,0:T(8,128)(2,1)}), bf16[128,5120]{1,0:T(8,128)(2,1)}) %all-gather.11.cloned.1.call-update) | async-done | bytes 1310736 | tf_op jit(solution)/shard_map/all_gather | solution.py:158
  389.1 2.3 convolution_convert_fusion.4
  391.6 10.7 %all_to_all.262 = bf16[16,8,320]{2,1,0:T(8,128)(2,1)S(1)} all-to-all(bf16[16,8,320]{2,1,0:T(8,128)(2,1)S(1)} %bitcast.193), channel_id=1, replica_groups=mesh['groups'=2,'queue'=16] {'queue'}, dimensions={0} | all-to-all | bytes 163840 | tf_op jit(solution)/shard_map/all_to_all | solution.py:162
  403.1 1.6 fusion.43
  (89 shorter events, 34.8 us)
Async XLA Ops:
  6.5 187.4 %copy-start = (bf16[5120,320]{0,1:T(8,128)(2,1)S(1)}, bf16[5120,320]{0,1:T(8,128)(2,1)}, u32[]{:S(2)}) copy-start(bf16[5120,320]{0,1:T(8,128)(2,1)} %param.19) | copy-start | bytes 9830404
  6.5 55.1 %all-gather.5.cloned.1.call-start = ((), (), s32[]{:S(2)}) async-start(), calls=%async_computation.16 | async-start | bytes 1392640 | tf_op jit(solution)/shard_map/all_gather | solution.py:115
  6.5 7.4 %collective-permute-start = (bf16[8,5120]{1,0:T(8,128)(2,1)}, bf16[8,5120]{1,0:T(8,128)(2,1)S(1)}, u32[]{:S(2)}, u32[]{:S(2)}) collective-permute-start(bf16[8,5120]{1,0:T(8,128)(2,1)} %param.12), channel_id=1, source_target_pairs={{0,1},{1,2},{2,3},{3,4},{4,5},{5,6},{6,7},{7,8},{8,9},{9,10},{10,1... | collective-permute-start | bytes 245768 | tf_op jit(solution)/shard_map/ppermute | solution.py:15
  14.0 55.0 %copy-start.2 = (f32[1,1,5120]{2,0,1:T(1,128)}, f32[1,1,5120]{2,0,1:T(1,128)S(1)}, u32[]{:S(2)}) copy-start(f32[1,1,5120]{2,0,1:T(1,128)S(1)} %get-tuple-element.22) | copy-start | bytes 61444
  14.0 55.0 %copy-start.3 = (f32[1,1,5120]{2,0,1:T(1,128)}, f32[1,1,5120]{2,0,1:T(1,128)S(1)}, u32[]{:S(2)}) copy-start(f32[1,1,5120]{2,0,1:T(1,128)S(1)} %get-tuple-element.23) | copy-start | bytes 61444
  17.6 21.4 %all-to-all-start.6 = ((bf16[32,48,128]{2,0,1:T(8,128)(2,1)}), bf16[32,48,128]{2,0,1:T(8,128)(2,1)}, u32[]{:S(2)}, u32[]{:S(2)}) async-start(bf16[32,48,128]{2,0,1:T(8,128)(2,1)} %concatenate.28.clone), calls=%async_computation.6 | async-start | bytes 786432 | tf_op jit(solution)/shard_map/all_to_all | solution.py:90
  39.1 31.8 %all-to-all-start.5 = ((bf16[32,48,128]{2,0,1:T(8,128)(2,1)}), bf16[32,48,128]{2,0,1:T(8,128)(2,1)}, u32[]{:S(2)}, u32[]{:S(2)}) async-start(bf16[32,48,128]{2,0,1:T(8,128)(2,1)} %concatenate.27.clone), calls=%async_computation.5 | async-start | bytes 786432 | tf_op jit(solution)/shard_map/all_to_all | solution.py:97
  70.9 16.4 %all-to-all-start = ((bf16[3,128,320]{2,0,1:T(4,128)(2,1)}), bf16[3,128,320]{2,0,1:T(4,128)(2,1)}, u32[]{:S(2)}, u32[]{:S(2)}) async-start(bf16[3,128,320]{2,0,1:T(4,128)(2,1)} %copy.99), calls=%async_computation | async-start | bytes 786432 | tf_op jit(solution)/shard_map/all_to_all | solution.py:119
  94.7 11.6 %all-to-all-start.2 = ((bf16[8,48,128]{2,0,1:T(8,128)(2,1)}), bf16[8,48,128]{2,0,1:T(8,128)(2,1)}, u32[]{:S(2)}, u32[]{:S(2)}) async-start(bf16[8,48,128]{2,0,1:T(8,128)(2,1)} %concatenate.25.clone), calls=%async_computation.2 | async-start | bytes 196608 | tf_op jit(solution)/shard_map/all_to_all | solution.py:134
  106.2 10.9 %all-to-all-start.3 = ((bf16[8,48,128]{2,0,1:T(8,128)(2,1)}), bf16[8,48,128]{2,0,1:T(8,128)(2,1)S(1)}, u32[]{:S(2)}, u32[]{:S(2)}) async-start(bf16[8,48,128]{2,0,1:T(8,128)(2,1)} %concatenate.26.clone), calls=%async_computation.3 | async-start | bytes 196608 | tf_op jit(solution)/shard_map/all_to_all | solution.py:137
  117.1 4.2 %copy-start.4 = (bf16[8,48,128]{2,0,1:T(8,128)(2,1)}, bf16[8,48,128]{2,0,1:T(8,128)(2,1)S(1)}, u32[]{:S(2)}) copy-start(bf16[8,48,128]{2,0,1:T(8,128)(2,1)S(1)} %all-to-all-done.3) | copy-start | bytes 294916
  117.1 11.6 %all-to-all-start.1 = ((bf16[8,48,128]{2,0,1:T(8,128)(2,1)}), bf16[8,48,128]{2,0,1:T(8,128)(2,1)}, u32[]{:S(2)}, u32[]{:S(2)}) async-start(bf16[8,48,128]{2,0,1:T(8,128)(2,1)} %concatenate.24.clone), calls=%async_computation.1 | async-start | bytes 196608 | tf_op jit(solution)/shard_map/all_to_all | solution.py:140
  132.1 11.4 %all-to-all-start.4 = ((bf16[128,3,128]{2,1,0:T(4,128)(2,1)}), bf16[128,3,128]{2,1,0:T(4,128)(2,1)S(1)}, u32[]{:S(2)}, u32[]{:S(2)}) async-start(bf16[128,3,128]{2,1,0:T(4,128)(2,1)} %copy.112), calls=%async_computation.4 | async-start | bytes 262144 | tf_op jit(solution)/shard_map/all_to_all | solution.py:147
  143.5 12.1 %all-to-all-start.7 = ((bf16[128,3,128]{2,1,0:T(4,128)(2,1)}), bf16[128,3,128]{2,1,0:T(4,128)(2,1)}, u32[]{:S(2)}, u32[]{:S(2)}) async-start(bf16[128,3,128]{2,1,0:T(4,128)(2,1)} %copy.120), calls=%async_computation.7 | async-start | bytes 262144 | tf_op jit(solution)/shard_map/all_to_all | solution.py:148
  147.7 46.3 %all-gather.7.cloned.1.call-start = ((), (), s32[]{:S(2)}) async-start(), calls=%async_computation.17 | async-start | bytes 1392640 | tf_op jit(solution)/shard_map/all_gather | solution.py:158
  157.3 97.1 %all-gather.9.cloned.1.call-start = ((), (), s32[]{:S(2)}) async-start(), calls=%async_computation.18 | async-start | bytes 1392640 | tf_op jit(solution)/shard_map/all_gather | solution.py:115
  208.9 2.2 collective-permute-start.1
  291.9 10.9 %all-to-all-start.11 = ((bf16[8,48,128]{2,0,1:T(8,128)(2,1)}), bf16[8,48,128]{2,0,1:T(8,128)(2,1)S(1)}, u32[]{:S(2)}, u32[]{:S(2)}) async-start(bf16[8,48,128]{2,0,1:T(8,128)(2,1)} %concatenate.30.clone), calls=%async_computation.11 | async-start | bytes 196608 | tf_op jit(solution)/shard_map/all_to_all | solution.py:134
  302.8 10.9 %all-to-all-start.12 = ((bf16[8,48,128]{2,0,1:T(8,128)(2,1)}), bf16[8,48,128]{2,0,1:T(8,128)(2,1)S(1)}, u32[]{:S(2)}, u32[]{:S(2)}) async-start(bf16[8,48,128]{2,0,1:T(8,128)(2,1)} %concatenate.31.clone), calls=%async_computation.12 | async-start | bytes 196608 | tf_op jit(solution)/shard_map/all_to_all | solution.py:137
  313.7 11.6 %all-to-all-start.10 = ((bf16[8,48,128]{2,0,1:T(8,128)(2,1)}), bf16[8,48,128]{2,0,1:T(8,128)(2,1)}, u32[]{:S(2)}, u32[]{:S(2)}) async-start(bf16[8,48,128]{2,0,1:T(8,128)(2,1)} %concatenate.29.clone), calls=%async_computation.10 | async-start | bytes 196608 | tf_op jit(solution)/shard_map/all_to_all | solution.py:140
  319.0 0.7 copy-start.1
  327.4 11.4 %all-to-all-start.13 = ((bf16[128,3,128]{2,1,0:T(4,128)(2,1)}), bf16[128,3,128]{2,1,0:T(4,128)(2,1)S(1)}, u32[]{:S(2)}, u32[]{:S(2)}) async-start(bf16[128,3,128]{2,1,0:T(4,128)(2,1)} %copy.138), calls=%async_computation.13 | async-start | bytes 262144 | tf_op jit(solution)/shard_map/all_to_all | solution.py:147
  338.8 12.1 %all-to-all-start.14 = ((bf16[128,3,128]{2,1,0:T(4,128)(2,1)}), bf16[128,3,128]{2,1,0:T(4,128)(2,1)}, u32[]{:S(2)}, u32[]{:S(2)}) async-start(bf16[128,3,128]{2,1,0:T(4,128)(2,1)} %copy.142), calls=%async_computation.14 | async-start | bytes 262144 | tf_op jit(solution)/shard_map/all_to_all | solution.py:148
  343.0 46.2 %all-gather.11.cloned.1.call-start = ((), (), s32[]{:S(2)}) async-start(), calls=%async_computation.19 | async-start | bytes 1392640 | tf_op jit(solution)/shard_map/all_gather | solution.py:158
Sparse Core Ops, SparseCore 0:
  15.9 45.7 all-gather.4
  157.4 36.5 all-gather.6
  213.9 40.5 all-gather.8
  352.6 36.4 all-gather.10
where the time goes:
time: 414 us; the launch traced here: 411 us
  waiting for transfers between devices  203 us (49%)
  starting transfers between devices  58.3 us (14%)
  local copies, waits for them, and re-layouts  39.1 us (9%)
  matrix products  38.4 us (9%)
  blocking collectives  37.2 us (9%)
  other arithmetic  19.5 us (5%)
  between operations  15.5 us (4%)
    all_gather x2, waiting for transfers between devices, per_device(): lax.all_gather(combined, 'queue', axis=0, tiled=True)  73.2 us
    all_gather x2, waiting for transfers between devices, per_device(): lax.all_gather(modulated, 'queue', axis=0, tiled=True)  59.1 us
    all_to_all x2, blocking collectives, per_device(): lax.all_to_all(out_columns.astype(jnp.bfloat16), 'queue', split_axis=0, c...  21.5 us
    all_to_all x1, blocking collectives, per_device(): lax.all_to_all(columns.astype(jnp.bfloat16), 'queue', split_axis=1, conca...  15.7 us
    all_to_all x2, waiting for transfers between devices, per_device(): lax.all_to_all(crossed_slots, 'queue', split_axis=0, concat_axis=1, tiled...  15.7 us
    dot_general x2, matrix products, per_device(): jnp.einsum('rd,cdw->crw', lax.all_gather(modulated, 'queue', axis=0, tile...  14.6 us
    all_to_all x1, waiting for transfers between devices, per_device(): lax.all_to_all(pad_slots(text_keys.reshape(text_local, HEADS, head_size),...  12.3 us
    all_to_all x2, waiting for transfers between devices, per_device(): lax.all_to_all(pad_slots(key_heads, slot_total), 'queue', split_axis=1, c...  10.4 us
  transfers between devices with their start and end apart: 19, of which 17 were waited for; matrix products, arithmetic and copies ran while one was open for 11% of the time, Pallas kernels for 0%

commit v1 on v0

--- a/solution.py
+++ b/solution.py
@@ -1,8 +1,11 @@
+import functools
 import math
 
 import jax
 import jax.numpy as jnp
 from jax import lax
+from jax.experimental import pallas as pl
+from jax.experimental.pallas import tpu as pltpu
 from jax.sharding import PartitionSpec as P
 
 HEADS = 40
@@ -166,6 +169,391 @@
     return queue_state
 
 
+def swapped(value, bit):
+    count = lax.axis_size("queue")
+    return lax.ppermute(value, "queue", [(source, source ^ bit) for source in range(count)])
+
+
+def gathered_over_chips(block):
+    chips = lax.axis_size("queue") // 2
+    blocks = {0: block}
+    bits = [1 << b for b in reversed(range(chips.bit_length() - 1))]
+    for bit in bits:
+        for mask in list(blocks):
+            blocks[mask | bit] = swapped(blocks[mask], 2 * bit)
+    return [blocks[mask] for mask in range(chips)]
+
+
+def contract_last(left, right):
+    return lax.dot_general(
+        left, right, (((1,), (1,)), ((), ())), preferred_element_type=jnp.float32
+    )
+
+
+VMEM_SPEC = pl.BlockSpec(memory_space=pltpu.VMEM)
+SMEM_SPEC = pl.BlockSpec(memory_space=pltpu.SMEM)
+ANY_SPEC = pl.BlockSpec(memory_space=pl.ANY)
+
+
+def kernel_params():
+    return pltpu.CompilerParams(vmem_limit_bytes=48 * 1024 * 1024)
+
+
+def project_kernel(
+    step, spans, place_ref, shift_ref, scale_ref, gain_ref, incoming_ref, *refs
+):
+    chips = spans // 2
+    mine, others = refs[:chips], refs[chips : 2 * chips]
+    refs = refs[2 * chips :]
+    weight_refs, refs = refs[:3], refs[3:]
+    own_ref, send_ref, squares_ref = refs[:3]
+    refs = refs[3:]
+    if step == 0:
+        current_ref, refs = refs[0], refs[1:]
+    state, modulated, held, sems = refs
+    chip, core = place_ref[0], place_ref[1]
+    tokens, width = state.shape
+    half = tokens // 2
+    rows = tokens // spans
+    pair = 2 * rows
+    cols = held.shape[1]
+    copies = [
+        pltpu.make_async_copy(weight_refs[i], held.at[i], sems.at[i]) for i in range(3)
+    ]
+    for copy in copies:
+        copy.start()
+    first = core == 0
+    for mask in range(chips):
+        other_chip = chip ^ mask
+        if step == 0:
+            at = pl.multiple_of(other_chip * pair, pair)
+            for low in range(0, width, width // 4):
+                part = pl.ds(low, width // 4)
+                a = mine[mask][:, part].astype(jnp.float32)
+                b = others[mask][:, part].astype(jnp.float32)
+                upper = jnp.where(first, b, a)
+                upper = jnp.where(
+                    other_chip == chips - 1, incoming_ref[:, part].astype(jnp.float32), upper
+                )
+                both = jnp.concatenate([jnp.where(first, a, b), upper], axis=0)
+                state[pl.ds(at, pair), part] = both.astype(jnp.bfloat16)
+        else:
+            lanes = pl.ds(pl.multiple_of(other_chip * 2 * cols, 2 * cols), 2 * cols)
+            state[pl.ds(pl.multiple_of(core * half, half), half), lanes] = mine[mask][...]
+            state[pl.ds(pl.multiple_of((1 - core) * half, half), half), lanes] = others[mask][...]
+    if step == 0:
+        lanes = pl.ds(pl.multiple_of(chip * 2 * cols, 2 * cols), 2 * cols)
+        current_ref[...] = state[pl.ds(pl.multiple_of(core * half, half), half), lanes]
+    pieces = 4
+    piece = width // pieces
+    for slab in range(chips):
+        band = slice(slab * pair, (slab + 1) * pair)
+        total = jnp.zeros((pair, 1), jnp.float32)
+        for low in range(0, width, piece):
+            x = state[band, low : low + piece].astype(jnp.float32)
+            total = total + jnp.sum(x * x, axis=1, keepdims=True)
+        factor = lax.rsqrt(total / width + 1e-06)
+        at = [(2 * slab + e + step + 1) % spans for e in range(2)]
+        for low in range(0, width, piece):
+            part = slice(low, low + piece)
+            x = state[band, part].astype(jnp.float32) * factor
+            scale, shift = (
+                jnp.concatenate(
+                    [jnp.broadcast_to(ref[s : s + 1, part], (rows, piece)) for s in at], axis=0
+                )
+                for ref in (scale_ref, shift_ref)
+            )
+            modulated[band, part] = (x * (1.0 + scale) + shift).astype(jnp.bfloat16)
+    ident = lax.broadcasted_iota(jnp.int32, (tokens, tokens), 0) == lax.broadcasted_iota(
+        jnp.int32, (tokens, tokens), 1
+    )
+    for i in range(3):
+        copies[i].wait()
+
+        def add(step_k, total):
+            part = pl.ds(pl.multiple_of(step_k * piece, piece), piece)
+            return total + contract_last(modulated[:, part], held[i, :, part])
+
+        product = lax.fori_loop(0, pieces, add, jnp.zeros((tokens, cols), jnp.float32))
+        if i < 2:
+            column = jnp.sum(product * product, axis=1, keepdims=True)
+            squares_ref[i : i + 1, :] = jnp.sum(
+                jnp.where(ident, column, 0.0), axis=0, keepdims=True
+            )
+            product = product * gain_ref[i : i + 1, :]
+        if i == 0:
+            low, high = product[:half], product[half:]
+            own_ref[:half, :] = jnp.where(first, low, high).astype(jnp.bfloat16)
+            send_ref[:half, :] = jnp.where(first, high, low).astype(jnp.bfloat16)
+        else:
+            band = slice(half + (i - 1) * tokens, half + i * tokens)
+            own_ref[band, :] = product.astype(jnp.bfloat16)
+            send_ref[band, :] = product.astype(jnp.bfloat16)
+
+
+def project(step, spans, place, shift, scale, gain, incoming, mine, others, weights):
+    tokens = spans * incoming.shape[0]
+    cols, width = weights[0].shape
+    half = tokens // 2
+    own = jax.ShapeDtypeStruct((half + 2 * tokens, cols), jnp.bfloat16)
+    out_shape = [own, own, jax.ShapeDtypeStruct((2, tokens), jnp.float32)]
+    if step == 0:
+        out_shape.append(jax.ShapeDtypeStruct((half, 2 * cols), jnp.bfloat16))
+    return pl.pallas_call(
+        functools.partial(project_kernel, step, spans),
+        out_shape=out_shape,
+        in_specs=[SMEM_SPEC] + [VMEM_SPEC] * (4 + len(mine) + len(others)) + [ANY_SPEC] * 3,
+        out_specs=[VMEM_SPEC] * len(out_shape),
+        scratch_shapes=[
+            pltpu.VMEM((tokens, width), jnp.bfloat16),
+            pltpu.VMEM((tokens, width), jnp.bfloat16),
+            pltpu.VMEM((3, cols, width), jnp.bfloat16),
+            pltpu.SemaphoreType.DMA((3,)),
+        ],
+        compiler_params=kernel_params(),
+        name="project",
+    )(place, shift, scale, gain, incoming, *mine, *others, *weights)
+
+
+def attend_kernel(step, spans, head_size, count, place_ref, own_ref, got_ref, text_ref, more_ref, *refs):
+    square_refs, (out_ref, queries, keys, values) = refs[:count], refs[count:]
+    core = place_ref[1]
+    first = core == 0
+    half, width = queries.shape
+    tokens = 2 * half
+    rows = tokens // spans
+    cols = width // 2
+    for target, low, size in (
+        (queries, 0, half),
+        (keys, half, tokens),
+        (values, half + tokens, tokens),
+    ):
+        mine = own_ref[low : low + size, :]
+        other = got_ref[low : low + size, :]
+        target[:, :cols] = jnp.where(first, mine, other)
+        target[:, cols:] = jnp.where(first, other, mine)
+    squares = square_refs[0][...]
+    for ref in square_refs[1:]:
+        squares = squares + ref[...]
+    factors = lax.rsqrt(squares / (width * (spans // 2)) + 1e-06)
+    ident = lax.broadcasted_iota(jnp.int32, (tokens, tokens), 0) == lax.broadcasted_iota(
+        jnp.int32, (tokens, tokens), 1
+    )
+    column = jnp.sum(jnp.where(ident, factors[0:1, :], 0.0), axis=1, keepdims=True)
+    column = jnp.where(first, column[:half], column[half:]) * (1.0 / math.sqrt(head_size))
+    row = factors[1:2, :]
+    shape = (half, tokens)
+    own_block = lax.broadcasted_iota(jnp.int32, shape, 0) // rows + core * (spans // 2)
+    key_block = lax.broadcasted_iota(jnp.int32, shape, 1) // rows
+    allowed = lax.rem(own_block + step + 1, spans) >= lax.rem(key_block + step + 1, spans)
+    text_rows = text_ref.shape[0] * text_ref.shape[2]
+    for head in range(width // head_size):
+        lanes = slice(head * head_size, (head + 1) * head_size)
+        q = queries[:, lanes]
+        scores = contract_last(q, keys[:, lanes]) * column * row
+        scores = jnp.where(allowed, scores, -1e30)
+        weights = jnp.exp(scores - jnp.max(scores, axis=1, keepdims=True))
+        weights = weights / jnp.sum(weights, axis=1, keepdims=True)
+        attended = jnp.dot(
+            weights.astype(jnp.bfloat16), values[:, lanes], preferred_element_type=jnp.float32
+        ).astype(jnp.bfloat16)
+        parts = []
+        for ref in (text_ref, more_ref):
+            text_keys = ref[:, 0, :, lanes].reshape(text_rows, head_size)
+            parts.append(contract_last(q, text_keys) * column)
+        most = jnp.maximum(
+            jnp.max(parts[0], axis=1, keepdims=True), jnp.max(parts[1], axis=1, keepdims=True)
+        )
+        parts = [jnp.exp(part - most) for part in parts]
+        total = jnp.sum(parts[0], axis=1, keepdims=True) + jnp.sum(parts[1], axis=1, keepdims=True)
+        crossed = jnp.zeros((half, head_size), jnp.float32)
+        for ref, part in zip((text_ref, more_ref), parts):
+            text_values = ref[:, 1, :, lanes].reshape(text_rows, head_size)
+            crossed = crossed + jnp.dot(
+                (part / total).astype(jnp.bfloat16), text_values, preferred_element_type=jnp.float32
+            )
+        crossed = crossed.astype(jnp.bfloat16)
+        out_ref[:, lanes] = (attended.astype(jnp.float32) + crossed.astype(jnp.float32)).astype(
+            jnp.bfloat16
+        )
+
+
+def attend(step, spans, head_size, place, own, got, text, more, squares):
+    cols = own.shape[1]
+    tokens = squares[0].shape[1]
+    half = tokens // 2
+    return pl.pallas_call(
+        functools.partial(attend_kernel, step, spans, head_size, len(squares)),
+        out_shape=jax.ShapeDtypeStruct((half, 2 * cols), jnp.bfloat16),
+        in_specs=[SMEM_SPEC] + [VMEM_SPEC] * (4 + len(squares)),
+        out_specs=VMEM_SPEC,
+        scratch_shapes=[
+            pltpu.VMEM((half, 2 * cols), jnp.bfloat16),
+            pltpu.VMEM((tokens, 2 * cols), jnp.bfloat16),
+            pltpu.VMEM((tokens, 2 * cols), jnp.bfloat16),
+        ],
+        compiler_params=kernel_params(),
+        name="attend",
+    )(place, own, got, text, more, *squares)
+
+
+def output_kernel(step, spans, last, place_ref, current_ref, gate_ref, incoming_ref, own_ref, other_ref, *refs):
+    chips = spans // 2
+    blocks, refs = refs[:chips], refs[chips:]
+    chip, core = place_ref[0], place_ref[1]
+    first = core == 0
+    half, width = current_ref.shape
+    cols = width // 2
+    rows = 2 * half // spans
+    mine = jnp.zeros((half, cols), jnp.float32)
+    other = jnp.zeros((half, cols), jnp.float32)
+    for mask in range(chips):
+        lanes = pl.ds(pl.multiple_of((chip ^ mask) * width, width), width)
+        block = blocks[mask][...]
+        mine = mine + contract_last(block, own_ref[:, lanes])
+        other = other + contract_last(block, other_ref[:, lanes])
+    totals = refs[-1]
+    totals[:, :cols] = jnp.where(first, mine, other)
+    totals[:, cols:] = jnp.where(first, other, mine)
+    for block in range(chips):
+        band = slice(block * rows, (block + 1) * rows)
+        places = [(block + e * chips + step + 1) % spans for e in range(2)]
+        gates = [gate_ref[s : s + 1, :] for s in places]
+        gate = jnp.where(first, gates[0], gates[1])
+        totals[band, :] = current_ref[band, :].astype(jnp.float32) + gate * totals[band, :]
+    if last:
+        for turn in range(chips):
+            at = pl.multiple_of((chip ^ turn) * rows, rows)
+            refs[turn][...] = totals[pl.ds(at, rows), :].astype(jnp.bfloat16)
+    else:
+        leaving = spans - 2 - step - chips
+        band = slice(leaving * rows, (leaving + 1) * rows)
+        lanes = pl.ds(pl.multiple_of(chip * width, width), width)
+        totals[band, :] = jnp.where(
+            first, totals[band, :], incoming_ref[:, lanes].astype(jnp.float32)
+        )
+        refs[0][...] = totals[...].astype(jnp.bfloat16)
+
+
+def output(step, spans, last, place, current, gate, incoming, own, other, blocks):
+    half, width = current.shape
+    chips = spans // 2
+    rows = 2 * half // spans
+    if last:
+        out_shape = [jax.ShapeDtypeStruct((rows, width), jnp.bfloat16)] * chips
+    else:
+        out_shape = [jax.ShapeDtypeStruct((half, width), jnp.bfloat16)]
+    return pl.pallas_call(
+        functools.partial(output_kernel, step, spans, last),
+        out_shape=out_shape,
+        in_specs=[SMEM_SPEC] + [VMEM_SPEC] * (5 + chips),
+        out_specs=[VMEM_SPEC] * len(out_shape),
+        scratch_shapes=[pltpu.VMEM((half, width), jnp.float32)],
+        compiler_params=kernel_params(),
+        name="output",
+    )(place, current, gate, incoming, own, other, *blocks)
+
+
+def join_kernel(place_ref, *refs):
+    out_ref = refs[-1]
+    for turn, ref in enumerate(refs[:-1]):
+        width = ref.shape[1]
+        lanes = pl.ds(pl.multiple_of((place_ref[2] ^ turn) * width, width), width)
+        out_ref[:, lanes] = ref[...]
+
+
+def join(place, blocks):
+    rows, width = blocks[0].shape
+    return pl.pallas_call(
+        join_kernel,
+        out_shape=jax.ShapeDtypeStruct((rows, width * len(blocks)), jnp.bfloat16),
+        in_specs=[SMEM_SPEC] + [VMEM_SPEC] * len(blocks),
+        out_specs=VMEM_SPEC,
+        compiler_params=kernel_params(),
+        name="join",
+    )(place, *blocks)
+
+
+def paired_device(
+    hidden,
+    incoming,
+    levels,
+    mod_table,
+    query_weight,
+    key_weight,
+    value_weight,
+    output_weight,
+    query_gain,
+    key_gain,
+    text_keys,
+    text_values,
+):
+    own_index = lax.axis_index("queue")
+    spans = lax.axis_size("queue")
+    chips = spans // 2
+    chip, core = own_index // 2, own_index % 2
+    rows, width = hidden.shape
+    cols = query_weight.shape[1]
+    head_size = width // HEADS
+    home = (own_index + spans - STEPS) % spans
+    place = jnp.stack([chip, core, home % chips]).astype(jnp.int32)
+    hidden_mine = gathered_over_chips(hidden)
+    hidden_others = [swapped(block, 1) for block in hidden_mine]
+    picked = (levels[:, None] == jnp.arange(mod_table.shape[0])[None, :]).astype(mod_table.dtype)
+    shift, scale, gate = jnp.einsum(
+        "sl,ltd->tsd", picked, mod_table, preferred_element_type=jnp.float32
+    )
+    gate = lax.dynamic_slice_in_dim(gate, chip * 2 * cols, 2 * cols, 1)
+    gain = lax.dynamic_slice_in_dim(jnp.stack([query_gain, key_gain]), own_index * cols, cols, 1)
+    weights = [w.T for w in (query_weight, key_weight, value_weight)]
+    output_own = output_weight.T
+    output_other = swapped(output_own, 1)
+    text_half = text_keys.shape[0] // 2
+    text = jnp.stack([text_keys, text_values]).reshape(2, 2, text_half, chips, 2 * cols)
+    text = text.transpose(3, 1, 0, 2, 4).reshape(spans, 2, text_half, 2 * cols)
+    text = lax.all_to_all(text, "queue", split_axis=0, concat_axis=0, tiled=True)
+    more = swapped(text, 1)
+    mine, others = hidden_mine, hidden_others
+    current = None
+    for step in range(STEPS):
+        own, send, squares, *rest = project(
+            step, spans, place, shift, scale, gain, incoming[step], mine, others, weights
+        )
+        if step == 0:
+            current = rest[0]
+        got = swapped(send, 1)
+        squares = gathered_over_chips(squares + swapped(squares, 1))
+        block = attend(step, spans, head_size, place, own, got, text, more, squares)
+        blocks = gathered_over_chips(block)
+        last = step == STEPS - 1
+        result = output(
+            step, spans, last, place, current, gate, incoming[min(step + 1, STEPS - 1)],
+            output_own, output_other, blocks,
+        )
+        if not last:
+            current = result[0]
+            mine = gathered_over_chips(current)
+            others = [swapped(block, 1) for block in mine]
+    rounds = []
+    for turn in range(chips):
+        pairs = []
+        for source in range(spans):
+            source_chip, source_core = source // 2, source % 2
+            ring = source_core * chips + (source_chip ^ turn)
+            pairs.append((source, (ring + STEPS) % spans))
+        rounds.append(lax.ppermute(result[turn], "queue", pairs))
+    return join(place, rounds)
+
+
+def held_in_pairs(mesh, hidden, query_weight):
+    spans = mesh.shape["queue"]
+    rows = hidden.shape[0] // (mesh.shape["groups"] * spans)
+    cols = query_weight.shape[1] // spans
+    head_size = query_weight.shape[0] // HEADS
+    power = spans & (spans - 1) == 0
+    return power and spans >= 4 and 2 * cols % head_size == 0 and rows * spans == 128 and rows == 8
+
+
 def solution(mesh):
     in_specs = (
         P(("groups", "queue"), None),
@@ -182,6 +570,11 @@
         P(("groups", "queue"), None),
     )
     out_specs = P(("groups", "queue"), None)
-    return jax.shard_map(
-        per_device, mesh=mesh, in_specs=in_specs, out_specs=out_specs, check_vma=False
-    )
+
+    def apply(*args):
+        body = paired_device if held_in_pairs(mesh, args[0], args[4]) else per_device
+        return jax.shard_map(
+            body, mesh=mesh, in_specs=in_specs, out_specs=out_specs, check_vma=False
+        )(*args)
+
+    return apply

time: 414 us -> 186 us (0.45)
  waiting for transfers between devices: 203 us -> 45.5 us
  matrix products: 38.4 us -> 0.55 us
  blocking collectives: 37.2 us -> 0 us
  Pallas kernels: 0 us -> 35.2 us
  starting transfers between devices: 58.3 us -> 87.4 us
  local copies, waits for them, and re-layouts: 39.1 us -> 14.4 us
  other arithmetic: 19.5 us -> 1.79 us
  between operations: 15.5 us -> 0.38 us
    all_gather x4 -> x0, waiting for transfers between devices: 132 us -> none  [the longest x2 73.2 us: per_device(): lax.all_gather(combined, 'queue', axis=0, tiled=True)]
    ppermute x2 -> x72, starting transfers between devices: 3.95 us -> 83.1 us  [the longest x64 59.5 us: swapped(): lax.ppermute(value, 'queue', [(source, source ^ bit) for source in range(...]
    all_to_all x13 -> x1, waiting for transfers between devices: 70 us -> 3.37 us  [paired_device(): lax.all_to_all(text, 'queue', split_axis=0, concat_axis=0, tiled=True)]
    all_to_all x13 -> x1, starting transfers between devices: 54.2 us -> 4.26 us  [paired_device(): lax.all_to_all(text, 'queue', split_axis=0, concat_axis=0, tiled=True)]
    ppermute x2 -> x72, waiting for transfers between devices: 0.9 us -> 42.2 us  [the longest x64 40.5 us: swapped(): lax.ppermute(value, 'queue', [(source, source ^ bit) for source in range(...]
    all_to_all x3 -> x0, blocking collectives: 37.2 us -> none  [the longest x2 21.5 us: per_device(): lax.all_to_all(out_columns.astype(jnp.bfloat16), 'queue', split_axis=0, c...]
    pallas_call x0 -> x7, Pallas kernels: none -> 35.2 us  [the longest x2 16.1 us: project(): pl.pallas_call(functools.partial(project_kernel, step, spans), out_shape=...]
    dot_general x12 -> x1, matrix products: 34.9 us -> 0.55 us  [paired_device(): jnp.einsum('sl,ltd->tsd', picked, mod_table, preferred_element_type=jnp.f...]
  transfers between devices with their start and end apart: 19 -> 73, of which waited for: 17 -> 34; matrix products, arithmetic and copies ran while one was open for 11% -> 4% of each run, Pallas kernels for 0% -> 7%
where the time goes in v1:
time: 186 us; the launch traced here: 185 us
  starting transfers between devices  87.4 us (47%)
  waiting for transfers between devices  45.5 us (24%)
  Pallas kernels  35.2 us (19%)
  local copies, waits for them, and re-layouts  14.4 us (8%)
    ppermute x64, starting transfers between devices, swapped(): lax.ppermute(value, 'queue', [(source, source ^ bit) for source in range(...  59.5 us
    ppermute x64, waiting for transfers between devices, swapped(): lax.ppermute(value, 'queue', [(source, source ^ bit) for source in range(...  40.5 us
    ppermute x8, starting transfers between devices, paired_device(): rounds.append(lax.ppermute(result[turn], 'queue', pairs))  23.6 us
    pallas_call x2, Pallas kernels, project(): pl.pallas_call(functools.partial(project_kernel, step, spans), out_shape=...  16.1 us
    unnamed x38, local copies, waits for them, and re-layouts  11.7 us
    pallas_call x2, Pallas kernels, attend(): pl.pallas_call(functools.partial(attend_kernel, step, spans, head_size, l...  9.6 us
    pallas_call x2, Pallas kernels, output(): pl.pallas_call(functools.partial(output_kernel, step, spans, last), out_s...  8.29 us
    all_to_all x1, starting transfers between devices, paired_device(): lax.all_to_all(text, 'queue', split_axis=0, concat_axis=0, tiled=True)  4.26 us
  transfers between devices with their start and end apart: 73, of which 34 were waited for; matrix products, arithmetic and copies ran while one was open for 4% of the time, Pallas kernels for 7%

profile of v1, /device:TPU:0, one launch (start us, length us, event | category | flops | bytes accessed | tf_op | source)
XLA Modules:
  0.0 185.2 jit_solution(10415126177244240250)
XLA Ops:
  0.0 4.0 %collective-permute-start.3 = (bf16[8,5120]{1,0:T(8,128)(2,1)}, bf16[8,5120]{1,0:T(8,128)(2,1)}, u32[]{:S(2)}, u32[]{:S(2)}) collective-permute-start(bf16[8,5120]{1,0:T(8,128)(2,1)} %refs_0_.1), channel_id=1, source_target_pairs={{0,8},{1,9},{2,10},{3,11},{4,12},{5,13},{6,14},{7,15},{8,0},{9,1},... | collective-permute-start | bytes 245768 | tf_op jit(solution)/shard_map/ppermute | solution.py:174
  4.0 1.6 collective-permute-start.1
  5.6 1.5 collective-permute-start
  10.2 4.3 %all-to-all-start = ((bf16[16,2,16,640]{3,2,1,0:T(8,128)(2,1)}), bf16[16,2,16,640]{3,2,1,0:T(8,128)(2,1)}, u32[]{:S(2)}, u32[]{:S(2)}) async-start(bf16[16,2,16,640]{3,2,1,0:T(8,128)(2,1)} %bitcast.43), calls=%async_computation | async-start | bytes 1310720 | tf_op jit(solution)/shard_map/all_to_all | solution.py:514
  15.7 1.8 collective-permute-start.5
  18.4 1.5 collective-permute-start.4
  21.4 1.7 collective-permute-start.2
  23.1 5.0 %collective-permute-done.5.refs_6_ = bf16[8,5120]{1,0:T(8,128)(2,1)} collective-permute-done((bf16[8,5120]{1,0:T(8,128)(2,1)}, bf16[8,5120]{1,0:T(8,128)(2,1)}, u32[]{:S(2)}, u32[]{:S(2)}) %collective-permute-start.5) | collective-permute-done | bytes 81952 | tf_op jit(solution)/shard_map/ppermute | solution.py:174
  28.1 3.4 %all-to-all-done.text_ref = bf16[16,2,16,640]{3,2,1,0:T(8,128)(2,1)} async-done(((bf16[16,2,16,640]{3,2,1,0:T(8,128)(2,1)}), bf16[16,2,16,640]{3,2,1,0:T(8,128)(2,1)}, u32[]{:S(2)}, u32[]{:S(2)}) %all-to-all-start) | async-done | bytes 655392 | tf_op jit(solution)/shard_map/all_to_all | solution.py:514
  33.1 1.0 collective-permute-start.6
  35.5 2.6 %collective-permute-done.6.refs_7_ = bf16[8,5120]{1,0:T(8,128)(2,1)S(1)} collective-permute-done((bf16[8,5120]{1,0:T(8,128)(2,1)}, bf16[8,5120]{1,0:T(8,128)(2,1)S(1)}, u32[]{:S(2)}, u32[]{:S(2)}) %collective-permute-start.6) | collective-permute-done | bytes 81952 | tf_op jit(solution)/shard_map/ppermute | solution.py:174
  38.2 1.2 collective-permute-done.14.refs_15_
  39.4 1.9 %copy-done.1 = bf16[5120,320]{0,1:T(8,128)(2,1)S(1)} copy-done((bf16[5120,320]{0,1:T(8,128)(2,1)S(1)}, bf16[5120,320]{0,1:T(8,128)(2,1)}, u32[]{:S(2)}) %copy-start.1) | copy-done | bytes 3276824
  45.0 8.3 %project.2 = (bf16[320,320]{1,0:T(8,128)(2,1)S(1)}, bf16[320,320]{1,0:T(8,128)(2,1)S(1)}, f32[2,128]{1,0:T(2,128)S(1)}, bf16[64,640]{1,0:T(8,128)(2,1)S(1)}) custom-call(s32[3]{0:T(128)S(1)} %pad_add_fusion.place_ref, f32[16,5120]{1,0:T(8,128)S(1)} %copy-done.5, f32[16,5120]{1,0:T(8,128)S(1)} %get-tuple-element.36.scale_ref, f32[2,320]{1,0:T(2,128)S(1)} %fusion.3.gain_ref, ...), custom_call_target="tpu_custom_call" | custom-call | tf_op jit(solution)/shard_map/project/pallas_call | solution.py:302
  54.9 2.5 %collective-permute-start.22 = (f32[2,128]{1,0:T(2,128)S(1)}, f32[2,128]{1,0:T(2,128)S(1)}, u32[]{:S(2)}, u32[]{:S(2)}) collective-permute-start(f32[2,128]{1,0:T(2,128)S(1)} %add.32.refs_0_), channel_id=1, source_target_pairs={{0,8},{1,9},{2,10},{3,11},{4,12},{5,13},{6,14},{7,15},{8,0},{9,1},... | collective-permute-start | bytes 3080 | tf_op jit(solution)/shard_map/ppermute | solution.py:174
  57.4 1.9 %collective-permute-done.22.refs_4_ = f32[2,128]{1,0:T(2,128)S(1)} collective-permute-done((f32[2,128]{1,0:T(2,128)S(1)}, f32[2,128]{1,0:T(2,128)S(1)}, u32[]{:S(2)}, u32[]{:S(2)}) %collective-permute-start.22) | collective-permute-done | bytes 1056 | tf_op jit(solution)/shard_map/ppermute | solution.py:174
  61.0 1.0 collective-permute-start.24
  65.0 1.5 collective-permute-done.23.refs_5_
  68.1 1.9 %collective-permute-done.25.refs_7_ = f32[2,128]{1,0:T(2,128)S(1)} collective-permute-done((f32[2,128]{1,0:T(2,128)S(1)}, f32[2,128]{1,0:T(2,128)S(1)}, u32[]{:S(2)}, u32[]{:S(2)}) %collective-permute-start.25) | collective-permute-done | bytes 1056 | tf_op jit(solution)/shard_map/ppermute | solution.py:174
  70.1 4.8 %attend.2.refs_0_ = bf16[64,640]{1,0:T(8,128)(2,1)S(1)} custom-call(s32[3]{0:T(128)S(1)} %pad_add_fusion.place_ref, bf16[320,320]{1,0:T(8,128)(2,1)S(1)} %get-tuple-element.21.own_ref, bf16[320,320]{1,0:T(8,128)(2,1)S(1)} %collective-permute-done.16.got_ref, bf16[16,2,16,640]{3,2,1,0:T(8,128)(2,1)} %all-to-all-done.text_ref, ...), custom_call_target="tpu_custom_call" | custom-call | tf_op jit(solution)/shard_map/attend/pallas_call | solution.py:385
  74.9 2.6 %collective-permute-start.29 = (bf16[64,640]{1,0:T(8,128)(2,1)S(1)}, bf16[64,640]{1,0:T(8,128)(2,1)S(1)}, u32[]{:S(2)}, u32[]{:S(2)}) collective-permute-start(bf16[64,640]{1,0:T(8,128)(2,1)S(1)} %attend.2.refs_0_), channel_id=1, source_target_pairs={{0,8},{1,9},{2,10},{3,11},{4,12},{5,13},{6,14},{7,15},{8,0},{9,1},... | collective-permute-start | bytes 245768 | tf_op jit(solution)/shard_map/ppermute | solution.py:174
  77.5 2.8 %collective-permute-done.29.refs_4_ = bf16[64,640]{1,0:T(8,128)(2,1)S(1)} collective-permute-done((bf16[64,640]{1,0:T(8,128)(2,1)S(1)}, bf16[64,640]{1,0:T(8,128)(2,1)S(1)}, u32[]{:S(2)}, u32[]{:S(2)}) %collective-permute-start.29) | collective-permute-done | bytes 81952 | tf_op jit(solution)/shard_map/ppermute | solution.py:174
  80.3 1.5 collective-permute-start.31
  81.8 1.1 collective-permute-start.26
  83.9 1.1 collective-permute-start.28
  87.4 1.1 collective-permute-done.28.refs_3_
  88.5 1.1 collective-permute-done.32.refs_7_
  89.7 1.9 %copy-done.3 = bf16[5120,320]{0,1:T(8,128)(2,1)S(1)} copy-done((bf16[5120,320]{0,1:T(8,128)(2,1)S(1)}, bf16[5120,320]{0,1:T(8,128)(2,1)}, u32[]{:S(2)}) %copy-start.3) | copy-done | bytes 3276824
  92.5 4.2 %output.2.refs_0_.current_ref = bf16[64,640]{1,0:T(8,128)(2,1)S(1)} custom-call(s32[3]{0:T(128)S(1)} %pad_add_fusion.place_ref, bf16[64,640]{1,0:T(8,128)(2,1)S(1)} %copy-done.15, f32[16,640]{1,0:T(8,128)S(1)} %dynamic-slice_bitcast_fusion.gate_ref, bf16[8,5120]{1,0:T(8,128)(2,1)S(1)} %get-tuple-element.38.incoming_ref, bf16[320,5120]{1,0:T(8,128)(2,1)S(1)} %bitcast.37, ...), custom_call_target="tpu_custom_call" | custom-call | tf_op jit(solution)/shard_map/output/pallas_call | solution.py:446
  96.7 2.5 %collective-permute-start.36 = (bf16[64,640]{1,0:T(8,128)(2,1)S(1)}, bf16[64,640]{1,0:T(8,128)(2,1)S(1)}, u32[]{:S(2)}, u32[]{:S(2)}) collective-permute-start(bf16[64,640]{1,0:T(8,128)(2,1)S(1)} %output.2.refs_0_.current_ref), channel_id=1, source_target_pairs={{0,8},{1,9},{2,10},{3,11},{4,12},{5,13},{6,14},{7,15},{8,0},{9,1},... | collective-permute-start | bytes 245768 | tf_op jit(solution)/shard_map/ppermute | solution.py:174
  99.7 2.0 %collective-permute-start.33 = (bf16[64,640]{1,0:T(8,128)(2,1)S(1)}, bf16[64,640]{1,0:T(8,128)(2,1)S(1)}, u32[]{:S(2)}, u32[]{:S(2)}) collective-permute-start(bf16[64,640]{1,0:T(8,128)(2,1)S(1)} %output.2.refs_0_.current_ref), channel_id=1, source_target_pairs={{0,2},{1,3},{2,0},{3,1},{4,6},{5,7},{6,4},{7,5},{8,10},{9,11},{10,... | collective-permute-start | bytes 245768 | tf_op jit(solution)/shard_map/ppermute | solution.py:174
  102.1 2.1 %collective-permute-start.38 = (bf16[64,640]{1,0:T(8,128)(2,1)S(1)}, bf16[64,640]{1,0:T(8,128)(2,1)S(1)}, u32[]{:S(2)}, u32[]{:S(2)}) collective-permute-start(bf16[64,640]{1,0:T(8,128)(2,1)S(1)} %collective-permute-done.36.refs_4_), channel_id=1, source_target_pairs={{0,4},{1,5},{2,6},{3,7},{4,0},{5,1},{6,2},{7,3},{8,12},{9,13},{10,... | collective-permute-start | bytes 245768 | tf_op jit(solution)/shard_map/ppermute | solution.py:174
  104.2 1.3 collective-permute-start.37
  106.6 1.3 collective-permute-start.39
  107.9 1.5 collective-permute-done.37.refs_5_
  110.0 1.2 collective-permute-done.35.refs_3_
  111.2 1.4 collective-permute-done.39.refs_7_
  112.6 1.2 collective-permute-done.47.refs_15_
  113.9 7.8 %project.3 = (bf16[320,320]{1,0:T(8,128)(2,1)S(1)}, bf16[320,320]{1,0:T(8,128)(2,1)S(1)}, f32[2,128]{1,0:T(2,128)S(1)}) custom-call(s32[3]{0:T(128)S(1)} %pad_add_fusion.place_ref, f32[16,5120]{1,0:T(8,128)S(1)} %copy-done.6, f32[16,5120]{1,0:T(8,128)S(1)} %get-tuple-element.36.scale_ref, f32[2,320]{1,0:T(2,128)S(1)} %fusion.3.gain_ref, ...), custom_call_target="tpu_custom_call" | custom-call | tf_op jit(solution)/shard_map/project/pallas_call | solution.py:302
  123.2 1.9 %collective-permute-start.53 = (f32[2,128]{1,0:T(2,128)S(1)}, f32[2,128]{1,0:T(2,128)S(1)}, u32[]{:S(2)}, u32[]{:S(2)}) collective-permute-start(f32[2,128]{1,0:T(2,128)S(1)} %add.33.refs_0_), channel_id=1, source_target_pairs={{0,8},{1,9},{2,10},{3,11},{4,12},{5,13},{6,14},{7,15},{8,0},{9,1},... | collective-permute-start | bytes 3080 | tf_op jit(solution)/shard_map/ppermute | solution.py:174
  125.1 1.3 collective-permute-start.51
  126.4 1.3 collective-permute-done.53.refs_4_
  128.2 1.3 collective-permute-start.50
  130.2 1.3 collective-permute-start.52
  131.5 1.0 collective-permute-start.56
  133.8 1.3 collective-permute-done.56.refs_7_
  135.1 4.8 %attend.3.refs_0_ = bf16[64,640]{1,0:T(8,128)(2,1)S(1)} custom-call(s32[3]{0:T(128)S(1)} %pad_add_fusion.place_ref, bf16[320,320]{1,0:T(8,128)(2,1)S(1)} %get-tuple-element.24.own_ref, bf16[320,320]{1,0:T(8,128)(2,1)S(1)} %collective-permute-done.48.got_ref, bf16[16,2,16,640]{3,2,1,0:T(8,128)(2,1)} %all-to-all-done.text_ref, ...), custom_call_target="tpu_custom_call" | custom-call | tf_op jit(solution)/shard_map/attend/pallas_call | solution.py:385
  139.9 2.5 %collective-permute-start.60 = (bf16[64,640]{1,0:T(8,128)(2,1)S(1)}, bf16[64,640]{1,0:T(8,128)(2,1)S(1)}, u32[]{:S(2)}, u32[]{:S(2)}) collective-permute-start(bf16[64,640]{1,0:T(8,128)(2,1)S(1)} %attend.3.refs_0_), channel_id=1, source_target_pairs={{0,8},{1,9},{2,10},{3,11},{4,12},{5,13},{6,14},{7,15},{8,0},{9,1},... | collective-permute-start | bytes 245768 | tf_op jit(solution)/shard_map/ppermute | solution.py:174
  142.3 1.5 collective-permute-start.58
  143.9 1.4 collective-permute-done.60.refs_4_
  145.3 2.0 %collective-permute-start.62 = (bf16[64,640]{1,0:T(8,128)(2,1)S(1)}, bf16[64,640]{1,0:T(8,128)(2,1)S(1)}, u32[]{:S(2)}, u32[]{:S(2)}) collective-permute-start(bf16[64,640]{1,0:T(8,128)(2,1)S(1)} %collective-permute-done.60.refs_4_), channel_id=1, source_target_pairs={{0,4},{1,5},{2,6},{3,7},{4,0},{5,1},{6,2},{7,3},{8,12},{9,13},{10,... | collective-permute-start | bytes 245768 | tf_op jit(solution)/shard_map/ppermute | solution.py:174
  148.1 1.2 collective-permute-start.61
  150.1 1.2 collective-permute-start.63
  152.6 1.2 collective-permute-done.59.refs_3_
  154.6 4.1 %output.3 = (bf16[8,640]{1,0:T(8,128)(2,1)S(1)}, bf16[8,640]{1,0:T(8,128)(2,1)S(1)}, bf16[8,640]{1,0:T(8,128)(2,1)S(1)}, bf16[8,640]{1,0:T(8,128)(2,1)S(1)}, bf1...) custom-call(s32[3]{0:T(128)S(1)} %pad_add_fusion.place_ref, ...), custom_call_target="tpu_custom_call" | custom-call | tf_op jit(solution)/shard_map/output/pallas_call | solution.py:446
  158.7 3.1 %collective-permute-start.64 = (bf16[8,640]{1,0:T(8,128)(2,1)S(1)}, bf16[8,640]{1,0:T(8,128)(2,1)S(1)}, u32[]{:S(2)}, u32[]{:S(2)}) collective-permute-start(bf16[8,640]{1,0:T(8,128)(2,1)S(1)} %get-tuple-element.27), channel_id=1, source_target_pairs={{0,2},{1,10},{2,3},{3,11},{4,4},{5,12},{6,5},{7,13},{8,6},{9,14},{... | collective-permute-start | bytes 30728 | tf_op jit(solution)/shard_map/ppermute | solution.py:544
  161.7 1.9 %collective-permute-start.65 = (bf16[8,640]{1,0:T(8,128)(2,1)S(1)}, bf16[8,640]{1,0:T(8,128)(2,1)S(1)}, u32[]{:S(2)}, u32[]{:S(2)}) collective-permute-start(bf16[8,640]{1,0:T(8,128)(2,1)S(1)} %get-tuple-element.28), channel_id=1, source_target_pairs={{0,3},{1,11},{2,2},{3,10},{4,5},{5,13},{6,4},{7,12},{8,7},{9,15},{... | collective-permute-start | bytes 30728 | tf_op jit(solution)/shard_map/ppermute | solution.py:544
  163.7 5.3 %collective-permute-start.66 = (bf16[8,640]{1,0:T(8,128)(2,1)S(1)}, bf16[8,640]{1,0:T(8,128)(2,1)S(1)}, u32[]{:S(2)}, u32[]{:S(2)}) collective-permute-start(bf16[8,640]{1,0:T(8,128)(2,1)S(1)} %get-tuple-element.29), channel_id=1, source_target_pairs={{0,4},{1,12},{2,5},{3,13},{4,2},{5,10},{6,3},{7,11},{8,8},{9,0},{1... | collective-permute-start | bytes 30728 | tf_op jit(solution)/shard_map/ppermute | solution.py:544
  169.0 4.4 %collective-permute-start.68 = (bf16[8,640]{1,0:T(8,128)(2,1)S(1)}, bf16[8,640]{1,0:T(8,128)(2,1)S(1)}, u32[]{:S(2)}, u32[]{:S(2)}) collective-permute-start(bf16[8,640]{1,0:T(8,128)(2,1)S(1)} %get-tuple-element.31), channel_id=1, source_target_pairs={{0,6},{1,14},{2,7},{3,15},{4,8},{5,0},{6,9},{7,1},{8,2},{9,10},{10... | collective-permute-start | bytes 30728 | tf_op jit(solution)/shard_map/ppermute | solution.py:544
  173.5 4.0 %collective-permute-start.69 = (bf16[8,640]{1,0:T(8,128)(2,1)S(1)}, bf16[8,640]{1,0:T(8,128)(2,1)S(1)}, u32[]{:S(2)}, u32[]{:S(2)}) collective-permute-start(bf16[8,640]{1,0:T(8,128)(2,1)S(1)} %get-tuple-element.32), channel_id=1, source_target_pairs={{0,7},{1,15},{2,6},{3,14},{4,9},{5,1},{6,8},{7,0},{8,3},{9,11},{10... | collective-permute-start | bytes 30728 | tf_op jit(solution)/shard_map/ppermute | solution.py:544
  177.4 1.6 collective-permute-start.70
  179.0 3.3 %collective-permute-start.71 = (bf16[8,640]{1,0:T(8,128)(2,1)S(1)}, bf16[8,640]{1,0:T(8,128)(2,1)S(1)}, u32[]{:S(2)}, u32[]{:S(2)}) collective-permute-start(bf16[8,640]{1,0:T(8,128)(2,1)S(1)} %get-tuple-element.34), channel_id=1, source_target_pairs={{0,9},{1,1},{2,8},{3,0},{4,7},{5,15},{6,6},{7,14},{8,5},{9,13},{10... | collective-permute-start | bytes 30728 | tf_op jit(solution)/shard_map/ppermute | solution.py:544
  182.4 1.6 collective-permute-done.71.refs_7_
  184.0 1.2 join.1
  (138 shorter events, 36.0 us)
Async XLA Ops:
  0.0 15.5 %collective-permute-start.3 = (bf16[8,5120]{1,0:T(8,128)(2,1)}, bf16[8,5120]{1,0:T(8,128)(2,1)}, u32[]{:S(2)}, u32[]{:S(2)}) collective-permute-start(bf16[8,5120]{1,0:T(8,128)(2,1)} %refs_0_.1), channel_id=1, source_target_pairs={{0,8},{1,9},{2,10},{3,11},{4,12},{5,13},{6,14},{7,15},{8,0},{9,1},... | collective-permute-start | bytes 245768 | tf_op jit(solution)/shard_map/ppermute | solution.py:174
  4.0 11.7 %collective-permute-start.1 = (bf16[8,5120]{1,0:T(8,128)(2,1)}, bf16[8,5120]{1,0:T(8,128)(2,1)}, u32[]{:S(2)}, u32[]{:S(2)}) collective-permute-start(bf16[8,5120]{1,0:T(8,128)(2,1)} %refs_0_.1), channel_id=1, source_target_pairs={{0,4},{1,5},{2,6},{3,7},{4,0},{5,1},{6,2},{7,3},{8,12},{9,13},{10,... | collective-permute-start | bytes 245768 | tf_op jit(solution)/shard_map/ppermute | solution.py:174
  5.6 12.8 %collective-permute-start = (bf16[8,5120]{1,0:T(8,128)(2,1)}, bf16[8,5120]{1,0:T(8,128)(2,1)S(1)}, u32[]{:S(2)}, u32[]{:S(2)}) collective-permute-start(bf16[8,5120]{1,0:T(8,128)(2,1)} %refs_0_.1), channel_id=1, source_target_pairs={{0,2},{1,3},{2,0},{3,1},{4,6},{5,7},{6,4},{7,5},{8,10},{9,11},{10,... | collective-permute-start | bytes 245768 | tf_op jit(solution)/shard_map/ppermute | solution.py:174
  7.1 12.7 %collective-permute-start.7 = (bf16[8,5120]{1,0:T(8,128)(2,1)}, bf16[8,5120]{1,0:T(8,128)(2,1)S(1)}, u32[]{:S(2)}, u32[]{:S(2)}) collective-permute-start(bf16[8,5120]{1,0:T(8,128)(2,1)} %refs_0_.1), channel_id=1, source_target_pairs={{0,1},{1,0},{2,3},{3,2},{4,5},{5,4},{6,7},{7,6},{8,9},{9,8},{10,11... | collective-permute-start | bytes 245768 | tf_op jit(solution)/shard_map/ppermute | solution.py:174
  10.2 21.2 %all-to-all-start = ((bf16[16,2,16,640]{3,2,1,0:T(8,128)(2,1)}), bf16[16,2,16,640]{3,2,1,0:T(8,128)(2,1)}, u32[]{:S(2)}, u32[]{:S(2)}) async-start(bf16[16,2,16,640]{3,2,1,0:T(8,128)(2,1)} %bitcast.43), calls=%async_computation | async-start | bytes 1310720 | tf_op jit(solution)/shard_map/all_to_all | solution.py:514
  14.5 75.1 %collective-permute-start.15 = (bf16[320,5120]{1,0:T(8,128)(2,1)}, bf16[320,5120]{1,0:T(8,128)(2,1)}, u32[]{:S(2)}, u32[]{:S(2)}) collective-permute-start(bf16[320,5120]{1,0:T(8,128)(2,1)} %bitcast.36), channel_id=1, source_target_pairs={{0,1},{1,0},{2,3},{3,2},{4,5},{5,4},{6,7},{7,6},{8,9},{9,8},{10,11... | collective-permute-start | bytes 9830408 | tf_op jit(solution)/shard_map/ppermute | solution.py:174
  15.5 5.2 %collective-permute-start.11 = (bf16[8,5120]{1,0:T(8,128)(2,1)}, bf16[8,5120]{1,0:T(8,128)(2,1)S(1)}, u32[]{:S(2)}, u32[]{:S(2)}) collective-permute-start(bf16[8,5120]{1,0:T(8,128)(2,1)} %collective-permute-done.3.refs_4_), channel_id=1, source_target_pairs={{0,1},{1,0},{2,3},{3,2},{4,5},{5,4},{6,7},{7,6},{8,9},{9,8},{10,11... | collective-permute-start | bytes 245768 | tf_op jit(solution)/shard_map/ppermute | solution.py:174
  15.7 12.4 %collective-permute-start.5 = (bf16[8,5120]{1,0:T(8,128)(2,1)}, bf16[8,5120]{1,0:T(8,128)(2,1)}, u32[]{:S(2)}, u32[]{:S(2)}) collective-permute-start(bf16[8,5120]{1,0:T(8,128)(2,1)} %collective-permute-done.3.refs_4_), channel_id=1, source_target_pairs={{0,4},{1,5},{2,6},{3,7},{4,0},{5,1},{6,2},{7,3},{8,12},{9,13},{10,... | collective-permute-start | bytes 245768 | tf_op jit(solution)/shard_map/ppermute | solution.py:174
  18.4 14.1 %collective-permute-start.4 = (bf16[8,5120]{1,0:T(8,128)(2,1)}, bf16[8,5120]{1,0:T(8,128)(2,1)}, u32[]{:S(2)}, u32[]{:S(2)}) collective-permute-start(bf16[8,5120]{1,0:T(8,128)(2,1)} %collective-permute-done.3.refs_4_), channel_id=1, source_target_pairs={{0,2},{1,3},{2,0},{3,1},{4,6},{5,7},{6,4},{7,5},{8,10},{9,11},{10,... | collective-permute-start | bytes 245768 | tf_op jit(solution)/shard_map/ppermute | solution.py:174
  20.5 12.5 %collective-permute-start.9 = (bf16[8,5120]{1,0:T(8,128)(2,1)}, bf16[8,5120]{1,0:T(8,128)(2,1)}, u32[]{:S(2)}, u32[]{:S(2)}) collective-permute-start(bf16[8,5120]{1,0:T(8,128)(2,1)} %collective-permute-done.1.refs_2_), channel_id=1, source_target_pairs={{0,1},{1,0},{2,3},{3,2},{4,5},{5,4},{6,7},{7,6},{8,9},{9,8},{10,11... | collective-permute-start | bytes 245768 | tf_op jit(solution)/shard_map/ppermute | solution.py:174
  21.4 11.7 %collective-permute-start.2 = (bf16[8,5120]{1,0:T(8,128)(2,1)}, bf16[8,5120]{1,0:T(8,128)(2,1)}, u32[]{:S(2)}, u32[]{:S(2)}) collective-permute-start(bf16[8,5120]{1,0:T(8,128)(2,1)} %collective-permute-done.1.refs_2_), channel_id=1, source_target_pairs={{0,2},{1,3},{2,0},{3,1},{4,6},{5,7},{6,4},{7,5},{8,10},{9,11},{10,... | collective-permute-start | bytes 245768 | tf_op jit(solution)/shard_map/ppermute | solution.py:174
  31.5 38.6 %collective-permute-start.17 = (bf16[16,2,16,640]{3,2,1,0:T(8,128)(2,1)}, bf16[16,2,16,640]{3,2,1,0:T(8,128)(2,1)}, u32[]{:S(2)}, u32[]{:S(2)}) collective-permute-start(bf16[16,2,16,640]{3,2,1,0:T(8,128)(2,1)} %all-to-all-done.text_ref), channel_id=1, source_target_pairs={{0,1},{1,0},{2,3},{3,2},{4,5},{5,4},{6,7},{7,6},{8,9},{9,8},{10,11... | collective-permute-start | bytes 1966088 | tf_op jit(solution)/shard_map/ppermute | solution.py:174
  33.1 5.0 %collective-permute-start.6 = (bf16[8,5120]{1,0:T(8,128)(2,1)}, bf16[8,5120]{1,0:T(8,128)(2,1)S(1)}, u32[]{:S(2)}, u32[]{:S(2)}) collective-permute-start(bf16[8,5120]{1,0:T(8,128)(2,1)} %collective-permute-done.5.refs_6_), channel_id=1, source_target_pairs={{0,2},{1,3},{2,0},{3,1},{4,6},{5,7},{6,4},{7,5},{8,10},{9,11},{10,... | collective-permute-start | bytes 245768 | tf_op jit(solution)/shard_map/ppermute | solution.py:174
  34.9 3.3 %collective-permute-start.12 = (bf16[8,5120]{1,0:T(8,128)(2,1)}, bf16[8,5120]{1,0:T(8,128)(2,1)S(1)}, u32[]{:S(2)}, u32[]{:S(2)}) collective-permute-start(bf16[8,5120]{1,0:T(8,128)(2,1)} %collective-permute-done.4.refs_5_), channel_id=1, source_target_pairs={{0,1},{1,0},{2,3},{3,2},{4,5},{5,4},{6,7},{7,6},{8,9},{9,8},{10,11... | collective-permute-start | bytes 245768 | tf_op jit(solution)/shard_map/ppermute | solution.py:174
  35.0 3.2 %collective-permute-start.10 = (bf16[8,5120]{1,0:T(8,128)(2,1)}, bf16[8,5120]{1,0:T(8,128)(2,1)S(1)}, u32[]{:S(2)}, u32[]{:S(2)}) collective-permute-start(bf16[8,5120]{1,0:T(8,128)(2,1)} %collective-permute-done.2.refs_3_), channel_id=1, source_target_pairs={{0,1},{1,0},{2,3},{3,2},{4,5},{5,4},{6,7},{7,6},{8,9},{9,8},{10,11... | collective-permute-start | bytes 245768 | tf_op jit(solution)/shard_map/ppermute | solution.py:174
  53.3 16.8 %collective-permute-start.16 = (bf16[320,320]{1,0:T(8,128)(2,1)S(1)}, bf16[320,320]{1,0:T(8,128)(2,1)S(1)}, u32[]{:S(2)}, u32[]{:S(2)}) collective-permute-start(bf16[320,320]{1,0:T(8,128)(2,1)S(1)} %get-tuple-element.22), channel_id=1, source_target_pairs={{0,1},{1,0},{2,3},{3,2},{4,5},{5,4},{6,7},{7,6},{8,9},{9,8},{10,11... | collective-permute-start | bytes 614408 | tf_op jit(solution)/shard_map/ppermute | solution.py:174
  54.9 4.5 %collective-permute-start.22 = (f32[2,128]{1,0:T(2,128)S(1)}, f32[2,128]{1,0:T(2,128)S(1)}, u32[]{:S(2)}, u32[]{:S(2)}) collective-permute-start(f32[2,128]{1,0:T(2,128)S(1)} %add.32.refs_0_), channel_id=1, source_target_pairs={{0,8},{1,9},{2,10},{3,11},{4,12},{5,13},{6,14},{7,15},{8,0},{9,1},... | collective-permute-start | bytes 3080 | tf_op jit(solution)/shard_map/ppermute | solution.py:174
  57.4 3.6 %collective-permute-start.20 = (f32[2,128]{1,0:T(2,128)S(1)}, f32[2,128]{1,0:T(2,128)S(1)}, u32[]{:S(2)}, u32[]{:S(2)}) collective-permute-start(f32[2,128]{1,0:T(2,128)S(1)} %add.32.refs_0_), channel_id=1, source_target_pairs={{0,4},{1,5},{2,6},{3,7},{4,0},{5,1},{6,2},{7,3},{8,12},{9,13},{10,... | collective-permute-start | bytes 3080 | tf_op jit(solution)/shard_map/ppermute | solution.py:174
  59.4 3.6 %collective-permute-start.19 = (f32[2,128]{1,0:T(2,128)S(1)}, f32[2,128]{1,0:T(2,128)S(1)}, u32[]{:S(2)}, u32[]{:S(2)}) collective-permute-start(f32[2,128]{1,0:T(2,128)S(1)} %add.32.refs_0_), channel_id=1, source_target_pairs={{0,2},{1,3},{2,0},{3,1},{4,6},{5,7},{6,4},{7,5},{8,10},{9,11},{10,... | collective-permute-start | bytes 3080 | tf_op jit(solution)/shard_map/ppermute | solution.py:174
  61.0 3.6 %collective-permute-start.24 = (f32[2,128]{1,0:T(2,128)S(1)}, f32[2,128]{1,0:T(2,128)S(1)}, u32[]{:S(2)}, u32[]{:S(2)}) collective-permute-start(f32[2,128]{1,0:T(2,128)S(1)} %collective-permute-done.22.refs_4_), channel_id=1, source_target_pairs={{0,4},{1,5},{2,6},{3,7},{4,0},{5,1},{6,2},{7,3},{8,12},{9,13},{10,... | collective-permute-start | bytes 3080 | tf_op jit(solution)/shard_map/ppermute | solution.py:174
  62.9 3.6 %collective-permute-start.23 = (f32[2,128]{1,0:T(2,128)S(1)}, f32[2,128]{1,0:T(2,128)S(1)}, u32[]{:S(2)}, u32[]{:S(2)}) collective-permute-start(f32[2,128]{1,0:T(2,128)S(1)} %collective-permute-done.22.refs_4_), channel_id=1, source_target_pairs={{0,2},{1,3},{2,0},{3,1},{4,6},{5,7},{6,4},{7,5},{8,10},{9,11},{10,... | collective-permute-start | bytes 3080 | tf_op jit(solution)/shard_map/ppermute | solution.py:174
  64.6 3.6 %collective-permute-start.21 = (f32[2,128]{1,0:T(2,128)S(1)}, f32[2,128]{1,0:T(2,128)S(1)}, u32[]{:S(2)}, u32[]{:S(2)}) collective-permute-start(f32[2,128]{1,0:T(2,128)S(1)} %collective-permute-done.20.refs_2_), channel_id=1, source_target_pairs={{0,2},{1,3},{2,0},{3,1},{4,6},{5,7},{6,4},{7,5},{8,10},{9,11},{10,... | collective-permute-start | bytes 3080 | tf_op jit(solution)/shard_map/ppermute | solution.py:174
  66.5 3.6 %collective-permute-start.25 = (f32[2,128]{1,0:T(2,128)S(1)}, f32[2,128]{1,0:T(2,128)S(1)}, u32[]{:S(2)}, u32[]{:S(2)}) collective-permute-start(f32[2,128]{1,0:T(2,128)S(1)} %collective-permute-done.24.refs_6_), channel_id=1, source_target_pairs={{0,2},{1,3},{2,0},{3,1},{4,6},{5,7},{6,4},{7,5},{8,10},{9,11},{10,... | collective-permute-start | bytes 3080 | tf_op jit(solution)/shard_map/ppermute | solution.py:174
  74.9 5.4 %collective-permute-start.29 = (bf16[64,640]{1,0:T(8,128)(2,1)S(1)}, bf16[64,640]{1,0:T(8,128)(2,1)S(1)}, u32[]{:S(2)}, u32[]{:S(2)}) collective-permute-start(bf16[64,640]{1,0:T(8,128)(2,1)S(1)} %attend.2.refs_0_), channel_id=1, source_target_pairs={{0,8},{1,9},{2,10},{3,11},{4,12},{5,13},{6,14},{7,15},{8,0},{9,1},... | collective-permute-start | bytes 245768 | tf_op jit(solution)/shard_map/ppermute | solution.py:174
  77.5 6.4 %collective-permute-start.27 = (bf16[64,640]{1,0:T(8,128)(2,1)S(1)}, bf16[64,640]{1,0:T(8,128)(2,1)}, u32[]{:S(2)}, u32[]{:S(2)}) collective-permute-start(bf16[64,640]{1,0:T(8,128)(2,1)S(1)} %attend.2.refs_0_), channel_id=1, source_target_pairs={{0,4},{1,5},{2,6},{3,7},{4,0},{5,1},{6,2},{7,3},{8,12},{9,13},{10,... | collective-permute-start | bytes 245768 | tf_op jit(solution)/shard_map/ppermute | solution.py:174
  80.3 4.7 %collective-permute-start.31 = (bf16[64,640]{1,0:T(8,128)(2,1)S(1)}, bf16[64,640]{1,0:T(8,128)(2,1)}, u32[]{:S(2)}, u32[]{:S(2)}) collective-permute-start(bf16[64,640]{1,0:T(8,128)(2,1)S(1)} %collective-permute-done.29.refs_4_), channel_id=1, source_target_pairs={{0,4},{1,5},{2,6},{3,7},{4,0},{5,1},{6,2},{7,3},{8,12},{9,13},{10,... | collective-permute-start | bytes 245768 | tf_op jit(solution)/shard_map/ppermute | solution.py:174
  81.8 4.8 %collective-permute-start.26 = (bf16[64,640]{1,0:T(8,128)(2,1)S(1)}, bf16[64,640]{1,0:T(8,128)(2,1)S(1)}, u32[]{:S(2)}, u32[]{:S(2)}) collective-permute-start(bf16[64,640]{1,0:T(8,128)(2,1)S(1)} %attend.2.refs_0_), channel_id=1, source_target_pairs={{0,2},{1,3},{2,0},{3,1},{4,6},{5,7},{6,4},{7,5},{8,10},{9,11},{10,... | collective-permute-start | bytes 245768 | tf_op jit(solution)/shard_map/ppermute | solution.py:174
  83.0 4.4 %collective-permute-start.30 = (bf16[64,640]{1,0:T(8,128)(2,1)S(1)}, bf16[64,640]{1,0:T(8,128)(2,1)S(1)}, u32[]{:S(2)}, u32[]{:S(2)}) collective-permute-start(bf16[64,640]{1,0:T(8,128)(2,1)S(1)} %collective-permute-done.29.refs_4_), channel_id=1, source_target_pairs={{0,2},{1,3},{2,0},{3,1},{4,6},{5,7},{6,4},{7,5},{8,10},{9,11},{10,... | collective-permute-start | bytes 245768 | tf_op jit(solution)/shard_map/ppermute | solution.py:174
  83.9 4.7 %collective-permute-start.28 = (bf16[64,640]{1,0:T(8,128)(2,1)}, bf16[64,640]{1,0:T(8,128)(2,1)S(1)}, u32[]{:S(2)}, u32[]{:S(2)}) collective-permute-start(bf16[64,640]{1,0:T(8,128)(2,1)} %collective-permute-done.27.refs_2_), channel_id=1, source_target_pairs={{0,2},{1,3},{2,0},{3,1},{4,6},{5,7},{6,4},{7,5},{8,10},{9,11},{10,... | collective-permute-start | bytes 245768 | tf_op jit(solution)/shard_map/ppermute | solution.py:174
  85.0 4.7 %collective-permute-start.32 = (bf16[64,640]{1,0:T(8,128)(2,1)}, bf16[64,640]{1,0:T(8,128)(2,1)S(1)}, u32[]{:S(2)}, u32[]{:S(2)}) collective-permute-start(bf16[64,640]{1,0:T(8,128)(2,1)} %collective-permute-done.31.refs_6_), channel_id=1, source_target_pairs={{0,2},{1,3},{2,0},{3,1},{4,6},{5,7},{6,4},{7,5},{8,10},{9,11},{10,... | collective-permute-start | bytes 245768 | tf_op jit(solution)/shard_map/ppermute | solution.py:174
  96.7 5.4 %collective-permute-start.36 = (bf16[64,640]{1,0:T(8,128)(2,1)S(1)}, bf16[64,640]{1,0:T(8,128)(2,1)S(1)}, u32[]{:S(2)}, u32[]{:S(2)}) collective-permute-start(bf16[64,640]{1,0:T(8,128)(2,1)S(1)} %output.2.refs_0_.current_ref), channel_id=1, source_target_pairs={{0,8},{1,9},{2,10},{3,11},{4,12},{5,13},{6,14},{7,15},{8,0},{9,1},... | collective-permute-start | bytes 245768 | tf_op jit(solution)/shard_map/ppermute | solution.py:174
  99.2 5.0 %collective-permute-start.40 = (bf16[64,640]{1,0:T(8,128)(2,1)S(1)}, bf16[64,640]{1,0:T(8,128)(2,1)S(1)}, u32[]{:S(2)}, u32[]{:S(2)}) collective-permute-start(bf16[64,640]{1,0:T(8,128)(2,1)S(1)} %output.2.refs_0_.current_ref), channel_id=1, source_target_pairs={{0,1},{1,0},{2,3},{3,2},{4,5},{5,4},{6,7},{7,6},{8,9},{9,8},{10,11... | collective-permute-start | bytes 245768 | tf_op jit(solution)/shard_map/ppermute | solution.py:174
  99.2 6.3 %collective-permute-start.34 = (bf16[64,640]{1,0:T(8,128)(2,1)S(1)}, bf16[64,640]{1,0:T(8,128)(2,1)S(1)}, u32[]{:S(2)}, u32[]{:S(2)}) collective-permute-start(bf16[64,640]{1,0:T(8,128)(2,1)S(1)} %output.2.refs_0_.current_ref), channel_id=1, source_target_pairs={{0,4},{1,5},{2,6},{3,7},{4,0},{5,1},{6,2},{7,3},{8,12},{9,13},{10,... | collective-permute-start | bytes 245768 | tf_op jit(solution)/shard_map/ppermute | solution.py:174
  99.7 6.0 %collective-permute-start.33 = (bf16[64,640]{1,0:T(8,128)(2,1)S(1)}, bf16[64,640]{1,0:T(8,128)(2,1)S(1)}, u32[]{:S(2)}, u32[]{:S(2)}) collective-permute-start(bf16[64,640]{1,0:T(8,128)(2,1)S(1)} %output.2.refs_0_.current_ref), channel_id=1, source_target_pairs={{0,2},{1,3},{2,0},{3,1},{4,6},{5,7},{6,4},{7,5},{8,10},{9,11},{10,... | collective-permute-start | bytes 245768 | tf_op jit(solution)/shard_map/ppermute | solution.py:174
  102.1 4.5 %collective-permute-start.38 = (bf16[64,640]{1,0:T(8,128)(2,1)S(1)}, bf16[64,640]{1,0:T(8,128)(2,1)S(1)}, u32[]{:S(2)}, u32[]{:S(2)}) collective-permute-start(bf16[64,640]{1,0:T(8,128)(2,1)S(1)} %collective-permute-done.36.refs_4_), channel_id=1, source_target_pairs={{0,4},{1,5},{2,6},{3,7},{4,0},{5,1},{6,2},{7,3},{8,12},{9,13},{10,... | collective-permute-start | bytes 245768 | tf_op jit(solution)/shard_map/ppermute | solution.py:174
  104.2 3.7 %collective-permute-start.44 = (bf16[64,640]{1,0:T(8,128)(2,1)S(1)}, bf16[64,640]{1,0:T(8,128)(2,1)S(1)}, u32[]{:S(2)}, u32[]{:S(2)}) collective-permute-start(bf16[64,640]{1,0:T(8,128)(2,1)S(1)} %collective-permute-done.36.refs_4_), channel_id=1, source_target_pairs={{0,1},{1,0},{2,3},{3,2},{4,5},{5,4},{6,7},{7,6},{8,9},{9,8},{10,11... | collective-permute-start | bytes 245768 | tf_op jit(solution)/shard_map/ppermute | solution.py:174
  104.2 5.2 %collective-permute-start.37 = (bf16[64,640]{1,0:T(8,128)(2,1)S(1)}, bf16[64,640]{1,0:T(8,128)(2,1)S(1)}, u32[]{:S(2)}, u32[]{:S(2)}) collective-permute-start(bf16[64,640]{1,0:T(8,128)(2,1)S(1)} %collective-permute-done.36.refs_4_), channel_id=1, source_target_pairs={{0,2},{1,3},{2,0},{3,1},{4,6},{5,7},{6,4},{7,5},{8,10},{9,11},{10,... | collective-permute-start | bytes 245768 | tf_op jit(solution)/shard_map/ppermute | solution.py:174
  105.5 4.0 %collective-permute-start.42 = (bf16[64,640]{1,0:T(8,128)(2,1)S(1)}, bf16[64,640]{1,0:T(8,128)(2,1)S(1)}, u32[]{:S(2)}, u32[]{:S(2)}) collective-permute-start(bf16[64,640]{1,0:T(8,128)(2,1)S(1)} %collective-permute-done.34.refs_2_), channel_id=1, source_target_pairs={{0,1},{1,0},{2,3},{3,2},{4,5},{5,4},{6,7},{7,6},{8,9},{9,8},{10,11... | collective-permute-start | bytes 245768 | tf_op jit(solution)/shard_map/ppermute | solution.py:174
  105.7 5.5 %collective-permute-start.35 = (bf16[64,640]{1,0:T(8,128)(2,1)S(1)}, bf16[64,640]{1,0:T(8,128)(2,1)S(1)}, u32[]{:S(2)}, u32[]{:S(2)}) collective-permute-start(bf16[64,640]{1,0:T(8,128)(2,1)S(1)} %collective-permute-done.34.refs_2_), channel_id=1, source_target_pairs={{0,2},{1,3},{2,0},{3,1},{4,6},{5,7},{6,4},{7,5},{8,10},{9,11},{10,... | collective-permute-start | bytes 245768 | tf_op jit(solution)/shard_map/ppermute | solution.py:174
  106.6 6.0 %collective-permute-start.39 = (bf16[64,640]{1,0:T(8,128)(2,1)S(1)}, bf16[64,640]{1,0:T(8,128)(2,1)S(1)}, u32[]{:S(2)}, u32[]{:S(2)}) collective-permute-start(bf16[64,640]{1,0:T(8,128)(2,1)S(1)} %collective-permute-done.38.refs_6_), channel_id=1, source_target_pairs={{0,2},{1,3},{2,0},{3,1},{4,6},{5,7},{6,4},{7,5},{8,10},{9,11},{10,... | collective-permute-start | bytes 245768 | tf_op jit(solution)/shard_map/ppermute | solution.py:174
  107.9 4.7 %collective-permute-start.41 = (bf16[64,640]{1,0:T(8,128)(2,1)S(1)}, bf16[64,640]{1,0:T(8,128)(2,1)S(1)}, u32[]{:S(2)}, u32[]{:S(2)}) collective-permute-start(bf16[64,640]{1,0:T(8,128)(2,1)S(1)} %collective-permute-done.33.refs_1_), channel_id=1, source_target_pairs={{0,1},{1,0},{2,3},{3,2},{4,5},{5,4},{6,7},{7,6},{8,9},{9,8},{10,11... | collective-permute-start | bytes 245768 | tf_op jit(solution)/shard_map/ppermute | solution.py:174
  121.6 13.4 %collective-permute-start.48 = (bf16[320,320]{1,0:T(8,128)(2,1)S(1)}, bf16[320,320]{1,0:T(8,128)(2,1)S(1)}, u32[]{:S(2)}, u32[]{:S(2)}) collective-permute-start(bf16[320,320]{1,0:T(8,128)(2,1)S(1)} %get-tuple-element.25), channel_id=1, source_target_pairs={{0,1},{1,0},{2,3},{3,2},{4,5},{5,4},{6,7},{7,6},{8,9},{9,8},{10,11... | collective-permute-start | bytes 614408 | tf_op jit(solution)/shard_map/ppermute | solution.py:174
  123.2 4.5 %collective-permute-start.53 = (f32[2,128]{1,0:T(2,128)S(1)}, f32[2,128]{1,0:T(2,128)S(1)}, u32[]{:S(2)}, u32[]{:S(2)}) collective-permute-start(f32[2,128]{1,0:T(2,128)S(1)} %add.33.refs_0_), channel_id=1, source_target_pairs={{0,8},{1,9},{2,10},{3,11},{4,12},{5,13},{6,14},{7,15},{8,0},{9,1},... | collective-permute-start | bytes 3080 | tf_op jit(solution)/shard_map/ppermute | solution.py:174
  125.1 5.1 %collective-permute-start.51 = (f32[2,128]{1,0:T(2,128)S(1)}, f32[2,128]{1,0:T(2,128)S(1)}, u32[]{:S(2)}, u32[]{:S(2)}) collective-permute-start(f32[2,128]{1,0:T(2,128)S(1)} %add.33.refs_0_), channel_id=1, source_target_pairs={{0,4},{1,5},{2,6},{3,7},{4,0},{5,1},{6,2},{7,3},{8,12},{9,13},{10,... | collective-permute-start | bytes 3080 | tf_op jit(solution)/shard_map/ppermute | solution.py:174
  127.7 3.8 %collective-permute-start.55 = (f32[2,128]{1,0:T(2,128)S(1)}, f32[2,128]{1,0:T(2,128)S(1)}, u32[]{:S(2)}, u32[]{:S(2)}) collective-permute-start(f32[2,128]{1,0:T(2,128)S(1)} %collective-permute-done.53.refs_4_), channel_id=1, source_target_pairs={{0,4},{1,5},{2,6},{3,7},{4,0},{5,1},{6,2},{7,3},{8,12},{9,13},{10,... | collective-permute-start | bytes 3080 | tf_op jit(solution)/shard_map/ppermute | solution.py:174
  128.2 4.3 %collective-permute-start.50 = (f32[2,128]{1,0:T(2,128)S(1)}, f32[2,128]{1,0:T(2,128)S(1)}, u32[]{:S(2)}, u32[]{:S(2)}) collective-permute-start(f32[2,128]{1,0:T(2,128)S(1)} %add.33.refs_0_), channel_id=1, source_target_pairs={{0,2},{1,3},{2,0},{3,1},{4,6},{5,7},{6,4},{7,5},{8,10},{9,11},{10,... | collective-permute-start | bytes 3080 | tf_op jit(solution)/shard_map/ppermute | solution.py:174
  129.5 3.6 %collective-permute-start.54 = (f32[2,128]{1,0:T(2,128)S(1)}, f32[2,128]{1,0:T(2,128)S(1)}, u32[]{:S(2)}, u32[]{:S(2)}) collective-permute-start(f32[2,128]{1,0:T(2,128)S(1)} %collective-permute-done.53.refs_4_), channel_id=1, source_target_pairs={{0,2},{1,3},{2,0},{3,1},{4,6},{5,7},{6,4},{7,5},{8,10},{9,11},{10,... | collective-permute-start | bytes 3080 | tf_op jit(solution)/shard_map/ppermute | solution.py:174
  130.2 3.6 %collective-permute-start.52 = (f32[2,128]{1,0:T(2,128)S(1)}, f32[2,128]{1,0:T(2,128)S(1)}, u32[]{:S(2)}, u32[]{:S(2)}) collective-permute-start(f32[2,128]{1,0:T(2,128)S(1)} %collective-permute-done.51.refs_2_), channel_id=1, source_target_pairs={{0,2},{1,3},{2,0},{3,1},{4,6},{5,7},{6,4},{7,5},{8,10},{9,11},{10,... | collective-permute-start | bytes 3080 | tf_op jit(solution)/shard_map/ppermute | solution.py:174
  131.5 3.6 %collective-permute-start.56 = (f32[2,128]{1,0:T(2,128)S(1)}, f32[2,128]{1,0:T(2,128)S(1)}, u32[]{:S(2)}, u32[]{:S(2)}) collective-permute-start(f32[2,128]{1,0:T(2,128)S(1)} %collective-permute-done.55.refs_6_), channel_id=1, source_target_pairs={{0,2},{1,3},{2,0},{3,1},{4,6},{5,7},{6,4},{7,5},{8,10},{9,11},{10,... | collective-permute-start | bytes 3080 | tf_op jit(solution)/shard_map/ppermute | solution.py:174
  139.9 5.4 %collective-permute-start.60 = (bf16[64,640]{1,0:T(8,128)(2,1)S(1)}, bf16[64,640]{1,0:T(8,128)(2,1)S(1)}, u32[]{:S(2)}, u32[]{:S(2)}) collective-permute-start(bf16[64,640]{1,0:T(8,128)(2,1)S(1)} %attend.3.refs_0_), channel_id=1, source_target_pairs={{0,8},{1,9},{2,10},{3,11},{4,12},{5,13},{6,14},{7,15},{8,0},{9,1},... | collective-permute-start | bytes 245768 | tf_op jit(solution)/shard_map/ppermute | solution.py:174
  142.3 6.9 %collective-permute-start.58 = (bf16[64,640]{1,0:T(8,128)(2,1)S(1)}, bf16[64,640]{1,0:T(8,128)(2,1)S(1)}, u32[]{:S(2)}, u32[]{:S(2)}) collective-permute-start(bf16[64,640]{1,0:T(8,128)(2,1)S(1)} %attend.3.refs_0_), channel_id=1, source_target_pairs={{0,4},{1,5},{2,6},{3,7},{4,0},{5,1},{6,2},{7,3},{8,12},{9,13},{10,... | collective-permute-start | bytes 245768 | tf_op jit(solution)/shard_map/ppermute | solution.py:174
  145.3 4.8 %collective-permute-start.62 = (bf16[64,640]{1,0:T(8,128)(2,1)S(1)}, bf16[64,640]{1,0:T(8,128)(2,1)S(1)}, u32[]{:S(2)}, u32[]{:S(2)}) collective-permute-start(bf16[64,640]{1,0:T(8,128)(2,1)S(1)} %collective-permute-done.60.refs_4_), channel_id=1, source_target_pairs={{0,4},{1,5},{2,6},{3,7},{4,0},{5,1},{6,2},{7,3},{8,12},{9,13},{10,... | collective-permute-start | bytes 245768 | tf_op jit(solution)/shard_map/ppermute | solution.py:174
  147.2 4.4 %collective-permute-start.57 = (bf16[64,640]{1,0:T(8,128)(2,1)S(1)}, bf16[64,640]{1,0:T(8,128)(2,1)S(1)}, u32[]{:S(2)}, u32[]{:S(2)}) collective-permute-start(bf16[64,640]{1,0:T(8,128)(2,1)S(1)} %attend.3.refs_0_), channel_id=1, source_target_pairs={{0,2},{1,3},{2,0},{3,1},{4,6},{5,7},{6,4},{7,5},{8,10},{9,11},{10,... | collective-permute-start | bytes 245768 | tf_op jit(solution)/shard_map/ppermute | solution.py:174
  148.1 4.5 %collective-permute-start.61 = (bf16[64,640]{1,0:T(8,128)(2,1)S(1)}, bf16[64,640]{1,0:T(8,128)(2,1)S(1)}, u32[]{:S(2)}, u32[]{:S(2)}) collective-permute-start(bf16[64,640]{1,0:T(8,128)(2,1)S(1)} %collective-permute-done.60.refs_4_), channel_id=1, source_target_pairs={{0,2},{1,3},{2,0},{3,1},{4,6},{5,7},{6,4},{7,5},{8,10},{9,11},{10,... | collective-permute-start | bytes 245768 | tf_op jit(solution)/shard_map/ppermute | solution.py:174
  149.3 4.4 %collective-permute-start.59 = (bf16[64,640]{1,0:T(8,128)(2,1)S(1)}, bf16[64,640]{1,0:T(8,128)(2,1)S(1)}, u32[]{:S(2)}, u32[]{:S(2)}) collective-permute-start(bf16[64,640]{1,0:T(8,128)(2,1)S(1)} %collective-permute-done.58.refs_2_), channel_id=1, source_target_pairs={{0,2},{1,3},{2,0},{3,1},{4,6},{5,7},{6,4},{7,5},{8,10},{9,11},{10,... | collective-permute-start | bytes 245768 | tf_op jit(solution)/shard_map/ppermute | solution.py:174
  150.1 4.5 %collective-permute-start.63 = (bf16[64,640]{1,0:T(8,128)(2,1)S(1)}, bf16[64,640]{1,0:T(8,128)(2,1)S(1)}, u32[]{:S(2)}, u32[]{:S(2)}) collective-permute-start(bf16[64,640]{1,0:T(8,128)(2,1)S(1)} %collective-permute-done.62.refs_6_), channel_id=1, source_target_pairs={{0,2},{1,3},{2,0},{3,1},{4,6},{5,7},{6,4},{7,5},{8,10},{9,11},{10,... | collective-permute-start | bytes 245768 | tf_op jit(solution)/shard_map/ppermute | solution.py:174
  158.7 14.8 %collective-permute-start.64 = (bf16[8,640]{1,0:T(8,128)(2,1)S(1)}, bf16[8,640]{1,0:T(8,128)(2,1)S(1)}, u32[]{:S(2)}, u32[]{:S(2)}) collective-permute-start(bf16[8,640]{1,0:T(8,128)(2,1)S(1)} %get-tuple-element.27), channel_id=1, source_target_pairs={{0,2},{1,10},{2,3},{3,11},{4,4},{5,12},{6,5},{7,13},{8,6},{9,14},{... | collective-permute-start | bytes 30728 | tf_op jit(solution)/shard_map/ppermute | solution.py:544
  161.7 15.7 %collective-permute-start.65 = (bf16[8,640]{1,0:T(8,128)(2,1)S(1)}, bf16[8,640]{1,0:T(8,128)(2,1)S(1)}, u32[]{:S(2)}, u32[]{:S(2)}) collective-permute-start(bf16[8,640]{1,0:T(8,128)(2,1)S(1)} %get-tuple-element.28), channel_id=1, source_target_pairs={{0,3},{1,11},{2,2},{3,10},{4,5},{5,13},{6,4},{7,12},{8,7},{9,15},{... | collective-permute-start | bytes 30728 | tf_op jit(solution)/shard_map/ppermute | solution.py:544
  163.7 15.4 %collective-permute-start.66 = (bf16[8,640]{1,0:T(8,128)(2,1)S(1)}, bf16[8,640]{1,0:T(8,128)(2,1)S(1)}, u32[]{:S(2)}, u32[]{:S(2)}) collective-permute-start(bf16[8,640]{1,0:T(8,128)(2,1)S(1)} %get-tuple-element.29), channel_id=1, source_target_pairs={{0,4},{1,12},{2,5},{3,13},{4,2},{5,10},{6,3},{7,11},{8,8},{9,0},{1... | collective-permute-start | bytes 30728 | tf_op jit(solution)/shard_map/ppermute | solution.py:544
  168.9 13.4 %collective-permute-start.67 = (bf16[8,640]{1,0:T(8,128)(2,1)S(1)}, bf16[8,640]{1,0:T(8,128)(2,1)S(1)}, u32[]{:S(2)}, u32[]{:S(2)}) collective-permute-start(bf16[8,640]{1,0:T(8,128)(2,1)S(1)} %get-tuple-element.30), channel_id=1, source_target_pairs={{0,5},{1,13},{2,4},{3,12},{4,3},{5,11},{6,2},{7,10},{8,9},{9,1},{1... | collective-permute-start | bytes 30728 | tf_op jit(solution)/shard_map/ppermute | solution.py:544
  169.0 13.3 %collective-permute-start.68 = (bf16[8,640]{1,0:T(8,128)(2,1)S(1)}, bf16[8,640]{1,0:T(8,128)(2,1)S(1)}, u32[]{:S(2)}, u32[]{:S(2)}) collective-permute-start(bf16[8,640]{1,0:T(8,128)(2,1)S(1)} %get-tuple-element.31), channel_id=1, source_target_pairs={{0,6},{1,14},{2,7},{3,15},{4,8},{5,0},{6,9},{7,1},{8,2},{9,10},{10... | collective-permute-start | bytes 30728 | tf_op jit(solution)/shard_map/ppermute | solution.py:544
  173.5 8.9 %collective-permute-start.69 = (bf16[8,640]{1,0:T(8,128)(2,1)S(1)}, bf16[8,640]{1,0:T(8,128)(2,1)S(1)}, u32[]{:S(2)}, u32[]{:S(2)}) collective-permute-start(bf16[8,640]{1,0:T(8,128)(2,1)S(1)} %get-tuple-element.32), channel_id=1, source_target_pairs={{0,7},{1,15},{2,6},{3,14},{4,9},{5,1},{6,8},{7,0},{8,3},{9,11},{10... | collective-permute-start | bytes 30728 | tf_op jit(solution)/shard_map/ppermute | solution.py:544
  177.4 4.9 %collective-permute-start.70 = (bf16[8,640]{1,0:T(8,128)(2,1)S(1)}, bf16[8,640]{1,0:T(8,128)(2,1)S(1)}, u32[]{:S(2)}, u32[]{:S(2)}) collective-permute-start(bf16[8,640]{1,0:T(8,128)(2,1)S(1)} %get-tuple-element.33), channel_id=1, source_target_pairs={{0,8},{1,0},{2,9},{3,1},{4,6},{5,14},{6,7},{7,15},{8,4},{9,12},{10... | collective-permute-start | bytes 30728 | tf_op jit(solution)/shard_map/ppermute | solution.py:544
  179.0 5.0 %collective-permute-start.71 = (bf16[8,640]{1,0:T(8,128)(2,1)S(1)}, bf16[8,640]{1,0:T(8,128)(2,1)S(1)}, u32[]{:S(2)}, u32[]{:S(2)}) collective-permute-start(bf16[8,640]{1,0:T(8,128)(2,1)S(1)} %get-tuple-element.34), channel_id=1, source_target_pairs={{0,9},{1,1},{2,8},{3,0},{4,7},{5,15},{6,6},{7,14},{8,5},{9,13},{10... | collective-permute-start | bytes 30728 | tf_op jit(solution)/shard_map/ppermute | solution.py:544
  (27 other events, 225.1 us)

commit v2 on v1

--- a/solution.py
+++ b/solution.py
@@ -195,68 +195,78 @@
 ANY_SPEC = pl.BlockSpec(memory_space=pl.ANY)
 
 
-def kernel_params():
-    return pltpu.CompilerParams(vmem_limit_bytes=48 * 1024 * 1024)
-
-
-def project_kernel(
-    step, spans, place_ref, shift_ref, scale_ref, gain_ref, incoming_ref, *refs
-):
+def kernel_params(mebibytes):
+    return pltpu.CompilerParams(vmem_limit_bytes=mebibytes * 1024 * 1024)
+
+
+def span_at(position, step, spans):
     chips = spans // 2
+    return (2 * (position % chips) + position // chips + step + 1) % spans
+
+
+def project_kernel(step, spans, place_ref, shift_ref, scale_ref, gain_ref, incoming_ref, *refs):
+    chips = spans // 2
+    weight_refs, refs = refs[:3], refs[3:]
     mine, others = refs[:chips], refs[chips : 2 * chips]
     refs = refs[2 * chips :]
-    weight_refs, refs = refs[:3], refs[3:]
     own_ref, send_ref, squares_ref = refs[:3]
     refs = refs[3:]
     if step == 0:
         current_ref, refs = refs[0], refs[1:]
-    state, modulated, held, sems = refs
+    state, modulated, sems = refs
     chip, core = place_ref[0], place_ref[1]
-    tokens, width = state.shape
+    tokens, width = modulated.shape
     half = tokens // 2
     rows = tokens // spans
     pair = 2 * rows
-    cols = held.shape[1]
-    copies = [
-        pltpu.make_async_copy(weight_refs[i], held.at[i], sems.at[i]) for i in range(3)
-    ]
+    cols = weight_refs[0].shape[0]
+    first = core == 0
+    copies = []
+    for side, blocks in enumerate((mine, others)):
+        owner = core if side == 0 else 1 - core
+        for mask in range(chips):
+            other_chip = chip ^ mask
+            if step == 0:
+                target = state.at[owner * chips + other_chip]
+            else:
+                lanes = pl.ds(pl.multiple_of(other_chip * 2 * cols, 2 * cols), 2 * cols)
+                target = state.at[pl.ds(pl.multiple_of(owner * half, half), half), lanes]
+            copies.append(
+                pltpu.make_async_copy(blocks[mask], target, sems.at[side * chips + mask])
+            )
     for copy in copies:
         copy.start()
-    first = core == 0
-    for mask in range(chips):
-        other_chip = chip ^ mask
-        if step == 0:
-            at = pl.multiple_of(other_chip * pair, pair)
-            for low in range(0, width, width // 4):
-                part = pl.ds(low, width // 4)
-                a = mine[mask][:, part].astype(jnp.float32)
-                b = others[mask][:, part].astype(jnp.float32)
-                upper = jnp.where(first, b, a)
-                upper = jnp.where(
-                    other_chip == chips - 1, incoming_ref[:, part].astype(jnp.float32), upper
-                )
-                both = jnp.concatenate([jnp.where(first, a, b), upper], axis=0)
-                state[pl.ds(at, pair), part] = both.astype(jnp.bfloat16)
-        else:
-            lanes = pl.ds(pl.multiple_of(other_chip * 2 * cols, 2 * cols), 2 * cols)
-            state[pl.ds(pl.multiple_of(core * half, half), half), lanes] = mine[mask][...]
-            state[pl.ds(pl.multiple_of((1 - core) * half, half), half), lanes] = others[mask][...]
+    for copy in copies:
+        copy.wait()
     if step == 0:
+        state[spans - 1] = incoming_ref[...]
         lanes = pl.ds(pl.multiple_of(chip * 2 * cols, 2 * cols), 2 * cols)
-        current_ref[...] = state[pl.ds(pl.multiple_of(core * half, half), half), lanes]
+        for slab in range(chips // 2):
+            at = core * chips + 2 * slab
+            both = [state[at + e, :, lanes].astype(jnp.float32) for e in range(2)]
+            current_ref[slab * pair : (slab + 1) * pair, :] = jnp.concatenate(
+                both, axis=0
+            ).astype(jnp.bfloat16)
     pieces = 4
     piece = width // pieces
     for slab in range(chips):
         band = slice(slab * pair, (slab + 1) * pair)
+
+        def load(part):
+            if step == 0:
+                both = [state[2 * slab + e, :, part].astype(jnp.float32) for e in range(2)]
+                return jnp.concatenate(both, axis=0)
+            return state[band, part].astype(jnp.float32)
+
         total = jnp.zeros((pair, 1), jnp.float32)
         for low in range(0, width, piece):
-            x = state[band, low : low + piece].astype(jnp.float32)
+            x = load(slice(low, low + piece))
             total = total + jnp.sum(x * x, axis=1, keepdims=True)
         factor = lax.rsqrt(total / width + 1e-06)
-        at = [(2 * slab + e + step + 1) % spans for e in range(2)]
+        at = [span_at(2 * slab + e, step, spans) for e in range(2)]
         for low in range(0, width, piece):
             part = slice(low, low + piece)
-            x = state[band, part].astype(jnp.float32) * factor
+            x = load(part) * factor
             scale, shift = (
                 jnp.concatenate(
                     [jnp.broadcast_to(ref[s : s + 1, part], (rows, piece)) for s in at], axis=0
@@ -264,23 +274,18 @@
                 for ref in (scale_ref, shift_ref)
             )
             modulated[band, part] = (x * (1.0 + scale) + shift).astype(jnp.bfloat16)
-    ident = lax.broadcasted_iota(jnp.int32, (tokens, tokens), 0) == lax.broadcasted_iota(
-        jnp.int32, (tokens, tokens), 1
-    )
     for i in range(3):
-        copies[i].wait()
 
         def add(step_k, total):
             part = pl.ds(pl.multiple_of(step_k * piece, piece), piece)
-            return total + contract_last(modulated[:, part], held[i, :, part])
-
-        product = lax.fori_loop(0, pieces, add, jnp.zeros((tokens, cols), jnp.float32))
+            return total + contract_last(weight_refs[i][:, part], modulated[:, part])
+
+        product = lax.fori_loop(0, pieces, add, jnp.zeros((cols, tokens), jnp.float32))
         if i < 2:
-            column = jnp.sum(product * product, axis=1, keepdims=True)
-            squares_ref[i : i + 1, :] = jnp.sum(
-                jnp.where(ident, column, 0.0), axis=0, keepdims=True
-            )
-            product = product * gain_ref[i : i + 1, :]
+            line = jnp.sum(product * product, axis=0, keepdims=True)
+            squares_ref[:, i : i + 1, :] = jnp.broadcast_to(line[None], (spans, 1, tokens))
+            product = product * gain_ref[:, i : i + 1]
+        product = product.T
         if i == 0:
             low, high = product[:half], product[half:]
             own_ref[:half, :] = jnp.where(first, low, high).astype(jnp.bfloat16)
@@ -292,31 +297,36 @@
 
 
 def project(step, spans, place, shift, scale, gain, incoming, mine, others, weights):
-    tokens = spans * incoming.shape[0]
+    rows = incoming.shape[0]
+    tokens = spans * rows
     cols, width = weights[0].shape
     half = tokens // 2
     own = jax.ShapeDtypeStruct((half + 2 * tokens, cols), jnp.bfloat16)
-    out_shape = [own, own, jax.ShapeDtypeStruct((2, tokens), jnp.float32)]
+    out_shape = [own, own, jax.ShapeDtypeStruct((spans, 2, tokens), jnp.float32)]
     if step == 0:
         out_shape.append(jax.ShapeDtypeStruct((half, 2 * cols), jnp.bfloat16))
+        state = (spans, rows, width)
+    else:
+        state = (tokens, width)
     return pl.pallas_call(
         functools.partial(project_kernel, step, spans),
         out_shape=out_shape,
-        in_specs=[SMEM_SPEC] + [VMEM_SPEC] * (4 + len(mine) + len(others)) + [ANY_SPEC] * 3,
+        in_specs=[SMEM_SPEC] + [VMEM_SPEC] * 7 + [ANY_SPEC] * (2 * len(mine)),
         out_specs=[VMEM_SPEC] * len(out_shape),
         scratch_shapes=[
+            pltpu.VMEM(state, jnp.bfloat16),
             pltpu.VMEM((tokens, width), jnp.bfloat16),
-            pltpu.VMEM((tokens, width), jnp.bfloat16),
-            pltpu.VMEM((3, cols, width), jnp.bfloat16),
-            pltpu.SemaphoreType.DMA((3,)),
+            pltpu.SemaphoreType.DMA((spans,)),
         ],
-        compiler_params=kernel_params(),
+        compiler_params=kernel_params(24),
         name="project",
-    )(place, shift, scale, gain, incoming, *mine, *others, *weights)
-
-
-def attend_kernel(step, spans, head_size, count, place_ref, own_ref, got_ref, text_ref, more_ref, *refs):
-    square_refs, (out_ref, queries, keys, values) = refs[:count], refs[count:]
+    )(place, shift, scale, gain, incoming, *weights, *mine, *others)
+
+
+def attend_kernel(
+    step, spans, head_size, place_ref, own_ref, got_ref, text_ref, more_ref, squares_ref,
+    out_ref, queries, keys, values,
+):
     core = place_ref[1]
     first = core == 0
     half, width = queries.shape
@@ -332,9 +342,7 @@
         other = got_ref[low : low + size, :]
         target[:, :cols] = jnp.where(first, mine, other)
         target[:, cols:] = jnp.where(first, other, mine)
-    squares = square_refs[0][...]
-    for ref in square_refs[1:]:
-        squares = squares + ref[...]
+    squares = jnp.sum(squares_ref[...], axis=0)
     factors = lax.rsqrt(squares / (width * (spans // 2)) + 1e-06)
     ident = lax.broadcasted_iota(jnp.int32, (tokens, tokens), 0) == lax.broadcasted_iota(
         jnp.int32, (tokens, tokens), 1
@@ -345,7 +353,7 @@
     shape = (half, tokens)
     own_block = lax.broadcasted_iota(jnp.int32, shape, 0) // rows + core * (spans // 2)
     key_block = lax.broadcasted_iota(jnp.int32, shape, 1) // rows
-    allowed = lax.rem(own_block + step + 1, spans) >= lax.rem(key_block + step + 1, spans)
+    allowed = span_at(own_block, step, spans) >= span_at(key_block, step, spans)
     text_rows = text_ref.shape[0] * text_ref.shape[2]
     for head in range(width // head_size):
         lanes = slice(head * head_size, (head + 1) * head_size)
@@ -380,98 +388,119 @@
 
 def attend(step, spans, head_size, place, own, got, text, more, squares):
     cols = own.shape[1]
-    tokens = squares[0].shape[1]
+    tokens = squares.shape[2]
     half = tokens // 2
     return pl.pallas_call(
-        functools.partial(attend_kernel, step, spans, head_size, len(squares)),
+        functools.partial(attend_kernel, step, spans, head_size),
         out_shape=jax.ShapeDtypeStruct((half, 2 * cols), jnp.bfloat16),
-        in_specs=[SMEM_SPEC] + [VMEM_SPEC] * (4 + len(squares)),
+        in_specs=[SMEM_SPEC] + [VMEM_SPEC] * 5,
         out_specs=VMEM_SPEC,
         scratch_shapes=[
             pltpu.VMEM((half, 2 * cols), jnp.bfloat16),
             pltpu.VMEM((tokens, 2 * cols), jnp.bfloat16),
             pltpu.VMEM((tokens, 2 * cols), jnp.bfloat16),
         ],
-        compiler_params=kernel_params(),
+        compiler_params=kernel_params(16),
         name="attend",
-    )(place, own, got, text, more, *squares)
-
-
-def output_kernel(step, spans, last, place_ref, current_ref, gate_ref, incoming_ref, own_ref, other_ref, *refs):
+    )(place, own, got, text, more, squares)
+
+
+def output_kernel(
+    step, spans, last, place_ref, current_ref, gate_ref, incoming_ref, own_ref, other_ref, *refs
+):
     chips = spans // 2
-    blocks, refs = refs[:chips], refs[chips:]
+    blocks, (out_ref, totals) = refs[:chips], refs[chips:]
     chip, core = place_ref[0], place_ref[1]
     first = core == 0
     half, width = current_ref.shape
     cols = width // 2
     rows = 2 * half // spans
-    mine = jnp.zeros((half, cols), jnp.float32)
-    other = jnp.zeros((half, cols), jnp.float32)
+    mine = jnp.zeros((cols, half), jnp.float32)
+    other = jnp.zeros((cols, half), jnp.float32)
     for mask in range(chips):
         lanes = pl.ds(pl.multiple_of((chip ^ mask) * width, width), width)
         block = blocks[mask][...]
-        mine = mine + contract_last(block, own_ref[:, lanes])
-        other = other + contract_last(block, other_ref[:, lanes])
-    totals = refs[-1]
-    totals[:, :cols] = jnp.where(first, mine, other)
-    totals[:, cols:] = jnp.where(first, other, mine)
+        mine = mine + contract_last(own_ref[:, lanes], block)
+        other = other + contract_last(other_ref[:, lanes], block)
+    both = jnp.concatenate([jnp.where(first, mine, other), jnp.where(first, other, mine)], axis=0)
+    totals[...] = both.T
     for block in range(chips):
         band = slice(block * rows, (block + 1) * rows)
-        places = [(block + e * chips + step + 1) % spans for e in range(2)]
+        places = [span_at(block + e * chips, step, spans) for e in range(2)]
         gates = [gate_ref[s : s + 1, :] for s in places]
         gate = jnp.where(first, gates[0], gates[1])
         totals[band, :] = current_ref[band, :].astype(jnp.float32) + gate * totals[band, :]
     if last:
-        for turn in range(chips):
-            at = pl.multiple_of((chip ^ turn) * rows, rows)
-            refs[turn][...] = totals[pl.ds(at, rows), :].astype(jnp.bfloat16)
+        for target in range(chips):
+            block = (target - STEPS // 2) % chips
+            out_ref[target] = totals[block * rows : (block + 1) * rows, :].astype(jnp.bfloat16)
     else:
-        leaving = spans - 2 - step - chips
-        band = slice(leaving * rows, (leaving + 1) * rows)
+        parity, block = (spans - 2 - step) % 2, (spans - 2 - step) // 2
+        band = slice(block * rows, (block + 1) * rows)
         lanes = pl.ds(pl.multiple_of(chip * width, width), width)
         totals[band, :] = jnp.where(
-            first, totals[band, :], incoming_ref[:, lanes].astype(jnp.float32)
-        )
-        refs[0][...] = totals[...].astype(jnp.bfloat16)
+            core == parity, incoming_ref[:, lanes].astype(jnp.float32), totals[band, :]
+        )
+        out_ref[...] = totals[...].astype(jnp.bfloat16)
 
 
 def output(step, spans, last, place, current, gate, incoming, own, other, blocks):
     half, width = current.shape
     chips = spans // 2
     rows = 2 * half // spans
-    if last:
-        out_shape = [jax.ShapeDtypeStruct((rows, width), jnp.bfloat16)] * chips
-    else:
-        out_shape = [jax.ShapeDtypeStruct((half, width), jnp.bfloat16)]
     return pl.pallas_call(
         functools.partial(output_kernel, step, spans, last),
-        out_shape=out_shape,
+        out_shape=jax.ShapeDtypeStruct(
+            (chips, rows, width) if last else (half, width), jnp.bfloat16
+        ),
         in_specs=[SMEM_SPEC] + [VMEM_SPEC] * (5 + chips),
-        out_specs=[VMEM_SPEC] * len(out_shape),
+        out_specs=VMEM_SPEC,
         scratch_shapes=[pltpu.VMEM((half, width), jnp.float32)],
-        compiler_params=kernel_params(),
+        compiler_params=kernel_params(16),
         name="output",
     )(place, current, gate, incoming, own, other, *blocks)
 
 
-def join_kernel(place_ref, *refs):
-    out_ref = refs[-1]
-    for turn, ref in enumerate(refs[:-1]):
-        width = ref.shape[1]
-        lanes = pl.ds(pl.multiple_of((place_ref[2] ^ turn) * width, width), width)
-        out_ref[:, lanes] = ref[...]
-
-
-def join(place, blocks):
-    rows, width = blocks[0].shape
+def join_kernel(in_ref, out_ref):
+    chips, _, width = in_ref.shape
+    for source in range(chips):
+        out_ref[:, source * width : (source + 1) * width] = in_ref[source]
+
+
+def join(blocks):
+    chips, rows, width = blocks.shape
     return pl.pallas_call(
         join_kernel,
-        out_shape=jax.ShapeDtypeStruct((rows, width * len(blocks)), jnp.bfloat16),
-        in_specs=[SMEM_SPEC] + [VMEM_SPEC] * len(blocks),
+        out_shape=jax.ShapeDtypeStruct((rows, width * chips), jnp.bfloat16),
+        in_specs=[VMEM_SPEC],
         out_specs=VMEM_SPEC,
-        compiler_params=kernel_params(),
+        compiler_params=kernel_params(4),
         name="join",
-    )(place, *blocks)
+    )(blocks)
+
+
+def arrange_kernel(spans, keys_ref, values_ref, out_ref):
+    width = out_ref.shape[3]
+    text_half = out_ref.shape[2]
+    for device in range(spans):
+        lanes = slice(device // 2 * width, (device // 2 + 1) * width)
+        band = slice(device % 2 * text_half, (device % 2 + 1) * text_half)
+        out_ref[device, 0] = keys_ref[band, lanes]
+        out_ref[device, 1] = values_ref[band, lanes]
+
+
+def arrange(spans, keys, values):
+    text_half = keys.shape[0] // 2
+    return pl.pallas_call(
+        functools.partial(arrange_kernel, spans),
+        out_shape=jax.ShapeDtypeStruct(
+            (spans, 2, text_half, 2 * keys.shape[1] // spans), jnp.bfloat16
+        ),
+        in_specs=[VMEM_SPEC] * 2,
+        out_specs=VMEM_SPEC,
+        compiler_params=kernel_params(8),
+        name="arrange",
+    )(keys, values)
 
 
 def paired_device(
@@ -492,57 +521,58 @@
     spans = lax.axis_size("queue")
     chips = spans // 2
     chip, core = own_index // 2, own_index % 2
-    rows, width = hidden.shape
+    width = hidden.shape[1]
     cols = query_weight.shape[1]
     head_size = width // HEADS
-    home = (own_index + spans - STEPS) % spans
-    place = jnp.stack([chip, core, home % chips]).astype(jnp.int32)
-    hidden_mine = gathered_over_chips(hidden)
-    hidden_others = [swapped(block, 1) for block in hidden_mine]
+    place = jnp.stack([chip, core]).astype(jnp.int32)
+    mine = gathered_over_chips(hidden)
+    others = [swapped(block, 1) for block in mine]
     picked = (levels[:, None] == jnp.arange(mod_table.shape[0])[None, :]).astype(mod_table.dtype)
     shift, scale, gate = jnp.einsum(
         "sl,ltd->tsd", picked, mod_table, preferred_element_type=jnp.float32
     )
     gate = lax.dynamic_slice_in_dim(gate, chip * 2 * cols, 2 * cols, 1)
-    gain = lax.dynamic_slice_in_dim(jnp.stack([query_gain, key_gain]), own_index * cols, cols, 1)
+    gain = lax.dynamic_slice_in_dim(jnp.stack([query_gain, key_gain]), own_index * cols, cols, 1).T
     weights = [w.T for w in (query_weight, key_weight, value_weight)]
     output_own = output_weight.T
     output_other = swapped(output_own, 1)
-    text_half = text_keys.shape[0] // 2
-    text = jnp.stack([text_keys, text_values]).reshape(2, 2, text_half, chips, 2 * cols)
-    text = text.transpose(3, 1, 0, 2, 4).reshape(spans, 2, text_half, 2 * cols)
+    text = arrange(spans, text_keys, text_values)
+    text, *mine = lax.optimization_barrier((text, *mine))
     text = lax.all_to_all(text, "queue", split_axis=0, concat_axis=0, tiled=True)
     more = swapped(text, 1)
-    mine, others = hidden_mine, hidden_others
     current = None
     for step in range(STEPS):
+        last = step == STEPS - 1
         own, send, squares, *rest = project(
             step, spans, place, shift, scale, gain, incoming[step], mine, others, weights
         )
+        got = swapped(send, 1)
+        squares = lax.all_to_all(squares, "queue", split_axis=0, concat_axis=0, tiled=True)
         if step == 0:
             current = rest[0]
-        got = swapped(send, 1)
-        squares = gathered_over_chips(squares + swapped(squares, 1))
+            got, output_other = lax.optimization_barrier((got, output_other))
         block = attend(step, spans, head_size, place, own, got, text, more, squares)
-        blocks = gathered_over_chips(block)
-        last = step == STEPS - 1
         result = output(
-            step, spans, last, place, current, gate, incoming[min(step + 1, STEPS - 1)],
-            output_own, output_other, blocks,
+            step,
+            spans,
+            last,
+            place,
+            current,
+            gate,
+            incoming[min(step + 1, STEPS - 1)],
+            output_own,
+            output_other,
+            gathered_over_chips(block),
         )
         if not last:
-            current = result[0]
+            current = result
             mine = gathered_over_chips(current)
             others = [swapped(block, 1) for block in mine]
-    rounds = []
-    for turn in range(chips):
-        pairs = []
-        for source in range(spans):
-            source_chip, source_core = source // 2, source % 2
-            ring = source_core * chips + (source_chip ^ turn)
-            pairs.append((source, (ring + STEPS) % spans))
-        rounds.append(lax.ppermute(result[turn], "queue", pairs))
-    return join(place, rounds)
+    same_core = [[2 * c + core_index for c in range(chips)] for core_index in range(2)]
+    result = lax.all_to_all(
+        result, "queue", split_axis=0, concat_axis=0, tiled=True, axis_index_groups=same_core
+    )
+    return join(result)
 
 
 def held_in_pairs(mesh, hidden, query_weight):
@@ -551,7 +581,7 @@
     cols = query_weight.shape[1] // spans
     head_size = query_weight.shape[0] // HEADS
     power = spans & (spans - 1) == 0
-    return power and spans >= 4 and 2 * cols % head_size == 0 and rows * spans == 128 and rows == 8
+    return STEPS % 2 == 0 and power and spans >= 4 and 2 * cols % head_size == 0 and rows * spans == 128 and rows == 8
 
 
 def solution(mesh):

time: 186 us -> 186 us (level)
  starting transfers between devices: 87.4 us -> 43.1 us
  blocking collectives: 0 us -> 19.4 us
  local copies, waits for them, and re-layouts: 14.4 us -> 27.8 us
  waiting for transfers between devices: 45.5 us -> 56.9 us
    ppermute x64 -> x48, starting transfers between devices: 59.5 us -> 32.7 us  [swapped(): lax.ppermute(value, 'queue', [(source, source ^ bit) for source in range(...]
    ppermute x8 -> x0, starting transfers between devices: 23.6 us -> none  [paired_device(): rounds.append(lax.ppermute(result[turn], 'queue', pairs))]
    all_to_all x0 -> x2, blocking collectives: none -> 19.4 us  [the longest x1 10.3 us: paired_device(): lax.all_to_all(result, 'queue', split_axis=0, concat_axis=0, tiled=True,...]
    unnamed x38 -> x61, local copies, waits for them, and re-layouts: 11.7 us -> 24.5 us
    all_to_all x1, waiting for transfers between devices: 3.37 us -> 14.2 us  [paired_device(): lax.all_to_all(text, 'queue', split_axis=0, concat_axis=0, tiled=True)]
    all_to_all x0 -> x1, waiting for transfers between devices: none -> 6.47 us  [paired_device(): lax.all_to_all(squares, 'queue', split_axis=0, concat_axis=0, tiled=True)]
    all_to_all x0 -> x1, starting transfers between devices: none -> 4.94 us  [paired_device(): lax.all_to_all(squares, 'queue', split_axis=0, concat_axis=0, tiled=True)]
    ppermute x64 -> x48, waiting for transfers between devices: 40.5 us -> 36.3 us  [swapped(): lax.ppermute(value, 'queue', [(source, source ^ bit) for source in range(...]
  transfers between devices with their start and end apart: 73 -> 50, of which waited for: 34 -> 25; matrix products, arithmetic and copies ran while one was open for 4% -> 3% of each run, Pallas kernels for 7% -> 5%
where the time goes in v2:
time: 186 us; the launch traced here: 185 us
  waiting for transfers between devices  56.9 us (31%)
  starting transfers between devices  43.1 us (23%)
  Pallas kernels  35.4 us (19%)
  local copies, waits for them, and re-layouts  27.8 us (15%)
  blocking collectives  19.4 us (10%)
    ppermute x48, waiting for transfers between devices, swapped(): lax.ppermute(value, 'queue', [(source, source ^ bit) for source in range(...  36.3 us
    ppermute x48, starting transfers between devices, swapped(): lax.ppermute(value, 'queue', [(source, source ^ bit) for source in range(...  32.7 us
    unnamed x61, local copies, waits for them, and re-layouts  24.5 us
    pallas_call x2, Pallas kernels, project(): pl.pallas_call(functools.partial(project_kernel, step, spans), out_shape=...  16.3 us
    all_to_all x1, waiting for transfers between devices, paired_device(): lax.all_to_all(text, 'queue', split_axis=0, concat_axis=0, tiled=True)  14.2 us
    pallas_call x2, Pallas kernels, attend(): pl.pallas_call(functools.partial(attend_kernel, step, spans, head_size),...  10.3 us
    all_to_all x1, blocking collectives, paired_device(): lax.all_to_all(result, 'queue', split_axis=0, concat_axis=0, tiled=True,...  10.3 us
    all_to_all x1, blocking collectives, paired_device(): lax.all_to_all(squares, 'queue', split_axis=0, concat_axis=0, tiled=True)  9.06 us
  transfers between devices with their start and end apart: 50, of which 25 were waited for; matrix products, arithmetic and copies ran while one was open for 3% of the time, Pallas kernels for 5%

profile of v2, /device:TPU:0, one launch (start us, length us, event | category | flops | bytes accessed | tf_op | source)
XLA Modules:
  0.0 184.9 jit_solution(3649547445373494057)
XLA Ops:
  0.5 3.7 %collective-permute-start.3 = (bf16[8,5120]{1,0:T(8,128)(2,1)}, bf16[8,5120]{1,0:T(8,128)(2,1)S(1)}, u32[]{:S(2)}, u32[]{:S(2)}) collective-permute-start(bf16[8,5120]{1,0:T(8,128)(2,1)} %refs_3_), channel_id=1, source_target_pairs={{0,8},{1,9},{2,10},{3,11},{4,12},{5,13},{6,14},{7,15},{8,0},{9,1},... | collective-permute-start | bytes 245768 | tf_op jit(solution)/shard_map/ppermute | solution.py:174
  4.1 1.6 collective-permute-start.1
  5.7 3.5 %collective-permute-done.3.refs_7_ = bf16[8,5120]{1,0:T(8,128)(2,1)S(1)} collective-permute-done((bf16[8,5120]{1,0:T(8,128)(2,1)}, bf16[8,5120]{1,0:T(8,128)(2,1)S(1)}, u32[]{:S(2)}, u32[]{:S(2)}) %collective-permute-start.3) | collective-permute-done | bytes 81952 | tf_op jit(solution)/shard_map/ppermute | solution.py:174
  10.0 1.5 collective-permute-start
  12.0 1.5 collective-permute-start.2
  13.8 1.6 collective-permute-start.6
  15.4 1.0 copy-done.13
  16.3 1.0 copy-done.14
  17.4 0.9 copy-done.11
  19.8 5.5 %all-to-all-start = ((bf16[16,2,16,640]{3,2,1,0:T(8,128)(2,1)}), bf16[16,2,16,640]{3,2,1,0:T(8,128)(2,1)}, u32[]{:S(2)}, u32[]{:S(2)}) async-start(bf16[16,2,16,640]{3,2,1,0:T(8,128)(2,1)} %copy-done.11), calls=%async_computation | async-start | bytes 1310720 | tf_op jit(solution)/shard_map/all_to_all | solution.py:541
  25.4 1.2 convolution_bitcast_fusion
  26.6 0.9 fusion.4
  27.8 14.2 %all-to-all-done.text_ref = bf16[16,2,16,640]{3,2,1,0:T(8,128)(2,1)} async-done(((bf16[16,2,16,640]{3,2,1,0:T(8,128)(2,1)}), bf16[16,2,16,640]{3,2,1,0:T(8,128)(2,1)}, u32[]{:S(2)}, u32[]{:S(2)}) %all-to-all-start) | async-done | bytes 655392 | tf_op jit(solution)/shard_map/all_to_all | solution.py:541
  42.1 1.6 slice_bitcast_fusion.2
  48.2 1.9 %copy-done.1 = bf16[5120,320]{0,1:T(8,128)(2,1)S(1)} copy-done((bf16[5120,320]{0,1:T(8,128)(2,1)S(1)}, bf16[5120,320]{0,1:T(8,128)(2,1)}, u32[]{:S(2)}) %copy-start.1) | copy-done | bytes 3276824
  50.2 1.9 %copy-done.3 = bf16[5120,320]{0,1:T(8,128)(2,1)S(1)} copy-done((bf16[5120,320]{0,1:T(8,128)(2,1)S(1)}, bf16[5120,320]{0,1:T(8,128)(2,1)}, u32[]{:S(2)}) %copy-start.3) | copy-done | bytes 3276824
  52.1 1.9 %copy-done.5 = bf16[5120,320]{0,1:T(8,128)(2,1)S(1)} copy-done((bf16[5120,320]{0,1:T(8,128)(2,1)S(1)}, bf16[5120,320]{0,1:T(8,128)(2,1)}, u32[]{:S(2)}) %copy-start.5) | copy-done | bytes 3276824
  54.0 1.0 copy-done.9
  55.0 0.9 copy-done.12
  55.9 0.9 copy-done.17
  56.8 0.9 copy-done.19
  57.7 0.9 copy-done.21
  58.5 0.9 copy-done.23
  59.4 0.9 copy-done.25
  60.3 9.2 %project.2 = (bf16[320,320]{1,0:T(8,128)(2,1)S(1)}, bf16[320,320]{1,0:T(8,128)(2,1)}, f32[16,2,128]{2,1,0:T(2,128)S(1)}, bf16[64,640]{1,0:T(8,128)(2,1)S(1)}) custom-call(s32[2]{0:T(128)S(1)} %pad_add_fusion.place_ref, f32[16,5120]{1,0:T(8,128)S(1)} %copy-done.9, f32[16,5120]{1,0:T(8,128)S(1)} %get-tuple-element.42.scale_ref, f32[320,2]{1,0:T(8,128)S(1)} %bitcast.34, ...), custom_call_target="tpu_custom_call" | custom-call | tf_op jit(solution)/shard_map/project/pallas_call | solution.py:311
  71.6 4.9 %all-to-all-start.1 = ((f32[16,2,128]{2,1,0:T(2,128)}), f32[16,2,128]{2,1,0:T(2,128)S(1)}, u32[]{:S(2)}, u32[]{:S(2)}) async-start(f32[16,2,128]{2,1,0:T(2,128)} %copy-done.28), calls=%async_computation.1 | async-start | bytes 32768 | tf_op jit(solution)/shard_map/all_to_all | solution.py:550
  76.6 6.5 %all-to-all-done.1.squares_ref = f32[16,2,128]{2,1,0:T(2,128)S(1)} async-done(((f32[16,2,128]{2,1,0:T(2,128)}), f32[16,2,128]{2,1,0:T(2,128)S(1)}, u32[]{:S(2)}, u32[]{:S(2)}) %all-to-all-start.1) | async-done | bytes 16416 | tf_op jit(solution)/shard_map/all_to_all | solution.py:550
  83.1 0.9 copy-done.16
  84.0 5.5 %attend.2.refs_0_ = bf16[64,640]{1,0:T(8,128)(2,1)} custom-call(s32[2]{0:T(128)S(1)} %pad_add_fusion.place_ref, bf16[320,320]{1,0:T(8,128)(2,1)S(1)} %copy-done.16, bf16[320,320]{1,0:T(8,128)(2,1)} %collective-permute-done.15.got_ref, bf16[16,2,16,640]{3,2,1,0:T(8,128)(2,1)} %all-to-all-done.text_ref, ...), custom_call_target="tpu_custom_call" | custom-call | tf_op jit(solution)/shard_map/attend/pallas_call | solution.py:393
  90.6 6.0 %collective-permute-done.21.refs_4_ = bf16[64,640]{1,0:T(8,128)(2,1)} collective-permute-done((bf16[64,640]{1,0:T(8,128)(2,1)}, bf16[64,640]{1,0:T(8,128)(2,1)}, u32[]{:S(2)}, u32[]{:S(2)}) %collective-permute-start.21) | collective-permute-done | bytes 81952 | tf_op jit(solution)/shard_map/ppermute | solution.py:174
  96.6 0.8 collective-permute-start.18
  97.4 1.2 collective-permute-start.22
  98.7 0.8 collective-permute-start.20
  99.5 1.9 %collective-permute-done.23.refs_6_ = bf16[64,640]{1,0:T(8,128)(2,1)} collective-permute-done((bf16[64,640]{1,0:T(8,128)(2,1)}, bf16[64,640]{1,0:T(8,128)(2,1)}, u32[]{:S(2)}, u32[]{:S(2)}) %collective-permute-start.23) | collective-permute-done | bytes 81952 | tf_op jit(solution)/shard_map/ppermute | solution.py:174
  101.4 0.8 collective-permute-start.24
  103.0 1.0 collective-permute-done.22.refs_5_
  103.9 1.4 collective-permute-done.20.refs_3_
  105.3 0.9 collective-permute-done.24.refs_7_
  106.2 1.9 %copy-done.7 = bf16[5120,320]{0,1:T(8,128)(2,1)S(1)} copy-done((bf16[5120,320]{0,1:T(8,128)(2,1)S(1)}, bf16[5120,320]{0,1:T(8,128)(2,1)}, u32[]{:S(2)}) %copy-start.7) | copy-done | bytes 3276824
  108.1 0.9 copy-done.27
  109.0 4.2 %output.2.refs_3_.current_ref = bf16[64,640]{1,0:T(8,128)(2,1)S(1)} custom-call(s32[2]{0:T(128)S(1)} %pad_add_fusion.place_ref, bf16[64,640]{1,0:T(8,128)(2,1)S(1)} %copy-done.27, f32[16,640]{1,0:T(8,128)S(1)} %dynamic-slice_bitcast_fusion.gate_ref, bf16[8,5120]{1,0:T(8,128)(2,1)S(1)} %get-tuple-element.44.incoming_ref, bf16[320,5120]{1,0:T(8,128)(2,1)S(1)} %bitcast.32, ...), custom_call_target="tpu_custom_call" | custom-call | tf_op jit(solution)/shard_map/output/pallas_call | solution.py:451
  113.4 1.8 collective-permute-start.26
  115.2 1.1 collective-permute-start.25
  116.2 2.5 %collective-permute-done.28.refs_7_ = bf16[64,640]{1,0:T(8,128)(2,1)S(1)} collective-permute-done((bf16[64,640]{1,0:T(8,128)(2,1)S(1)}, bf16[64,640]{1,0:T(8,128)(2,1)S(1)}, u32[]{:S(2)}, u32[]{:S(2)}) %collective-permute-start.28) | collective-permute-done | bytes 81952 | tf_op jit(solution)/shard_map/ppermute | solution.py:174
  118.7 2.3 %collective-permute-start.30 = (bf16[64,640]{1,0:T(8,128)(2,1)S(1)}, bf16[64,640]{1,0:T(8,128)(2,1)S(1)}, u32[]{:S(2)}, u32[]{:S(2)}) collective-permute-start(bf16[64,640]{1,0:T(8,128)(2,1)S(1)} %collective-permute-done.28.refs_7_), channel_id=1, source_target_pairs={{0,4},{1,5},{2,6},{3,7},{4,0},{5,1},{6,2},{7,3},{8,12},{9,13},{10,... | collective-permute-start | bytes 245768 | tf_op jit(solution)/shard_map/ppermute | solution.py:174
  121.0 1.1 collective-permute-start.29
  122.3 1.0 collective-permute-start.27
  123.5 1.1 collective-permute-start.31
  124.5 1.8 collective-permute-done.29.refs_8_
  126.8 1.2 collective-permute-done.27.refs_6_
  128.0 1.4 collective-permute-done.31.refs_10_
  129.4 1.2 collective-permute-done.39.refs_18_
  130.7 1.9 %copy-done.6 = bf16[5120,320]{0,1:T(8,128)(2,1)S(1)} copy-done((bf16[5120,320]{0,1:T(8,128)(2,1)S(1)}, bf16[5120,320]{0,1:T(8,128)(2,1)}, u32[]{:S(2)}) %copy-start.6) | copy-done | bytes 3276824
  132.6 7.1 %project.3 = (bf16[320,320]{1,0:T(8,128)(2,1)S(1)}, bf16[320,320]{1,0:T(8,128)(2,1)S(1)}, f32[16,2,128]{2,1,0:T(2,128)S(1)}) custom-call(s32[2]{0:T(128)S(1)} %pad_add_fusion.place_ref, f32[16,5120]{1,0:T(8,128)S(1)} %copy-done.10, f32[16,5120]{1,0:T(8,128)S(1)} %get-tuple-element.42.scale_ref, f32[320,2]{1,0:T(8,128)S(1)} %bitcast.35, ...), custom_call_target="tpu_custom_call" | custom-call | tf_op jit(solution)/shard_map/project/pallas_call | solution.py:311
  139.9 9.1 %all_to_all.20.squares_ref = f32[16,2,128]{2,1,0:T(2,128)S(1)} all-to-all(f32[16,2,128]{2,1,0:T(2,128)S(1)} %get-tuple-element.40), channel_id=1, replica_groups=mesh['groups'=2,'queue'=16] {'queue'}, dimensions={0} | all-to-all | bytes 32768 | tf_op jit(solution)/shard_map/all_to_all | solution.py:550
  149.0 4.8 %attend.3.refs_0_ = bf16[64,640]{1,0:T(8,128)(2,1)S(1)} custom-call(s32[2]{0:T(128)S(1)} %pad_add_fusion.place_ref, bf16[320,320]{1,0:T(8,128)(2,1)S(1)} %get-tuple-element.38.own_ref, bf16[320,320]{1,0:T(8,128)(2,1)S(1)} %collective-permute-done.40.got_ref, bf16[16,2,16,640]{3,2,1,0:T(8,128)(2,1)} %all-to-all-done.text_ref, ...), custom_call_target="tpu_custom_call" | custom-call | tf_op jit(solution)/shard_map/attend/pallas_call | solution.py:393
  154.9 5.7 %collective-permute-done.44.refs_4_ = bf16[64,640]{1,0:T(8,128)(2,1)S(1)} collective-permute-done((bf16[64,640]{1,0:T(8,128)(2,1)S(1)}, bf16[64,640]{1,0:T(8,128)(2,1)S(1)}, u32[]{:S(2)}, u32[]{:S(2)}) %collective-permute-start.44) | collective-permute-done | bytes 81952 | tf_op jit(solution)/shard_map/ppermute | solution.py:174
  161.4 1.2 collective-permute-start.45
  163.5 1.6 collective-permute-done.46.refs_6_
  166.0 1.8 collective-permute-done.45.refs_5_
  167.7 1.4 collective-permute-done.43.refs_3_
  169.1 0.9 collective-permute-done.47.refs_7_
  170.0 3.9 %output.3 = bf16[8,8,640]{2,1,0:T(8,128)(2,1)S(1)} custom-call(s32[2]{0:T(128)S(1)} %pad_add_fusion.place_ref, bf16[64,640]{1,0:T(8,128)(2,1)S(1)} %output.2.refs_3_.current_ref, f32[16,640]{1,0:T(8,128)S(1)} %dynamic-slice_bitcast_fusion.gate_ref, bf16[8,5120]{1,0:T(8,128)(2,1)S(1)} %get-tuple-element.44.incoming_ref, bf16[320,5120]{1,0:T(8,128)(2,1)S(1)} %bitcast.33, ...), custom_call_target="tpu_custom_call" | custom-call | tf_op jit(solution)/shard_map/output/pallas_call | solution.py:451
  173.9 10.3 %all_to_all.21.in_ref = bf16[8,8,640]{2,1,0:T(8,128)(2,1)S(1)} all-to-all(bf16[8,8,640]{2,1,0:T(8,128)(2,1)S(1)} %output.3), channel_id=1, replica_groups={{0,2,4,6,8,10,12,14},{1,3,5,7,9,11,13,15},{16,18,20,22,24,26,28,30},{17..., dimensions={0} | all-to-all | bytes 163840 | tf_op jit(solution)/shard_map/all_to_all | solution.py:572
  (113 shorter events, 18.2 us)
Async XLA Ops:
  0.0 25.3 %copy-start = (bf16[96,3,5120]{2,0,1:T(8,128)(2,1)S(1)}, bf16[96,3,5120]{2,0,1:T(8,128)(2,1)}, u32[]{:S(2)}) copy-start(bf16[96,3,5120]{2,0,1:T(8,128)(2,1)} %param.15) | copy-start | bytes 8847364
  0.0 76.6 %collective-permute-start.16 = (bf16[320,5120]{1,0:T(8,128)(2,1)}, bf16[320,5120]{1,0:T(8,128)(2,1)}, u32[]{:S(2)}, u32[]{:S(2)}) collective-permute-start(bf16[320,5120]{1,0:T(8,128)(2,1)} %bitcast.31), channel_id=1, source_target_pairs={{0,1},{1,0},{2,3},{3,2},{4,5},{5,4},{6,7},{7,6},{8,9},{9,8},{10,11... | collective-permute-start | bytes 9830408 | tf_op jit(solution)/shard_map/ppermute | solution.py:174
  0.5 8.8 %collective-permute-start.3 = (bf16[8,5120]{1,0:T(8,128)(2,1)}, bf16[8,5120]{1,0:T(8,128)(2,1)S(1)}, u32[]{:S(2)}, u32[]{:S(2)}) collective-permute-start(bf16[8,5120]{1,0:T(8,128)(2,1)} %refs_3_), channel_id=1, source_target_pairs={{0,8},{1,9},{2,10},{3,11},{4,12},{5,13},{6,14},{7,15},{8,0},{9,1},... | collective-permute-start | bytes 245768 | tf_op jit(solution)/shard_map/ppermute | solution.py:174
  4.1 7.9 %collective-permute-start.1 = (bf16[8,5120]{1,0:T(8,128)(2,1)}, bf16[8,5120]{1,0:T(8,128)(2,1)}, u32[]{:S(2)}, u32[]{:S(2)}) collective-permute-start(bf16[8,5120]{1,0:T(8,128)(2,1)} %refs_3_), channel_id=1, source_target_pairs={{0,4},{1,5},{2,6},{3,7},{4,0},{5,1},{6,2},{7,3},{8,12},{9,13},{10,... | collective-permute-start | bytes 245768 | tf_op jit(solution)/shard_map/ppermute | solution.py:174
  9.2 18.2 %copy-start.18 = (bf16[8,5120]{1,0:T(8,128)(2,1)}, bf16[8,5120]{1,0:T(8,128)(2,1)S(1)}, u32[]{:S(2)}) copy-start(bf16[8,5120]{1,0:T(8,128)(2,1)S(1)} %collective-permute-done.3.refs_7_) | copy-start | bytes 245764
  9.2 4.5 %collective-permute-start.5 = (bf16[8,5120]{1,0:T(8,128)(2,1)S(1)}, bf16[8,5120]{1,0:T(8,128)(2,1)}, u32[]{:S(2)}, u32[]{:S(2)}) collective-permute-start(bf16[8,5120]{1,0:T(8,128)(2,1)S(1)} %collective-permute-done.3.refs_7_), channel_id=1, source_target_pairs={{0,4},{1,5},{2,6},{3,7},{4,0},{5,1},{6,2},{7,3},{8,12},{9,13},{10,... | collective-permute-start | bytes 245768 | tf_op jit(solution)/shard_map/ppermute | solution.py:174
  10.0 8.3 %collective-permute-start = (bf16[8,5120]{1,0:T(8,128)(2,1)}, bf16[8,5120]{1,0:T(8,128)(2,1)}, u32[]{:S(2)}, u32[]{:S(2)}) collective-permute-start(bf16[8,5120]{1,0:T(8,128)(2,1)} %refs_3_), channel_id=1, source_target_pairs={{0,2},{1,3},{2,0},{3,1},{4,6},{5,7},{6,4},{7,5},{8,10},{9,11},{10,... | collective-permute-start | bytes 245768 | tf_op jit(solution)/shard_map/ppermute | solution.py:174
  11.5 6.8 %collective-permute-start.4 = (bf16[8,5120]{1,0:T(8,128)(2,1)S(1)}, bf16[8,5120]{1,0:T(8,128)(2,1)S(1)}, u32[]{:S(2)}, u32[]{:S(2)}) collective-permute-start(bf16[8,5120]{1,0:T(8,128)(2,1)S(1)} %collective-permute-done.3.refs_7_), channel_id=1, source_target_pairs={{0,2},{1,3},{2,0},{3,1},{4,6},{5,7},{6,4},{7,5},{8,10},{9,11},{10,... | collective-permute-start | bytes 245768 | tf_op jit(solution)/shard_map/ppermute | solution.py:174
  12.0 6.9 %collective-permute-start.2 = (bf16[8,5120]{1,0:T(8,128)(2,1)}, bf16[8,5120]{1,0:T(8,128)(2,1)S(1)}, u32[]{:S(2)}, u32[]{:S(2)}) collective-permute-start(bf16[8,5120]{1,0:T(8,128)(2,1)} %collective-permute-done.1.refs_5_), channel_id=1, source_target_pairs={{0,2},{1,3},{2,0},{3,1},{4,6},{5,7},{6,4},{7,5},{8,10},{9,11},{10,... | collective-permute-start | bytes 245768 | tf_op jit(solution)/shard_map/ppermute | solution.py:174
  13.8 6.0 %collective-permute-start.6 = (bf16[8,5120]{1,0:T(8,128)(2,1)}, bf16[8,5120]{1,0:T(8,128)(2,1)}, u32[]{:S(2)}, u32[]{:S(2)}) collective-permute-start(bf16[8,5120]{1,0:T(8,128)(2,1)} %collective-permute-done.5.refs_9_), channel_id=1, source_target_pairs={{0,2},{1,3},{2,0},{3,1},{4,6},{5,7},{6,4},{7,5},{8,10},{9,11},{10,... | collective-permute-start | bytes 245768 | tf_op jit(solution)/shard_map/ppermute | solution.py:174
  15.3 1.0 copy-start.13
  16.3 1.0 copy-start.14
  18.2 25.9 %collective-permute-start.7 = (bf16[8,5120]{1,0:T(8,128)(2,1)}, bf16[8,5120]{1,0:T(8,128)(2,1)S(1)}, u32[]{:S(2)}, u32[]{:S(2)}) collective-permute-start(bf16[8,5120]{1,0:T(8,128)(2,1)} %refs_3_), channel_id=1, source_target_pairs={{0,1},{1,0},{2,3},{3,2},{4,5},{5,4},{6,7},{7,6},{8,9},{9,8},{10,11... | collective-permute-start | bytes 245768 | tf_op jit(solution)/shard_map/ppermute | solution.py:174
  19.8 22.2 %all-to-all-start = ((bf16[16,2,16,640]{3,2,1,0:T(8,128)(2,1)}), bf16[16,2,16,640]{3,2,1,0:T(8,128)(2,1)}, u32[]{:S(2)}, u32[]{:S(2)}) async-start(bf16[16,2,16,640]{3,2,1,0:T(8,128)(2,1)} %copy-done.11), calls=%async_computation | async-start | bytes 1310720 | tf_op jit(solution)/shard_map/all_to_all | solution.py:541
  25.3 19.9 %copy-start.29 = (f32[5120]{0:T(1024)S(1)}, f32[5120]{0:T(1024)}, u32[]{:S(2)}) copy-start(f32[5120]{0:T(1024)} %param.20) | copy-start | bytes 61444
  27.5 17.3 %collective-permute-start.11 = (bf16[8,5120]{1,0:T(8,128)(2,1)S(1)}, bf16[8,5120]{1,0:T(8,128)(2,1)}, u32[]{:S(2)}, u32[]{:S(2)}) collective-permute-start(bf16[8,5120]{1,0:T(8,128)(2,1)S(1)} %collective-permute-done.3.refs_7_), channel_id=1, source_target_pairs={{0,1},{1,0},{2,3},{3,2},{4,5},{5,4},{6,7},{7,6},{8,9},{9,8},{10,11... | collective-permute-start | bytes 245768 | tf_op jit(solution)/shard_map/ppermute | solution.py:174
  42.0 41.1 %collective-permute-start.17 = (bf16[16,2,16,640]{3,2,1,0:T(8,128)(2,1)}, bf16[16,2,16,640]{3,2,1,0:T(8,128)(2,1)}, u32[]{:S(2)}, u32[]{:S(2)}) collective-permute-start(bf16[16,2,16,640]{3,2,1,0:T(8,128)(2,1)} %all-to-all-done.text_ref), channel_id=1, source_target_pairs={{0,1},{1,0},{2,3},{3,2},{4,5},{5,4},{6,7},{7,6},{8,9},{9,8},{10,11... | collective-permute-start | bytes 1966088 | tf_op jit(solution)/shard_map/ppermute | solution.py:174
  43.7 2.5 %collective-permute-start.9 = (bf16[8,5120]{1,0:T(8,128)(2,1)}, bf16[8,5120]{1,0:T(8,128)(2,1)}, u32[]{:S(2)}, u32[]{:S(2)}) collective-permute-start(bf16[8,5120]{1,0:T(8,128)(2,1)} %collective-permute-done.1.refs_5_), channel_id=1, source_target_pairs={{0,1},{1,0},{2,3},{3,2},{4,5},{5,4},{6,7},{7,6},{8,9},{9,8},{10,11... | collective-permute-start | bytes 245768 | tf_op jit(solution)/shard_map/ppermute | solution.py:174
  44.7 1.6 collective-permute-start.8
  44.8 2.0 %collective-permute-start.13 = (bf16[8,5120]{1,0:T(8,128)(2,1)}, bf16[8,5120]{1,0:T(8,128)(2,1)}, u32[]{:S(2)}, u32[]{:S(2)}) collective-permute-start(bf16[8,5120]{1,0:T(8,128)(2,1)} %collective-permute-done.5.refs_9_), channel_id=1, source_target_pairs={{0,1},{1,0},{2,3},{3,2},{4,5},{5,4},{6,7},{7,6},{8,9},{9,8},{10,11... | collective-permute-start | bytes 245768 | tf_op jit(solution)/shard_map/ppermute | solution.py:174
  46.2 1.6 collective-permute-start.12
  46.3 1.5 collective-permute-start.10
  46.7 1.5 collective-permute-start.14
  48.2 1.9 %copy-start.1 = (bf16[5120,320]{0,1:T(8,128)(2,1)S(1)}, bf16[5120,320]{0,1:T(8,128)(2,1)}, u32[]{:S(2)}) copy-start(bf16[5120,320]{0,1:T(8,128)(2,1)} %param.16) | copy-start | bytes 9830404
  50.2 1.9 %copy-start.3 = (bf16[5120,320]{0,1:T(8,128)(2,1)S(1)}, bf16[5120,320]{0,1:T(8,128)(2,1)}, u32[]{:S(2)}) copy-start(bf16[5120,320]{0,1:T(8,128)(2,1)} %param.17) | copy-start | bytes 9830404
  52.1 1.9 %copy-start.5 = (bf16[5120,320]{0,1:T(8,128)(2,1)S(1)}, bf16[5120,320]{0,1:T(8,128)(2,1)}, u32[]{:S(2)}) copy-start(bf16[5120,320]{0,1:T(8,128)(2,1)} %param.18) | copy-start | bytes 9830404
  71.5 5.1 %collective-permute-start.15 = (bf16[320,320]{1,0:T(8,128)(2,1)}, bf16[320,320]{1,0:T(8,128)(2,1)}, u32[]{:S(2)}, u32[]{:S(2)}) collective-permute-start(bf16[320,320]{1,0:T(8,128)(2,1)} %get-tuple-element.32), channel_id=1, source_target_pairs={{0,1},{1,0},{2,3},{3,2},{4,5},{5,4},{6,7},{7,6},{8,9},{9,8},{10,11... | collective-permute-start | bytes 614408 | tf_op jit(solution)/shard_map/ppermute | solution.py:174
  71.6 11.4 %all-to-all-start.1 = ((f32[16,2,128]{2,1,0:T(2,128)}), f32[16,2,128]{2,1,0:T(2,128)S(1)}, u32[]{:S(2)}, u32[]{:S(2)}) async-start(f32[16,2,128]{2,1,0:T(2,128)} %copy-done.28), calls=%async_computation.1 | async-start | bytes 32768 | tf_op jit(solution)/shard_map/all_to_all | solution.py:550
  89.5 7.1 %collective-permute-start.21 = (bf16[64,640]{1,0:T(8,128)(2,1)}, bf16[64,640]{1,0:T(8,128)(2,1)}, u32[]{:S(2)}, u32[]{:S(2)}) collective-permute-start(bf16[64,640]{1,0:T(8,128)(2,1)} %attend.2.refs_0_), channel_id=1, source_target_pairs={{0,8},{1,9},{2,10},{3,11},{4,12},{5,13},{6,14},{7,15},{8,0},{9,1},... | collective-permute-start | bytes 245768 | tf_op jit(solution)/shard_map/ppermute | solution.py:174
  90.0 8.6 %collective-permute-start.19 = (bf16[64,640]{1,0:T(8,128)(2,1)}, bf16[64,640]{1,0:T(8,128)(2,1)}, u32[]{:S(2)}, u32[]{:S(2)}) collective-permute-start(bf16[64,640]{1,0:T(8,128)(2,1)} %attend.2.refs_0_), channel_id=1, source_target_pairs={{0,4},{1,5},{2,6},{3,7},{4,0},{5,1},{6,2},{7,3},{8,12},{9,13},{10,... | collective-permute-start | bytes 245768 | tf_op jit(solution)/shard_map/ppermute | solution.py:174
  96.6 4.8 %collective-permute-start.23 = (bf16[64,640]{1,0:T(8,128)(2,1)}, bf16[64,640]{1,0:T(8,128)(2,1)}, u32[]{:S(2)}, u32[]{:S(2)}) collective-permute-start(bf16[64,640]{1,0:T(8,128)(2,1)} %collective-permute-done.21.refs_4_), channel_id=1, source_target_pairs={{0,4},{1,5},{2,6},{3,7},{4,0},{5,1},{6,2},{7,3},{8,12},{9,13},{10,... | collective-permute-start | bytes 245768 | tf_op jit(solution)/shard_map/ppermute | solution.py:174
  96.6 6.4 %collective-permute-start.18 = (bf16[64,640]{1,0:T(8,128)(2,1)}, bf16[64,640]{1,0:T(8,128)(2,1)S(1)}, u32[]{:S(2)}, u32[]{:S(2)}) collective-permute-start(bf16[64,640]{1,0:T(8,128)(2,1)} %attend.2.refs_0_), channel_id=1, source_target_pairs={{0,2},{1,3},{2,0},{3,1},{4,6},{5,7},{6,4},{7,5},{8,10},{9,11},{10,... | collective-permute-start | bytes 245768 | tf_op jit(solution)/shard_map/ppermute | solution.py:174
  97.4 6.5 %collective-permute-start.22 = (bf16[64,640]{1,0:T(8,128)(2,1)}, bf16[64,640]{1,0:T(8,128)(2,1)S(1)}, u32[]{:S(2)}, u32[]{:S(2)}) collective-permute-start(bf16[64,640]{1,0:T(8,128)(2,1)} %collective-permute-done.21.refs_4_), channel_id=1, source_target_pairs={{0,2},{1,3},{2,0},{3,1},{4,6},{5,7},{6,4},{7,5},{8,10},{9,11},{10,... | collective-permute-start | bytes 245768 | tf_op jit(solution)/shard_map/ppermute | solution.py:174
  98.7 6.7 %collective-permute-start.20 = (bf16[64,640]{1,0:T(8,128)(2,1)}, bf16[64,640]{1,0:T(8,128)(2,1)S(1)}, u32[]{:S(2)}, u32[]{:S(2)}) collective-permute-start(bf16[64,640]{1,0:T(8,128)(2,1)} %collective-permute-done.19.refs_2_), channel_id=1, source_target_pairs={{0,2},{1,3},{2,0},{3,1},{4,6},{5,7},{6,4},{7,5},{8,10},{9,11},{10,... | collective-permute-start | bytes 245768 | tf_op jit(solution)/shard_map/ppermute | solution.py:174
  101.4 4.8 %collective-permute-start.24 = (bf16[64,640]{1,0:T(8,128)(2,1)}, bf16[64,640]{1,0:T(8,128)(2,1)S(1)}, u32[]{:S(2)}, u32[]{:S(2)}) collective-permute-start(bf16[64,640]{1,0:T(8,128)(2,1)} %collective-permute-done.23.refs_6_), channel_id=1, source_target_pairs={{0,2},{1,3},{2,0},{3,1},{4,6},{5,7},{6,4},{7,5},{8,10},{9,11},{10,... | collective-permute-start | bytes 245768 | tf_op jit(solution)/shard_map/ppermute | solution.py:174
  106.2 1.9 %copy-start.7 = (bf16[5120,320]{0,1:T(8,128)(2,1)S(1)}, bf16[5120,320]{0,1:T(8,128)(2,1)}, u32[]{:S(2)}) copy-start(bf16[5120,320]{0,1:T(8,128)(2,1)} %param.19) | copy-start | bytes 9830404
  109.0 21.7 %copy-start.2 = (bf16[5120,320]{0,1:T(8,128)(2,1)S(1)}, bf16[5120,320]{0,1:T(8,128)(2,1)}, u32[]{:S(2)}) copy-start(bf16[5120,320]{0,1:T(8,128)(2,1)} %param.16) | copy-start | bytes 9830404
  109.0 21.7 %copy-start.4 = (bf16[5120,320]{0,1:T(8,128)(2,1)S(1)}, bf16[5120,320]{0,1:T(8,128)(2,1)}, u32[]{:S(2)}) copy-start(bf16[5120,320]{0,1:T(8,128)(2,1)} %param.17) | copy-start | bytes 9830404
  109.0 21.7 %copy-start.10 = (f32[16,5120]{1,0:T(8,128)S(1)}, f32[16,5120]{1,0:T(8,128)}, u32[]{:S(2)}) copy-start(f32[16,5120]{1,0:T(8,128)} %get-tuple-element.43.shift_ref) | copy-start | bytes 983044
  113.2 5.5 %collective-permute-start.28 = (bf16[64,640]{1,0:T(8,128)(2,1)S(1)}, bf16[64,640]{1,0:T(8,128)(2,1)S(1)}, u32[]{:S(2)}, u32[]{:S(2)}) collective-permute-start(bf16[64,640]{1,0:T(8,128)(2,1)S(1)} %output.2.refs_3_.current_ref), channel_id=1, source_target_pairs={{0,8},{1,9},{2,10},{3,11},{4,12},{5,13},{6,14},{7,15},{8,0},{9,1},... | collective-permute-start | bytes 245768 | tf_op jit(solution)/shard_map/ppermute | solution.py:174
  113.4 7.7 %collective-permute-start.32 = (bf16[64,640]{1,0:T(8,128)(2,1)S(1)}, bf16[64,640]{1,0:T(8,128)(2,1)S(1)}, u32[]{:S(2)}, u32[]{:S(2)}) collective-permute-start(bf16[64,640]{1,0:T(8,128)(2,1)S(1)} %output.2.refs_3_.current_ref), channel_id=1, source_target_pairs={{0,1},{1,0},{2,3},{3,2},{4,5},{5,4},{6,7},{7,6},{8,9},{9,8},{10,11... | collective-permute-start | bytes 245768 | tf_op jit(solution)/shard_map/ppermute | solution.py:174
  113.4 8.7 %collective-permute-start.26 = (bf16[64,640]{1,0:T(8,128)(2,1)S(1)}, bf16[64,640]{1,0:T(8,128)(2,1)S(1)}, u32[]{:S(2)}, u32[]{:S(2)}) collective-permute-start(bf16[64,640]{1,0:T(8,128)(2,1)S(1)} %output.2.refs_3_.current_ref), channel_id=1, source_target_pairs={{0,4},{1,5},{2,6},{3,7},{4,0},{5,1},{6,2},{7,3},{8,12},{9,13},{10,... | collective-permute-start | bytes 245768 | tf_op jit(solution)/shard_map/ppermute | solution.py:174
  115.2 7.2 %collective-permute-start.25 = (bf16[64,640]{1,0:T(8,128)(2,1)S(1)}, bf16[64,640]{1,0:T(8,128)(2,1)S(1)}, u32[]{:S(2)}, u32[]{:S(2)}) collective-permute-start(bf16[64,640]{1,0:T(8,128)(2,1)S(1)} %output.2.refs_3_.current_ref), channel_id=1, source_target_pairs={{0,2},{1,3},{2,0},{3,1},{4,6},{5,7},{6,4},{7,5},{8,10},{9,11},{10,... | collective-permute-start | bytes 245768 | tf_op jit(solution)/shard_map/ppermute | solution.py:174
  118.7 4.8 %collective-permute-start.30 = (bf16[64,640]{1,0:T(8,128)(2,1)S(1)}, bf16[64,640]{1,0:T(8,128)(2,1)S(1)}, u32[]{:S(2)}, u32[]{:S(2)}) collective-permute-start(bf16[64,640]{1,0:T(8,128)(2,1)S(1)} %collective-permute-done.28.refs_7_), channel_id=1, source_target_pairs={{0,4},{1,5},{2,6},{3,7},{4,0},{5,1},{6,2},{7,3},{8,12},{9,13},{10,... | collective-permute-start | bytes 245768 | tf_op jit(solution)/shard_map/ppermute | solution.py:174
  121.0 3.5 %collective-permute-start.36 = (bf16[64,640]{1,0:T(8,128)(2,1)S(1)}, bf16[64,640]{1,0:T(8,128)(2,1)S(1)}, u32[]{:S(2)}, u32[]{:S(2)}) collective-permute-start(bf16[64,640]{1,0:T(8,128)(2,1)S(1)} %collective-permute-done.28.refs_7_), channel_id=1, source_target_pairs={{0,1},{1,0},{2,3},{3,2},{4,5},{5,4},{6,7},{7,6},{8,9},{9,8},{10,11... | collective-permute-start | bytes 245768 | tf_op jit(solution)/shard_map/ppermute | solution.py:174
  121.0 5.2 %collective-permute-start.29 = (bf16[64,640]{1,0:T(8,128)(2,1)S(1)}, bf16[64,640]{1,0:T(8,128)(2,1)S(1)}, u32[]{:S(2)}, u32[]{:S(2)}) collective-permute-start(bf16[64,640]{1,0:T(8,128)(2,1)S(1)} %collective-permute-done.28.refs_7_), channel_id=1, source_target_pairs={{0,2},{1,3},{2,0},{3,1},{4,6},{5,7},{6,4},{7,5},{8,10},{9,11},{10,... | collective-permute-start | bytes 245768 | tf_op jit(solution)/shard_map/ppermute | solution.py:174
  122.1 4.2 %collective-permute-start.34 = (bf16[64,640]{1,0:T(8,128)(2,1)S(1)}, bf16[64,640]{1,0:T(8,128)(2,1)S(1)}, u32[]{:S(2)}, u32[]{:S(2)}) collective-permute-start(bf16[64,640]{1,0:T(8,128)(2,1)S(1)} %collective-permute-done.26.refs_5_), channel_id=1, source_target_pairs={{0,1},{1,0},{2,3},{3,2},{4,5},{5,4},{6,7},{7,6},{8,9},{9,8},{10,11... | collective-permute-start | bytes 245768 | tf_op jit(solution)/shard_map/ppermute | solution.py:174
  122.3 5.7 %collective-permute-start.27 = (bf16[64,640]{1,0:T(8,128)(2,1)S(1)}, bf16[64,640]{1,0:T(8,128)(2,1)S(1)}, u32[]{:S(2)}, u32[]{:S(2)}) collective-permute-start(bf16[64,640]{1,0:T(8,128)(2,1)S(1)} %collective-permute-done.26.refs_5_), channel_id=1, source_target_pairs={{0,2},{1,3},{2,0},{3,1},{4,6},{5,7},{6,4},{7,5},{8,10},{9,11},{10,... | collective-permute-start | bytes 245768 | tf_op jit(solution)/shard_map/ppermute | solution.py:174
  123.5 6.0 %collective-permute-start.31 = (bf16[64,640]{1,0:T(8,128)(2,1)S(1)}, bf16[64,640]{1,0:T(8,128)(2,1)S(1)}, u32[]{:S(2)}, u32[]{:S(2)}) collective-permute-start(bf16[64,640]{1,0:T(8,128)(2,1)S(1)} %collective-permute-done.30.refs_9_), channel_id=1, source_target_pairs={{0,2},{1,3},{2,0},{3,1},{4,6},{5,7},{6,4},{7,5},{8,10},{9,11},{10,... | collective-permute-start | bytes 245768 | tf_op jit(solution)/shard_map/ppermute | solution.py:174
  124.5 4.9 %collective-permute-start.33 = (bf16[64,640]{1,0:T(8,128)(2,1)S(1)}, bf16[64,640]{1,0:T(8,128)(2,1)S(1)}, u32[]{:S(2)}, u32[]{:S(2)}) collective-permute-start(bf16[64,640]{1,0:T(8,128)(2,1)S(1)} %collective-permute-done.25.refs_4_), channel_id=1, source_target_pairs={{0,1},{1,0},{2,3},{3,2},{4,5},{5,4},{6,7},{7,6},{8,9},{9,8},{10,11... | collective-permute-start | bytes 245768 | tf_op jit(solution)/shard_map/ppermute | solution.py:174
  126.3 3.1 %collective-permute-start.38 = (bf16[64,640]{1,0:T(8,128)(2,1)S(1)}, bf16[64,640]{1,0:T(8,128)(2,1)S(1)}, u32[]{:S(2)}, u32[]{:S(2)}) collective-permute-start(bf16[64,640]{1,0:T(8,128)(2,1)S(1)} %collective-permute-done.30.refs_9_), channel_id=1, source_target_pairs={{0,1},{1,0},{2,3},{3,2},{4,5},{5,4},{6,7},{7,6},{8,9},{9,8},{10,11... | collective-permute-start | bytes 245768 | tf_op jit(solution)/shard_map/ppermute | solution.py:174
  126.3 3.1 %collective-permute-start.37 = (bf16[64,640]{1,0:T(8,128)(2,1)S(1)}, bf16[64,640]{1,0:T(8,128)(2,1)S(1)}, u32[]{:S(2)}, u32[]{:S(2)}) collective-permute-start(bf16[64,640]{1,0:T(8,128)(2,1)S(1)} %collective-permute-done.29.refs_8_), channel_id=1, source_target_pairs={{0,1},{1,0},{2,3},{3,2},{4,5},{5,4},{6,7},{7,6},{8,9},{9,8},{10,11... | collective-permute-start | bytes 245768 | tf_op jit(solution)/shard_map/ppermute | solution.py:174
  128.0 1.4 collective-permute-start.35
  129.4 1.3 collective-permute-start.39
  130.7 1.9 %copy-start.6 = (bf16[5120,320]{0,1:T(8,128)(2,1)S(1)}, bf16[5120,320]{0,1:T(8,128)(2,1)}, u32[]{:S(2)}) copy-start(bf16[5120,320]{0,1:T(8,128)(2,1)} %param.18) | copy-start | bytes 9830404
  132.6 37.4 %copy-start.8 = (bf16[5120,320]{0,1:T(8,128)(2,1)S(1)}, bf16[5120,320]{0,1:T(8,128)(2,1)}, u32[]{:S(2)}) copy-start(bf16[5120,320]{0,1:T(8,128)(2,1)} %param.19) | copy-start | bytes 9830404
  139.7 9.3 %collective-permute-start.40 = (bf16[320,320]{1,0:T(8,128)(2,1)S(1)}, bf16[320,320]{1,0:T(8,128)(2,1)S(1)}, u32[]{:S(2)}, u32[]{:S(2)}) collective-permute-start(bf16[320,320]{1,0:T(8,128)(2,1)S(1)} %get-tuple-element.39), channel_id=1, source_target_pairs={{0,1},{1,0},{2,3},{3,2},{4,5},{5,4},{6,7},{7,6},{8,9},{9,8},{10,11... | collective-permute-start | bytes 614408 | tf_op jit(solution)/shard_map/ppermute | solution.py:174
  153.8 6.8 %collective-permute-start.44 = (bf16[64,640]{1,0:T(8,128)(2,1)S(1)}, bf16[64,640]{1,0:T(8,128)(2,1)S(1)}, u32[]{:S(2)}, u32[]{:S(2)}) collective-permute-start(bf16[64,640]{1,0:T(8,128)(2,1)S(1)} %attend.3.refs_0_), channel_id=1, source_target_pairs={{0,8},{1,9},{2,10},{3,11},{4,12},{5,13},{6,14},{7,15},{8,0},{9,1},... | collective-permute-start | bytes 245768 | tf_op jit(solution)/shard_map/ppermute | solution.py:174
  154.3 8.3 %collective-permute-start.42 = (bf16[64,640]{1,0:T(8,128)(2,1)S(1)}, bf16[64,640]{1,0:T(8,128)(2,1)S(1)}, u32[]{:S(2)}, u32[]{:S(2)}) collective-permute-start(bf16[64,640]{1,0:T(8,128)(2,1)S(1)} %attend.3.refs_0_), channel_id=1, source_target_pairs={{0,4},{1,5},{2,6},{3,7},{4,0},{5,1},{6,2},{7,3},{8,12},{9,13},{10,... | collective-permute-start | bytes 245768 | tf_op jit(solution)/shard_map/ppermute | solution.py:174
  160.6 4.4 %collective-permute-start.46 = (bf16[64,640]{1,0:T(8,128)(2,1)S(1)}, bf16[64,640]{1,0:T(8,128)(2,1)S(1)}, u32[]{:S(2)}, u32[]{:S(2)}) collective-permute-start(bf16[64,640]{1,0:T(8,128)(2,1)S(1)} %collective-permute-done.44.refs_4_), channel_id=1, source_target_pairs={{0,4},{1,5},{2,6},{3,7},{4,0},{5,1},{6,2},{7,3},{8,12},{9,13},{10,... | collective-permute-start | bytes 245768 | tf_op jit(solution)/shard_map/ppermute | solution.py:174
  160.6 5.3 %collective-permute-start.41 = (bf16[64,640]{1,0:T(8,128)(2,1)S(1)}, bf16[64,640]{1,0:T(8,128)(2,1)S(1)}, u32[]{:S(2)}, u32[]{:S(2)}) collective-permute-start(bf16[64,640]{1,0:T(8,128)(2,1)S(1)} %attend.3.refs_0_), channel_id=1, source_target_pairs={{0,2},{1,3},{2,0},{3,1},{4,6},{5,7},{6,4},{7,5},{8,10},{9,11},{10,... | collective-permute-start | bytes 245768 | tf_op jit(solution)/shard_map/ppermute | solution.py:174
  161.4 6.3 %collective-permute-start.45 = (bf16[64,640]{1,0:T(8,128)(2,1)S(1)}, bf16[64,640]{1,0:T(8,128)(2,1)S(1)}, u32[]{:S(2)}, u32[]{:S(2)}) collective-permute-start(bf16[64,640]{1,0:T(8,128)(2,1)S(1)} %collective-permute-done.44.refs_4_), channel_id=1, source_target_pairs={{0,2},{1,3},{2,0},{3,1},{4,6},{5,7},{6,4},{7,5},{8,10},{9,11},{10,... | collective-permute-start | bytes 245768 | tf_op jit(solution)/shard_map/ppermute | solution.py:174
  162.7 6.4 %collective-permute-start.43 = (bf16[64,640]{1,0:T(8,128)(2,1)S(1)}, bf16[64,640]{1,0:T(8,128)(2,1)S(1)}, u32[]{:S(2)}, u32[]{:S(2)}) collective-permute-start(bf16[64,640]{1,0:T(8,128)(2,1)S(1)} %collective-permute-done.42.refs_2_), channel_id=1, source_target_pairs={{0,2},{1,3},{2,0},{3,1},{4,6},{5,7},{6,4},{7,5},{8,10},{9,11},{10,... | collective-permute-start | bytes 245768 | tf_op jit(solution)/shard_map/ppermute | solution.py:174
  165.1 4.9 %collective-permute-start.47 = (bf16[64,640]{1,0:T(8,128)(2,1)S(1)}, bf16[64,640]{1,0:T(8,128)(2,1)S(1)}, u32[]{:S(2)}, u32[]{:S(2)}) collective-permute-start(bf16[64,640]{1,0:T(8,128)(2,1)S(1)} %collective-permute-done.46.refs_6_), channel_id=1, source_target_pairs={{0,2},{1,3},{2,0},{3,1},{4,6},{5,7},{6,4},{7,5},{8,10},{9,11},{10,... | collective-permute-start | bytes 245768 | tf_op jit(solution)/shard_map/ppermute | solution.py:174
  (16 other events, 12.8 us)

commit v3 on v2

--- a/solution.py
+++ b/solution.py
@@ -192,7 +192,7 @@
 
 VMEM_SPEC = pl.BlockSpec(memory_space=pltpu.VMEM)
 SMEM_SPEC = pl.BlockSpec(memory_space=pltpu.SMEM)
-ANY_SPEC = pl.BlockSpec(memory_space=pl.ANY)
+HBM_SPEC = pl.BlockSpec(memory_space=pltpu.HBM)
 
 
 def kernel_params(mebibytes):
@@ -204,7 +204,7 @@
     return (2 * (position % chips) + position // chips + step + 1) % spans
 
 
-def project_kernel(step, spans, place_ref, shift_ref, scale_ref, gain_ref, incoming_ref, *refs):
+def project_kernel(step, spans, place_ref, gain_ref, table_ref, incoming_ref, *refs):
     chips = spans // 2
     weight_refs, refs = refs[:3], refs[3:]
     mine, others = refs[:chips], refs[chips : 2 * chips]
@@ -213,7 +213,7 @@
     refs = refs[3:]
     if step == 0:
         current_ref, refs = refs[0], refs[1:]
-    state, modulated, sems = refs
+    state, modulated, table, entering, shift_ref, scale_ref, weights, sems = refs
     chip, core = place_ref[0], place_ref[1]
     tokens, width = modulated.shape
     half = tokens // 2
@@ -221,7 +221,9 @@
     pair = 2 * rows
     cols = weight_refs[0].shape[0]
     first = core == 0
-    copies = []
+    copies = [pltpu.make_async_copy(table_ref, table, sems.at[spans])]
+    if step == 0:
+        copies.append(pltpu.make_async_copy(incoming_ref, entering, sems.at[spans + 1]))
     for side, blocks in enumerate((mine, others)):
         owner = core if side == 0 else 1 - core
         for mask in range(chips):
@@ -234,12 +236,18 @@
             copies.append(
                 pltpu.make_async_copy(blocks[mask], target, sems.at[side * chips + mask])
             )
-    for copy in copies:
+    fetches = [
+        pltpu.make_async_copy(weight_refs[i], weights.at[i], sems.at[spans + 2 + i])
+        for i in range(3)
+    ]
+    for copy in copies + fetches:
         copy.start()
     for copy in copies:
         copy.wait()
+    shift_ref[...] = table[0].astype(jnp.float32)
+    scale_ref[...] = table[1].astype(jnp.float32) + 1.0
     if step == 0:
-        state[spans - 1] = incoming_ref[...]
+        state[spans - 1] = entering[step]
         lanes = pl.ds(pl.multiple_of(chip * 2 * cols, 2 * cols), 2 * cols)
         for slab in range(chips // 2):
             at = core * chips + 2 * slab
@@ -273,12 +281,13 @@
                 )
                 for ref in (scale_ref, shift_ref)
             )
-            modulated[band, part] = (x * (1.0 + scale) + shift).astype(jnp.bfloat16)
+            modulated[band, part] = (x * scale + shift).astype(jnp.bfloat16)
     for i in range(3):
+        fetches[i].wait()
 
         def add(step_k, total):
             part = pl.ds(pl.multiple_of(step_k * piece, piece), piece)
-            return total + contract_last(weight_refs[i][:, part], modulated[:, part])
+            return total + contract_last(weights[i, :, part], modulated[:, part])
 
         product = lax.fori_loop(0, pieces, add, jnp.zeros((cols, tokens), jnp.float32))
         if i < 2:
@@ -296,8 +305,8 @@
             send_ref[band, :] = product.astype(jnp.bfloat16)
 
 
-def project(step, spans, place, shift, scale, gain, incoming, mine, others, weights):
-    rows = incoming.shape[0]
+def project(step, spans, place, gain, table, incoming, mine, others, weights):
+    rows = incoming.shape[1]
     tokens = spans * rows
     cols, width = weights[0].shape
     half = tokens // 2
@@ -311,22 +320,33 @@
     return pl.pallas_call(
         functools.partial(project_kernel, step, spans),
         out_shape=out_shape,
-        in_specs=[SMEM_SPEC] + [VMEM_SPEC] * 7 + [ANY_SPEC] * (2 * len(mine)),
+        in_specs=[SMEM_SPEC, VMEM_SPEC] + [HBM_SPEC] * (5 + 2 * len(mine)),
         out_specs=[VMEM_SPEC] * len(out_shape),
         scratch_shapes=[
             pltpu.VMEM(state, jnp.bfloat16),
             pltpu.VMEM((tokens, width), jnp.bfloat16),
-            pltpu.SemaphoreType.DMA((spans,)),
+            pltpu.VMEM(table.shape, jnp.bfloat16),
+            pltpu.VMEM(incoming.shape, jnp.bfloat16),
+            pltpu.VMEM((spans, width), jnp.float32),
+            pltpu.VMEM((spans, width), jnp.float32),
+            pltpu.VMEM((3, cols, width), jnp.bfloat16),
+            pltpu.SemaphoreType.DMA((spans + 5,)),
         ],
         compiler_params=kernel_params(24),
         name="project",
-    )(place, shift, scale, gain, incoming, *weights, *mine, *others)
+    )(place, gain, table, incoming, *weights, *mine, *others)
 
 
 def attend_kernel(
-    step, spans, head_size, place_ref, own_ref, got_ref, text_ref, more_ref, squares_ref,
-    out_ref, queries, keys, values,
+    step, spans, head_size, place_ref, own_ref, got_ref, squares_ref, text_hbm, more_hbm,
+    out_ref, queries, keys, values, text_ref, more_ref, sems,
 ):
+    copies = [
+        pltpu.make_async_copy(text_hbm, text_ref, sems.at[0]),
+        pltpu.make_async_copy(more_hbm, more_ref, sems.at[1]),
+    ]
+    for copy in copies:
+        copy.start()
     core = place_ref[1]
     first = core == 0
     half, width = queries.shape
@@ -355,6 +375,8 @@
     key_block = lax.broadcasted_iota(jnp.int32, shape, 1) // rows
     allowed = span_at(own_block, step, spans) >= span_at(key_block, step, spans)
     text_rows = text_ref.shape[0] * text_ref.shape[2]
+    for copy in copies:
+        copy.wait()
     for head in range(width // head_size):
         lanes = slice(head * head_size, (head + 1) * head_size)
         q = queries[:, lanes]
@@ -393,37 +415,52 @@
     return pl.pallas_call(
         functools.partial(attend_kernel, step, spans, head_size),
         out_shape=jax.ShapeDtypeStruct((half, 2 * cols), jnp.bfloat16),
-        in_specs=[SMEM_SPEC] + [VMEM_SPEC] * 5,
+        in_specs=[SMEM_SPEC] + [VMEM_SPEC] * 3 + [HBM_SPEC] * 2,
         out_specs=VMEM_SPEC,
         scratch_shapes=[
             pltpu.VMEM((half, 2 * cols), jnp.bfloat16),
             pltpu.VMEM((tokens, 2 * cols), jnp.bfloat16),
             pltpu.VMEM((tokens, 2 * cols), jnp.bfloat16),
+            pltpu.VMEM(text.shape, jnp.bfloat16),
+            pltpu.VMEM(more.shape, jnp.bfloat16),
+            pltpu.SemaphoreType.DMA((2,)),
         ],
         compiler_params=kernel_params(16),
         name="attend",
-    )(place, own, got, text, more, squares)
+    )(place, own, got, squares, text, more)
 
 
 def output_kernel(
     step, spans, last, place_ref, current_ref, gate_ref, incoming_ref, own_ref, other_ref, *refs
 ):
     chips = spans // 2
-    blocks, (out_ref, totals) = refs[:chips], refs[chips:]
+    blocks, (out_ref, totals, weights, sems) = refs[:chips], refs[chips:]
     chip, core = place_ref[0], place_ref[1]
     first = core == 0
     half, width = current_ref.shape
     cols = width // 2
     rows = 2 * half // spans
-    mine = jnp.zeros((cols, half), jnp.float32)
-    other = jnp.zeros((cols, half), jnp.float32)
+    fetches = []
     for mask in range(chips):
         lanes = pl.ds(pl.multiple_of((chip ^ mask) * width, width), width)
+        for side, ref in enumerate((own_ref, other_ref)):
+            fetches.append(
+                pltpu.make_async_copy(
+                    ref.at[:, lanes], weights.at[mask, side], sems.at[mask, side]
+                )
+            )
+    for fetch in fetches:
+        fetch.start()
+    mine = jnp.zeros((half, cols), jnp.float32)
+    other = jnp.zeros((half, cols), jnp.float32)
+    for mask in range(chips):
         block = blocks[mask][...]
-        mine = mine + contract_last(own_ref[:, lanes], block)
-        other = other + contract_last(other_ref[:, lanes], block)
-    both = jnp.concatenate([jnp.where(first, mine, other), jnp.where(first, other, mine)], axis=0)
-    totals[...] = both.T
+        fetches[2 * mask].wait()
+        mine = mine + contract_last(block, weights[mask, 0])
+        fetches[2 * mask + 1].wait()
+        other = other + contract_last(block, weights[mask, 1])
+    totals[:, :cols] = jnp.where(first, mine, other)
+    totals[:, cols:] = jnp.where(first, other, mine)
     for block in range(chips):
         band = slice(block * rows, (block + 1) * rows)
         places = [span_at(block + e * chips, step, spans) for e in range(2)]
@@ -453,9 +490,13 @@
         out_shape=jax.ShapeDtypeStruct(
             (chips, rows, width) if last else (half, width), jnp.bfloat16
         ),
-        in_specs=[SMEM_SPEC] + [VMEM_SPEC] * (5 + chips),
+        in_specs=[SMEM_SPEC] + [VMEM_SPEC] * 3 + [HBM_SPEC] * 2 + [VMEM_SPEC] * chips,
         out_specs=VMEM_SPEC,
-        scratch_shapes=[pltpu.VMEM((half, width), jnp.float32)],
+        scratch_shapes=[
+            pltpu.VMEM((half, width), jnp.float32),
+            pltpu.VMEM((chips, 2, width // 2, width), jnp.bfloat16),
+            pltpu.SemaphoreType.DMA((chips, 2)),
+        ],
         compiler_params=kernel_params(16),
         name="output",
     )(place, current, gate, incoming, own, other, *blocks)
@@ -528,29 +569,28 @@
     mine = gathered_over_chips(hidden)
     others = [swapped(block, 1) for block in mine]
     picked = (levels[:, None] == jnp.arange(mod_table.shape[0])[None, :]).astype(mod_table.dtype)
-    shift, scale, gate = jnp.einsum(
-        "sl,ltd->tsd", picked, mod_table, preferred_element_type=jnp.float32
-    )
-    gate = lax.dynamic_slice_in_dim(gate, chip * 2 * cols, 2 * cols, 1)
+    table = jnp.einsum("sl,ltd->tsd", picked, mod_table, preferred_element_type=jnp.float32)
+    table = table.astype(jnp.bfloat16)
+    gate = lax.dynamic_slice_in_dim(table[2], chip * 2 * cols, 2 * cols, 1).astype(jnp.float32)
     gain = lax.dynamic_slice_in_dim(jnp.stack([query_gain, key_gain]), own_index * cols, cols, 1).T
     weights = [w.T for w in (query_weight, key_weight, value_weight)]
     output_own = output_weight.T
     output_other = swapped(output_own, 1)
     text = arrange(spans, text_keys, text_values)
-    text, *mine = lax.optimization_barrier((text, *mine))
+    text = lax.optimization_barrier((text, *mine))[0]
     text = lax.all_to_all(text, "queue", split_axis=0, concat_axis=0, tiled=True)
-    more = swapped(text, 1)
     current = None
     for step in range(STEPS):
         last = step == STEPS - 1
         own, send, squares, *rest = project(
-            step, spans, place, shift, scale, gain, incoming[step], mine, others, weights
+            step, spans, place, gain, table, incoming, mine, others, weights
         )
         got = swapped(send, 1)
         squares = lax.all_to_all(squares, "queue", split_axis=0, concat_axis=0, tiled=True)
         if step == 0:
             current = rest[0]
-            got, output_other = lax.optimization_barrier((got, output_other))
+            text = lax.optimization_barrier((text, send))[0]
+            more = swapped(text, 1)
         block = attend(step, spans, head_size, place, own, got, text, more, squares)
         result = output(
             step,

time: 186 us -> 175 us (0.941)
  waiting for transfers between devices: 56.9 us -> 35.9 us
  blocking collectives: 19.4 us -> 31.4 us
  Pallas kernels: 35.4 us -> 41.3 us
  local copies, waits for them, and re-layouts: 27.8 us -> 23.2 us
  starting transfers between devices: 43.1 us -> 39.4 us
    all_to_all x1, waiting for transfers between devices: 14.2 us -> 0.01 us  [paired_device(): lax.all_to_all(text, 'queue', split_axis=0, concat_axis=0, tiled=True)]
    all_to_all x1 -> x2, blocking collectives: 9.06 us -> 21.1 us  [paired_device(): lax.all_to_all(squares, 'queue', split_axis=0, concat_axis=0, tiled=True)]
    all_to_all x1 -> x0, waiting for transfers between devices: 6.47 us -> none  [paired_device(): lax.all_to_all(squares, 'queue', split_axis=0, concat_axis=0, tiled=True)]
    all_to_all x1 -> x0, starting transfers between devices: 4.94 us -> none  [paired_device(): lax.all_to_all(squares, 'queue', split_axis=0, concat_axis=0, tiled=True)]
    pallas_call x2, Pallas kernels: 8.11 us -> 11.8 us  [output(): pl.pallas_call(functools.partial(output_kernel, step, spans, last), out_s...]
    unnamed x61 -> x57, local copies, waits for them, and re-layouts: 24.5 us -> 21.6 us
  transfers between devices with their start and end apart: 50 -> 49, of which waited for: 25 -> 25; matrix products, arithmetic and copies ran while one was open for 3% -> 3% of each run, Pallas kernels for 5% -> 9%
where the time goes in v3:
time: 175 us; the launch traced here: 174 us
  Pallas kernels  41.3 us (24%)
  starting transfers between devices  39.4 us (23%)
  waiting for transfers between devices  35.9 us (21%)
  blocking collectives  31.4 us (18%)
  local copies, waits for them, and re-layouts  23.2 us (13%)
    ppermute x48, waiting for transfers between devices, swapped(): lax.ppermute(value, 'queue', [(source, source ^ bit) for source in range(...  35.9 us
    ppermute x48, starting transfers between devices, swapped(): lax.ppermute(value, 'queue', [(source, source ^ bit) for source in range(...  33.8 us
    unnamed x57, local copies, waits for them, and re-layouts  21.6 us
    all_to_all x2, blocking collectives, paired_device(): lax.all_to_all(squares, 'queue', split_axis=0, concat_axis=0, tiled=True)  21.1 us
    pallas_call x2, Pallas kernels, project(): pl.pallas_call(functools.partial(project_kernel, step, spans), out_shape=...  18 us
    pallas_call x2, Pallas kernels, output(): pl.pallas_call(functools.partial(output_kernel, step, spans, last), out_s...  11.8 us
    pallas_call x2, Pallas kernels, attend(): pl.pallas_call(functools.partial(attend_kernel, step, spans, head_size),...  10.8 us
    all_to_all x1, blocking collectives, paired_device(): lax.all_to_all(result, 'queue', split_axis=0, concat_axis=0, tiled=True,...  10.3 us
  transfers between devices with their start and end apart: 49, of which 25 were waited for; matrix products, arithmetic and copies ran while one was open for 3% of the time, Pallas kernels for 9%

profile of v3, /device:TPU:0, one launch (start us, length us, event | category | flops | bytes accessed | tf_op | source)
XLA Modules:
  0.0 173.5 jit_solution(8792306242845830092)
XLA Ops:
  0.0 4.0 %collective-permute-start.3 = (bf16[8,5120]{1,0:T(8,128)(2,1)}, bf16[8,5120]{1,0:T(8,128)(2,1)}, u32[]{:S(2)}, u32[]{:S(2)}) collective-permute-start(bf16[8,5120]{1,0:T(8,128)(2,1)} %refs_3_.1), channel_id=1, source_target_pairs={{0,8},{1,9},{2,10},{3,11},{4,12},{5,13},{6,14},{7,15},{8,0},{9,1},... | collective-permute-start | bytes 245768 | tf_op jit(solution)/shard_map/ppermute | solution.py:174
  4.0 1.6 collective-permute-start.1
  5.6 2.5 %collective-permute-done.3.refs_7_ = bf16[8,5120]{1,0:T(8,128)(2,1)} collective-permute-done((bf16[8,5120]{1,0:T(8,128)(2,1)}, bf16[8,5120]{1,0:T(8,128)(2,1)}, u32[]{:S(2)}, u32[]{:S(2)}) %collective-permute-start.3) | collective-permute-done | bytes 81952 | tf_op jit(solution)/shard_map/ppermute | solution.py:174
  8.1 1.2 collective-permute-start.5
  9.3 1.5 collective-permute-start
  11.3 1.5 collective-permute-start.2
  12.9 1.8 %collective-permute-start.6 = (bf16[8,5120]{1,0:T(8,128)(2,1)S(1)}, bf16[8,5120]{1,0:T(8,128)(2,1)}, u32[]{:S(2)}, u32[]{:S(2)}) collective-permute-start(bf16[8,5120]{1,0:T(8,128)(2,1)S(1)} %collective-permute-done.5.refs_9_), channel_id=1, source_target_pairs={{0,2},{1,3},{2,0},{3,1},{4,6},{5,7},{6,4},{7,5},{8,10},{9,11},{10,... | collective-permute-start | bytes 245768 | tf_op jit(solution)/shard_map/ppermute | solution.py:174
  14.6 1.0 copy-done.16
  15.6 1.0 copy-done.17
  16.7 0.8 copy-done.11
  18.1 0.9 collective-permute-done.6.refs_10_
  19.0 5.5 %all-to-all-start.1 = ((bf16[16,2,16,640]{3,2,1,0:T(8,128)(2,1)}), bf16[16,2,16,640]{3,2,1,0:T(8,128)(2,1)}, u32[]{:S(2)}, u32[]{:S(2)}) async-start(bf16[16,2,16,640]{3,2,1,0:T(8,128)(2,1)} %copy-done.11), calls=%async_computation.1 | async-start | bytes 1310720 | tf_op jit(solution)/shard_map/all_to_all | solution.py:581
  24.9 1.2 fusion.table_ref
  27.0 0.8 copy.16
  30.1 1.9 %copy-done.1 = bf16[5120,320]{0,1:T(8,128)(2,1)S(1)} copy-done((bf16[5120,320]{0,1:T(8,128)(2,1)S(1)}, bf16[5120,320]{0,1:T(8,128)(2,1)}, u32[]{:S(2)}) %copy-start.1) | copy-done | bytes 3276824
  32.1 1.9 %copy-done.3 = bf16[5120,320]{0,1:T(8,128)(2,1)S(1)} copy-done((bf16[5120,320]{0,1:T(8,128)(2,1)S(1)}, bf16[5120,320]{0,1:T(8,128)(2,1)}, u32[]{:S(2)}) %copy-start.3) | copy-done | bytes 3276824
  34.0 1.9 %copy-done.5 = bf16[5120,320]{0,1:T(8,128)(2,1)S(1)} copy-done((bf16[5120,320]{0,1:T(8,128)(2,1)S(1)}, bf16[5120,320]{0,1:T(8,128)(2,1)}, u32[]{:S(2)}) %copy-start.5) | copy-done | bytes 3276824
  35.9 0.9 copy-done.12
  36.8 0.9 copy-done.14
  37.8 0.9 copy-done.22
  38.6 9.4 %project.2 = (bf16[320,320]{1,0:T(8,128)(2,1)S(1)}, bf16[320,320]{1,0:T(8,128)(2,1)S(1)}, f32[16,2,128]{2,1,0:T(2,128)S(1)}, bf16[64,640]{1,0:T(8,128)(2,1)S(1)}) custom-call(s32[2]{0:T(128)S(1)} %pad_add_fusion.place_ref, f32[320,2]{1,0:T(8,128)S(1)} %bitcast.29, bf16[3,16,5120]{2,1,0:T(8,128)(2,1)S(1)} %fusion.table_ref, ...), custom_call_target="tpu_custom_call" | custom-call | tf_op jit(solution)/shard_map/project/pallas_call | solution.py:320
  50.6 12.0 %all_to_all.20.squares_ref = f32[16,2,128]{2,1,0:T(2,128)S(1)} all-to-all(f32[16,2,128]{2,1,0:T(2,128)S(1)} %get-tuple-element.17), channel_id=1, replica_groups=mesh['groups'=2,'queue'=16] {'queue'}, dimensions={0} | all-to-all | bytes 32768 | tf_op jit(solution)/shard_map/all_to_all | solution.py:589
  62.6 0.9 copy-done.19
  63.6 5.7 %attend.2.refs_0_ = bf16[64,640]{1,0:T(8,128)(2,1)} custom-call(s32[2]{0:T(128)S(1)} %pad_add_fusion.place_ref, bf16[320,320]{1,0:T(8,128)(2,1)S(1)} %copy-done.19, bf16[320,320]{1,0:T(8,128)(2,1)S(1)} %collective-permute-done.16.got_ref, f32[16,2,128]{2,1,0:T(2,128)S(1)} %all_to_all.20.squares_ref, bf16[16,2,16,640]{3,2,1,0:T(8,128)(2,1)} %all-to-all-done.1.text_hbm, ...), custom_call_target="tpu_custom_call" | custom-call | tf_op jit(solution)/shard_map/attend/pallas_call | solution.py:415
  69.3 0.8 copy-done.9
  71.2 6.0 %collective-permute-done.21.refs_4_ = bf16[64,640]{1,0:T(8,128)(2,1)} collective-permute-done((bf16[64,640]{1,0:T(8,128)(2,1)}, bf16[64,640]{1,0:T(8,128)(2,1)}, u32[]{:S(2)}, u32[]{:S(2)}) %collective-permute-start.21) | collective-permute-done | bytes 81952 | tf_op jit(solution)/shard_map/ppermute | solution.py:174
  77.2 0.9 slice_bitcast_fusion.incoming_ref
  78.8 0.8 collective-permute-start.18
  79.6 1.2 collective-permute-start.22
  80.8 0.8 collective-permute-start.20
  82.0 0.9 collective-permute-start.24
  84.4 1.8 %collective-permute-done.22.refs_5_ = bf16[64,640]{1,0:T(8,128)(2,1)S(1)} collective-permute-done((bf16[64,640]{1,0:T(8,128)(2,1)}, bf16[64,640]{1,0:T(8,128)(2,1)S(1)}, u32[]{:S(2)}, u32[]{:S(2)}) %collective-permute-start.22) | collective-permute-done | bytes 81952 | tf_op jit(solution)/shard_map/ppermute | solution.py:174
  86.1 1.4 collective-permute-done.20.refs_3_
  87.5 0.9 collective-permute-done.24.refs_7_
  88.4 1.9 %copy-done.7 = bf16[5120,320]{0,1:T(8,128)(2,1)S(1)} copy-done((bf16[5120,320]{0,1:T(8,128)(2,1)S(1)}, bf16[5120,320]{0,1:T(8,128)(2,1)}, u32[]{:S(2)}) %copy-start.7) | copy-done | bytes 3276824
  90.3 0.9 copy-done.24
  91.2 6.5 %output.2.refs_3_.current_ref = bf16[64,640]{1,0:T(8,128)(2,1)S(1)} custom-call(s32[2]{0:T(128)S(1)} %pad_add_fusion.place_ref, bf16[64,640]{1,0:T(8,128)(2,1)S(1)} %copy-done.24, f32[16,640]{1,0:T(8,128)S(1)} %bitcast_convert_fusion.gate_ref, bf16[8,5120]{1,0:T(8,128)(2,1)S(1)} %slice_bitcast_fusion.incoming_ref, bf16[320,5120]{1,0:T(8,128)(2,1)S(1)} %bitcast.27, ...), custom_call_target="tpu_custom_call" | custom-call | tf_op jit(solution)/shard_map/output/pallas_call | solution.py:488
  97.9 1.8 %collective-permute-start.26 = (bf16[64,640]{1,0:T(8,128)(2,1)S(1)}, bf16[64,640]{1,0:T(8,128)(2,1)S(1)}, u32[]{:S(2)}, u32[]{:S(2)}) collective-permute-start(bf16[64,640]{1,0:T(8,128)(2,1)S(1)} %output.2.refs_3_.current_ref), channel_id=1, source_target_pairs={{0,4},{1,5},{2,6},{3,7},{4,0},{5,1},{6,2},{7,3},{8,12},{9,13},{10,... | collective-permute-start | bytes 245768 | tf_op jit(solution)/shard_map/ppermute | solution.py:174
  99.7 1.1 collective-permute-start.25
  100.8 2.5 %collective-permute-done.28.refs_7_ = bf16[64,640]{1,0:T(8,128)(2,1)S(1)} collective-permute-done((bf16[64,640]{1,0:T(8,128)(2,1)S(1)}, bf16[64,640]{1,0:T(8,128)(2,1)S(1)}, u32[]{:S(2)}, u32[]{:S(2)}) %collective-permute-start.28) | collective-permute-done | bytes 81952 | tf_op jit(solution)/shard_map/ppermute | solution.py:174
  103.3 2.3 %collective-permute-start.30 = (bf16[64,640]{1,0:T(8,128)(2,1)S(1)}, bf16[64,640]{1,0:T(8,128)(2,1)S(1)}, u32[]{:S(2)}, u32[]{:S(2)}) collective-permute-start(bf16[64,640]{1,0:T(8,128)(2,1)S(1)} %collective-permute-done.28.refs_7_), channel_id=1, source_target_pairs={{0,4},{1,5},{2,6},{3,7},{4,0},{5,1},{6,2},{7,3},{8,12},{9,13},{10,... | collective-permute-start | bytes 245768 | tf_op jit(solution)/shard_map/ppermute | solution.py:174
  105.6 1.1 collective-permute-start.29
  106.9 1.0 collective-permute-start.27
  108.0 1.1 collective-permute-start.31
  109.1 1.8 %collective-permute-done.29.refs_8_ = bf16[64,640]{1,0:T(8,128)(2,1)S(1)} collective-permute-done((bf16[64,640]{1,0:T(8,128)(2,1)S(1)}, bf16[64,640]{1,0:T(8,128)(2,1)S(1)}, u32[]{:S(2)}, u32[]{:S(2)}) %collective-permute-start.29) | collective-permute-done | bytes 81952 | tf_op jit(solution)/shard_map/ppermute | solution.py:174
  111.4 1.2 collective-permute-done.27.refs_6_
  112.6 1.4 collective-permute-done.31.refs_10_
  114.0 1.2 collective-permute-done.39.refs_18_
  115.3 1.9 %copy-done.6 = bf16[5120,320]{0,1:T(8,128)(2,1)S(1)} copy-done((bf16[5120,320]{0,1:T(8,128)(2,1)S(1)}, bf16[5120,320]{0,1:T(8,128)(2,1)}, u32[]{:S(2)}) %copy-start.6) | copy-done | bytes 3276824
  117.2 0.9 copy-done.15
  118.1 8.6 %project.3 = (bf16[320,320]{1,0:T(8,128)(2,1)S(1)}, bf16[320,320]{1,0:T(8,128)(2,1)S(1)}, f32[16,2,128]{2,1,0:T(2,128)S(1)}) custom-call(s32[2]{0:T(128)S(1)} %pad_add_fusion.place_ref, f32[320,2]{1,0:T(8,128)S(1)} %bitcast.30, bf16[3,16,5120]{2,1,0:T(8,128)(2,1)S(1)} %fusion.table_ref, bf16[2,8,5120]{2,1,0:T(8,128)(2,1)S(1)} %copy-done.15, ...), custom_call_target="tpu_custom_call" | custom-call | tf_op jit(solution)/shard_map/project/pallas_call | solution.py:320
  127.0 9.1 %all_to_all.21.squares_ref = f32[16,2,128]{2,1,0:T(2,128)S(1)} all-to-all(f32[16,2,128]{2,1,0:T(2,128)S(1)} %get-tuple-element.22), channel_id=1, replica_groups=mesh['groups'=2,'queue'=16] {'queue'}, dimensions={0} | all-to-all | bytes 32768 | tf_op jit(solution)/shard_map/all_to_all | solution.py:589
  136.0 5.1 %attend.3.refs_0_ = bf16[64,640]{1,0:T(8,128)(2,1)S(1)} custom-call(s32[2]{0:T(128)S(1)} %pad_add_fusion.place_ref, bf16[320,320]{1,0:T(8,128)(2,1)S(1)} %get-tuple-element.20.own_ref, bf16[320,320]{1,0:T(8,128)(2,1)S(1)} %collective-permute-done.40.got_ref, f32[16,2,128]{2,1,0:T(2,128)S(1)} %all_to_all.21.squares_ref, ...), custom_call_target="tpu_custom_call" | custom-call | tf_op jit(solution)/shard_map/attend/pallas_call | solution.py:415
  142.2 5.7 %collective-permute-done.44.refs_4_ = bf16[64,640]{1,0:T(8,128)(2,1)S(1)} collective-permute-done((bf16[64,640]{1,0:T(8,128)(2,1)S(1)}, bf16[64,640]{1,0:T(8,128)(2,1)S(1)}, u32[]{:S(2)}, u32[]{:S(2)}) %collective-permute-start.44) | collective-permute-done | bytes 81952 | tf_op jit(solution)/shard_map/ppermute | solution.py:174
  147.9 0.8 collective-permute-start.41
  148.7 1.2 collective-permute-start.45
  149.9 0.8 collective-permute-start.43
  150.8 1.6 collective-permute-done.46.refs_6_
  152.4 0.8 collective-permute-start.47
  153.3 1.8 %collective-permute-done.45.refs_5_ = bf16[64,640]{1,0:T(8,128)(2,1)S(1)} collective-permute-done((bf16[64,640]{1,0:T(8,128)(2,1)S(1)}, bf16[64,640]{1,0:T(8,128)(2,1)S(1)}, u32[]{:S(2)}, u32[]{:S(2)}) %collective-permute-start.45) | collective-permute-done | bytes 81952 | tf_op jit(solution)/shard_map/ppermute | solution.py:174
  155.0 1.4 collective-permute-done.43.refs_3_
  156.4 0.9 collective-permute-done.47.refs_7_
  157.3 5.3 %output.3 = bf16[8,8,640]{2,1,0:T(8,128)(2,1)S(1)} custom-call(s32[2]{0:T(128)S(1)} %pad_add_fusion.place_ref, bf16[64,640]{1,0:T(8,128)(2,1)S(1)} %output.2.refs_3_.current_ref, f32[16,640]{1,0:T(8,128)S(1)} %bitcast_convert_fusion.gate_ref, bf16[8,5120]{1,0:T(8,128)(2,1)S(1)} %slice_bitcast_fusion.incoming_ref, bf16[320,5120]{1,0:T(8,128)(2,1)S(1)} %bitcast.28, ...), custom_call_target="tpu_custom_call" | custom-call | tf_op jit(solution)/shard_map/output/pallas_call | solution.py:488
  162.6 10.3 %all_to_all.22.in_ref = bf16[8,8,640]{2,1,0:T(8,128)(2,1)S(1)} all-to-all(bf16[8,8,640]{2,1,0:T(8,128)(2,1)S(1)} %output.3), channel_id=1, replica_groups={{0,2,4,6,8,10,12,14},{1,3,5,7,9,11,13,15},{16,18,20,22,24,26,28,30},{17..., dimensions={0} | all-to-all | bytes 163840 | tf_op jit(solution)/shard_map/all_to_all | solution.py:612
  (108 shorter events, 14.0 us)
Async XLA Ops:
  0.0 24.9 %copy-start = (bf16[96,3,5120]{2,0,1:T(8,128)(2,1)S(1)}, bf16[96,3,5120]{2,0,1:T(8,128)(2,1)}, u32[]{:S(2)}) copy-start(bf16[96,3,5120]{2,0,1:T(8,128)(2,1)} %param.15) | copy-start | bytes 8847364
  0.0 8.1 %collective-permute-start.3 = (bf16[8,5120]{1,0:T(8,128)(2,1)}, bf16[8,5120]{1,0:T(8,128)(2,1)}, u32[]{:S(2)}, u32[]{:S(2)}) collective-permute-start(bf16[8,5120]{1,0:T(8,128)(2,1)} %refs_3_.1), channel_id=1, source_target_pairs={{0,8},{1,9},{2,10},{3,11},{4,12},{5,13},{6,14},{7,15},{8,0},{9,1},... | collective-permute-start | bytes 245768 | tf_op jit(solution)/shard_map/ppermute | solution.py:174
  4.0 7.3 %collective-permute-start.1 = (bf16[8,5120]{1,0:T(8,128)(2,1)}, bf16[8,5120]{1,0:T(8,128)(2,1)}, u32[]{:S(2)}, u32[]{:S(2)}) collective-permute-start(bf16[8,5120]{1,0:T(8,128)(2,1)} %refs_3_.1), channel_id=1, source_target_pairs={{0,4},{1,5},{2,6},{3,7},{4,0},{5,1},{6,2},{7,3},{8,12},{9,13},{10,... | collective-permute-start | bytes 245768 | tf_op jit(solution)/shard_map/ppermute | solution.py:174
  8.1 4.8 %collective-permute-start.5 = (bf16[8,5120]{1,0:T(8,128)(2,1)}, bf16[8,5120]{1,0:T(8,128)(2,1)S(1)}, u32[]{:S(2)}, u32[]{:S(2)}) collective-permute-start(bf16[8,5120]{1,0:T(8,128)(2,1)} %collective-permute-done.3.refs_7_), channel_id=1, source_target_pairs={{0,4},{1,5},{2,6},{3,7},{4,0},{5,1},{6,2},{7,3},{8,12},{9,13},{10,... | collective-permute-start | bytes 245768 | tf_op jit(solution)/shard_map/ppermute | solution.py:174
  9.3 8.2 %collective-permute-start = (bf16[8,5120]{1,0:T(8,128)(2,1)}, bf16[8,5120]{1,0:T(8,128)(2,1)}, u32[]{:S(2)}, u32[]{:S(2)}) collective-permute-start(bf16[8,5120]{1,0:T(8,128)(2,1)} %refs_3_.1), channel_id=1, source_target_pairs={{0,2},{1,3},{2,0},{3,1},{4,6},{5,7},{6,4},{7,5},{8,10},{9,11},{10,... | collective-permute-start | bytes 245768 | tf_op jit(solution)/shard_map/ppermute | solution.py:174
  10.8 6.7 %collective-permute-start.4 = (bf16[8,5120]{1,0:T(8,128)(2,1)}, bf16[8,5120]{1,0:T(8,128)(2,1)}, u32[]{:S(2)}, u32[]{:S(2)}) collective-permute-start(bf16[8,5120]{1,0:T(8,128)(2,1)} %collective-permute-done.3.refs_7_), channel_id=1, source_target_pairs={{0,2},{1,3},{2,0},{3,1},{4,6},{5,7},{6,4},{7,5},{8,10},{9,11},{10,... | collective-permute-start | bytes 245768 | tf_op jit(solution)/shard_map/ppermute | solution.py:174
  11.3 6.8 %collective-permute-start.2 = (bf16[8,5120]{1,0:T(8,128)(2,1)}, bf16[8,5120]{1,0:T(8,128)(2,1)}, u32[]{:S(2)}, u32[]{:S(2)}) collective-permute-start(bf16[8,5120]{1,0:T(8,128)(2,1)} %collective-permute-done.1.refs_5_), channel_id=1, source_target_pairs={{0,2},{1,3},{2,0},{3,1},{4,6},{5,7},{6,4},{7,5},{8,10},{9,11},{10,... | collective-permute-start | bytes 245768 | tf_op jit(solution)/shard_map/ppermute | solution.py:174
  12.9 3.8 %copy-start.21 = (bf16[8,5120]{1,0:T(8,128)(2,1)}, bf16[8,5120]{1,0:T(8,128)(2,1)S(1)}, u32[]{:S(2)}) copy-start(bf16[8,5120]{1,0:T(8,128)(2,1)S(1)} %collective-permute-done.5.refs_9_) | copy-start | bytes 245764
  12.9 6.1 %collective-permute-start.6 = (bf16[8,5120]{1,0:T(8,128)(2,1)S(1)}, bf16[8,5120]{1,0:T(8,128)(2,1)}, u32[]{:S(2)}, u32[]{:S(2)}) collective-permute-start(bf16[8,5120]{1,0:T(8,128)(2,1)S(1)} %collective-permute-done.5.refs_9_), channel_id=1, source_target_pairs={{0,2},{1,3},{2,0},{3,1},{4,6},{5,7},{6,4},{7,5},{8,10},{9,11},{10,... | collective-permute-start | bytes 245768 | tf_op jit(solution)/shard_map/ppermute | solution.py:174
  14.6 73.7 %collective-permute-start.15 = (bf16[320,5120]{1,0:T(8,128)(2,1)}, bf16[320,5120]{1,0:T(8,128)(2,1)}, u32[]{:S(2)}, u32[]{:S(2)}) collective-permute-start(bf16[320,5120]{1,0:T(8,128)(2,1)} %bitcast.26), channel_id=1, source_target_pairs={{0,1},{1,0},{2,3},{3,2},{4,5},{5,4},{6,7},{7,6},{8,9},{9,8},{10,11... | collective-permute-start | bytes 9830408 | tf_op jit(solution)/shard_map/ppermute | solution.py:174
  16.6 10.3 %copy-start.26 = (f32[5120]{0:T(1024)S(1)}, f32[5120]{0:T(1024)}, u32[]{:S(2)}) copy-start(f32[5120]{0:T(1024)} %param.20) | copy-start | bytes 61444
  16.6 13.5 %copy-start.20 = (bf16[8,5120]{1,0:T(8,128)(2,1)S(1)}, bf16[8,5120]{1,0:T(8,128)(2,1)}, u32[]{:S(2)}) copy-start(bf16[8,5120]{1,0:T(8,128)(2,1)} %refs_3_.1) | copy-start | bytes 245764
  19.0 31.1 %all-to-all-start.1 = ((bf16[16,2,16,640]{3,2,1,0:T(8,128)(2,1)}), bf16[16,2,16,640]{3,2,1,0:T(8,128)(2,1)}, u32[]{:S(2)}, u32[]{:S(2)}) async-start(bf16[16,2,16,640]{3,2,1,0:T(8,128)(2,1)} %copy-done.11), calls=%async_computation.1 | async-start | bytes 1310720 | tf_op jit(solution)/shard_map/all_to_all | solution.py:581
  24.6 3.3 %collective-permute-start.7 = (bf16[8,5120]{1,0:T(8,128)(2,1)}, bf16[8,5120]{1,0:T(8,128)(2,1)}, u32[]{:S(2)}, u32[]{:S(2)}) collective-permute-start(bf16[8,5120]{1,0:T(8,128)(2,1)} %refs_3_.1), channel_id=1, source_target_pairs={{0,1},{1,0},{2,3},{3,2},{4,5},{5,4},{6,7},{7,6},{8,9},{9,8},{10,11... | collective-permute-start | bytes 245768 | tf_op jit(solution)/shard_map/ppermute | solution.py:174
  24.9 2.0 %copy-start.27 = (f32[5120]{0:T(1024)S(1)}, f32[5120]{0:T(1024)}, u32[]{:S(2)}) copy-start(f32[5120]{0:T(1024)} %param.21) | copy-start | bytes 61444
  26.1 2.0 %collective-permute-start.11 = (bf16[8,5120]{1,0:T(8,128)(2,1)}, bf16[8,5120]{1,0:T(8,128)(2,1)}, u32[]{:S(2)}, u32[]{:S(2)}) collective-permute-start(bf16[8,5120]{1,0:T(8,128)(2,1)} %collective-permute-done.3.refs_7_), channel_id=1, source_target_pairs={{0,1},{1,0},{2,3},{3,2},{4,5},{5,4},{6,7},{7,6},{8,9},{9,8},{10,11... | collective-permute-start | bytes 245768 | tf_op jit(solution)/shard_map/ppermute | solution.py:174
  26.4 1.9 %collective-permute-start.9 = (bf16[8,5120]{1,0:T(8,128)(2,1)}, bf16[8,5120]{1,0:T(8,128)(2,1)}, u32[]{:S(2)}, u32[]{:S(2)}) collective-permute-start(bf16[8,5120]{1,0:T(8,128)(2,1)} %collective-permute-done.1.refs_5_), channel_id=1, source_target_pairs={{0,1},{1,0},{2,3},{3,2},{4,5},{5,4},{6,7},{7,6},{8,9},{9,8},{10,11... | collective-permute-start | bytes 245768 | tf_op jit(solution)/shard_map/ppermute | solution.py:174
  26.7 1.9 %collective-permute-start.8 = (bf16[8,5120]{1,0:T(8,128)(2,1)}, bf16[8,5120]{1,0:T(8,128)(2,1)}, u32[]{:S(2)}, u32[]{:S(2)}) collective-permute-start(bf16[8,5120]{1,0:T(8,128)(2,1)} %collective-permute-done.refs_4_), channel_id=1, source_target_pairs={{0,1},{1,0},{2,3},{3,2},{4,5},{5,4},{6,7},{7,6},{8,9},{9,8},{10,11... | collective-permute-start | bytes 245768 | tf_op jit(solution)/shard_map/ppermute | solution.py:174
  27.8 1.5 collective-permute-start.13
  28.1 1.5 collective-permute-start.12
  28.3 1.5 collective-permute-start.10
  28.7 1.5 collective-permute-start.14
  30.1 1.9 %copy-start.1 = (bf16[5120,320]{0,1:T(8,128)(2,1)S(1)}, bf16[5120,320]{0,1:T(8,128)(2,1)}, u32[]{:S(2)}) copy-start(bf16[5120,320]{0,1:T(8,128)(2,1)} %param.16) | copy-start | bytes 9830404
  32.1 1.9 %copy-start.3 = (bf16[5120,320]{0,1:T(8,128)(2,1)S(1)}, bf16[5120,320]{0,1:T(8,128)(2,1)}, u32[]{:S(2)}) copy-start(bf16[5120,320]{0,1:T(8,128)(2,1)} %param.17) | copy-start | bytes 9830404
  34.0 1.9 %copy-start.5 = (bf16[5120,320]{0,1:T(8,128)(2,1)S(1)}, bf16[5120,320]{0,1:T(8,128)(2,1)}, u32[]{:S(2)}) copy-start(bf16[5120,320]{0,1:T(8,128)(2,1)} %param.18) | copy-start | bytes 9830404
  50.1 12.6 %collective-permute-start.17 = (bf16[16,2,16,640]{3,2,1,0:T(8,128)(2,1)}, bf16[16,2,16,640]{3,2,1,0:T(8,128)(2,1)S(1)}, u32[]{:S(2)}, u32[]{:S(2)}) collective-permute-start(bf16[16,2,16,640]{3,2,1,0:T(8,128)(2,1)} %all-to-all-done.1.text_hbm), channel_id=1, source_target_pairs={{0,1},{1,0},{2,3},{3,2},{4,5},{5,4},{6,7},{7,6},{8,9},{9,8},{10,11... | collective-permute-start | bytes 1966088 | tf_op jit(solution)/shard_map/ppermute | solution.py:174
  50.3 12.4 %collective-permute-start.16 = (bf16[320,320]{1,0:T(8,128)(2,1)}, bf16[320,320]{1,0:T(8,128)(2,1)S(1)}, u32[]{:S(2)}, u32[]{:S(2)}) collective-permute-start(bf16[320,320]{1,0:T(8,128)(2,1)} %copy-done.25), channel_id=1, source_target_pairs={{0,1},{1,0},{2,3},{3,2},{4,5},{5,4},{6,7},{7,6},{8,9},{9,8},{10,11... | collective-permute-start | bytes 614408 | tf_op jit(solution)/shard_map/ppermute | solution.py:174
  70.1 7.1 %collective-permute-start.21 = (bf16[64,640]{1,0:T(8,128)(2,1)}, bf16[64,640]{1,0:T(8,128)(2,1)}, u32[]{:S(2)}, u32[]{:S(2)}) collective-permute-start(bf16[64,640]{1,0:T(8,128)(2,1)} %attend.2.refs_0_), channel_id=1, source_target_pairs={{0,8},{1,9},{2,10},{3,11},{4,12},{5,13},{6,14},{7,15},{8,0},{9,1},... | collective-permute-start | bytes 245768 | tf_op jit(solution)/shard_map/ppermute | solution.py:174
  70.6 10.2 %collective-permute-start.19 = (bf16[64,640]{1,0:T(8,128)(2,1)}, bf16[64,640]{1,0:T(8,128)(2,1)}, u32[]{:S(2)}, u32[]{:S(2)}) collective-permute-start(bf16[64,640]{1,0:T(8,128)(2,1)} %attend.2.refs_0_), channel_id=1, source_target_pairs={{0,4},{1,5},{2,6},{3,7},{4,0},{5,1},{6,2},{7,3},{8,12},{9,13},{10,... | collective-permute-start | bytes 245768 | tf_op jit(solution)/shard_map/ppermute | solution.py:174
  77.2 4.8 %collective-permute-start.23 = (bf16[64,640]{1,0:T(8,128)(2,1)}, bf16[64,640]{1,0:T(8,128)(2,1)}, u32[]{:S(2)}, u32[]{:S(2)}) collective-permute-start(bf16[64,640]{1,0:T(8,128)(2,1)} %collective-permute-done.21.refs_4_), channel_id=1, source_target_pairs={{0,4},{1,5},{2,6},{3,7},{4,0},{5,1},{6,2},{7,3},{8,12},{9,13},{10,... | collective-permute-start | bytes 245768 | tf_op jit(solution)/shard_map/ppermute | solution.py:174
  78.8 5.6 %collective-permute-start.18 = (bf16[64,640]{1,0:T(8,128)(2,1)}, bf16[64,640]{1,0:T(8,128)(2,1)S(1)}, u32[]{:S(2)}, u32[]{:S(2)}) collective-permute-start(bf16[64,640]{1,0:T(8,128)(2,1)} %attend.2.refs_0_), channel_id=1, source_target_pairs={{0,2},{1,3},{2,0},{3,1},{4,6},{5,7},{6,4},{7,5},{8,10},{9,11},{10,... | collective-permute-start | bytes 245768 | tf_op jit(solution)/shard_map/ppermute | solution.py:174
  79.6 6.5 %collective-permute-start.22 = (bf16[64,640]{1,0:T(8,128)(2,1)}, bf16[64,640]{1,0:T(8,128)(2,1)S(1)}, u32[]{:S(2)}, u32[]{:S(2)}) collective-permute-start(bf16[64,640]{1,0:T(8,128)(2,1)} %collective-permute-done.21.refs_4_), channel_id=1, source_target_pairs={{0,2},{1,3},{2,0},{3,1},{4,6},{5,7},{6,4},{7,5},{8,10},{9,11},{10,... | collective-permute-start | bytes 245768 | tf_op jit(solution)/shard_map/ppermute | solution.py:174
  80.8 6.7 %collective-permute-start.20 = (bf16[64,640]{1,0:T(8,128)(2,1)}, bf16[64,640]{1,0:T(8,128)(2,1)S(1)}, u32[]{:S(2)}, u32[]{:S(2)}) collective-permute-start(bf16[64,640]{1,0:T(8,128)(2,1)} %collective-permute-done.19.refs_2_), channel_id=1, source_target_pairs={{0,2},{1,3},{2,0},{3,1},{4,6},{5,7},{6,4},{7,5},{8,10},{9,11},{10,... | collective-permute-start | bytes 245768 | tf_op jit(solution)/shard_map/ppermute | solution.py:174
  82.0 6.4 %collective-permute-start.24 = (bf16[64,640]{1,0:T(8,128)(2,1)}, bf16[64,640]{1,0:T(8,128)(2,1)S(1)}, u32[]{:S(2)}, u32[]{:S(2)}) collective-permute-start(bf16[64,640]{1,0:T(8,128)(2,1)} %collective-permute-done.23.refs_6_), channel_id=1, source_target_pairs={{0,2},{1,3},{2,0},{3,1},{4,6},{5,7},{6,4},{7,5},{8,10},{9,11},{10,... | collective-permute-start | bytes 245768 | tf_op jit(solution)/shard_map/ppermute | solution.py:174
  88.4 1.9 %copy-start.7 = (bf16[5120,320]{0,1:T(8,128)(2,1)S(1)}, bf16[5120,320]{0,1:T(8,128)(2,1)}, u32[]{:S(2)}) copy-start(bf16[5120,320]{0,1:T(8,128)(2,1)} %param.19) | copy-start | bytes 9830404
  91.2 24.1 %copy-start.2 = (bf16[5120,320]{0,1:T(8,128)(2,1)S(1)}, bf16[5120,320]{0,1:T(8,128)(2,1)}, u32[]{:S(2)}) copy-start(bf16[5120,320]{0,1:T(8,128)(2,1)} %param.16) | copy-start | bytes 9830404
  91.2 24.1 %copy-start.4 = (bf16[5120,320]{0,1:T(8,128)(2,1)S(1)}, bf16[5120,320]{0,1:T(8,128)(2,1)}, u32[]{:S(2)}) copy-start(bf16[5120,320]{0,1:T(8,128)(2,1)} %param.17) | copy-start | bytes 9830404
  91.2 24.1 %copy-start.13 = (f32[2,320]{0,1:T(8,128)S(1)}, f32[2,320]{0,1:T(8,128)}, u32[]{:S(2)}) copy-start(f32[2,320]{0,1:T(8,128)} %copy.16) | copy-start | bytes 7684
  91.2 44.8 %copy-start.10 = (bf16[16,2,16,640]{3,2,1,0:T(8,128)(2,1)S(1)}, bf16[16,2,16,640]{3,2,1,0:T(8,128)(2,1)}, u32[]{:S(2)}) copy-start(bf16[16,2,16,640]{3,2,1,0:T(8,128)(2,1)} %copy-done.9) | copy-start | bytes 1966084
  97.7 5.5 %collective-permute-start.28 = (bf16[64,640]{1,0:T(8,128)(2,1)S(1)}, bf16[64,640]{1,0:T(8,128)(2,1)S(1)}, u32[]{:S(2)}, u32[]{:S(2)}) collective-permute-start(bf16[64,640]{1,0:T(8,128)(2,1)S(1)} %output.2.refs_3_.current_ref), channel_id=1, source_target_pairs={{0,8},{1,9},{2,10},{3,11},{4,12},{5,13},{6,14},{7,15},{8,0},{9,1},... | collective-permute-start | bytes 245768 | tf_op jit(solution)/shard_map/ppermute | solution.py:174
  97.8 7.8 %collective-permute-start.32 = (bf16[64,640]{1,0:T(8,128)(2,1)S(1)}, bf16[64,640]{1,0:T(8,128)(2,1)S(1)}, u32[]{:S(2)}, u32[]{:S(2)}) collective-permute-start(bf16[64,640]{1,0:T(8,128)(2,1)S(1)} %output.2.refs_3_.current_ref), channel_id=1, source_target_pairs={{0,1},{1,0},{2,3},{3,2},{4,5},{5,4},{6,7},{7,6},{8,9},{9,8},{10,11... | collective-permute-start | bytes 245768 | tf_op jit(solution)/shard_map/ppermute | solution.py:174
  97.9 8.8 %collective-permute-start.26 = (bf16[64,640]{1,0:T(8,128)(2,1)S(1)}, bf16[64,640]{1,0:T(8,128)(2,1)S(1)}, u32[]{:S(2)}, u32[]{:S(2)}) collective-permute-start(bf16[64,640]{1,0:T(8,128)(2,1)S(1)} %output.2.refs_3_.current_ref), channel_id=1, source_target_pairs={{0,4},{1,5},{2,6},{3,7},{4,0},{5,1},{6,2},{7,3},{8,12},{9,13},{10,... | collective-permute-start | bytes 245768 | tf_op jit(solution)/shard_map/ppermute | solution.py:174
  99.7 7.2 %collective-permute-start.25 = (bf16[64,640]{1,0:T(8,128)(2,1)S(1)}, bf16[64,640]{1,0:T(8,128)(2,1)S(1)}, u32[]{:S(2)}, u32[]{:S(2)}) collective-permute-start(bf16[64,640]{1,0:T(8,128)(2,1)S(1)} %output.2.refs_3_.current_ref), channel_id=1, source_target_pairs={{0,2},{1,3},{2,0},{3,1},{4,6},{5,7},{6,4},{7,5},{8,10},{9,11},{10,... | collective-permute-start | bytes 245768 | tf_op jit(solution)/shard_map/ppermute | solution.py:174
  103.3 4.8 %collective-permute-start.30 = (bf16[64,640]{1,0:T(8,128)(2,1)S(1)}, bf16[64,640]{1,0:T(8,128)(2,1)S(1)}, u32[]{:S(2)}, u32[]{:S(2)}) collective-permute-start(bf16[64,640]{1,0:T(8,128)(2,1)S(1)} %collective-permute-done.28.refs_7_), channel_id=1, source_target_pairs={{0,4},{1,5},{2,6},{3,7},{4,0},{5,1},{6,2},{7,3},{8,12},{9,13},{10,... | collective-permute-start | bytes 245768 | tf_op jit(solution)/shard_map/ppermute | solution.py:174
  105.6 3.5 %collective-permute-start.36 = (bf16[64,640]{1,0:T(8,128)(2,1)S(1)}, bf16[64,640]{1,0:T(8,128)(2,1)S(1)}, u32[]{:S(2)}, u32[]{:S(2)}) collective-permute-start(bf16[64,640]{1,0:T(8,128)(2,1)S(1)} %collective-permute-done.28.refs_7_), channel_id=1, source_target_pairs={{0,1},{1,0},{2,3},{3,2},{4,5},{5,4},{6,7},{7,6},{8,9},{9,8},{10,11... | collective-permute-start | bytes 245768 | tf_op jit(solution)/shard_map/ppermute | solution.py:174
  105.6 5.2 %collective-permute-start.29 = (bf16[64,640]{1,0:T(8,128)(2,1)S(1)}, bf16[64,640]{1,0:T(8,128)(2,1)S(1)}, u32[]{:S(2)}, u32[]{:S(2)}) collective-permute-start(bf16[64,640]{1,0:T(8,128)(2,1)S(1)} %collective-permute-done.28.refs_7_), channel_id=1, source_target_pairs={{0,2},{1,3},{2,0},{3,1},{4,6},{5,7},{6,4},{7,5},{8,10},{9,11},{10,... | collective-permute-start | bytes 245768 | tf_op jit(solution)/shard_map/ppermute | solution.py:174
  106.7 4.2 %collective-permute-start.34 = (bf16[64,640]{1,0:T(8,128)(2,1)S(1)}, bf16[64,640]{1,0:T(8,128)(2,1)S(1)}, u32[]{:S(2)}, u32[]{:S(2)}) collective-permute-start(bf16[64,640]{1,0:T(8,128)(2,1)S(1)} %collective-permute-done.26.refs_5_), channel_id=1, source_target_pairs={{0,1},{1,0},{2,3},{3,2},{4,5},{5,4},{6,7},{7,6},{8,9},{9,8},{10,11... | collective-permute-start | bytes 245768 | tf_op jit(solution)/shard_map/ppermute | solution.py:174
  106.9 5.7 %collective-permute-start.27 = (bf16[64,640]{1,0:T(8,128)(2,1)S(1)}, bf16[64,640]{1,0:T(8,128)(2,1)S(1)}, u32[]{:S(2)}, u32[]{:S(2)}) collective-permute-start(bf16[64,640]{1,0:T(8,128)(2,1)S(1)} %collective-permute-done.26.refs_5_), channel_id=1, source_target_pairs={{0,2},{1,3},{2,0},{3,1},{4,6},{5,7},{6,4},{7,5},{8,10},{9,11},{10,... | collective-permute-start | bytes 245768 | tf_op jit(solution)/shard_map/ppermute | solution.py:174
  108.0 6.0 %collective-permute-start.31 = (bf16[64,640]{1,0:T(8,128)(2,1)S(1)}, bf16[64,640]{1,0:T(8,128)(2,1)S(1)}, u32[]{:S(2)}, u32[]{:S(2)}) collective-permute-start(bf16[64,640]{1,0:T(8,128)(2,1)S(1)} %collective-permute-done.30.refs_9_), channel_id=1, source_target_pairs={{0,2},{1,3},{2,0},{3,1},{4,6},{5,7},{6,4},{7,5},{8,10},{9,11},{10,... | collective-permute-start | bytes 245768 | tf_op jit(solution)/shard_map/ppermute | solution.py:174
  109.1 4.9 %collective-permute-start.33 = (bf16[64,640]{1,0:T(8,128)(2,1)S(1)}, bf16[64,640]{1,0:T(8,128)(2,1)S(1)}, u32[]{:S(2)}, u32[]{:S(2)}) collective-permute-start(bf16[64,640]{1,0:T(8,128)(2,1)S(1)} %collective-permute-done.25.refs_4_), channel_id=1, source_target_pairs={{0,1},{1,0},{2,3},{3,2},{4,5},{5,4},{6,7},{7,6},{8,9},{9,8},{10,11... | collective-permute-start | bytes 245768 | tf_op jit(solution)/shard_map/ppermute | solution.py:174
  110.8 3.1 %collective-permute-start.38 = (bf16[64,640]{1,0:T(8,128)(2,1)S(1)}, bf16[64,640]{1,0:T(8,128)(2,1)S(1)}, u32[]{:S(2)}, u32[]{:S(2)}) collective-permute-start(bf16[64,640]{1,0:T(8,128)(2,1)S(1)} %collective-permute-done.30.refs_9_), channel_id=1, source_target_pairs={{0,1},{1,0},{2,3},{3,2},{4,5},{5,4},{6,7},{7,6},{8,9},{9,8},{10,11... | collective-permute-start | bytes 245768 | tf_op jit(solution)/shard_map/ppermute | solution.py:174
  110.8 3.1 %collective-permute-start.37 = (bf16[64,640]{1,0:T(8,128)(2,1)S(1)}, bf16[64,640]{1,0:T(8,128)(2,1)S(1)}, u32[]{:S(2)}, u32[]{:S(2)}) collective-permute-start(bf16[64,640]{1,0:T(8,128)(2,1)S(1)} %collective-permute-done.29.refs_8_), channel_id=1, source_target_pairs={{0,1},{1,0},{2,3},{3,2},{4,5},{5,4},{6,7},{7,6},{8,9},{9,8},{10,11... | collective-permute-start | bytes 245768 | tf_op jit(solution)/shard_map/ppermute | solution.py:174
  112.6 1.4 collective-permute-start.35
  114.0 1.3 collective-permute-start.39
  115.3 1.9 %copy-start.6 = (bf16[5120,320]{0,1:T(8,128)(2,1)S(1)}, bf16[5120,320]{0,1:T(8,128)(2,1)}, u32[]{:S(2)}) copy-start(bf16[5120,320]{0,1:T(8,128)(2,1)} %param.18) | copy-start | bytes 9830404
  118.1 39.2 %copy-start.8 = (bf16[5120,320]{0,1:T(8,128)(2,1)S(1)}, bf16[5120,320]{0,1:T(8,128)(2,1)}, u32[]{:S(2)}) copy-start(bf16[5120,320]{0,1:T(8,128)(2,1)} %param.19) | copy-start | bytes 9830404
  126.7 9.3 %collective-permute-start.40 = (bf16[320,320]{1,0:T(8,128)(2,1)S(1)}, bf16[320,320]{1,0:T(8,128)(2,1)S(1)}, u32[]{:S(2)}, u32[]{:S(2)}) collective-permute-start(bf16[320,320]{1,0:T(8,128)(2,1)S(1)} %get-tuple-element.21), channel_id=1, source_target_pairs={{0,1},{1,0},{2,3},{3,2},{4,5},{5,4},{6,7},{7,6},{8,9},{9,8},{10,11... | collective-permute-start | bytes 614408 | tf_op jit(solution)/shard_map/ppermute | solution.py:174
  141.1 6.8 %collective-permute-start.44 = (bf16[64,640]{1,0:T(8,128)(2,1)S(1)}, bf16[64,640]{1,0:T(8,128)(2,1)S(1)}, u32[]{:S(2)}, u32[]{:S(2)}) collective-permute-start(bf16[64,640]{1,0:T(8,128)(2,1)S(1)} %attend.3.refs_0_), channel_id=1, source_target_pairs={{0,8},{1,9},{2,10},{3,11},{4,12},{5,13},{6,14},{7,15},{8,0},{9,1},... | collective-permute-start | bytes 245768 | tf_op jit(solution)/shard_map/ppermute | solution.py:174
  141.6 8.3 %collective-permute-start.42 = (bf16[64,640]{1,0:T(8,128)(2,1)S(1)}, bf16[64,640]{1,0:T(8,128)(2,1)S(1)}, u32[]{:S(2)}, u32[]{:S(2)}) collective-permute-start(bf16[64,640]{1,0:T(8,128)(2,1)S(1)} %attend.3.refs_0_), channel_id=1, source_target_pairs={{0,4},{1,5},{2,6},{3,7},{4,0},{5,1},{6,2},{7,3},{8,12},{9,13},{10,... | collective-permute-start | bytes 245768 | tf_op jit(solution)/shard_map/ppermute | solution.py:174
  147.9 4.4 %collective-permute-start.46 = (bf16[64,640]{1,0:T(8,128)(2,1)S(1)}, bf16[64,640]{1,0:T(8,128)(2,1)S(1)}, u32[]{:S(2)}, u32[]{:S(2)}) collective-permute-start(bf16[64,640]{1,0:T(8,128)(2,1)S(1)} %collective-permute-done.44.refs_4_), channel_id=1, source_target_pairs={{0,4},{1,5},{2,6},{3,7},{4,0},{5,1},{6,2},{7,3},{8,12},{9,13},{10,... | collective-permute-start | bytes 245768 | tf_op jit(solution)/shard_map/ppermute | solution.py:174
  147.9 5.3 %collective-permute-start.41 = (bf16[64,640]{1,0:T(8,128)(2,1)S(1)}, bf16[64,640]{1,0:T(8,128)(2,1)S(1)}, u32[]{:S(2)}, u32[]{:S(2)}) collective-permute-start(bf16[64,640]{1,0:T(8,128)(2,1)S(1)} %attend.3.refs_0_), channel_id=1, source_target_pairs={{0,2},{1,3},{2,0},{3,1},{4,6},{5,7},{6,4},{7,5},{8,10},{9,11},{10,... | collective-permute-start | bytes 245768 | tf_op jit(solution)/shard_map/ppermute | solution.py:174
  148.7 6.3 %collective-permute-start.45 = (bf16[64,640]{1,0:T(8,128)(2,1)S(1)}, bf16[64,640]{1,0:T(8,128)(2,1)S(1)}, u32[]{:S(2)}, u32[]{:S(2)}) collective-permute-start(bf16[64,640]{1,0:T(8,128)(2,1)S(1)} %collective-permute-done.44.refs_4_), channel_id=1, source_target_pairs={{0,2},{1,3},{2,0},{3,1},{4,6},{5,7},{6,4},{7,5},{8,10},{9,11},{10,... | collective-permute-start | bytes 245768 | tf_op jit(solution)/shard_map/ppermute | solution.py:174
  149.9 6.4 %collective-permute-start.43 = (bf16[64,640]{1,0:T(8,128)(2,1)S(1)}, bf16[64,640]{1,0:T(8,128)(2,1)S(1)}, u32[]{:S(2)}, u32[]{:S(2)}) collective-permute-start(bf16[64,640]{1,0:T(8,128)(2,1)S(1)} %collective-permute-done.42.refs_2_), channel_id=1, source_target_pairs={{0,2},{1,3},{2,0},{3,1},{4,6},{5,7},{6,4},{7,5},{8,10},{9,11},{10,... | collective-permute-start | bytes 245768 | tf_op jit(solution)/shard_map/ppermute | solution.py:174
  152.4 4.9 %collective-permute-start.47 = (bf16[64,640]{1,0:T(8,128)(2,1)S(1)}, bf16[64,640]{1,0:T(8,128)(2,1)S(1)}, u32[]{:S(2)}, u32[]{:S(2)}) collective-permute-start(bf16[64,640]{1,0:T(8,128)(2,1)S(1)} %collective-permute-done.46.refs_6_), channel_id=1, source_target_pairs={{0,2},{1,3},{2,0},{3,1},{4,6},{5,7},{6,4},{7,5},{8,10},{9,11},{10,... | collective-permute-start | bytes 245768 | tf_op jit(solution)/shard_map/ppermute | solution.py:174
  (13 other events, 11.1 us)

commit v4 on v3

--- a/solution.py
+++ b/solution.py
@@ -177,10 +177,10 @@
 def gathered_over_chips(block):
     chips = lax.axis_size("queue") // 2
     blocks = {0: block}
-    bits = [1 << b for b in reversed(range(chips.bit_length() - 1))]
-    for bit in bits:
-        for mask in list(blocks):
-            blocks[mask | bit] = swapped(blocks[mask], 2 * bit)
+    for mask in range(2, chips, 2):
+        blocks[mask] = swapped(block, 2 * mask)
+    for mask in range(0, chips, 2):
+        blocks[mask + 1] = swapped(blocks[mask], 2)
     return [blocks[mask] for mask in range(chips)]
 
 
@@ -190,13 +190,9 @@
     )
 
 
+HBM_SPEC = pl.BlockSpec(memory_space=pltpu.HBM)
 VMEM_SPEC = pl.BlockSpec(memory_space=pltpu.VMEM)
-SMEM_SPEC = pl.BlockSpec(memory_space=pltpu.SMEM)
-HBM_SPEC = pl.BlockSpec(memory_space=pltpu.HBM)
-
-
-def kernel_params(mebibytes):
-    return pltpu.CompilerParams(vmem_limit_bytes=mebibytes * 1024 * 1024)
+PARAMS = pltpu.CompilerParams(vmem_limit_bytes=60 * 1024 * 1024)
 
 
 def span_at(position, step, spans):
@@ -204,26 +200,44 @@
     return (2 * (position % chips) + position // chips + step + 1) % spans
 
 
-def project_kernel(step, spans, place_ref, gain_ref, table_ref, incoming_ref, *refs):
+def own_place():
+    own_index = lax.axis_index("queue")
+    return own_index // 2, own_index % 2
+
+
+def started(pairs, sems):
+    copies = [
+        pltpu.make_async_copy(source, target, sems.at[i]) for i, (source, target) in enumerate(pairs)
+    ]
+    for copy in copies:
+        copy.start()
+    return copies
+
+
+def finished(copies):
+    for copy in copies:
+        copy.wait()
+
+
+def project_kernel(step, spans, gain_hbm, table_hbm, incoming_hbm, *refs):
     chips = spans // 2
     weight_refs, refs = refs[:3], refs[3:]
     mine, others = refs[:chips], refs[chips : 2 * chips]
     refs = refs[2 * chips :]
-    own_ref, send_ref, squares_ref = refs[:3]
+    own_hbm, send_hbm, squares_ref = refs[:3]
     refs = refs[3:]
     if step == 0:
-        current_ref, refs = refs[0], refs[1:]
-    state, modulated, table, entering, shift_ref, scale_ref, weights, sems = refs
-    chip, core = place_ref[0], place_ref[1]
+        current_hbm, refs = refs[0], refs[1:]
+    state, modulated, table, entering, gain, scale_ref, shift_ref, weights, own, send, current, sems = refs
+    chip, core = own_place()
     tokens, width = modulated.shape
     half = tokens // 2
     rows = tokens // spans
     pair = 2 * rows
     cols = weight_refs[0].shape[0]
     first = core == 0
-    copies = [pltpu.make_async_copy(table_ref, table, sems.at[spans])]
-    if step == 0:
-        copies.append(pltpu.make_async_copy(incoming_ref, entering, sems.at[spans + 1]))
+    own_lanes = pl.ds(pl.multiple_of(chip * 2 * cols, 2 * cols), 2 * cols)
+    pairs = []
     for side, blocks in enumerate((mine, others)):
         owner = core if side == 0 else 1 - core
         for mask in range(chips):
@@ -233,28 +247,24 @@
             else:
                 lanes = pl.ds(pl.multiple_of(other_chip * 2 * cols, 2 * cols), 2 * cols)
                 target = state.at[pl.ds(pl.multiple_of(owner * half, half), half), lanes]
-            copies.append(
-                pltpu.make_async_copy(blocks[mask], target, sems.at[side * chips + mask])
-            )
-    fetches = [
-        pltpu.make_async_copy(weight_refs[i], weights.at[i], sems.at[spans + 2 + i])
-        for i in range(3)
-    ]
-    for copy in copies + fetches:
-        copy.start()
-    for copy in copies:
-        copy.wait()
+            pairs.append((blocks[mask], target))
+    pairs += [(table_hbm, table), (gain_hbm.at[:, own_lanes], gain), (incoming_hbm, entering)]
+    pairs += [(weight_refs[i], weights.at[i]) for i in range(3)]
+    copies = started(pairs, sems)
+    copies, fetches = copies[:-3], copies[-3:]
+    finished(copies)
     shift_ref[...] = table[0].astype(jnp.float32)
     scale_ref[...] = table[1].astype(jnp.float32) + 1.0
+    leaving = []
     if step == 0:
         state[spans - 1] = entering[step]
-        lanes = pl.ds(pl.multiple_of(chip * 2 * cols, 2 * cols), 2 * cols)
         for slab in range(chips // 2):
             at = core * chips + 2 * slab
-            both = [state[at + e, :, lanes].astype(jnp.float32) for e in range(2)]
-            current_ref[slab * pair : (slab + 1) * pair, :] = jnp.concatenate(
-                both, axis=0
-            ).astype(jnp.bfloat16)
+            both = [state[at + e, :, own_lanes].astype(jnp.float32) for e in range(2)]
+            current[slab * pair : (slab + 1) * pair, :] = jnp.concatenate(both, axis=0).astype(
+                jnp.bfloat16
+            )
+        leaving += started([(current, current_hbm)], sems.at[pl.ds(0, 1)])
     pieces = 4
     piece = width // pieces
     for slab in range(chips):
@@ -282,36 +292,43 @@
                 for ref in (scale_ref, shift_ref)
             )
             modulated[band, part] = (x * scale + shift).astype(jnp.bfloat16)
+    ident = lax.broadcasted_iota(jnp.int32, (tokens, tokens), 0) == lax.broadcasted_iota(
+        jnp.int32, (tokens, tokens), 1
+    )
     for i in range(3):
         fetches[i].wait()
-
-        def add(step_k, total):
-            part = pl.ds(pl.multiple_of(step_k * piece, piece), piece)
-            return total + contract_last(weights[i, :, part], modulated[:, part])
-
-        product = lax.fori_loop(0, pieces, add, jnp.zeros((cols, tokens), jnp.float32))
+        product = contract_last(modulated[...], weights[i])
         if i < 2:
-            line = jnp.sum(product * product, axis=0, keepdims=True)
+            column = jnp.sum(product * product, axis=1, keepdims=True)
+            line = jnp.sum(jnp.where(ident, column, 0.0), axis=0, keepdims=True)
             squares_ref[:, i : i + 1, :] = jnp.broadcast_to(line[None], (spans, 1, tokens))
-            product = product * gain_ref[:, i : i + 1]
-        product = product.T
+            line = gain[i : i + 1, :]
+            product = product * jnp.where(first, line[:, :cols], line[:, cols:])
         if i == 0:
             low, high = product[:half], product[half:]
-            own_ref[:half, :] = jnp.where(first, low, high).astype(jnp.bfloat16)
-            send_ref[:half, :] = jnp.where(first, high, low).astype(jnp.bfloat16)
+            own[...] = jnp.where(first, low, high).astype(jnp.bfloat16)
+            send[:half, :] = jnp.where(first, high, low).astype(jnp.bfloat16)
+            leaving += started(
+                [(own, own_hbm), (send.at[pl.ds(0, half)], send_hbm.at[pl.ds(0, half)])],
+                sems.at[pl.ds(1, 2)],
+            )
         else:
-            band = slice(half + (i - 1) * tokens, half + i * tokens)
-            own_ref[band, :] = product.astype(jnp.bfloat16)
-            send_ref[band, :] = product.astype(jnp.bfloat16)
-
-
-def project(step, spans, place, gain, table, incoming, mine, others, weights):
+            band = pl.ds(half + (i - 1) * tokens, tokens)
+            send[band, :] = product.astype(jnp.bfloat16)
+            leaving += started([(send.at[band], send_hbm.at[band])], sems.at[pl.ds(2 + i, 1)])
+    finished(leaving)
+
+
+def project(step, spans, gain, table, incoming, mine, others, weights):
     rows = incoming.shape[1]
     tokens = spans * rows
     cols, width = weights[0].shape
     half = tokens // 2
-    own = jax.ShapeDtypeStruct((half + 2 * tokens, cols), jnp.bfloat16)
-    out_shape = [own, own, jax.ShapeDtypeStruct((spans, 2, tokens), jnp.float32)]
+    out_shape = [
+        jax.ShapeDtypeStruct((half, cols), jnp.bfloat16),
+        jax.ShapeDtypeStruct((half + 2 * tokens, cols), jnp.bfloat16),
+        jax.ShapeDtypeStruct((spans, 2, tokens), jnp.float32),
+    ]
     if step == 0:
         out_shape.append(jax.ShapeDtypeStruct((half, 2 * cols), jnp.bfloat16))
         state = (spans, rows, width)
@@ -320,50 +337,60 @@
     return pl.pallas_call(
         functools.partial(project_kernel, step, spans),
         out_shape=out_shape,
-        in_specs=[SMEM_SPEC, VMEM_SPEC] + [HBM_SPEC] * (5 + 2 * len(mine)),
-        out_specs=[VMEM_SPEC] * len(out_shape),
+        in_specs=[HBM_SPEC] * (6 + 2 * len(mine)),
+        out_specs=[HBM_SPEC, HBM_SPEC, VMEM_SPEC, HBM_SPEC][: len(out_shape)],
         scratch_shapes=[
             pltpu.VMEM(state, jnp.bfloat16),
             pltpu.VMEM((tokens, width), jnp.bfloat16),
             pltpu.VMEM(table.shape, jnp.bfloat16),
             pltpu.VMEM(incoming.shape, jnp.bfloat16),
+            pltpu.VMEM((2, 2 * cols), jnp.float32),
             pltpu.VMEM((spans, width), jnp.float32),
             pltpu.VMEM((spans, width), jnp.float32),
             pltpu.VMEM((3, cols, width), jnp.bfloat16),
-            pltpu.SemaphoreType.DMA((spans + 5,)),
+            pltpu.VMEM((half, cols), jnp.bfloat16),
+            pltpu.VMEM((half + 2 * tokens, cols), jnp.bfloat16),
+            pltpu.VMEM((half, 2 * cols), jnp.bfloat16),
+            pltpu.SemaphoreType.DMA((spans + 6,)),
         ],
-        compiler_params=kernel_params(24),
+        compiler_params=PARAMS,
         name="project",
-    )(place, gain, table, incoming, *weights, *mine, *others)
+    )(gain, table, incoming, *weights, *mine, *others)
 
 
 def attend_kernel(
-    step, spans, head_size, place_ref, own_ref, got_ref, squares_ref, text_hbm, more_hbm,
-    out_ref, queries, keys, values, text_ref, more_ref, sems,
+    step, spans, head_size, own_hbm, sent_hbm, got_hbm, squares_hbm, text_hbm, more_hbm,
+    out_ref, own, sent, got, squares_ref, queries, keys, values, text_ref, more_ref, sems,
 ):
-    copies = [
-        pltpu.make_async_copy(text_hbm, text_ref, sems.at[0]),
-        pltpu.make_async_copy(more_hbm, more_ref, sems.at[1]),
-    ]
-    for copy in copies:
-        copy.start()
-    core = place_ref[1]
+    copies = started(
+        [
+            (own_hbm, own),
+            (sent_hbm, sent),
+            (got_hbm, got),
+            (squares_hbm, squares_ref),
+            (text_hbm, text_ref),
+            (more_hbm, more_ref),
+        ],
+        sems,
+    )
+    chip, core = own_place()
     first = core == 0
     half, width = queries.shape
     tokens = 2 * half
     rows = tokens // spans
     cols = width // 2
-    for target, low, size in (
-        (queries, 0, half),
-        (keys, half, tokens),
-        (values, half + tokens, tokens),
+    finished(copies[:3])
+    for target, mine_ref, low, size in (
+        (queries, own, 0, half),
+        (keys, sent, half, tokens),
+        (values, sent, half + tokens, tokens),
     ):
-        mine = own_ref[low : low + size, :]
-        other = got_ref[low : low + size, :]
+        mine = mine_ref[low : low + size, :]
+        other = got[low : low + size, :]
         target[:, :cols] = jnp.where(first, mine, other)
         target[:, cols:] = jnp.where(first, other, mine)
-    squares = jnp.sum(squares_ref[...], axis=0)
-    factors = lax.rsqrt(squares / (width * (spans // 2)) + 1e-06)
+    copies[3].wait()
+    factors = lax.rsqrt(jnp.sum(squares_ref[...], axis=0) / (width * (spans // 2)) + 1e-06)
     ident = lax.broadcasted_iota(jnp.int32, (tokens, tokens), 0) == lax.broadcasted_iota(
         jnp.int32, (tokens, tokens), 1
     )
@@ -375,15 +402,14 @@
     key_block = lax.broadcasted_iota(jnp.int32, shape, 1) // rows
     allowed = span_at(own_block, step, spans) >= span_at(key_block, step, spans)
     text_rows = text_ref.shape[0] * text_ref.shape[2]
-    for copy in copies:
-        copy.wait()
+    finished(copies[4:])
     for head in range(width // head_size):
         lanes = slice(head * head_size, (head + 1) * head_size)
         q = queries[:, lanes]
         scores = contract_last(q, keys[:, lanes]) * column * row
         scores = jnp.where(allowed, scores, -1e30)
         weights = jnp.exp(scores - jnp.max(scores, axis=1, keepdims=True))
-        weights = weights / jnp.sum(weights, axis=1, keepdims=True)
+        weights = weights * (1.0 / jnp.sum(weights, axis=1, keepdims=True))
         attended = jnp.dot(
             weights.astype(jnp.bfloat16), values[:, lanes], preferred_element_type=jnp.float32
         ).astype(jnp.bfloat16)
@@ -396,11 +422,12 @@
         )
         parts = [jnp.exp(part - most) for part in parts]
         total = jnp.sum(parts[0], axis=1, keepdims=True) + jnp.sum(parts[1], axis=1, keepdims=True)
+        share = 1.0 / total
         crossed = jnp.zeros((half, head_size), jnp.float32)
         for ref, part in zip((text_ref, more_ref), parts):
             text_values = ref[:, 1, :, lanes].reshape(text_rows, head_size)
             crossed = crossed + jnp.dot(
-                (part / total).astype(jnp.bfloat16), text_values, preferred_element_type=jnp.float32
+                (part * share).astype(jnp.bfloat16), text_values, preferred_element_type=jnp.float32
             )
         crossed = crossed.astype(jnp.bfloat16)
         out_ref[:, lanes] = (attended.astype(jnp.float32) + crossed.astype(jnp.float32)).astype(
@@ -408,65 +435,70 @@
         )
 
 
-def attend(step, spans, head_size, place, own, got, text, more, squares):
-    cols = own.shape[1]
-    tokens = squares.shape[2]
-    half = tokens // 2
+def attend(step, spans, head_size, own, sent, got, squares, text, more):
+    half, cols = own.shape
+    tokens = 2 * half
     return pl.pallas_call(
         functools.partial(attend_kernel, step, spans, head_size),
         out_shape=jax.ShapeDtypeStruct((half, 2 * cols), jnp.bfloat16),
-        in_specs=[SMEM_SPEC] + [VMEM_SPEC] * 3 + [HBM_SPEC] * 2,
+        in_specs=[HBM_SPEC] * 6,
         out_specs=VMEM_SPEC,
         scratch_shapes=[
+            pltpu.VMEM(own.shape, jnp.bfloat16),
+            pltpu.VMEM(sent.shape, jnp.bfloat16),
+            pltpu.VMEM(got.shape, jnp.bfloat16),
+            pltpu.VMEM(squares.shape, jnp.float32),
             pltpu.VMEM((half, 2 * cols), jnp.bfloat16),
             pltpu.VMEM((tokens, 2 * cols), jnp.bfloat16),
             pltpu.VMEM((tokens, 2 * cols), jnp.bfloat16),
             pltpu.VMEM(text.shape, jnp.bfloat16),
             pltpu.VMEM(more.shape, jnp.bfloat16),
-            pltpu.SemaphoreType.DMA((2,)),
+            pltpu.SemaphoreType.DMA((6,)),
         ],
-        compiler_params=kernel_params(16),
+        compiler_params=PARAMS,
         name="attend",
-    )(place, own, got, squares, text, more)
+    )(own, sent, got, squares, text, more)
 
 
 def output_kernel(
-    step, spans, last, place_ref, current_ref, gate_ref, incoming_ref, own_ref, other_ref, *refs
+    step, spans, last, current_hbm, table_hbm, incoming_hbm, own_hbm, other_hbm, *refs
 ):
     chips = spans // 2
-    blocks, (out_ref, totals, weights, sems) = refs[:chips], refs[chips:]
-    chip, core = place_ref[0], place_ref[1]
+    block_refs, refs = refs[:chips], refs[chips:]
+    out_ref, blocks, current, gate_ref, entering, totals, weights, sems = refs
+    chip, core = own_place()
     first = core == 0
-    half, width = current_ref.shape
+    half, width = current.shape
     cols = width // 2
     rows = 2 * half // spans
-    fetches = []
+    own_lanes = pl.ds(pl.multiple_of(chip * width, width), width)
+    pairs = []
     for mask in range(chips):
         lanes = pl.ds(pl.multiple_of((chip ^ mask) * width, width), width)
-        for side, ref in enumerate((own_ref, other_ref)):
-            fetches.append(
-                pltpu.make_async_copy(
-                    ref.at[:, lanes], weights.at[mask, side], sems.at[mask, side]
-                )
-            )
-    for fetch in fetches:
-        fetch.start()
+        pairs.append((block_refs[mask], blocks.at[mask]))
+        for side, ref in enumerate((own_hbm, other_hbm)):
+            pairs.append((ref.at[:, lanes], weights.at[mask, side]))
+    pairs.append((current_hbm, current))
+    pairs.append((table_hbm.at[2, :, own_lanes], gate_ref))
+    if not last:
+        pairs.append((incoming_hbm.at[step + 1, :, own_lanes], entering))
+    copies = started(pairs, sems)
     mine = jnp.zeros((half, cols), jnp.float32)
     other = jnp.zeros((half, cols), jnp.float32)
     for mask in range(chips):
-        block = blocks[mask][...]
-        fetches[2 * mask].wait()
+        finished(copies[3 * mask : 3 * mask + 3])
+        block = blocks[mask]
         mine = mine + contract_last(block, weights[mask, 0])
-        fetches[2 * mask + 1].wait()
         other = other + contract_last(block, weights[mask, 1])
     totals[:, :cols] = jnp.where(first, mine, other)
     totals[:, cols:] = jnp.where(first, other, mine)
+    finished(copies[3 * chips :])
+    gates = gate_ref[...].astype(jnp.float32)
     for block in range(chips):
         band = slice(block * rows, (block + 1) * rows)
         places = [span_at(block + e * chips, step, spans) for e in range(2)]
-        gates = [gate_ref[s : s + 1, :] for s in places]
-        gate = jnp.where(first, gates[0], gates[1])
-        totals[band, :] = current_ref[band, :].astype(jnp.float32) + gate * totals[band, :]
+        gate = jnp.where(first, *(gates[s : s + 1, :] for s in places))
+        totals[band, :] = current[band, :].astype(jnp.float32) + gate * totals[band, :]
     if last:
         for target in range(chips):
             block = (target - STEPS // 2) % chips
@@ -474,14 +506,13 @@
     else:
         parity, block = (spans - 2 - step) % 2, (spans - 2 - step) // 2
         band = slice(block * rows, (block + 1) * rows)
-        lanes = pl.ds(pl.multiple_of(chip * width, width), width)
         totals[band, :] = jnp.where(
-            core == parity, incoming_ref[:, lanes].astype(jnp.float32), totals[band, :]
+            core == parity, entering[...].astype(jnp.float32), totals[band, :]
         )
         out_ref[...] = totals[...].astype(jnp.bfloat16)
 
 
-def output(step, spans, last, place, current, gate, incoming, own, other, blocks):
+def output(step, spans, last, current, table, incoming, own, other, blocks):
     half, width = current.shape
     chips = spans // 2
     rows = 2 * half // spans
@@ -490,16 +521,20 @@
         out_shape=jax.ShapeDtypeStruct(
             (chips, rows, width) if last else (half, width), jnp.bfloat16
         ),
-        in_specs=[SMEM_SPEC] + [VMEM_SPEC] * 3 + [HBM_SPEC] * 2 + [VMEM_SPEC] * chips,
+        in_specs=[HBM_SPEC] * (5 + chips),
         out_specs=VMEM_SPEC,
         scratch_shapes=[
+            pltpu.VMEM((chips, half, width), jnp.bfloat16),
+            pltpu.VMEM((half, width), jnp.bfloat16),
+            pltpu.VMEM((spans, width), jnp.bfloat16),
+            pltpu.VMEM((rows, width), jnp.bfloat16),
             pltpu.VMEM((half, width), jnp.float32),
             pltpu.VMEM((chips, 2, width // 2, width), jnp.bfloat16),
-            pltpu.SemaphoreType.DMA((chips, 2)),
+            pltpu.SemaphoreType.DMA((3 * chips + 3,)),
         ],
-        compiler_params=kernel_params(16),
+        compiler_params=PARAMS,
         name="output",
-    )(place, current, gate, incoming, own, other, *blocks)
+    )(current, table, incoming, own, other, *blocks)
 
 
 def join_kernel(in_ref, out_ref):
@@ -515,7 +550,7 @@
         out_shape=jax.ShapeDtypeStruct((rows, width * chips), jnp.bfloat16),
         in_specs=[VMEM_SPEC],
         out_specs=VMEM_SPEC,
-        compiler_params=kernel_params(4),
+        compiler_params=PARAMS,
         name="join",
     )(blocks)
 
@@ -539,7 +574,7 @@
         ),
         in_specs=[VMEM_SPEC] * 2,
         out_specs=VMEM_SPEC,
-        compiler_params=kernel_params(8),
+        compiler_params=PARAMS,
         name="arrange",
     )(keys, values)
 
@@ -558,32 +593,26 @@
     text_keys,
     text_values,
 ):
-    own_index = lax.axis_index("queue")
     spans = lax.axis_size("queue")
     chips = spans // 2
-    chip, core = own_index // 2, own_index % 2
-    width = hidden.shape[1]
-    cols = query_weight.shape[1]
-    head_size = width // HEADS
-    place = jnp.stack([chip, core]).astype(jnp.int32)
+    head_size = hidden.shape[1] // HEADS
     mine = gathered_over_chips(hidden)
     others = [swapped(block, 1) for block in mine]
     picked = (levels[:, None] == jnp.arange(mod_table.shape[0])[None, :]).astype(mod_table.dtype)
     table = jnp.einsum("sl,ltd->tsd", picked, mod_table, preferred_element_type=jnp.float32)
     table = table.astype(jnp.bfloat16)
-    gate = lax.dynamic_slice_in_dim(table[2], chip * 2 * cols, 2 * cols, 1).astype(jnp.float32)
-    gain = lax.dynamic_slice_in_dim(jnp.stack([query_gain, key_gain]), own_index * cols, cols, 1).T
+    gain = jnp.stack([query_gain, key_gain])
     weights = [w.T for w in (query_weight, key_weight, value_weight)]
     output_own = output_weight.T
     output_other = swapped(output_own, 1)
     text = arrange(spans, text_keys, text_values)
-    text = lax.optimization_barrier((text, *mine))[0]
+    text, table, gain = lax.optimization_barrier((text, table, gain, *mine))[:3]
     text = lax.all_to_all(text, "queue", split_axis=0, concat_axis=0, tiled=True)
     current = None
     for step in range(STEPS):
         last = step == STEPS - 1
         own, send, squares, *rest = project(
-            step, spans, place, gain, table, incoming, mine, others, weights
+            step, spans, gain, table, incoming, mine, others, weights
         )
         got = swapped(send, 1)
         squares = lax.all_to_all(squares, "queue", split_axis=0, concat_axis=0, tiled=True)
@@ -591,24 +620,16 @@
             current = rest[0]
             text = lax.optimization_barrier((text, send))[0]
             more = swapped(text, 1)
-        block = attend(step, spans, head_size, place, own, got, text, more, squares)
+        block = attend(step, spans, head_size, own, send, got, squares, text, more)
+        blocks = gathered_over_chips(block)
         result = output(
-            step,
-            spans,
-            last,
-            place,
-            current,
-            gate,
-            incoming[min(step + 1, STEPS - 1)],
-            output_own,
-            output_other,
-            gathered_over_chips(block),
+            step, spans, last, current, table, incoming, output_own, output_other, blocks
         )
         if not last:
             current = result
             mine = gathered_over_chips(current)
             others = [swapped(block, 1) for block in mine]
-    same_core = [[2 * c + core_index for c in range(chips)] for core_index in range(2)]
+    same_core = [[2 * c + core for c in range(chips)] for core in range(2)]
     result = lax.all_to_all(
         result, "queue", split_axis=0, concat_axis=0, tiled=True, axis_index_groups=same_core
     )

time: 175 us -> 159 us (0.909)
  local copies, waits for them, and re-layouts: 23.2 us -> 3.51 us
  waiting for transfers between devices: 35.9 us -> 33.2 us
  starting transfers between devices: 39.4 us -> 42 us
    unnamed x57 -> x94, local copies, waits for them, and re-layouts: 21.6 us -> 3.51 us
    ppermute x48, waiting for transfers between devices: 35.9 us -> 29.6 us  [swapped(): lax.ppermute(value, 'queue', [(source, source ^ bit) for source in range(...]
    all_to_all x1, waiting for transfers between devices: 0.01 us -> 3.6 us  [paired_device(): lax.all_to_all(text, 'queue', split_axis=0, concat_axis=0, tiled=True)]
    ppermute x48, starting transfers between devices: 33.8 us -> 37.3 us  [swapped(): lax.ppermute(value, 'queue', [(source, source ^ bit) for source in range(...]
    pallas_call x1, Pallas kernels: 0.05 us -> 1.99 us  [arrange(): pl.pallas_call(functools.partial(arrange_kernel, spans), out_shape=jax.Sh...]
  transfers between devices with their start and end apart: 49 -> 49, of which waited for: 25 -> 23; matrix products, arithmetic and copies ran while one was open for 3% -> 2% of each run, Pallas kernels for 9% -> 10%
where the time goes in v4:
time: 159 us; the launch traced here: 158 us
  Pallas kernels  42.7 us (27%)
  starting transfers between devices  42 us (26%)
  waiting for transfers between devices  33.2 us (21%)
  blocking collectives  32.9 us (21%)
  local copies, waits for them, and re-layouts  3.51 us (2%)
  matrix products  2.02 us (1%)
    ppermute x48, starting transfers between devices, swapped(): lax.ppermute(value, 'queue', [(source, source ^ bit) for source in range(...  37.3 us
    ppermute x48, waiting for transfers between devices, swapped(): lax.ppermute(value, 'queue', [(source, source ^ bit) for source in range(...  29.6 us
    all_to_all x2, blocking collectives, paired_device(): lax.all_to_all(squares, 'queue', split_axis=0, concat_axis=0, tiled=True)  21.9 us
    pallas_call x2, Pallas kernels, project(): pl.pallas_call(functools.partial(project_kernel, step, spans), out_shape=...  17.4 us
    pallas_call x2, Pallas kernels, attend(): pl.pallas_call(functools.partial(attend_kernel, step, spans, head_size),...  11.4 us
    all_to_all x1, blocking collectives, paired_device(): lax.all_to_all(result, 'queue', split_axis=0, concat_axis=0, tiled=True,...  11 us
    pallas_call x2, Pallas kernels, output(): pl.pallas_call(functools.partial(output_kernel, step, spans, last), out_s...  10.4 us
    all_to_all x1, starting transfers between devices, paired_device(): lax.all_to_all(text, 'queue', split_axis=0, concat_axis=0, tiled=True)  4.73 us
  transfers between devices with their start and end apart: 49, of which 23 were waited for; matrix products, arithmetic and copies ran while one was open for 2% of the time, Pallas kernels for 10%

profile of v4, /device:TPU:0, one launch (start us, length us, event | category | flops | bytes accessed | tf_op | source)
XLA Modules:
  0.0 158.2 jit_solution(8458382063410308713)
XLA Ops:
  0.0 0.5 collective-permute-start.15
  0.5 4.7 %collective-permute-start.5 = (bf16[8,5120]{1,0:T(8,128)(2,1)}, bf16[8,5120]{1,0:T(8,128)(2,1)S(1)}, u32[]{:S(2)}, u32[]{:S(2)}) collective-permute-start(bf16[8,5120]{1,0:T(8,128)(2,1)} %refs_3_.1), channel_id=1, source_target_pairs={{0,12},{1,13},{2,14},{3,15},{4,8},{5,9},{6,10},{7,11},{8,4},{9,5},... | collective-permute-start | bytes 245768 | tf_op jit(solution)/shard_map/ppermute | solution.py:174
  5.1 0.7 collective-permute-start.1
  5.8 1.6 %collective-permute-start = (bf16[8,5120]{1,0:T(8,128)(2,1)}, bf16[8,5120]{1,0:T(8,128)(2,1)S(1)}, u32[]{:S(2)}, u32[]{:S(2)}) collective-permute-start(bf16[8,5120]{1,0:T(8,128)(2,1)} %refs_3_.1), channel_id=1, source_target_pairs={{0,2},{1,3},{2,0},{3,1},{4,6},{5,7},{6,4},{7,5},{8,10},{9,11},{10,... | collective-permute-start | bytes 245768 | tf_op jit(solution)/shard_map/ppermute | solution.py:174
  7.4 1.4 pad_maximum_fusion.gain_hbm
  8.8 1.6 collective-permute-start.6
  10.4 2.4 %collective-permute-done.3.refs_7_ = bf16[8,5120]{1,0:T(8,128)(2,1)S(1)} collective-permute-done((bf16[8,5120]{1,0:T(8,128)(2,1)}, bf16[8,5120]{1,0:T(8,128)(2,1)S(1)}, u32[]{:S(2)}, u32[]{:S(2)}) %collective-permute-start.3) | collective-permute-done | bytes 81952 | tf_op jit(solution)/shard_map/ppermute | solution.py:174
  12.8 1.5 collective-permute-start.4
  14.3 0.5 collective-permute-start.2
  14.9 2.0 %fusion.table_hbm = bf16[3,16,5120]{2,1,0:T(8,128)(2,1)} fusion(bf16[96,3,5120]{2,0,1:T(8,128)(2,1)S(1)} %copy-done, s32[16]{0:T(128)} %param.14), kind=kOutput, calls=%fused_computation.1 | convolution fusion | flops 47433216 | bytes 3440704 | tf_op jit(solution)/shard_map/sl,ltd->tsd/dot_general | solution.py:602
  16.9 2.0 %arrange.1 = bf16[16,2,16,640]{3,2,1,0:T(8,128)(2,1)} custom-call(bf16[32,5120]{1,0:T(8,128)(2,1)} %keys_ref.1, bf16[32,5120]{1,0:T(8,128)(2,1)} %values_ref.1), custom_call_target="tpu_custom_call" | custom-call | tf_op jit(solution)/shard_map/arrange/pallas_call | solution.py:570
  19.1 4.7 %all-to-all-start.1 = ((bf16[16,2,16,640]{3,2,1,0:T(8,128)(2,1)}), bf16[16,2,16,640]{3,2,1,0:T(8,128)(2,1)}, u32[]{:S(2)}, u32[]{:S(2)}) async-start(bf16[16,2,16,640]{3,2,1,0:T(8,128)(2,1)} %arrange.1), calls=%async_computation.1 | async-start | bytes 1310720 | tf_op jit(solution)/shard_map/all_to_all | solution.py:610
  23.8 0.4 collective-permute-start.7
  24.4 0.4 collective-permute-start.11
  26.4 0.4 collective-permute-done.14.refs_18_
  27.0 0.6 collective-permute-done.10.refs_14_
  27.6 0.5 copy-done.42
  28.2 8.7 %project.2 = (bf16[64,320]{1,0:T(8,128)(2,1)}, bf16[320,320]{1,0:T(8,128)(2,1)}, f32[16,2,128]{2,1,0:T(2,128)}, bf16[64,640]{1,0:T(8,128)(2,1)}) custom-call(f32[2,5120]{1,0:T(2,128)} %pad_maximum_fusion.gain_hbm, bf16[3,16,5120]{2,1,0:T(8,128)(2,1)} %fusion.table_hbm, bf16[2,8,5120]{2,1,0:T(8,128)(2,1)} %incoming_hbm.7, bf16[320,5120]{1,0:T(8,128)(2,1)} %bitcast.12, ...), custom_call_target="tpu_custom_call" | custom-call | tf_op jit(solution)/shard_map/project/pallas_call | solution.py:337
  36.9 3.6 %all-to-all-done.1.text_hbm = bf16[16,2,16,640]{3,2,1,0:T(8,128)(2,1)} async-done(((bf16[16,2,16,640]{3,2,1,0:T(8,128)(2,1)}), bf16[16,2,16,640]{3,2,1,0:T(8,128)(2,1)}, u32[]{:S(2)}, u32[]{:S(2)}) %all-to-all-start.1) | async-done | bytes 655392 | tf_op jit(solution)/shard_map/all_to_all | solution.py:610
  40.5 0.4 collective-permute-start.16
  41.0 11.4 %all_to_all.20.squares_hbm = f32[16,2,128]{2,1,0:T(2,128)} all-to-all(f32[16,2,128]{2,1,0:T(2,128)} %get-tuple-element.21), channel_id=1, replica_groups=mesh['groups'=2,'queue'=16] {'queue'}, dimensions={0} | all-to-all | bytes 32768 | tf_op jit(solution)/shard_map/all_to_all | solution.py:618
  52.3 0.7 copy-done.2
  53.3 5.7 %attend.2.refs_0_ = bf16[64,640]{1,0:T(8,128)(2,1)} custom-call(bf16[64,320]{1,0:T(8,128)(2,1)} %get-tuple-element.19.own_hbm, bf16[320,320]{1,0:T(8,128)(2,1)} %get-tuple-element.20.sent_hbm, bf16[320,320]{1,0:T(8,128)(2,1)} %copy-done.2, f32[16,2,128]{2,1,0:T(2,128)} %all_to_all.20.squares_hbm, bf16[16,2,16,640]{3,2,1,0:T(8,128)(2,1)} %all-to-all-done.1.text_hbm, ...), custom_call_target="tpu_custom_call" | custom-call | tf_op jit(solution)/shard_map/attend/pallas_call | solution.py:441
  59.0 0.6 collective-permute-start.23
  59.5 1.4 collective-permute-start.21
  61.0 2.5 %collective-permute-start.19 = (bf16[64,640]{1,0:T(8,128)(2,1)}, bf16[64,640]{1,0:T(8,128)(2,1)S(1)}, u32[]{:S(2)}, u32[]{:S(2)}) collective-permute-start(bf16[64,640]{1,0:T(8,128)(2,1)} %attend.2.refs_0_), channel_id=1, source_target_pairs={{0,4},{1,5},{2,6},{3,7},{4,0},{5,1},{6,2},{7,3},{8,12},{9,13},{10,... | collective-permute-start | bytes 245768 | tf_op jit(solution)/shard_map/ppermute | solution.py:174
  63.4 0.5 collective-permute-start.18
  63.9 2.5 %collective-permute-done.23.refs_6_ = bf16[64,640]{1,0:T(8,128)(2,1)S(1)} collective-permute-done((bf16[64,640]{1,0:T(8,128)(2,1)}, bf16[64,640]{1,0:T(8,128)(2,1)S(1)}, u32[]{:S(2)}, u32[]{:S(2)}) %collective-permute-start.23) | collective-permute-done | bytes 81952 | tf_op jit(solution)/shard_map/ppermute | solution.py:174
  66.4 0.5 collective-permute-start.24
  66.9 2.0 %collective-permute-done.21.refs_4_ = bf16[64,640]{1,0:T(8,128)(2,1)S(1)} collective-permute-done((bf16[64,640]{1,0:T(8,128)(2,1)}, bf16[64,640]{1,0:T(8,128)(2,1)S(1)}, u32[]{:S(2)}, u32[]{:S(2)}) %collective-permute-start.21) | collective-permute-done | bytes 81952 | tf_op jit(solution)/shard_map/ppermute | solution.py:174
  68.9 0.6 collective-permute-start.22
  69.5 1.4 collective-permute-start.20
  70.9 2.7 %collective-permute-done.22.refs_5_ = bf16[64,640]{1,0:T(8,128)(2,1)S(1)} collective-permute-done((bf16[64,640]{1,0:T(8,128)(2,1)S(1)}, bf16[64,640]{1,0:T(8,128)(2,1)S(1)}, u32[]{:S(2)}, u32[]{:S(2)}) %collective-permute-start.22) | collective-permute-done | bytes 81952 | tf_op jit(solution)/shard_map/ppermute | solution.py:174
  73.6 0.9 collective-permute-done.20.refs_3_
  74.5 0.6 copy-done.45
  75.1 5.2 %output.2.refs_3_.current_hbm = bf16[64,640]{1,0:T(8,128)(2,1)} custom-call(bf16[64,640]{1,0:T(8,128)(2,1)} %get-tuple-element.18.current_hbm, bf16[3,16,5120]{2,1,0:T(8,128)(2,1)} %fusion.table_hbm, bf16[2,8,5120]{2,1,0:T(8,128)(2,1)} %incoming_hbm.7, bf16[320,5120]{1,0:T(8,128)(2,1)} %bitcast.19, bf16[320,5120]{1,0:T(8,128)(2,1)} %collective-permute-done.15.other_hbm, ...), custom_call_target="tpu_custom_call" | custom-call | tf_op jit(solution)/shard_map/output/pallas_call | solution.py:519
  80.3 1.4 collective-permute-start.30
  81.8 3.0 %collective-permute-start.26 = (bf16[64,640]{1,0:T(8,128)(2,1)}, bf16[64,640]{1,0:T(8,128)(2,1)S(1)}, u32[]{:S(2)}, u32[]{:S(2)}) collective-permute-start(bf16[64,640]{1,0:T(8,128)(2,1)} %output.2.refs_3_.current_hbm), channel_id=1, source_target_pairs={{0,4},{1,5},{2,6},{3,7},{4,0},{5,1},{6,2},{7,3},{8,12},{9,13},{10,... | collective-permute-start | bytes 245768 | tf_op jit(solution)/shard_map/ppermute | solution.py:174
  84.8 0.9 collective-permute-start.25
  85.7 2.1 %collective-permute-done.30.refs_9_ = bf16[64,640]{1,0:T(8,128)(2,1)S(1)} collective-permute-done((bf16[64,640]{1,0:T(8,128)(2,1)}, bf16[64,640]{1,0:T(8,128)(2,1)S(1)}, u32[]{:S(2)}, u32[]{:S(2)}) %collective-permute-start.30) | collective-permute-done | bytes 81952 | tf_op jit(solution)/shard_map/ppermute | solution.py:174
  87.8 0.9 collective-permute-start.31
  88.7 1.5 collective-permute-done.28.refs_7_
  90.4 0.9 collective-permute-start.29
  91.3 1.1 collective-permute-start.27
  93.2 2.5 %collective-permute-done.29.refs_8_ = bf16[64,640]{1,0:T(8,128)(2,1)S(1)} collective-permute-done((bf16[64,640]{1,0:T(8,128)(2,1)S(1)}, bf16[64,640]{1,0:T(8,128)(2,1)S(1)}, u32[]{:S(2)}, u32[]{:S(2)}) %collective-permute-start.29) | collective-permute-done | bytes 81952 | tf_op jit(solution)/shard_map/ppermute | solution.py:174
  95.7 1.2 collective-permute-done.27.refs_6_
  97.0 1.3 collective-permute-done.35.refs_14_
  98.4 8.7 %project.3 = (bf16[64,320]{1,0:T(8,128)(2,1)}, bf16[320,320]{1,0:T(8,128)(2,1)}, f32[16,2,128]{2,1,0:T(2,128)}) custom-call(f32[2,5120]{1,0:T(2,128)} %pad_maximum_fusion.gain_hbm, bf16[3,16,5120]{2,1,0:T(8,128)(2,1)} %fusion.table_hbm, bf16[2,8,5120]{2,1,0:T(8,128)(2,1)} %incoming_hbm.7, bf16[320,5120]{1,0:T(8,128)(2,1)} %bitcast.13, ...), custom_call_target="tpu_custom_call" | custom-call | tf_op jit(solution)/shard_map/project/pallas_call | solution.py:337
  107.3 10.5 %all_to_all.21.squares_hbm = f32[16,2,128]{2,1,0:T(2,128)} all-to-all(f32[16,2,128]{2,1,0:T(2,128)} %get-tuple-element.26), channel_id=1, replica_groups=mesh['groups'=2,'queue'=16] {'queue'}, dimensions={0} | all-to-all | bytes 32768 | tf_op jit(solution)/shard_map/all_to_all | solution.py:618
  117.9 0.7 copy-done.3
  118.6 5.7 %attend.3.refs_0_ = bf16[64,640]{1,0:T(8,128)(2,1)} custom-call(bf16[64,320]{1,0:T(8,128)(2,1)} %get-tuple-element.24.own_hbm, bf16[320,320]{1,0:T(8,128)(2,1)} %get-tuple-element.25.sent_hbm, bf16[320,320]{1,0:T(8,128)(2,1)} %copy-done.3, f32[16,2,128]{2,1,0:T(2,128)} %all_to_all.21.squares_hbm, bf16[16,2,16,640]{3,2,1,0:T(8,128)(2,1)} %all-to-all-done.1.text_hbm, ...), custom_call_target="tpu_custom_call" | custom-call | tf_op jit(solution)/shard_map/attend/pallas_call | solution.py:441
  124.3 0.6 collective-permute-start.46
  124.8 1.4 collective-permute-start.44
  126.2 2.5 %collective-permute-start.42 = (bf16[64,640]{1,0:T(8,128)(2,1)}, bf16[64,640]{1,0:T(8,128)(2,1)S(1)}, u32[]{:S(2)}, u32[]{:S(2)}) collective-permute-start(bf16[64,640]{1,0:T(8,128)(2,1)} %attend.3.refs_0_), channel_id=1, source_target_pairs={{0,4},{1,5},{2,6},{3,7},{4,0},{5,1},{6,2},{7,3},{8,12},{9,13},{10,... | collective-permute-start | bytes 245768 | tf_op jit(solution)/shard_map/ppermute | solution.py:174
  129.0 2.7 %collective-permute-done.46.refs_6_ = bf16[64,640]{1,0:T(8,128)(2,1)S(1)} collective-permute-done((bf16[64,640]{1,0:T(8,128)(2,1)}, bf16[64,640]{1,0:T(8,128)(2,1)S(1)}, u32[]{:S(2)}, u32[]{:S(2)}) %collective-permute-start.46) | collective-permute-done | bytes 81952 | tf_op jit(solution)/shard_map/ppermute | solution.py:174
  132.0 2.1 %collective-permute-done.44.refs_4_ = bf16[64,640]{1,0:T(8,128)(2,1)S(1)} collective-permute-done((bf16[64,640]{1,0:T(8,128)(2,1)}, bf16[64,640]{1,0:T(8,128)(2,1)S(1)}, u32[]{:S(2)}, u32[]{:S(2)}) %collective-permute-start.44) | collective-permute-done | bytes 81952 | tf_op jit(solution)/shard_map/ppermute | solution.py:174
  134.2 0.6 collective-permute-start.45
  134.7 1.5 collective-permute-start.43
  136.2 2.7 %collective-permute-done.45.refs_5_ = bf16[64,640]{1,0:T(8,128)(2,1)S(1)} collective-permute-done((bf16[64,640]{1,0:T(8,128)(2,1)S(1)}, bf16[64,640]{1,0:T(8,128)(2,1)S(1)}, u32[]{:S(2)}, u32[]{:S(2)}) %collective-permute-start.45) | collective-permute-done | bytes 81952 | tf_op jit(solution)/shard_map/ppermute | solution.py:174
  139.0 0.9 collective-permute-done.43.refs_3_
  139.9 0.6 copy-done.46
  140.5 5.2 %output.3 = bf16[8,8,640]{2,1,0:T(8,128)(2,1)} custom-call(bf16[64,640]{1,0:T(8,128)(2,1)} %output.2.refs_3_.current_hbm, bf16[3,16,5120]{2,1,0:T(8,128)(2,1)} %fusion.table_hbm, bf16[2,8,5120]{2,1,0:T(8,128)(2,1)} %incoming_hbm.7, bf16[320,5120]{1,0:T(8,128)(2,1)} %bitcast.20, bf16[320,5120]{1,0:T(8,128)(2,1)} %collective-permute-done.15.other_hbm, ...), custom_call_target="tpu_custom_call" | custom-call | tf_op jit(solution)/shard_map/output/pallas_call | solution.py:519
  145.7 11.0 %all_to_all.22.in_ref = bf16[8,8,640]{2,1,0:T(8,128)(2,1)} all-to-all(bf16[8,8,640]{2,1,0:T(8,128)(2,1)} %output.3), channel_id=1, replica_groups={{0,2,4,6,8,10,12,14},{1,3,5,7,9,11,13,15},{16,18,20,22,24,26,28,30},{17..., dimensions={0} | all-to-all | bytes 163840 | tf_op jit(solution)/shard_map/all_to_all | solution.py:633
  156.7 1.5 join.1
  (141 shorter events, 4.5 us)
Async XLA Ops:
  0.0 14.9 %copy-start = (bf16[96,3,5120]{2,0,1:T(8,128)(2,1)S(1)}, bf16[96,3,5120]{2,0,1:T(8,128)(2,1)}, u32[]{:S(2)}) copy-start(bf16[96,3,5120]{2,0,1:T(8,128)(2,1)} %param.15) | copy-start | bytes 8847364
  0.0 23.8 %copy-start.4 = (bf16[8,5120]{1,0:T(8,128)(2,1)S(1)}, bf16[8,5120]{1,0:T(8,128)(2,1)}, u32[]{:S(2)}) copy-start(bf16[8,5120]{1,0:T(8,128)(2,1)} %refs_3_.1) | copy-start | bytes 245764
  0.0 74.5 %collective-permute-start.15 = (bf16[320,5120]{1,0:T(8,128)(2,1)}, bf16[320,5120]{1,0:T(8,128)(2,1)}, u32[]{:S(2)}, u32[]{:S(2)}) collective-permute-start(bf16[320,5120]{1,0:T(8,128)(2,1)} %bitcast.18), channel_id=1, source_target_pairs={{0,1},{1,0},{2,3},{3,2},{4,5},{5,4},{6,7},{7,6},{8,9},{9,8},{10,11... | collective-permute-start | bytes 9830408 | tf_op jit(solution)/shard_map/ppermute | solution.py:174
  0.5 8.4 %collective-permute-start.5 = (bf16[8,5120]{1,0:T(8,128)(2,1)}, bf16[8,5120]{1,0:T(8,128)(2,1)S(1)}, u32[]{:S(2)}, u32[]{:S(2)}) collective-permute-start(bf16[8,5120]{1,0:T(8,128)(2,1)} %refs_3_.1), channel_id=1, source_target_pairs={{0,12},{1,13},{2,14},{3,15},{4,8},{5,9},{6,10},{7,11},{8,4},{9,5},... | collective-permute-start | bytes 245768 | tf_op jit(solution)/shard_map/ppermute | solution.py:174
  5.1 7.7 %collective-permute-start.3 = (bf16[8,5120]{1,0:T(8,128)(2,1)}, bf16[8,5120]{1,0:T(8,128)(2,1)S(1)}, u32[]{:S(2)}, u32[]{:S(2)}) collective-permute-start(bf16[8,5120]{1,0:T(8,128)(2,1)} %refs_3_.1), channel_id=1, source_target_pairs={{0,8},{1,9},{2,10},{3,11},{4,12},{5,13},{6,14},{7,15},{8,0},{9,1},... | collective-permute-start | bytes 245768 | tf_op jit(solution)/shard_map/ppermute | solution.py:174
  5.1 9.2 %collective-permute-start.1 = (bf16[8,5120]{1,0:T(8,128)(2,1)}, bf16[8,5120]{1,0:T(8,128)(2,1)S(1)}, u32[]{:S(2)}, u32[]{:S(2)}) collective-permute-start(bf16[8,5120]{1,0:T(8,128)(2,1)} %refs_3_.1), channel_id=1, source_target_pairs={{0,4},{1,5},{2,6},{3,7},{4,0},{5,1},{6,2},{7,3},{8,12},{9,13},{10,... | collective-permute-start | bytes 245768 | tf_op jit(solution)/shard_map/ppermute | solution.py:174
  5.8 13.1 %collective-permute-start = (bf16[8,5120]{1,0:T(8,128)(2,1)}, bf16[8,5120]{1,0:T(8,128)(2,1)S(1)}, u32[]{:S(2)}, u32[]{:S(2)}) collective-permute-start(bf16[8,5120]{1,0:T(8,128)(2,1)} %refs_3_.1), channel_id=1, source_target_pairs={{0,2},{1,3},{2,0},{3,1},{4,6},{5,7},{6,4},{7,5},{8,10},{9,11},{10,... | collective-permute-start | bytes 245768 | tf_op jit(solution)/shard_map/ppermute | solution.py:174
  8.8 18.7 %copy-start.5 = (bf16[8,5120]{1,0:T(8,128)(2,1)}, bf16[8,5120]{1,0:T(8,128)(2,1)S(1)}, u32[]{:S(2)}) copy-start(bf16[8,5120]{1,0:T(8,128)(2,1)S(1)} %collective-permute-done.5.refs_9_) | copy-start | bytes 245764
  8.8 10.0 %collective-permute-start.6 = (bf16[8,5120]{1,0:T(8,128)(2,1)S(1)}, bf16[8,5120]{1,0:T(8,128)(2,1)S(1)}, u32[]{:S(2)}, u32[]{:S(2)}) collective-permute-start(bf16[8,5120]{1,0:T(8,128)(2,1)S(1)} %collective-permute-done.5.refs_9_), channel_id=1, source_target_pairs={{0,2},{1,3},{2,0},{3,1},{4,6},{5,7},{6,4},{7,5},{8,10},{9,11},{10,... | collective-permute-start | bytes 245768 | tf_op jit(solution)/shard_map/ppermute | solution.py:174
  12.8 14.7 %copy-start.6 = (bf16[8,5120]{1,0:T(8,128)(2,1)}, bf16[8,5120]{1,0:T(8,128)(2,1)S(1)}, u32[]{:S(2)}) copy-start(bf16[8,5120]{1,0:T(8,128)(2,1)S(1)} %collective-permute-done.3.refs_7_) | copy-start | bytes 245764
  12.8 6.1 %collective-permute-start.4 = (bf16[8,5120]{1,0:T(8,128)(2,1)S(1)}, bf16[8,5120]{1,0:T(8,128)(2,1)S(1)}, u32[]{:S(2)}, u32[]{:S(2)}) collective-permute-start(bf16[8,5120]{1,0:T(8,128)(2,1)S(1)} %collective-permute-done.3.refs_7_), channel_id=1, source_target_pairs={{0,2},{1,3},{2,0},{3,1},{4,6},{5,7},{6,4},{7,5},{8,10},{9,11},{10,... | collective-permute-start | bytes 245768 | tf_op jit(solution)/shard_map/ppermute | solution.py:174
  14.3 13.2 %copy-start.7 = (bf16[8,5120]{1,0:T(8,128)(2,1)}, bf16[8,5120]{1,0:T(8,128)(2,1)S(1)}, u32[]{:S(2)}) copy-start(bf16[8,5120]{1,0:T(8,128)(2,1)S(1)} %collective-permute-done.1.refs_5_) | copy-start | bytes 245764
  14.3 4.7 %collective-permute-start.2 = (bf16[8,5120]{1,0:T(8,128)(2,1)S(1)}, bf16[8,5120]{1,0:T(8,128)(2,1)}, u32[]{:S(2)}, u32[]{:S(2)}) collective-permute-start(bf16[8,5120]{1,0:T(8,128)(2,1)S(1)} %collective-permute-done.1.refs_5_), channel_id=1, source_target_pairs={{0,2},{1,3},{2,0},{3,1},{4,6},{5,7},{6,4},{7,5},{8,10},{9,11},{10,... | collective-permute-start | bytes 245768 | tf_op jit(solution)/shard_map/ppermute | solution.py:174
  18.9 8.7 %copy-start.9 = (bf16[8,5120]{1,0:T(8,128)(2,1)}, bf16[8,5120]{1,0:T(8,128)(2,1)S(1)}, u32[]{:S(2)}) copy-start(bf16[8,5120]{1,0:T(8,128)(2,1)S(1)} %collective-permute-done.refs_4_) | copy-start | bytes 245764
  18.9 8.7 %copy-start.12 = (bf16[8,5120]{1,0:T(8,128)(2,1)}, bf16[8,5120]{1,0:T(8,128)(2,1)S(1)}, u32[]{:S(2)}) copy-start(bf16[8,5120]{1,0:T(8,128)(2,1)S(1)} %collective-permute-done.6.refs_10_) | copy-start | bytes 245764
  18.9 8.7 %copy-start.15 = (bf16[8,5120]{1,0:T(8,128)(2,1)}, bf16[8,5120]{1,0:T(8,128)(2,1)S(1)}, u32[]{:S(2)}) copy-start(bf16[8,5120]{1,0:T(8,128)(2,1)S(1)} %collective-permute-done.4.refs_8_) | copy-start | bytes 245764
  19.1 21.4 %all-to-all-start.1 = ((bf16[16,2,16,640]{3,2,1,0:T(8,128)(2,1)}), bf16[16,2,16,640]{3,2,1,0:T(8,128)(2,1)}, u32[]{:S(2)}, u32[]{:S(2)}) async-start(bf16[16,2,16,640]{3,2,1,0:T(8,128)(2,1)} %arrange.1), calls=%async_computation.1 | async-start | bytes 1310720 | tf_op jit(solution)/shard_map/all_to_all | solution.py:610
  23.8 1.3 collective-permute-start.7
  24.2 1.3 collective-permute-start.13
  24.4 1.3 collective-permute-start.11
  24.7 1.3 collective-permute-start.9
  25.2 1.3 collective-permute-start.8
  25.5 1.3 collective-permute-start.14
  25.7 1.3 collective-permute-start.12
  26.0 1.5 collective-permute-start.10
  40.5 11.9 %collective-permute-start.17 = (bf16[16,2,16,640]{3,2,1,0:T(8,128)(2,1)}, bf16[16,2,16,640]{3,2,1,0:T(8,128)(2,1)S(1)}, u32[]{:S(2)}, u32[]{:S(2)}) collective-permute-start(bf16[16,2,16,640]{3,2,1,0:T(8,128)(2,1)} %all-to-all-done.1.text_hbm), channel_id=1, source_target_pairs={{0,1},{1,0},{2,3},{3,2},{4,5},{5,4},{6,7},{7,6},{8,9},{9,8},{10,11... | collective-permute-start | bytes 1966088 | tf_op jit(solution)/shard_map/ppermute | solution.py:174
  40.5 11.8 %collective-permute-start.16 = (bf16[320,320]{1,0:T(8,128)(2,1)}, bf16[320,320]{1,0:T(8,128)(2,1)S(1)}, u32[]{:S(2)}, u32[]{:S(2)}) collective-permute-start(bf16[320,320]{1,0:T(8,128)(2,1)} %get-tuple-element.20.sent_hbm), channel_id=1, source_target_pairs={{0,1},{1,0},{2,3},{3,2},{4,5},{5,4},{6,7},{7,6},{8,9},{9,8},{10,11... | collective-permute-start | bytes 614408 | tf_op jit(solution)/shard_map/ppermute | solution.py:174
  59.0 7.4 %collective-permute-start.23 = (bf16[64,640]{1,0:T(8,128)(2,1)}, bf16[64,640]{1,0:T(8,128)(2,1)S(1)}, u32[]{:S(2)}, u32[]{:S(2)}) collective-permute-start(bf16[64,640]{1,0:T(8,128)(2,1)} %attend.2.refs_0_), channel_id=1, source_target_pairs={{0,12},{1,13},{2,14},{3,15},{4,8},{5,9},{6,10},{7,11},{8,4},{9,5},... | collective-permute-start | bytes 245768 | tf_op jit(solution)/shard_map/ppermute | solution.py:174
  59.5 9.3 %collective-permute-start.21 = (bf16[64,640]{1,0:T(8,128)(2,1)}, bf16[64,640]{1,0:T(8,128)(2,1)S(1)}, u32[]{:S(2)}, u32[]{:S(2)}) collective-permute-start(bf16[64,640]{1,0:T(8,128)(2,1)} %attend.2.refs_0_), channel_id=1, source_target_pairs={{0,8},{1,9},{2,10},{3,11},{4,12},{5,13},{6,14},{7,15},{8,0},{9,1},... | collective-permute-start | bytes 245768 | tf_op jit(solution)/shard_map/ppermute | solution.py:174
  61.0 8.5 %collective-permute-start.19 = (bf16[64,640]{1,0:T(8,128)(2,1)}, bf16[64,640]{1,0:T(8,128)(2,1)S(1)}, u32[]{:S(2)}, u32[]{:S(2)}) collective-permute-start(bf16[64,640]{1,0:T(8,128)(2,1)} %attend.2.refs_0_), channel_id=1, source_target_pairs={{0,4},{1,5},{2,6},{3,7},{4,0},{5,1},{6,2},{7,3},{8,12},{9,13},{10,... | collective-permute-start | bytes 245768 | tf_op jit(solution)/shard_map/ppermute | solution.py:174
  63.4 7.5 %collective-permute-start.18 = (bf16[64,640]{1,0:T(8,128)(2,1)}, bf16[64,640]{1,0:T(8,128)(2,1)S(1)}, u32[]{:S(2)}, u32[]{:S(2)}) collective-permute-start(bf16[64,640]{1,0:T(8,128)(2,1)} %attend.2.refs_0_), channel_id=1, source_target_pairs={{0,2},{1,3},{2,0},{3,1},{4,6},{5,7},{6,4},{7,5},{8,10},{9,11},{10,... | collective-permute-start | bytes 245768 | tf_op jit(solution)/shard_map/ppermute | solution.py:174
  66.4 8.1 %copy-start.26 = (bf16[64,640]{1,0:T(8,128)(2,1)}, bf16[64,640]{1,0:T(8,128)(2,1)S(1)}, u32[]{:S(2)}) copy-start(bf16[64,640]{1,0:T(8,128)(2,1)S(1)} %collective-permute-done.23.refs_6_) | copy-start | bytes 245764
  66.4 4.5 %collective-permute-start.24 = (bf16[64,640]{1,0:T(8,128)(2,1)S(1)}, bf16[64,640]{1,0:T(8,128)(2,1)S(1)}, u32[]{:S(2)}, u32[]{:S(2)}) collective-permute-start(bf16[64,640]{1,0:T(8,128)(2,1)S(1)} %collective-permute-done.23.refs_6_), channel_id=1, source_target_pairs={{0,2},{1,3},{2,0},{3,1},{4,6},{5,7},{6,4},{7,5},{8,10},{9,11},{10,... | collective-permute-start | bytes 245768 | tf_op jit(solution)/shard_map/ppermute | solution.py:174
  68.9 4.7 %collective-permute-start.22 = (bf16[64,640]{1,0:T(8,128)(2,1)S(1)}, bf16[64,640]{1,0:T(8,128)(2,1)S(1)}, u32[]{:S(2)}, u32[]{:S(2)}) collective-permute-start(bf16[64,640]{1,0:T(8,128)(2,1)S(1)} %collective-permute-done.21.refs_4_), channel_id=1, source_target_pairs={{0,2},{1,3},{2,0},{3,1},{4,6},{5,7},{6,4},{7,5},{8,10},{9,11},{10,... | collective-permute-start | bytes 245768 | tf_op jit(solution)/shard_map/ppermute | solution.py:174
  69.5 5.0 %collective-permute-start.20 = (bf16[64,640]{1,0:T(8,128)(2,1)S(1)}, bf16[64,640]{1,0:T(8,128)(2,1)S(1)}, u32[]{:S(2)}, u32[]{:S(2)}) collective-permute-start(bf16[64,640]{1,0:T(8,128)(2,1)S(1)} %collective-permute-done.19.refs_2_), channel_id=1, source_target_pairs={{0,2},{1,3},{2,0},{3,1},{4,6},{5,7},{6,4},{7,5},{8,10},{9,11},{10,... | collective-permute-start | bytes 245768 | tf_op jit(solution)/shard_map/ppermute | solution.py:174
  80.3 7.4 %collective-permute-start.30 = (bf16[64,640]{1,0:T(8,128)(2,1)}, bf16[64,640]{1,0:T(8,128)(2,1)S(1)}, u32[]{:S(2)}, u32[]{:S(2)}) collective-permute-start(bf16[64,640]{1,0:T(8,128)(2,1)} %output.2.refs_3_.current_hbm), channel_id=1, source_target_pairs={{0,12},{1,13},{2,14},{3,15},{4,8},{5,9},{6,10},{7,11},{8,4},{9,5},... | collective-permute-start | bytes 245768 | tf_op jit(solution)/shard_map/ppermute | solution.py:174
  81.8 6.0 %collective-permute-start.32 = (bf16[64,640]{1,0:T(8,128)(2,1)}, bf16[64,640]{1,0:T(8,128)(2,1)S(1)}, u32[]{:S(2)}, u32[]{:S(2)}) collective-permute-start(bf16[64,640]{1,0:T(8,128)(2,1)} %output.2.refs_3_.current_hbm), channel_id=1, source_target_pairs={{0,1},{1,0},{2,3},{3,2},{4,5},{5,4},{6,7},{7,6},{8,9},{9,8},{10,11... | collective-permute-start | bytes 245768 | tf_op jit(solution)/shard_map/ppermute | solution.py:174
  81.8 8.5 %collective-permute-start.28 = (bf16[64,640]{1,0:T(8,128)(2,1)}, bf16[64,640]{1,0:T(8,128)(2,1)S(1)}, u32[]{:S(2)}, u32[]{:S(2)}) collective-permute-start(bf16[64,640]{1,0:T(8,128)(2,1)} %output.2.refs_3_.current_hbm), channel_id=1, source_target_pairs={{0,8},{1,9},{2,10},{3,11},{4,12},{5,13},{6,14},{7,15},{8,0},{9,1},... | collective-permute-start | bytes 245768 | tf_op jit(solution)/shard_map/ppermute | solution.py:174
  81.8 8.7 %collective-permute-start.26 = (bf16[64,640]{1,0:T(8,128)(2,1)}, bf16[64,640]{1,0:T(8,128)(2,1)S(1)}, u32[]{:S(2)}, u32[]{:S(2)}) collective-permute-start(bf16[64,640]{1,0:T(8,128)(2,1)} %output.2.refs_3_.current_hbm), channel_id=1, source_target_pairs={{0,4},{1,5},{2,6},{3,7},{4,0},{5,1},{6,2},{7,3},{8,12},{9,13},{10,... | collective-permute-start | bytes 245768 | tf_op jit(solution)/shard_map/ppermute | solution.py:174
  84.8 6.5 %collective-permute-start.25 = (bf16[64,640]{1,0:T(8,128)(2,1)}, bf16[64,640]{1,0:T(8,128)(2,1)S(1)}, u32[]{:S(2)}, u32[]{:S(2)}) collective-permute-start(bf16[64,640]{1,0:T(8,128)(2,1)} %output.2.refs_3_.current_hbm), channel_id=1, source_target_pairs={{0,2},{1,3},{2,0},{3,1},{4,6},{5,7},{6,4},{7,5},{8,10},{9,11},{10,... | collective-permute-start | bytes 245768 | tf_op jit(solution)/shard_map/ppermute | solution.py:174
  87.7 10.5 %copy-start.8 = (bf16[64,640]{1,0:T(8,128)(2,1)}, bf16[64,640]{1,0:T(8,128)(2,1)S(1)}, u32[]{:S(2)}) copy-start(bf16[64,640]{1,0:T(8,128)(2,1)S(1)} %collective-permute-done.30.refs_9_) | copy-start | bytes 245764
  87.8 4.7 %collective-permute-start.38 = (bf16[64,640]{1,0:T(8,128)(2,1)S(1)}, bf16[64,640]{1,0:T(8,128)(2,1)S(1)}, u32[]{:S(2)}, u32[]{:S(2)}) collective-permute-start(bf16[64,640]{1,0:T(8,128)(2,1)S(1)} %collective-permute-done.30.refs_9_), channel_id=1, source_target_pairs={{0,1},{1,0},{2,3},{3,2},{4,5},{5,4},{6,7},{7,6},{8,9},{9,8},{10,11... | collective-permute-start | bytes 245768 | tf_op jit(solution)/shard_map/ppermute | solution.py:174
  87.8 10.5 %copy-start.10 = (bf16[64,640]{1,0:T(8,128)(2,1)}, bf16[64,640]{1,0:T(8,128)(2,1)S(1)}, u32[]{:S(2)}) copy-start(bf16[64,640]{1,0:T(8,128)(2,1)S(1)} %collective-permute-done.32.refs_11_) | copy-start | bytes 245764
  87.8 4.9 %collective-permute-start.31 = (bf16[64,640]{1,0:T(8,128)(2,1)S(1)}, bf16[64,640]{1,0:T(8,128)(2,1)S(1)}, u32[]{:S(2)}, u32[]{:S(2)}) collective-permute-start(bf16[64,640]{1,0:T(8,128)(2,1)S(1)} %collective-permute-done.30.refs_9_), channel_id=1, source_target_pairs={{0,2},{1,3},{2,0},{3,1},{4,6},{5,7},{6,4},{7,5},{8,10},{9,11},{10,... | collective-permute-start | bytes 245768 | tf_op jit(solution)/shard_map/ppermute | solution.py:174
  90.2 8.0 %copy-start.11 = (bf16[64,640]{1,0:T(8,128)(2,1)}, bf16[64,640]{1,0:T(8,128)(2,1)S(1)}, u32[]{:S(2)}) copy-start(bf16[64,640]{1,0:T(8,128)(2,1)S(1)} %collective-permute-done.28.refs_7_) | copy-start | bytes 245764
  90.2 2.7 %collective-permute-start.36 = (bf16[64,640]{1,0:T(8,128)(2,1)S(1)}, bf16[64,640]{1,0:T(8,128)(2,1)S(1)}, u32[]{:S(2)}, u32[]{:S(2)}) collective-permute-start(bf16[64,640]{1,0:T(8,128)(2,1)S(1)} %collective-permute-done.28.refs_7_), channel_id=1, source_target_pairs={{0,1},{1,0},{2,3},{3,2},{4,5},{5,4},{6,7},{7,6},{8,9},{9,8},{10,11... | collective-permute-start | bytes 245768 | tf_op jit(solution)/shard_map/ppermute | solution.py:174
  90.4 7.9 %copy-start.13 = (bf16[64,640]{1,0:T(8,128)(2,1)}, bf16[64,640]{1,0:T(8,128)(2,1)S(1)}, u32[]{:S(2)}) copy-start(bf16[64,640]{1,0:T(8,128)(2,1)S(1)} %collective-permute-done.26.refs_5_) | copy-start | bytes 245764
  90.4 5.3 %collective-permute-start.29 = (bf16[64,640]{1,0:T(8,128)(2,1)S(1)}, bf16[64,640]{1,0:T(8,128)(2,1)S(1)}, u32[]{:S(2)}, u32[]{:S(2)}) collective-permute-start(bf16[64,640]{1,0:T(8,128)(2,1)S(1)} %collective-permute-done.28.refs_7_), channel_id=1, source_target_pairs={{0,2},{1,3},{2,0},{3,1},{4,6},{5,7},{6,4},{7,5},{8,10},{9,11},{10,... | collective-permute-start | bytes 245768 | tf_op jit(solution)/shard_map/ppermute | solution.py:174
  91.3 7.0 %copy-start.14 = (bf16[64,640]{1,0:T(8,128)(2,1)}, bf16[64,640]{1,0:T(8,128)(2,1)S(1)}, u32[]{:S(2)}) copy-start(bf16[64,640]{1,0:T(8,128)(2,1)S(1)} %collective-permute-done.25.refs_4_) | copy-start | bytes 245764
  91.3 5.6 %collective-permute-start.27 = (bf16[64,640]{1,0:T(8,128)(2,1)S(1)}, bf16[64,640]{1,0:T(8,128)(2,1)S(1)}, u32[]{:S(2)}, u32[]{:S(2)}) collective-permute-start(bf16[64,640]{1,0:T(8,128)(2,1)S(1)} %collective-permute-done.26.refs_5_), channel_id=1, source_target_pairs={{0,2},{1,3},{2,0},{3,1},{4,6},{5,7},{6,4},{7,5},{8,10},{9,11},{10,... | collective-permute-start | bytes 245768 | tf_op jit(solution)/shard_map/ppermute | solution.py:174
  92.5 4.4 %collective-permute-start.34 = (bf16[64,640]{1,0:T(8,128)(2,1)S(1)}, bf16[64,640]{1,0:T(8,128)(2,1)S(1)}, u32[]{:S(2)}, u32[]{:S(2)}) collective-permute-start(bf16[64,640]{1,0:T(8,128)(2,1)S(1)} %collective-permute-done.26.refs_5_), channel_id=1, source_target_pairs={{0,1},{1,0},{2,3},{3,2},{4,5},{5,4},{6,7},{7,6},{8,9},{9,8},{10,11... | collective-permute-start | bytes 245768 | tf_op jit(solution)/shard_map/ppermute | solution.py:174
  92.6 4.3 %collective-permute-start.33 = (bf16[64,640]{1,0:T(8,128)(2,1)S(1)}, bf16[64,640]{1,0:T(8,128)(2,1)S(1)}, u32[]{:S(2)}, u32[]{:S(2)}) collective-permute-start(bf16[64,640]{1,0:T(8,128)(2,1)S(1)} %collective-permute-done.25.refs_4_), channel_id=1, source_target_pairs={{0,1},{1,0},{2,3},{3,2},{4,5},{5,4},{6,7},{7,6},{8,9},{9,8},{10,11... | collective-permute-start | bytes 245768 | tf_op jit(solution)/shard_map/ppermute | solution.py:174
  93.0 3.9 %collective-permute-start.39 = (bf16[64,640]{1,0:T(8,128)(2,1)S(1)}, bf16[64,640]{1,0:T(8,128)(2,1)S(1)}, u32[]{:S(2)}, u32[]{:S(2)}) collective-permute-start(bf16[64,640]{1,0:T(8,128)(2,1)S(1)} %collective-permute-done.31.refs_10_), channel_id=1, source_target_pairs={{0,1},{1,0},{2,3},{3,2},{4,5},{5,4},{6,7},{7,6},{8,9},{9,8},{10,11... | collective-permute-start | bytes 245768 | tf_op jit(solution)/shard_map/ppermute | solution.py:174
  95.7 1.3 collective-permute-start.37
  96.9 1.4 collective-permute-start.35
  107.1 10.8 %collective-permute-start.40 = (bf16[320,320]{1,0:T(8,128)(2,1)}, bf16[320,320]{1,0:T(8,128)(2,1)S(1)}, u32[]{:S(2)}, u32[]{:S(2)}) collective-permute-start(bf16[320,320]{1,0:T(8,128)(2,1)} %get-tuple-element.25.sent_hbm), channel_id=1, source_target_pairs={{0,1},{1,0},{2,3},{3,2},{4,5},{5,4},{6,7},{7,6},{8,9},{9,8},{10,11... | collective-permute-start | bytes 614408 | tf_op jit(solution)/shard_map/ppermute | solution.py:174
  124.3 7.4 %collective-permute-start.46 = (bf16[64,640]{1,0:T(8,128)(2,1)}, bf16[64,640]{1,0:T(8,128)(2,1)S(1)}, u32[]{:S(2)}, u32[]{:S(2)}) collective-permute-start(bf16[64,640]{1,0:T(8,128)(2,1)} %attend.3.refs_0_), channel_id=1, source_target_pairs={{0,12},{1,13},{2,14},{3,15},{4,8},{5,9},{6,10},{7,11},{8,4},{9,5},... | collective-permute-start | bytes 245768 | tf_op jit(solution)/shard_map/ppermute | solution.py:174
  124.8 9.3 %collective-permute-start.44 = (bf16[64,640]{1,0:T(8,128)(2,1)}, bf16[64,640]{1,0:T(8,128)(2,1)S(1)}, u32[]{:S(2)}, u32[]{:S(2)}) collective-permute-start(bf16[64,640]{1,0:T(8,128)(2,1)} %attend.3.refs_0_), channel_id=1, source_target_pairs={{0,8},{1,9},{2,10},{3,11},{4,12},{5,13},{6,14},{7,15},{8,0},{9,1},... | collective-permute-start | bytes 245768 | tf_op jit(solution)/shard_map/ppermute | solution.py:174
  126.2 8.5 %collective-permute-start.42 = (bf16[64,640]{1,0:T(8,128)(2,1)}, bf16[64,640]{1,0:T(8,128)(2,1)S(1)}, u32[]{:S(2)}, u32[]{:S(2)}) collective-permute-start(bf16[64,640]{1,0:T(8,128)(2,1)} %attend.3.refs_0_), channel_id=1, source_target_pairs={{0,4},{1,5},{2,6},{3,7},{4,0},{5,1},{6,2},{7,3},{8,12},{9,13},{10,... | collective-permute-start | bytes 245768 | tf_op jit(solution)/shard_map/ppermute | solution.py:174
  128.7 7.5 %collective-permute-start.41 = (bf16[64,640]{1,0:T(8,128)(2,1)}, bf16[64,640]{1,0:T(8,128)(2,1)S(1)}, u32[]{:S(2)}, u32[]{:S(2)}) collective-permute-start(bf16[64,640]{1,0:T(8,128)(2,1)} %attend.3.refs_0_), channel_id=1, source_target_pairs={{0,2},{1,3},{2,0},{3,1},{4,6},{5,7},{6,4},{7,5},{8,10},{9,11},{10,... | collective-permute-start | bytes 245768 | tf_op jit(solution)/shard_map/ppermute | solution.py:174
  131.7 8.2 %copy-start.28 = (bf16[64,640]{1,0:T(8,128)(2,1)}, bf16[64,640]{1,0:T(8,128)(2,1)S(1)}, u32[]{:S(2)}) copy-start(bf16[64,640]{1,0:T(8,128)(2,1)S(1)} %collective-permute-done.46.refs_6_) | copy-start | bytes 245764
  131.7 4.5 %collective-permute-start.47 = (bf16[64,640]{1,0:T(8,128)(2,1)S(1)}, bf16[64,640]{1,0:T(8,128)(2,1)S(1)}, u32[]{:S(2)}, u32[]{:S(2)}) collective-permute-start(bf16[64,640]{1,0:T(8,128)(2,1)S(1)} %collective-permute-done.46.refs_6_), channel_id=1, source_target_pairs={{0,2},{1,3},{2,0},{3,1},{4,6},{5,7},{6,4},{7,5},{8,10},{9,11},{10,... | collective-permute-start | bytes 245768 | tf_op jit(solution)/shard_map/ppermute | solution.py:174
  134.2 4.8 %collective-permute-start.45 = (bf16[64,640]{1,0:T(8,128)(2,1)S(1)}, bf16[64,640]{1,0:T(8,128)(2,1)S(1)}, u32[]{:S(2)}, u32[]{:S(2)}) collective-permute-start(bf16[64,640]{1,0:T(8,128)(2,1)S(1)} %collective-permute-done.44.refs_4_), channel_id=1, source_target_pairs={{0,2},{1,3},{2,0},{3,1},{4,6},{5,7},{6,4},{7,5},{8,10},{9,11},{10,... | collective-permute-start | bytes 245768 | tf_op jit(solution)/shard_map/ppermute | solution.py:174
  134.7 5.1 %collective-permute-start.43 = (bf16[64,640]{1,0:T(8,128)(2,1)S(1)}, bf16[64,640]{1,0:T(8,128)(2,1)S(1)}, u32[]{:S(2)}, u32[]{:S(2)}) collective-permute-start(bf16[64,640]{1,0:T(8,128)(2,1)S(1)} %collective-permute-done.42.refs_2_), channel_id=1, source_target_pairs={{0,2},{1,3},{2,0},{3,1},{4,6},{5,7},{6,4},{7,5},{8,10},{9,11},{10,... | collective-permute-start | bytes 245768 | tf_op jit(solution)/shard_map/ppermute | solution.py:174
  (32 other events, 79.5 us)

commit v5 on v4

--- a/solution.py
+++ b/solution.py
@@ -631,9 +631,9 @@
             others = [swapped(block, 1) for block in mine]
     same_core = [[2 * c + core for c in range(chips)] for core in range(2)]
     result = lax.all_to_all(
-        result, "queue", split_axis=0, concat_axis=0, tiled=True, axis_index_groups=same_core
-    )
-    return join(result)
+        result, "queue", split_axis=0, concat_axis=2, tiled=True, axis_index_groups=same_core
+    )
+    return result[0]
 
 
 def held_in_pairs(mesh, hidden, query_weight):

time: 159 us -> 157 us (0.987)
    unnamed x94 -> x95, local copies, waits for them, and re-layouts: 3.51 us -> 4.14 us
where the time goes in v5:
time: 157 us
  starting transfers between devices  42 us (27%)
  Pallas kernels  41.2 us (26%)
  waiting for transfers between devices  33.2 us (21%)
  blocking collectives  32.2 us (21%)
  local copies, waits for them, and re-layouts  4.14 us (3%)
  matrix products  2.02 us (1%)
    ppermute x48, starting transfers between devices, swapped(): lax.ppermute(value, 'queue', [(source, source ^ bit) for source in range(...  37.3 us
    ppermute x48, waiting for transfers between devices, swapped(): lax.ppermute(value, 'queue', [(source, source ^ bit) for source in range(...  29.6 us
    all_to_all x2, blocking collectives, paired_device(): lax.all_to_all(squares, 'queue', split_axis=0, concat_axis=0, tiled=True)  21.9 us
    pallas_call x2, Pallas kernels, project(): pl.pallas_call(functools.partial(project_kernel, step, spans), out_shape=...  17.4 us
    pallas_call x2, Pallas kernels, attend(): pl.pallas_call(functools.partial(attend_kernel, step, spans, head_size),...  11.4 us
    pallas_call x2, Pallas kernels, output(): pl.pallas_call(functools.partial(output_kernel, step, spans, last), out_s...  10.4 us
    all_to_all x1, blocking collectives, paired_device(): lax.all_to_all(result, 'queue', split_axis=0, concat_axis=2, tiled=True,...  10.3 us
    all_to_all x1, starting transfers between devices, paired_device(): lax.all_to_all(text, 'queue', split_axis=0, concat_axis=0, tiled=True)  4.73 us
  transfers between devices with their start and end apart: 49, of which 23 were waited for; matrix products, arithmetic and copies ran while one was open for 2% of the time, Pallas kernels for 10%

profile of v5, /device:TPU:0, one launch (start us, length us, event | category | flops | bytes accessed | tf_op | source)
XLA Modules:
  0.0 156.6 jit_solution(14179311756579907007)
XLA Ops:
  0.0 0.5 collective-permute-start.15
  0.5 4.7 %collective-permute-start.5 = (bf16[8,5120]{1,0:T(8,128)(2,1)}, bf16[8,5120]{1,0:T(8,128)(2,1)S(1)}, u32[]{:S(2)}, u32[]{:S(2)}) collective-permute-start(bf16[8,5120]{1,0:T(8,128)(2,1)} %refs_3_.1), channel_id=1, source_target_pairs={{0,12},{1,13},{2,14},{3,15},{4,8},{5,9},{6,10},{7,11},{8,4},{9,5},... | collective-permute-start | bytes 245768 | tf_op jit(solution)/shard_map/ppermute | solution.py:174
  5.1 0.7 collective-permute-start.1
  5.8 1.6 %collective-permute-start = (bf16[8,5120]{1,0:T(8,128)(2,1)}, bf16[8,5120]{1,0:T(8,128)(2,1)S(1)}, u32[]{:S(2)}, u32[]{:S(2)}) collective-permute-start(bf16[8,5120]{1,0:T(8,128)(2,1)} %refs_3_.1), channel_id=1, source_target_pairs={{0,2},{1,3},{2,0},{3,1},{4,6},{5,7},{6,4},{7,5},{8,10},{9,11},{10,... | collective-permute-start | bytes 245768 | tf_op jit(solution)/shard_map/ppermute | solution.py:174
  7.4 1.4 pad_maximum_fusion.gain_hbm
  8.8 1.6 collective-permute-start.6
  10.4 2.4 %collective-permute-done.3.refs_7_ = bf16[8,5120]{1,0:T(8,128)(2,1)S(1)} collective-permute-done((bf16[8,5120]{1,0:T(8,128)(2,1)}, bf16[8,5120]{1,0:T(8,128)(2,1)S(1)}, u32[]{:S(2)}, u32[]{:S(2)}) %collective-permute-start.3) | collective-permute-done | bytes 81952 | tf_op jit(solution)/shard_map/ppermute | solution.py:174
  12.8 1.5 collective-permute-start.4
  14.3 0.5 collective-permute-start.2
  14.9 2.0 %fusion.table_hbm = bf16[3,16,5120]{2,1,0:T(8,128)(2,1)} fusion(bf16[96,3,5120]{2,0,1:T(8,128)(2,1)S(1)} %copy-done, s32[16]{0:T(128)} %param.14), kind=kOutput, calls=%fused_computation.1 | convolution fusion | flops 47433216 | bytes 3440704 | tf_op jit(solution)/shard_map/sl,ltd->tsd/dot_general | solution.py:602
  16.9 2.0 %arrange.1 = bf16[16,2,16,640]{3,2,1,0:T(8,128)(2,1)} custom-call(bf16[32,5120]{1,0:T(8,128)(2,1)} %keys_ref.1, bf16[32,5120]{1,0:T(8,128)(2,1)} %values_ref.1), custom_call_target="tpu_custom_call" | custom-call | tf_op jit(solution)/shard_map/arrange/pallas_call | solution.py:570
  19.1 4.7 %all-to-all-start.1 = ((bf16[16,2,16,640]{3,2,1,0:T(8,128)(2,1)}), bf16[16,2,16,640]{3,2,1,0:T(8,128)(2,1)}, u32[]{:S(2)}, u32[]{:S(2)}) async-start(bf16[16,2,16,640]{3,2,1,0:T(8,128)(2,1)} %arrange.1), calls=%async_computation.1 | async-start | bytes 1310720 | tf_op jit(solution)/shard_map/all_to_all | solution.py:610
  23.8 0.4 collective-permute-start.7
  24.4 0.4 collective-permute-start.11
  26.4 0.4 collective-permute-done.14.refs_18_
  27.0 0.6 collective-permute-done.10.refs_14_
  27.6 0.5 copy-done.42
  28.2 8.7 %project.2 = (bf16[64,320]{1,0:T(8,128)(2,1)}, bf16[320,320]{1,0:T(8,128)(2,1)}, f32[16,2,128]{2,1,0:T(2,128)}, bf16[64,640]{1,0:T(8,128)(2,1)}) custom-call(f32[2,5120]{1,0:T(2,128)} %pad_maximum_fusion.gain_hbm, bf16[3,16,5120]{2,1,0:T(8,128)(2,1)} %fusion.table_hbm, bf16[2,8,5120]{2,1,0:T(8,128)(2,1)} %incoming_hbm.7, bf16[320,5120]{1,0:T(8,128)(2,1)} %bitcast.17, ...), custom_call_target="tpu_custom_call" | custom-call | tf_op jit(solution)/shard_map/project/pallas_call | solution.py:337
  36.9 3.6 %all-to-all-done.1.text_hbm = bf16[16,2,16,640]{3,2,1,0:T(8,128)(2,1)} async-done(((bf16[16,2,16,640]{3,2,1,0:T(8,128)(2,1)}), bf16[16,2,16,640]{3,2,1,0:T(8,128)(2,1)}, u32[]{:S(2)}, u32[]{:S(2)}) %all-to-all-start.1) | async-done | bytes 655392 | tf_op jit(solution)/shard_map/all_to_all | solution.py:610
  40.5 0.4 collective-permute-start.16
  41.0 11.4 %all_to_all.30.squares_hbm = f32[16,2,128]{2,1,0:T(2,128)} all-to-all(f32[16,2,128]{2,1,0:T(2,128)} %get-tuple-element.21), channel_id=1, replica_groups=mesh['groups'=2,'queue'=16] {'queue'}, dimensions={0} | all-to-all | bytes 32768 | tf_op jit(solution)/shard_map/all_to_all | solution.py:618
  52.3 0.7 copy-done.2
  53.3 5.7 %attend.2.refs_0_ = bf16[64,640]{1,0:T(8,128)(2,1)} custom-call(bf16[64,320]{1,0:T(8,128)(2,1)} %get-tuple-element.19.own_hbm, bf16[320,320]{1,0:T(8,128)(2,1)} %get-tuple-element.20.sent_hbm, bf16[320,320]{1,0:T(8,128)(2,1)} %copy-done.2, f32[16,2,128]{2,1,0:T(2,128)} %all_to_all.30.squares_hbm, bf16[16,2,16,640]{3,2,1,0:T(8,128)(2,1)} %all-to-all-done.1.text_hbm, ...), custom_call_target="tpu_custom_call" | custom-call | tf_op jit(solution)/shard_map/attend/pallas_call | solution.py:441
  59.0 0.6 collective-permute-start.23
  59.5 1.4 collective-permute-start.21
  61.0 2.5 %collective-permute-start.19 = (bf16[64,640]{1,0:T(8,128)(2,1)}, bf16[64,640]{1,0:T(8,128)(2,1)S(1)}, u32[]{:S(2)}, u32[]{:S(2)}) collective-permute-start(bf16[64,640]{1,0:T(8,128)(2,1)} %attend.2.refs_0_), channel_id=1, source_target_pairs={{0,4},{1,5},{2,6},{3,7},{4,0},{5,1},{6,2},{7,3},{8,12},{9,13},{10,... | collective-permute-start | bytes 245768 | tf_op jit(solution)/shard_map/ppermute | solution.py:174
  63.4 0.5 collective-permute-start.18
  63.9 2.5 %collective-permute-done.23.refs_6_ = bf16[64,640]{1,0:T(8,128)(2,1)S(1)} collective-permute-done((bf16[64,640]{1,0:T(8,128)(2,1)}, bf16[64,640]{1,0:T(8,128)(2,1)S(1)}, u32[]{:S(2)}, u32[]{:S(2)}) %collective-permute-start.23) | collective-permute-done | bytes 81952 | tf_op jit(solution)/shard_map/ppermute | solution.py:174
  66.4 0.5 collective-permute-start.24
  66.9 2.0 %collective-permute-done.21.refs_4_ = bf16[64,640]{1,0:T(8,128)(2,1)S(1)} collective-permute-done((bf16[64,640]{1,0:T(8,128)(2,1)}, bf16[64,640]{1,0:T(8,128)(2,1)S(1)}, u32[]{:S(2)}, u32[]{:S(2)}) %collective-permute-start.21) | collective-permute-done | bytes 81952 | tf_op jit(solution)/shard_map/ppermute | solution.py:174
  68.9 0.6 collective-permute-start.22
  69.5 1.4 collective-permute-start.20
  70.9 2.7 %collective-permute-done.22.refs_5_ = bf16[64,640]{1,0:T(8,128)(2,1)S(1)} collective-permute-done((bf16[64,640]{1,0:T(8,128)(2,1)S(1)}, bf16[64,640]{1,0:T(8,128)(2,1)S(1)}, u32[]{:S(2)}, u32[]{:S(2)}) %collective-permute-start.22) | collective-permute-done | bytes 81952 | tf_op jit(solution)/shard_map/ppermute | solution.py:174
  73.6 0.9 collective-permute-done.20.refs_3_
  74.5 0.6 copy-done.45
  75.1 5.2 %output.2.refs_3_.current_hbm = bf16[64,640]{1,0:T(8,128)(2,1)} custom-call(bf16[64,640]{1,0:T(8,128)(2,1)} %get-tuple-element.18.current_hbm, bf16[3,16,5120]{2,1,0:T(8,128)(2,1)} %fusion.table_hbm, bf16[2,8,5120]{2,1,0:T(8,128)(2,1)} %incoming_hbm.7, bf16[320,5120]{1,0:T(8,128)(2,1)} %bitcast.24, bf16[320,5120]{1,0:T(8,128)(2,1)} %collective-permute-done.15.other_hbm, ...), custom_call_target="tpu_custom_call" | custom-call | tf_op jit(solution)/shard_map/output/pallas_call | solution.py:519
  80.3 1.4 collective-permute-start.30
  81.8 3.0 %collective-permute-start.26 = (bf16[64,640]{1,0:T(8,128)(2,1)}, bf16[64,640]{1,0:T(8,128)(2,1)S(1)}, u32[]{:S(2)}, u32[]{:S(2)}) collective-permute-start(bf16[64,640]{1,0:T(8,128)(2,1)} %output.2.refs_3_.current_hbm), channel_id=1, source_target_pairs={{0,4},{1,5},{2,6},{3,7},{4,0},{5,1},{6,2},{7,3},{8,12},{9,13},{10,... | collective-permute-start | bytes 245768 | tf_op jit(solution)/shard_map/ppermute | solution.py:174
  84.8 0.9 collective-permute-start.25
  85.7 2.1 %collective-permute-done.30.refs_9_ = bf16[64,640]{1,0:T(8,128)(2,1)S(1)} collective-permute-done((bf16[64,640]{1,0:T(8,128)(2,1)}, bf16[64,640]{1,0:T(8,128)(2,1)S(1)}, u32[]{:S(2)}, u32[]{:S(2)}) %collective-permute-start.30) | collective-permute-done | bytes 81952 | tf_op jit(solution)/shard_map/ppermute | solution.py:174
  87.8 0.9 collective-permute-start.31
  88.7 1.5 collective-permute-done.28.refs_7_
  90.4 0.9 collective-permute-start.29
  91.3 1.1 collective-permute-start.27
  93.2 2.5 %collective-permute-done.29.refs_8_ = bf16[64,640]{1,0:T(8,128)(2,1)S(1)} collective-permute-done((bf16[64,640]{1,0:T(8,128)(2,1)S(1)}, bf16[64,640]{1,0:T(8,128)(2,1)S(1)}, u32[]{:S(2)}, u32[]{:S(2)}) %collective-permute-start.29) | collective-permute-done | bytes 81952 | tf_op jit(solution)/shard_map/ppermute | solution.py:174
  95.7 1.2 collective-permute-done.27.refs_6_
  97.0 1.3 collective-permute-done.35.refs_14_
  98.4 8.7 %project.3 = (bf16[64,320]{1,0:T(8,128)(2,1)}, bf16[320,320]{1,0:T(8,128)(2,1)}, f32[16,2,128]{2,1,0:T(2,128)}) custom-call(f32[2,5120]{1,0:T(2,128)} %pad_maximum_fusion.gain_hbm, bf16[3,16,5120]{2,1,0:T(8,128)(2,1)} %fusion.table_hbm, bf16[2,8,5120]{2,1,0:T(8,128)(2,1)} %incoming_hbm.7, bf16[320,5120]{1,0:T(8,128)(2,1)} %bitcast.18, ...), custom_call_target="tpu_custom_call" | custom-call | tf_op jit(solution)/shard_map/project/pallas_call | solution.py:337
  107.3 10.5 %all_to_all.31.squares_hbm = f32[16,2,128]{2,1,0:T(2,128)} all-to-all(f32[16,2,128]{2,1,0:T(2,128)} %get-tuple-element.26), channel_id=1, replica_groups=mesh['groups'=2,'queue'=16] {'queue'}, dimensions={0} | all-to-all | bytes 32768 | tf_op jit(solution)/shard_map/all_to_all | solution.py:618
  117.9 0.7 copy-done.3
  118.6 5.7 %attend.3.refs_0_ = bf16[64,640]{1,0:T(8,128)(2,1)} custom-call(bf16[64,320]{1,0:T(8,128)(2,1)} %get-tuple-element.24.own_hbm, bf16[320,320]{1,0:T(8,128)(2,1)} %get-tuple-element.25.sent_hbm, bf16[320,320]{1,0:T(8,128)(2,1)} %copy-done.3, f32[16,2,128]{2,1,0:T(2,128)} %all_to_all.31.squares_hbm, bf16[16,2,16,640]{3,2,1,0:T(8,128)(2,1)} %all-to-all-done.1.text_hbm, ...), custom_call_target="tpu_custom_call" | custom-call | tf_op jit(solution)/shard_map/attend/pallas_call | solution.py:441
  124.3 0.6 collective-permute-start.46
  124.8 1.4 collective-permute-start.44
  126.2 2.5 %collective-permute-start.42 = (bf16[64,640]{1,0:T(8,128)(2,1)}, bf16[64,640]{1,0:T(8,128)(2,1)S(1)}, u32[]{:S(2)}, u32[]{:S(2)}) collective-permute-start(bf16[64,640]{1,0:T(8,128)(2,1)} %attend.3.refs_0_), channel_id=1, source_target_pairs={{0,4},{1,5},{2,6},{3,7},{4,0},{5,1},{6,2},{7,3},{8,12},{9,13},{10,... | collective-permute-start | bytes 245768 | tf_op jit(solution)/shard_map/ppermute | solution.py:174
  129.0 2.7 %collective-permute-done.46.refs_6_ = bf16[64,640]{1,0:T(8,128)(2,1)S(1)} collective-permute-done((bf16[64,640]{1,0:T(8,128)(2,1)}, bf16[64,640]{1,0:T(8,128)(2,1)S(1)}, u32[]{:S(2)}, u32[]{:S(2)}) %collective-permute-start.46) | collective-permute-done | bytes 81952 | tf_op jit(solution)/shard_map/ppermute | solution.py:174
  132.0 2.1 %collective-permute-done.44.refs_4_ = bf16[64,640]{1,0:T(8,128)(2,1)S(1)} collective-permute-done((bf16[64,640]{1,0:T(8,128)(2,1)}, bf16[64,640]{1,0:T(8,128)(2,1)S(1)}, u32[]{:S(2)}, u32[]{:S(2)}) %collective-permute-start.44) | collective-permute-done | bytes 81952 | tf_op jit(solution)/shard_map/ppermute | solution.py:174
  134.2 0.6 collective-permute-start.45
  134.7 1.5 collective-permute-start.43
  136.2 2.7 %collective-permute-done.45.refs_5_ = bf16[64,640]{1,0:T(8,128)(2,1)S(1)} collective-permute-done((bf16[64,640]{1,0:T(8,128)(2,1)S(1)}, bf16[64,640]{1,0:T(8,128)(2,1)S(1)}, u32[]{:S(2)}, u32[]{:S(2)}) %collective-permute-start.45) | collective-permute-done | bytes 81952 | tf_op jit(solution)/shard_map/ppermute | solution.py:174
  139.0 0.9 collective-permute-done.43.refs_3_
  139.9 0.6 copy-done.46
  140.5 5.2 %output.3 = bf16[8,8,640]{2,1,0:T(8,128)(2,1)} custom-call(bf16[64,640]{1,0:T(8,128)(2,1)} %output.2.refs_3_.current_hbm, bf16[3,16,5120]{2,1,0:T(8,128)(2,1)} %fusion.table_hbm, bf16[2,8,5120]{2,1,0:T(8,128)(2,1)} %incoming_hbm.7, bf16[320,5120]{1,0:T(8,128)(2,1)} %bitcast.25, bf16[320,5120]{1,0:T(8,128)(2,1)} %collective-permute-done.15.other_hbm, ...), custom_call_target="tpu_custom_call" | custom-call | tf_op jit(solution)/shard_map/output/pallas_call | solution.py:519
  145.7 10.3 %all_to_all.32 = bf16[8,8,640]{2,1,0:T(8,128)(2,1)S(1)} all-to-all(bf16[8,8,640]{2,1,0:T(8,128)(2,1)} %output.3), channel_id=1, replica_groups={{0,2,4,6,8,10,12,14},{1,3,5,7,9,11,13,15},{16,18,20,22,24,26,28,30},{17..., dimensions={0} | all-to-all | bytes 163840 | tf_op jit(solution)/shard_map/all_to_all | solution.py:633
  156.0 0.6 copy.14
  (141 shorter events, 4.5 us)
Async XLA Ops:
  0.0 14.9 %copy-start = (bf16[96,3,5120]{2,0,1:T(8,128)(2,1)S(1)}, bf16[96,3,5120]{2,0,1:T(8,128)(2,1)}, u32[]{:S(2)}) copy-start(bf16[96,3,5120]{2,0,1:T(8,128)(2,1)} %param.15) | copy-start | bytes 8847364
  0.0 23.8 %copy-start.4 = (bf16[8,5120]{1,0:T(8,128)(2,1)S(1)}, bf16[8,5120]{1,0:T(8,128)(2,1)}, u32[]{:S(2)}) copy-start(bf16[8,5120]{1,0:T(8,128)(2,1)} %refs_3_.1) | copy-start | bytes 245764
  0.0 74.5 %collective-permute-start.15 = (bf16[320,5120]{1,0:T(8,128)(2,1)}, bf16[320,5120]{1,0:T(8,128)(2,1)}, u32[]{:S(2)}, u32[]{:S(2)}) collective-permute-start(bf16[320,5120]{1,0:T(8,128)(2,1)} %bitcast.23), channel_id=1, source_target_pairs={{0,1},{1,0},{2,3},{3,2},{4,5},{5,4},{6,7},{7,6},{8,9},{9,8},{10,11... | collective-permute-start | bytes 9830408 | tf_op jit(solution)/shard_map/ppermute | solution.py:174
  0.5 8.4 %collective-permute-start.5 = (bf16[8,5120]{1,0:T(8,128)(2,1)}, bf16[8,5120]{1,0:T(8,128)(2,1)S(1)}, u32[]{:S(2)}, u32[]{:S(2)}) collective-permute-start(bf16[8,5120]{1,0:T(8,128)(2,1)} %refs_3_.1), channel_id=1, source_target_pairs={{0,12},{1,13},{2,14},{3,15},{4,8},{5,9},{6,10},{7,11},{8,4},{9,5},... | collective-permute-start | bytes 245768 | tf_op jit(solution)/shard_map/ppermute | solution.py:174
  5.1 7.7 %collective-permute-start.3 = (bf16[8,5120]{1,0:T(8,128)(2,1)}, bf16[8,5120]{1,0:T(8,128)(2,1)S(1)}, u32[]{:S(2)}, u32[]{:S(2)}) collective-permute-start(bf16[8,5120]{1,0:T(8,128)(2,1)} %refs_3_.1), channel_id=1, source_target_pairs={{0,8},{1,9},{2,10},{3,11},{4,12},{5,13},{6,14},{7,15},{8,0},{9,1},... | collective-permute-start | bytes 245768 | tf_op jit(solution)/shard_map/ppermute | solution.py:174
  5.1 9.2 %collective-permute-start.1 = (bf16[8,5120]{1,0:T(8,128)(2,1)}, bf16[8,5120]{1,0:T(8,128)(2,1)S(1)}, u32[]{:S(2)}, u32[]{:S(2)}) collective-permute-start(bf16[8,5120]{1,0:T(8,128)(2,1)} %refs_3_.1), channel_id=1, source_target_pairs={{0,4},{1,5},{2,6},{3,7},{4,0},{5,1},{6,2},{7,3},{8,12},{9,13},{10,... | collective-permute-start | bytes 245768 | tf_op jit(solution)/shard_map/ppermute | solution.py:174
  5.8 13.1 %collective-permute-start = (bf16[8,5120]{1,0:T(8,128)(2,1)}, bf16[8,5120]{1,0:T(8,128)(2,1)S(1)}, u32[]{:S(2)}, u32[]{:S(2)}) collective-permute-start(bf16[8,5120]{1,0:T(8,128)(2,1)} %refs_3_.1), channel_id=1, source_target_pairs={{0,2},{1,3},{2,0},{3,1},{4,6},{5,7},{6,4},{7,5},{8,10},{9,11},{10,... | collective-permute-start | bytes 245768 | tf_op jit(solution)/shard_map/ppermute | solution.py:174
  8.8 18.7 %copy-start.5 = (bf16[8,5120]{1,0:T(8,128)(2,1)}, bf16[8,5120]{1,0:T(8,128)(2,1)S(1)}, u32[]{:S(2)}) copy-start(bf16[8,5120]{1,0:T(8,128)(2,1)S(1)} %collective-permute-done.5.refs_9_) | copy-start | bytes 245764
  8.8 10.0 %collective-permute-start.6 = (bf16[8,5120]{1,0:T(8,128)(2,1)S(1)}, bf16[8,5120]{1,0:T(8,128)(2,1)S(1)}, u32[]{:S(2)}, u32[]{:S(2)}) collective-permute-start(bf16[8,5120]{1,0:T(8,128)(2,1)S(1)} %collective-permute-done.5.refs_9_), channel_id=1, source_target_pairs={{0,2},{1,3},{2,0},{3,1},{4,6},{5,7},{6,4},{7,5},{8,10},{9,11},{10,... | collective-permute-start | bytes 245768 | tf_op jit(solution)/shard_map/ppermute | solution.py:174
  12.8 14.7 %copy-start.6 = (bf16[8,5120]{1,0:T(8,128)(2,1)}, bf16[8,5120]{1,0:T(8,128)(2,1)S(1)}, u32[]{:S(2)}) copy-start(bf16[8,5120]{1,0:T(8,128)(2,1)S(1)} %collective-permute-done.3.refs_7_) | copy-start | bytes 245764
  12.8 6.1 %collective-permute-start.4 = (bf16[8,5120]{1,0:T(8,128)(2,1)S(1)}, bf16[8,5120]{1,0:T(8,128)(2,1)S(1)}, u32[]{:S(2)}, u32[]{:S(2)}) collective-permute-start(bf16[8,5120]{1,0:T(8,128)(2,1)S(1)} %collective-permute-done.3.refs_7_), channel_id=1, source_target_pairs={{0,2},{1,3},{2,0},{3,1},{4,6},{5,7},{6,4},{7,5},{8,10},{9,11},{10,... | collective-permute-start | bytes 245768 | tf_op jit(solution)/shard_map/ppermute | solution.py:174
  14.3 13.2 %copy-start.7 = (bf16[8,5120]{1,0:T(8,128)(2,1)}, bf16[8,5120]{1,0:T(8,128)(2,1)S(1)}, u32[]{:S(2)}) copy-start(bf16[8,5120]{1,0:T(8,128)(2,1)S(1)} %collective-permute-done.1.refs_5_) | copy-start | bytes 245764
  14.3 4.7 %collective-permute-start.2 = (bf16[8,5120]{1,0:T(8,128)(2,1)S(1)}, bf16[8,5120]{1,0:T(8,128)(2,1)}, u32[]{:S(2)}, u32[]{:S(2)}) collective-permute-start(bf16[8,5120]{1,0:T(8,128)(2,1)S(1)} %collective-permute-done.1.refs_5_), channel_id=1, source_target_pairs={{0,2},{1,3},{2,0},{3,1},{4,6},{5,7},{6,4},{7,5},{8,10},{9,11},{10,... | collective-permute-start | bytes 245768 | tf_op jit(solution)/shard_map/ppermute | solution.py:174
  18.9 8.7 %copy-start.9 = (bf16[8,5120]{1,0:T(8,128)(2,1)}, bf16[8,5120]{1,0:T(8,128)(2,1)S(1)}, u32[]{:S(2)}) copy-start(bf16[8,5120]{1,0:T(8,128)(2,1)S(1)} %collective-permute-done.refs_4_) | copy-start | bytes 245764
  18.9 8.7 %copy-start.12 = (bf16[8,5120]{1,0:T(8,128)(2,1)}, bf16[8,5120]{1,0:T(8,128)(2,1)S(1)}, u32[]{:S(2)}) copy-start(bf16[8,5120]{1,0:T(8,128)(2,1)S(1)} %collective-permute-done.6.refs_10_) | copy-start | bytes 245764
  18.9 8.7 %copy-start.15 = (bf16[8,5120]{1,0:T(8,128)(2,1)}, bf16[8,5120]{1,0:T(8,128)(2,1)S(1)}, u32[]{:S(2)}) copy-start(bf16[8,5120]{1,0:T(8,128)(2,1)S(1)} %collective-permute-done.4.refs_8_) | copy-start | bytes 245764
  19.1 21.4 %all-to-all-start.1 = ((bf16[16,2,16,640]{3,2,1,0:T(8,128)(2,1)}), bf16[16,2,16,640]{3,2,1,0:T(8,128)(2,1)}, u32[]{:S(2)}, u32[]{:S(2)}) async-start(bf16[16,2,16,640]{3,2,1,0:T(8,128)(2,1)} %arrange.1), calls=%async_computation.1 | async-start | bytes 1310720 | tf_op jit(solution)/shard_map/all_to_all | solution.py:610
  23.8 1.3 collective-permute-start.7
  24.2 1.3 collective-permute-start.13
  24.4 1.3 collective-permute-start.11
  24.7 1.3 collective-permute-start.9
  25.2 1.3 collective-permute-start.8
  25.5 1.3 collective-permute-start.14
  25.7 1.3 collective-permute-start.12
  26.0 1.5 collective-permute-start.10
  40.5 11.9 %collective-permute-start.17 = (bf16[16,2,16,640]{3,2,1,0:T(8,128)(2,1)}, bf16[16,2,16,640]{3,2,1,0:T(8,128)(2,1)S(1)}, u32[]{:S(2)}, u32[]{:S(2)}) collective-permute-start(bf16[16,2,16,640]{3,2,1,0:T(8,128)(2,1)} %all-to-all-done.1.text_hbm), channel_id=1, source_target_pairs={{0,1},{1,0},{2,3},{3,2},{4,5},{5,4},{6,7},{7,6},{8,9},{9,8},{10,11... | collective-permute-start | bytes 1966088 | tf_op jit(solution)/shard_map/ppermute | solution.py:174
  40.5 11.8 %collective-permute-start.16 = (bf16[320,320]{1,0:T(8,128)(2,1)}, bf16[320,320]{1,0:T(8,128)(2,1)S(1)}, u32[]{:S(2)}, u32[]{:S(2)}) collective-permute-start(bf16[320,320]{1,0:T(8,128)(2,1)} %get-tuple-element.20.sent_hbm), channel_id=1, source_target_pairs={{0,1},{1,0},{2,3},{3,2},{4,5},{5,4},{6,7},{7,6},{8,9},{9,8},{10,11... | collective-permute-start | bytes 614408 | tf_op jit(solution)/shard_map/ppermute | solution.py:174
  59.0 7.4 %collective-permute-start.23 = (bf16[64,640]{1,0:T(8,128)(2,1)}, bf16[64,640]{1,0:T(8,128)(2,1)S(1)}, u32[]{:S(2)}, u32[]{:S(2)}) collective-permute-start(bf16[64,640]{1,0:T(8,128)(2,1)} %attend.2.refs_0_), channel_id=1, source_target_pairs={{0,12},{1,13},{2,14},{3,15},{4,8},{5,9},{6,10},{7,11},{8,4},{9,5},... | collective-permute-start | bytes 245768 | tf_op jit(solution)/shard_map/ppermute | solution.py:174
  59.5 9.3 %collective-permute-start.21 = (bf16[64,640]{1,0:T(8,128)(2,1)}, bf16[64,640]{1,0:T(8,128)(2,1)S(1)}, u32[]{:S(2)}, u32[]{:S(2)}) collective-permute-start(bf16[64,640]{1,0:T(8,128)(2,1)} %attend.2.refs_0_), channel_id=1, source_target_pairs={{0,8},{1,9},{2,10},{3,11},{4,12},{5,13},{6,14},{7,15},{8,0},{9,1},... | collective-permute-start | bytes 245768 | tf_op jit(solution)/shard_map/ppermute | solution.py:174
  61.0 8.5 %collective-permute-start.19 = (bf16[64,640]{1,0:T(8,128)(2,1)}, bf16[64,640]{1,0:T(8,128)(2,1)S(1)}, u32[]{:S(2)}, u32[]{:S(2)}) collective-permute-start(bf16[64,640]{1,0:T(8,128)(2,1)} %attend.2.refs_0_), channel_id=1, source_target_pairs={{0,4},{1,5},{2,6},{3,7},{4,0},{5,1},{6,2},{7,3},{8,12},{9,13},{10,... | collective-permute-start | bytes 245768 | tf_op jit(solution)/shard_map/ppermute | solution.py:174
  63.4 7.5 %collective-permute-start.18 = (bf16[64,640]{1,0:T(8,128)(2,1)}, bf16[64,640]{1,0:T(8,128)(2,1)S(1)}, u32[]{:S(2)}, u32[]{:S(2)}) collective-permute-start(bf16[64,640]{1,0:T(8,128)(2,1)} %attend.2.refs_0_), channel_id=1, source_target_pairs={{0,2},{1,3},{2,0},{3,1},{4,6},{5,7},{6,4},{7,5},{8,10},{9,11},{10,... | collective-permute-start | bytes 245768 | tf_op jit(solution)/shard_map/ppermute | solution.py:174
  66.4 8.1 %copy-start.26 = (bf16[64,640]{1,0:T(8,128)(2,1)}, bf16[64,640]{1,0:T(8,128)(2,1)S(1)}, u32[]{:S(2)}) copy-start(bf16[64,640]{1,0:T(8,128)(2,1)S(1)} %collective-permute-done.23.refs_6_) | copy-start | bytes 245764
  66.4 4.5 %collective-permute-start.24 = (bf16[64,640]{1,0:T(8,128)(2,1)S(1)}, bf16[64,640]{1,0:T(8,128)(2,1)S(1)}, u32[]{:S(2)}, u32[]{:S(2)}) collective-permute-start(bf16[64,640]{1,0:T(8,128)(2,1)S(1)} %collective-permute-done.23.refs_6_), channel_id=1, source_target_pairs={{0,2},{1,3},{2,0},{3,1},{4,6},{5,7},{6,4},{7,5},{8,10},{9,11},{10,... | collective-permute-start | bytes 245768 | tf_op jit(solution)/shard_map/ppermute | solution.py:174
  68.9 4.7 %collective-permute-start.22 = (bf16[64,640]{1,0:T(8,128)(2,1)S(1)}, bf16[64,640]{1,0:T(8,128)(2,1)S(1)}, u32[]{:S(2)}, u32[]{:S(2)}) collective-permute-start(bf16[64,640]{1,0:T(8,128)(2,1)S(1)} %collective-permute-done.21.refs_4_), channel_id=1, source_target_pairs={{0,2},{1,3},{2,0},{3,1},{4,6},{5,7},{6,4},{7,5},{8,10},{9,11},{10,... | collective-permute-start | bytes 245768 | tf_op jit(solution)/shard_map/ppermute | solution.py:174
  69.5 5.0 %collective-permute-start.20 = (bf16[64,640]{1,0:T(8,128)(2,1)S(1)}, bf16[64,640]{1,0:T(8,128)(2,1)S(1)}, u32[]{:S(2)}, u32[]{:S(2)}) collective-permute-start(bf16[64,640]{1,0:T(8,128)(2,1)S(1)} %collective-permute-done.19.refs_2_), channel_id=1, source_target_pairs={{0,2},{1,3},{2,0},{3,1},{4,6},{5,7},{6,4},{7,5},{8,10},{9,11},{10,... | collective-permute-start | bytes 245768 | tf_op jit(solution)/shard_map/ppermute | solution.py:174
  80.3 7.4 %collective-permute-start.30 = (bf16[64,640]{1,0:T(8,128)(2,1)}, bf16[64,640]{1,0:T(8,128)(2,1)S(1)}, u32[]{:S(2)}, u32[]{:S(2)}) collective-permute-start(bf16[64,640]{1,0:T(8,128)(2,1)} %output.2.refs_3_.current_hbm), channel_id=1, source_target_pairs={{0,12},{1,13},{2,14},{3,15},{4,8},{5,9},{6,10},{7,11},{8,4},{9,5},... | collective-permute-start | bytes 245768 | tf_op jit(solution)/shard_map/ppermute | solution.py:174
  81.8 6.0 %collective-permute-start.32 = (bf16[64,640]{1,0:T(8,128)(2,1)}, bf16[64,640]{1,0:T(8,128)(2,1)S(1)}, u32[]{:S(2)}, u32[]{:S(2)}) collective-permute-start(bf16[64,640]{1,0:T(8,128)(2,1)} %output.2.refs_3_.current_hbm), channel_id=1, source_target_pairs={{0,1},{1,0},{2,3},{3,2},{4,5},{5,4},{6,7},{7,6},{8,9},{9,8},{10,11... | collective-permute-start | bytes 245768 | tf_op jit(solution)/shard_map/ppermute | solution.py:174
  81.8 8.5 %collective-permute-start.28 = (bf16[64,640]{1,0:T(8,128)(2,1)}, bf16[64,640]{1,0:T(8,128)(2,1)S(1)}, u32[]{:S(2)}, u32[]{:S(2)}) collective-permute-start(bf16[64,640]{1,0:T(8,128)(2,1)} %output.2.refs_3_.current_hbm), channel_id=1, source_target_pairs={{0,8},{1,9},{2,10},{3,11},{4,12},{5,13},{6,14},{7,15},{8,0},{9,1},... | collective-permute-start | bytes 245768 | tf_op jit(solution)/shard_map/ppermute | solution.py:174
  81.8 8.7 %collective-permute-start.26 = (bf16[64,640]{1,0:T(8,128)(2,1)}, bf16[64,640]{1,0:T(8,128)(2,1)S(1)}, u32[]{:S(2)}, u32[]{:S(2)}) collective-permute-start(bf16[64,640]{1,0:T(8,128)(2,1)} %output.2.refs_3_.current_hbm), channel_id=1, source_target_pairs={{0,4},{1,5},{2,6},{3,7},{4,0},{5,1},{6,2},{7,3},{8,12},{9,13},{10,... | collective-permute-start | bytes 245768 | tf_op jit(solution)/shard_map/ppermute | solution.py:174
  84.8 6.5 %collective-permute-start.25 = (bf16[64,640]{1,0:T(8,128)(2,1)}, bf16[64,640]{1,0:T(8,128)(2,1)S(1)}, u32[]{:S(2)}, u32[]{:S(2)}) collective-permute-start(bf16[64,640]{1,0:T(8,128)(2,1)} %output.2.refs_3_.current_hbm), channel_id=1, source_target_pairs={{0,2},{1,3},{2,0},{3,1},{4,6},{5,7},{6,4},{7,5},{8,10},{9,11},{10,... | collective-permute-start | bytes 245768 | tf_op jit(solution)/shard_map/ppermute | solution.py:174
  87.7 10.5 %copy-start.8 = (bf16[64,640]{1,0:T(8,128)(2,1)}, bf16[64,640]{1,0:T(8,128)(2,1)S(1)}, u32[]{:S(2)}) copy-start(bf16[64,640]{1,0:T(8,128)(2,1)S(1)} %collective-permute-done.30.refs_9_) | copy-start | bytes 245764
  87.8 4.7 %collective-permute-start.38 = (bf16[64,640]{1,0:T(8,128)(2,1)S(1)}, bf16[64,640]{1,0:T(8,128)(2,1)S(1)}, u32[]{:S(2)}, u32[]{:S(2)}) collective-permute-start(bf16[64,640]{1,0:T(8,128)(2,1)S(1)} %collective-permute-done.30.refs_9_), channel_id=1, source_target_pairs={{0,1},{1,0},{2,3},{3,2},{4,5},{5,4},{6,7},{7,6},{8,9},{9,8},{10,11... | collective-permute-start | bytes 245768 | tf_op jit(solution)/shard_map/ppermute | solution.py:174
  87.8 10.5 %copy-start.10 = (bf16[64,640]{1,0:T(8,128)(2,1)}, bf16[64,640]{1,0:T(8,128)(2,1)S(1)}, u32[]{:S(2)}) copy-start(bf16[64,640]{1,0:T(8,128)(2,1)S(1)} %collective-permute-done.32.refs_11_) | copy-start | bytes 245764
  87.8 4.9 %collective-permute-start.31 = (bf16[64,640]{1,0:T(8,128)(2,1)S(1)}, bf16[64,640]{1,0:T(8,128)(2,1)S(1)}, u32[]{:S(2)}, u32[]{:S(2)}) collective-permute-start(bf16[64,640]{1,0:T(8,128)(2,1)S(1)} %collective-permute-done.30.refs_9_), channel_id=1, source_target_pairs={{0,2},{1,3},{2,0},{3,1},{4,6},{5,7},{6,4},{7,5},{8,10},{9,11},{10,... | collective-permute-start | bytes 245768 | tf_op jit(solution)/shard_map/ppermute | solution.py:174
  90.2 8.0 %copy-start.11 = (bf16[64,640]{1,0:T(8,128)(2,1)}, bf16[64,640]{1,0:T(8,128)(2,1)S(1)}, u32[]{:S(2)}) copy-start(bf16[64,640]{1,0:T(8,128)(2,1)S(1)} %collective-permute-done.28.refs_7_) | copy-start | bytes 245764
  90.2 2.7 %collective-permute-start.36 = (bf16[64,640]{1,0:T(8,128)(2,1)S(1)}, bf16[64,640]{1,0:T(8,128)(2,1)S(1)}, u32[]{:S(2)}, u32[]{:S(2)}) collective-permute-start(bf16[64,640]{1,0:T(8,128)(2,1)S(1)} %collective-permute-done.28.refs_7_), channel_id=1, source_target_pairs={{0,1},{1,0},{2,3},{3,2},{4,5},{5,4},{6,7},{7,6},{8,9},{9,8},{10,11... | collective-permute-start | bytes 245768 | tf_op jit(solution)/shard_map/ppermute | solution.py:174
  90.4 7.9 %copy-start.13 = (bf16[64,640]{1,0:T(8,128)(2,1)}, bf16[64,640]{1,0:T(8,128)(2,1)S(1)}, u32[]{:S(2)}) copy-start(bf16[64,640]{1,0:T(8,128)(2,1)S(1)} %collective-permute-done.26.refs_5_) | copy-start | bytes 245764
  90.4 5.3 %collective-permute-start.29 = (bf16[64,640]{1,0:T(8,128)(2,1)S(1)}, bf16[64,640]{1,0:T(8,128)(2,1)S(1)}, u32[]{:S(2)}, u32[]{:S(2)}) collective-permute-start(bf16[64,640]{1,0:T(8,128)(2,1)S(1)} %collective-permute-done.28.refs_7_), channel_id=1, source_target_pairs={{0,2},{1,3},{2,0},{3,1},{4,6},{5,7},{6,4},{7,5},{8,10},{9,11},{10,... | collective-permute-start | bytes 245768 | tf_op jit(solution)/shard_map/ppermute | solution.py:174
  91.3 7.0 %copy-start.14 = (bf16[64,640]{1,0:T(8,128)(2,1)}, bf16[64,640]{1,0:T(8,128)(2,1)S(1)}, u32[]{:S(2)}) copy-start(bf16[64,640]{1,0:T(8,128)(2,1)S(1)} %collective-permute-done.25.refs_4_) | copy-start | bytes 245764
  91.3 5.6 %collective-permute-start.27 = (bf16[64,640]{1,0:T(8,128)(2,1)S(1)}, bf16[64,640]{1,0:T(8,128)(2,1)S(1)}, u32[]{:S(2)}, u32[]{:S(2)}) collective-permute-start(bf16[64,640]{1,0:T(8,128)(2,1)S(1)} %collective-permute-done.26.refs_5_), channel_id=1, source_target_pairs={{0,2},{1,3},{2,0},{3,1},{4,6},{5,7},{6,4},{7,5},{8,10},{9,11},{10,... | collective-permute-start | bytes 245768 | tf_op jit(solution)/shard_map/ppermute | solution.py:174
  92.5 4.4 %collective-permute-start.34 = (bf16[64,640]{1,0:T(8,128)(2,1)S(1)}, bf16[64,640]{1,0:T(8,128)(2,1)S(1)}, u32[]{:S(2)}, u32[]{:S(2)}) collective-permute-start(bf16[64,640]{1,0:T(8,128)(2,1)S(1)} %collective-permute-done.26.refs_5_), channel_id=1, source_target_pairs={{0,1},{1,0},{2,3},{3,2},{4,5},{5,4},{6,7},{7,6},{8,9},{9,8},{10,11... | collective-permute-start | bytes 245768 | tf_op jit(solution)/shard_map/ppermute | solution.py:174
  92.6 4.3 %collective-permute-start.33 = (bf16[64,640]{1,0:T(8,128)(2,1)S(1)}, bf16[64,640]{1,0:T(8,128)(2,1)S(1)}, u32[]{:S(2)}, u32[]{:S(2)}) collective-permute-start(bf16[64,640]{1,0:T(8,128)(2,1)S(1)} %collective-permute-done.25.refs_4_), channel_id=1, source_target_pairs={{0,1},{1,0},{2,3},{3,2},{4,5},{5,4},{6,7},{7,6},{8,9},{9,8},{10,11... | collective-permute-start | bytes 245768 | tf_op jit(solution)/shard_map/ppermute | solution.py:174
  93.0 3.9 %collective-permute-start.39 = (bf16[64,640]{1,0:T(8,128)(2,1)S(1)}, bf16[64,640]{1,0:T(8,128)(2,1)S(1)}, u32[]{:S(2)}, u32[]{:S(2)}) collective-permute-start(bf16[64,640]{1,0:T(8,128)(2,1)S(1)} %collective-permute-done.31.refs_10_), channel_id=1, source_target_pairs={{0,1},{1,0},{2,3},{3,2},{4,5},{5,4},{6,7},{7,6},{8,9},{9,8},{10,11... | collective-permute-start | bytes 245768 | tf_op jit(solution)/shard_map/ppermute | solution.py:174
  95.7 1.3 collective-permute-start.37
  96.9 1.4 collective-permute-start.35
  107.1 10.8 %collective-permute-start.40 = (bf16[320,320]{1,0:T(8,128)(2,1)}, bf16[320,320]{1,0:T(8,128)(2,1)S(1)}, u32[]{:S(2)}, u32[]{:S(2)}) collective-permute-start(bf16[320,320]{1,0:T(8,128)(2,1)} %get-tuple-element.25.sent_hbm), channel_id=1, source_target_pairs={{0,1},{1,0},{2,3},{3,2},{4,5},{5,4},{6,7},{7,6},{8,9},{9,8},{10,11... | collective-permute-start | bytes 614408 | tf_op jit(solution)/shard_map/ppermute | solution.py:174
  124.3 7.4 %collective-permute-start.46 = (bf16[64,640]{1,0:T(8,128)(2,1)}, bf16[64,640]{1,0:T(8,128)(2,1)S(1)}, u32[]{:S(2)}, u32[]{:S(2)}) collective-permute-start(bf16[64,640]{1,0:T(8,128)(2,1)} %attend.3.refs_0_), channel_id=1, source_target_pairs={{0,12},{1,13},{2,14},{3,15},{4,8},{5,9},{6,10},{7,11},{8,4},{9,5},... | collective-permute-start | bytes 245768 | tf_op jit(solution)/shard_map/ppermute | solution.py:174
  124.8 9.3 %collective-permute-start.44 = (bf16[64,640]{1,0:T(8,128)(2,1)}, bf16[64,640]{1,0:T(8,128)(2,1)S(1)}, u32[]{:S(2)}, u32[]{:S(2)}) collective-permute-start(bf16[64,640]{1,0:T(8,128)(2,1)} %attend.3.refs_0_), channel_id=1, source_target_pairs={{0,8},{1,9},{2,10},{3,11},{4,12},{5,13},{6,14},{7,15},{8,0},{9,1},... | collective-permute-start | bytes 245768 | tf_op jit(solution)/shard_map/ppermute | solution.py:174
  126.2 8.5 %collective-permute-start.42 = (bf16[64,640]{1,0:T(8,128)(2,1)}, bf16[64,640]{1,0:T(8,128)(2,1)S(1)}, u32[]{:S(2)}, u32[]{:S(2)}) collective-permute-start(bf16[64,640]{1,0:T(8,128)(2,1)} %attend.3.refs_0_), channel_id=1, source_target_pairs={{0,4},{1,5},{2,6},{3,7},{4,0},{5,1},{6,2},{7,3},{8,12},{9,13},{10,... | collective-permute-start | bytes 245768 | tf_op jit(solution)/shard_map/ppermute | solution.py:174
  128.7 7.5 %collective-permute-start.41 = (bf16[64,640]{1,0:T(8,128)(2,1)}, bf16[64,640]{1,0:T(8,128)(2,1)S(1)}, u32[]{:S(2)}, u32[]{:S(2)}) collective-permute-start(bf16[64,640]{1,0:T(8,128)(2,1)} %attend.3.refs_0_), channel_id=1, source_target_pairs={{0,2},{1,3},{2,0},{3,1},{4,6},{5,7},{6,4},{7,5},{8,10},{9,11},{10,... | collective-permute-start | bytes 245768 | tf_op jit(solution)/shard_map/ppermute | solution.py:174
  131.7 8.2 %copy-start.28 = (bf16[64,640]{1,0:T(8,128)(2,1)}, bf16[64,640]{1,0:T(8,128)(2,1)S(1)}, u32[]{:S(2)}) copy-start(bf16[64,640]{1,0:T(8,128)(2,1)S(1)} %collective-permute-done.46.refs_6_) | copy-start | bytes 245764
  131.7 4.5 %collective-permute-start.47 = (bf16[64,640]{1,0:T(8,128)(2,1)S(1)}, bf16[64,640]{1,0:T(8,128)(2,1)S(1)}, u32[]{:S(2)}, u32[]{:S(2)}) collective-permute-start(bf16[64,640]{1,0:T(8,128)(2,1)S(1)} %collective-permute-done.46.refs_6_), channel_id=1, source_target_pairs={{0,2},{1,3},{2,0},{3,1},{4,6},{5,7},{6,4},{7,5},{8,10},{9,11},{10,... | collective-permute-start | bytes 245768 | tf_op jit(solution)/shard_map/ppermute | solution.py:174
  134.2 4.8 %collective-permute-start.45 = (bf16[64,640]{1,0:T(8,128)(2,1)S(1)}, bf16[64,640]{1,0:T(8,128)(2,1)S(1)}, u32[]{:S(2)}, u32[]{:S(2)}) collective-permute-start(bf16[64,640]{1,0:T(8,128)(2,1)S(1)} %collective-permute-done.44.refs_4_), channel_id=1, source_target_pairs={{0,2},{1,3},{2,0},{3,1},{4,6},{5,7},{6,4},{7,5},{8,10},{9,11},{10,... | collective-permute-start | bytes 245768 | tf_op jit(solution)/shard_map/ppermute | solution.py:174
  134.7 5.1 %collective-permute-start.43 = (bf16[64,640]{1,0:T(8,128)(2,1)S(1)}, bf16[64,640]{1,0:T(8,128)(2,1)S(1)}, u32[]{:S(2)}, u32[]{:S(2)}) collective-permute-start(bf16[64,640]{1,0:T(8,128)(2,1)S(1)} %collective-permute-done.42.refs_2_), channel_id=1, source_target_pairs={{0,2},{1,3},{2,0},{3,1},{4,6},{5,7},{6,4},{7,5},{8,10},{9,11},{10,... | collective-permute-start | bytes 245768 | tf_op jit(solution)/shard_map/ppermute | solution.py:174
  (32 other events, 79.5 us)

commit v6 on v5

--- a/solution.py
+++ b/solution.py
@@ -295,27 +295,24 @@
     ident = lax.broadcasted_iota(jnp.int32, (tokens, tokens), 0) == lax.broadcasted_iota(
         jnp.int32, (tokens, tokens), 1
     )
-    for i in range(3):
-        fetches[i].wait()
-        product = contract_last(modulated[...], weights[i])
-        if i < 2:
-            column = jnp.sum(product * product, axis=1, keepdims=True)
-            line = jnp.sum(jnp.where(ident, column, 0.0), axis=0, keepdims=True)
-            squares_ref[:, i : i + 1, :] = jnp.broadcast_to(line[None], (spans, 1, tokens))
-            line = gain[i : i + 1, :]
-            product = product * jnp.where(first, line[:, :cols], line[:, cols:])
-        if i == 0:
-            low, high = product[:half], product[half:]
-            own[...] = jnp.where(first, low, high).astype(jnp.bfloat16)
-            send[:half, :] = jnp.where(first, high, low).astype(jnp.bfloat16)
-            leaving += started(
-                [(own, own_hbm), (send.at[pl.ds(0, half)], send_hbm.at[pl.ds(0, half)])],
-                sems.at[pl.ds(1, 2)],
-            )
-        else:
-            band = pl.ds(half + (i - 1) * tokens, tokens)
-            send[band, :] = product.astype(jnp.bfloat16)
-            leaving += started([(send.at[band], send_hbm.at[band])], sems.at[pl.ds(2 + i, 1)])
+    products = []
+    for fetch, weight in ((fetches[:1], 0), (fetches[1:], 1), ([], 2)):
+        finished(fetch)
+        products.append(contract_last(modulated[...], weights[weight]))
+    shape = (tokens, tokens)
+    ident = lax.broadcasted_iota(jnp.int32, shape, 0) == lax.broadcasted_iota(jnp.int32, shape, 1)
+    for i in range(2):
+        column = jnp.sum(products[i] * products[i], axis=1, keepdims=True)
+        line = jnp.sum(jnp.where(ident, column, 0.0), axis=0, keepdims=True)
+        squares_ref[:, i : i + 1, :] = jnp.broadcast_to(line[None], (spans, 1, tokens))
+        line = gain[i : i + 1, :]
+        products[i] = products[i] * jnp.where(first, line[:, :cols], line[:, cols:])
+    low, high = products[0][:half], products[0][half:]
+    own[...] = jnp.where(first, low, high).astype(jnp.bfloat16)
+    send[:half, :] = jnp.where(first, high, low).astype(jnp.bfloat16)
+    send[half : half + tokens, :] = products[1].astype(jnp.bfloat16)
+    send[half + tokens :, :] = products[2].astype(jnp.bfloat16)
+    leaving += started([(own, own_hbm), (send, send_hbm)], sems.at[pl.ds(1, 2)])
     finished(leaving)
 
 
@@ -403,36 +400,39 @@
     allowed = span_at(own_block, step, spans) >= span_at(key_block, step, spans)
     text_rows = text_ref.shape[0] * text_ref.shape[2]
     finished(copies[4:])
-    for head in range(width // head_size):
-        lanes = slice(head * head_size, (head + 1) * head_size)
-        q = queries[:, lanes]
-        scores = contract_last(q, keys[:, lanes]) * column * row
-        scores = jnp.where(allowed, scores, -1e30)
-        weights = jnp.exp(scores - jnp.max(scores, axis=1, keepdims=True))
-        weights = weights * (1.0 / jnp.sum(weights, axis=1, keepdims=True))
-        attended = jnp.dot(
-            weights.astype(jnp.bfloat16), values[:, lanes], preferred_element_type=jnp.float32
-        ).astype(jnp.bfloat16)
-        parts = []
-        for ref in (text_ref, more_ref):
-            text_keys = ref[:, 0, :, lanes].reshape(text_rows, head_size)
-            parts.append(contract_last(q, text_keys) * column)
-        most = jnp.maximum(
-            jnp.max(parts[0], axis=1, keepdims=True), jnp.max(parts[1], axis=1, keepdims=True)
-        )
-        parts = [jnp.exp(part - most) for part in parts]
-        total = jnp.sum(parts[0], axis=1, keepdims=True) + jnp.sum(parts[1], axis=1, keepdims=True)
-        share = 1.0 / total
+    heads = width // head_size
+    lanes = [slice(head * head_size, (head + 1) * head_size) for head in range(heads)]
+    stacked = jnp.concatenate([column] * heads, axis=0)
+    scores = jnp.concatenate([contract_last(queries[:, at], keys[:, at]) for at in lanes], axis=0)
+    scores = scores * stacked * row
+    scores = jnp.where(jnp.concatenate([allowed] * heads, axis=0), scores, -1e30)
+    parts = []
+    for ref in (text_ref, more_ref):
+        products = [
+            contract_last(queries[:, at], ref[:, 0, :, at].reshape(text_rows, head_size))
+            for at in lanes
+        ]
+        parts.append(jnp.concatenate(products, axis=0) * stacked)
+    weights = jnp.exp(scores - jnp.max(scores, axis=1, keepdims=True))
+    weights = weights * (1.0 / jnp.sum(weights, axis=1, keepdims=True))
+    weights = weights.astype(jnp.bfloat16)
+    most = jnp.max(jnp.maximum(*parts), axis=1, keepdims=True)
+    parts = [jnp.exp(part - most) for part in parts]
+    share = 1.0 / jnp.sum(parts[0] + parts[1], axis=1, keepdims=True)
+    parts = [(part * share).astype(jnp.bfloat16) for part in parts]
+    for head, at in enumerate(lanes):
+        band = slice(head * half, (head + 1) * half)
+        attended = jnp.dot(weights[band], values[:, at], preferred_element_type=jnp.float32)
         crossed = jnp.zeros((half, head_size), jnp.float32)
         for ref, part in zip((text_ref, more_ref), parts):
-            text_values = ref[:, 1, :, lanes].reshape(text_rows, head_size)
+            text_values = ref[:, 1, :, at].reshape(text_rows, head_size)
             crossed = crossed + jnp.dot(
-                (part * share).astype(jnp.bfloat16), text_values, preferred_element_type=jnp.float32
+                part[band], text_values, preferred_element_type=jnp.float32
             )
-        crossed = crossed.astype(jnp.bfloat16)
-        out_ref[:, lanes] = (attended.astype(jnp.float32) + crossed.astype(jnp.float32)).astype(
-            jnp.bfloat16
-        )
+        attended, crossed = (
+            value.astype(jnp.bfloat16).astype(jnp.float32) for value in (attended, crossed)
+        )
+        out_ref[:, at] = (attended + crossed).astype(jnp.bfloat16)
 
 
 def attend(step, spans, head_size, own, sent, got, squares, text, more):
@@ -486,7 +486,8 @@
     mine = jnp.zeros((half, cols), jnp.float32)
     other = jnp.zeros((half, cols), jnp.float32)
     for mask in range(chips):
-        finished(copies[3 * mask : 3 * mask + 3])
+        if mask % (chips // 2) == 0:
+            finished(copies[3 * mask : 3 * (mask + chips // 2)])
         block = blocks[mask]
         mine = mine + contract_last(block, weights[mask, 0])
         other = other + contract_last(block, weights[mask, 1])
@@ -494,22 +495,22 @@
     totals[:, cols:] = jnp.where(first, other, mine)
     finished(copies[3 * chips :])
     gates = gate_ref[...].astype(jnp.float32)
+    gate = []
     for block in range(chips):
-        band = slice(block * rows, (block + 1) * rows)
         places = [span_at(block + e * chips, step, spans) for e in range(2)]
-        gate = jnp.where(first, *(gates[s : s + 1, :] for s in places))
-        totals[band, :] = current[band, :].astype(jnp.float32) + gate * totals[band, :]
+        row = jnp.where(first, *(gates[s : s + 1, :] for s in places))
+        gate.append(jnp.broadcast_to(row, (rows, width)))
+    state = current[...].astype(jnp.float32) + jnp.concatenate(gate, axis=0) * totals[...]
     if last:
         for target in range(chips):
             block = (target - STEPS // 2) % chips
-            out_ref[target] = totals[block * rows : (block + 1) * rows, :].astype(jnp.bfloat16)
+            out_ref[target] = state[block * rows : (block + 1) * rows, :].astype(jnp.bfloat16)
     else:
         parity, block = (spans - 2 - step) % 2, (spans - 2 - step) // 2
-        band = slice(block * rows, (block + 1) * rows)
-        totals[band, :] = jnp.where(
-            core == parity, entering[...].astype(jnp.float32), totals[band, :]
-        )
-        out_ref[...] = totals[...].astype(jnp.bfloat16)
+        replaced = lax.broadcasted_iota(jnp.int32, (half, width), 0) // rows == block
+        fresh = jnp.concatenate([entering[...].astype(jnp.float32)] * chips, axis=0)
+        state = jnp.where(replaced & (core == parity), fresh, state)
+        out_ref[...] = state.astype(jnp.bfloat16)
 
 
 def output(step, spans, last, current, table, incoming, own, other, blocks):

time: 157 us -> 152 us (0.968)
  Pallas kernels: 41.2 us -> 36 us
    pallas_call x2, Pallas kernels: 11.4 us -> 6.27 us  [attend(): pl.pallas_call(functools.partial(attend_kernel, step, spans, head_size),...]
  transfers between devices with their start and end apart: 49 -> 49, of which waited for: 23 -> 23; matrix products, arithmetic and copies ran while one was open for 2% -> 2% of each run, Pallas kernels for 10% -> 9%
where the time goes in v6:
time: 152 us; the launch traced here: 151 us
  starting transfers between devices  42 us (28%)
  Pallas kernels  36 us (24%)
  waiting for transfers between devices  33.2 us (22%)
  blocking collectives  32.2 us (21%)
  local copies, waits for them, and re-layouts  4.14 us (3%)
  matrix products  2.02 us (1%)
    ppermute x48, starting transfers between devices, swapped(): lax.ppermute(value, 'queue', [(source, source ^ bit) for source in range(...  37.3 us
    ppermute x48, waiting for transfers between devices, swapped(): lax.ppermute(value, 'queue', [(source, source ^ bit) for source in range(...  29.6 us
    all_to_all x2, blocking collectives, paired_device(): lax.all_to_all(squares, 'queue', split_axis=0, concat_axis=0, tiled=True)  21.9 us
    pallas_call x2, Pallas kernels, project(): pl.pallas_call(functools.partial(project_kernel, step, spans), out_shape=...  17.5 us
    all_to_all x1, blocking collectives, paired_device(): lax.all_to_all(result, 'queue', split_axis=0, concat_axis=2, tiled=True,...  10.3 us
    pallas_call x2, Pallas kernels, output(): pl.pallas_call(functools.partial(output_kernel, step, spans, last), out_s...  10.2 us
    pallas_call x2, Pallas kernels, attend(): pl.pallas_call(functools.partial(attend_kernel, step, spans, head_size),...  6.27 us
    all_to_all x1, starting transfers between devices, paired_device(): lax.all_to_all(text, 'queue', split_axis=0, concat_axis=0, tiled=True)  4.73 us
  transfers between devices with their start and end apart: 49, of which 23 were waited for; matrix products, arithmetic and copies ran while one was open for 2% of the time, Pallas kernels for 9%

profile of v6, /device:TPU:0, one launch (start us, length us, event | category | flops | bytes accessed | tf_op | source)
XLA Modules:
  0.0 151.4 jit_solution(15781209651263717031)
XLA Ops:
  0.0 0.5 collective-permute-start.15
  0.5 4.7 %collective-permute-start.5 = (bf16[8,5120]{1,0:T(8,128)(2,1)}, bf16[8,5120]{1,0:T(8,128)(2,1)S(1)}, u32[]{:S(2)}, u32[]{:S(2)}) collective-permute-start(bf16[8,5120]{1,0:T(8,128)(2,1)} %refs_3_.1), channel_id=1, source_target_pairs={{0,12},{1,13},{2,14},{3,15},{4,8},{5,9},{6,10},{7,11},{8,4},{9,5},... | collective-permute-start | bytes 245768 | tf_op jit(solution)/shard_map/ppermute | solution.py:174
  5.1 0.7 collective-permute-start.1
  5.8 1.6 %collective-permute-start = (bf16[8,5120]{1,0:T(8,128)(2,1)}, bf16[8,5120]{1,0:T(8,128)(2,1)S(1)}, u32[]{:S(2)}, u32[]{:S(2)}) collective-permute-start(bf16[8,5120]{1,0:T(8,128)(2,1)} %refs_3_.1), channel_id=1, source_target_pairs={{0,2},{1,3},{2,0},{3,1},{4,6},{5,7},{6,4},{7,5},{8,10},{9,11},{10,... | collective-permute-start | bytes 245768 | tf_op jit(solution)/shard_map/ppermute | solution.py:174
  7.4 1.4 pad_maximum_fusion.gain_hbm
  8.8 1.6 %collective-permute-start.6 = (bf16[8,5120]{1,0:T(8,128)(2,1)S(1)}, bf16[8,5120]{1,0:T(8,128)(2,1)S(1)}, u32[]{:S(2)}, u32[]{:S(2)}) collective-permute-start(bf16[8,5120]{1,0:T(8,128)(2,1)S(1)} %collective-permute-done.5.refs_9_), channel_id=1, source_target_pairs={{0,2},{1,3},{2,0},{3,1},{4,6},{5,7},{6,4},{7,5},{8,10},{9,11},{10,... | collective-permute-start | bytes 245768 | tf_op jit(solution)/shard_map/ppermute | solution.py:174
  10.4 2.4 %collective-permute-done.3.refs_7_ = bf16[8,5120]{1,0:T(8,128)(2,1)S(1)} collective-permute-done((bf16[8,5120]{1,0:T(8,128)(2,1)}, bf16[8,5120]{1,0:T(8,128)(2,1)S(1)}, u32[]{:S(2)}, u32[]{:S(2)}) %collective-permute-start.3) | collective-permute-done | bytes 81952 | tf_op jit(solution)/shard_map/ppermute | solution.py:174
  12.8 1.5 %collective-permute-start.4 = (bf16[8,5120]{1,0:T(8,128)(2,1)S(1)}, bf16[8,5120]{1,0:T(8,128)(2,1)S(1)}, u32[]{:S(2)}, u32[]{:S(2)}) collective-permute-start(bf16[8,5120]{1,0:T(8,128)(2,1)S(1)} %collective-permute-done.3.refs_7_), channel_id=1, source_target_pairs={{0,2},{1,3},{2,0},{3,1},{4,6},{5,7},{6,4},{7,5},{8,10},{9,11},{10,... | collective-permute-start | bytes 245768 | tf_op jit(solution)/shard_map/ppermute | solution.py:174
  14.3 0.5 collective-permute-start.2
  14.9 2.0 %fusion.table_hbm = bf16[3,16,5120]{2,1,0:T(8,128)(2,1)} fusion(bf16[96,3,5120]{2,0,1:T(8,128)(2,1)S(1)} %copy-done, s32[16]{0:T(128)} %param.14), kind=kOutput, calls=%fused_computation.1 | convolution fusion | flops 47433216 | bytes 3440704 | tf_op jit(solution)/shard_map/sl,ltd->tsd/dot_general | solution.py:603
  16.9 2.0 %arrange.1 = bf16[16,2,16,640]{3,2,1,0:T(8,128)(2,1)} custom-call(bf16[32,5120]{1,0:T(8,128)(2,1)} %keys_ref.1, bf16[32,5120]{1,0:T(8,128)(2,1)} %values_ref.1), custom_call_target="tpu_custom_call" | custom-call | tf_op jit(solution)/shard_map/arrange/pallas_call | solution.py:571
  19.1 4.7 %all-to-all-start.1 = ((bf16[16,2,16,640]{3,2,1,0:T(8,128)(2,1)}), bf16[16,2,16,640]{3,2,1,0:T(8,128)(2,1)}, u32[]{:S(2)}, u32[]{:S(2)}) async-start(bf16[16,2,16,640]{3,2,1,0:T(8,128)(2,1)} %arrange.1), calls=%async_computation.1 | async-start | bytes 1310720 | tf_op jit(solution)/shard_map/all_to_all | solution.py:611
  23.8 0.4 collective-permute-start.7
  24.4 0.4 collective-permute-start.11
  26.4 0.4 collective-permute-done.14.refs_18_
  27.0 0.6 collective-permute-done.10.refs_14_
  27.6 0.5 copy-done.42
  28.2 8.8 %project.2 = (bf16[64,320]{1,0:T(8,128)(2,1)}, bf16[320,320]{1,0:T(8,128)(2,1)}, f32[16,2,128]{2,1,0:T(2,128)}, bf16[64,640]{1,0:T(8,128)(2,1)}) custom-call(f32[2,5120]{1,0:T(2,128)} %pad_maximum_fusion.gain_hbm, bf16[3,16,5120]{2,1,0:T(8,128)(2,1)} %fusion.table_hbm, bf16[2,8,5120]{2,1,0:T(8,128)(2,1)} %incoming_hbm.7, bf16[320,5120]{1,0:T(8,128)(2,1)} %bitcast.17, ...), custom_call_target="tpu_custom_call" | custom-call | tf_op jit(solution)/shard_map/project/pallas_call | solution.py:334
  36.9 3.5 %all-to-all-done.1.text_hbm = bf16[16,2,16,640]{3,2,1,0:T(8,128)(2,1)} async-done(((bf16[16,2,16,640]{3,2,1,0:T(8,128)(2,1)}), bf16[16,2,16,640]{3,2,1,0:T(8,128)(2,1)}, u32[]{:S(2)}, u32[]{:S(2)}) %all-to-all-start.1) | async-done | bytes 655392 | tf_op jit(solution)/shard_map/all_to_all | solution.py:611
  40.5 0.4 collective-permute-start.16
  41.0 11.4 %all_to_all.30.squares_hbm = f32[16,2,128]{2,1,0:T(2,128)} all-to-all(f32[16,2,128]{2,1,0:T(2,128)} %get-tuple-element.21), channel_id=1, replica_groups=mesh['groups'=2,'queue'=16] {'queue'}, dimensions={0} | all-to-all | bytes 32768 | tf_op jit(solution)/shard_map/all_to_all | solution.py:619
  52.3 0.7 copy-done.2
  53.3 3.1 %attend.2.refs_0_ = bf16[64,640]{1,0:T(8,128)(2,1)} custom-call(bf16[64,320]{1,0:T(8,128)(2,1)} %get-tuple-element.19.own_hbm, bf16[320,320]{1,0:T(8,128)(2,1)} %get-tuple-element.20.sent_hbm, bf16[320,320]{1,0:T(8,128)(2,1)} %copy-done.2, f32[16,2,128]{2,1,0:T(2,128)} %all_to_all.30.squares_hbm, bf16[16,2,16,640]{3,2,1,0:T(8,128)(2,1)} %all-to-all-done.1.text_hbm, ...), custom_call_target="tpu_custom_call" | custom-call | tf_op jit(solution)/shard_map/attend/pallas_call | solution.py:441
  56.4 0.6 collective-permute-start.23
  57.0 1.4 collective-permute-start.21
  58.4 2.5 %collective-permute-start.19 = (bf16[64,640]{1,0:T(8,128)(2,1)}, bf16[64,640]{1,0:T(8,128)(2,1)S(1)}, u32[]{:S(2)}, u32[]{:S(2)}) collective-permute-start(bf16[64,640]{1,0:T(8,128)(2,1)} %attend.2.refs_0_), channel_id=1, source_target_pairs={{0,4},{1,5},{2,6},{3,7},{4,0},{5,1},{6,2},{7,3},{8,12},{9,13},{10,... | collective-permute-start | bytes 245768 | tf_op jit(solution)/shard_map/ppermute | solution.py:174
  60.9 0.5 collective-permute-start.18
  61.4 2.5 %collective-permute-done.23.refs_6_ = bf16[64,640]{1,0:T(8,128)(2,1)S(1)} collective-permute-done((bf16[64,640]{1,0:T(8,128)(2,1)}, bf16[64,640]{1,0:T(8,128)(2,1)S(1)}, u32[]{:S(2)}, u32[]{:S(2)}) %collective-permute-start.23) | collective-permute-done | bytes 81952 | tf_op jit(solution)/shard_map/ppermute | solution.py:174
  63.9 0.5 collective-permute-start.24
  64.4 2.0 %collective-permute-done.21.refs_4_ = bf16[64,640]{1,0:T(8,128)(2,1)S(1)} collective-permute-done((bf16[64,640]{1,0:T(8,128)(2,1)}, bf16[64,640]{1,0:T(8,128)(2,1)S(1)}, u32[]{:S(2)}, u32[]{:S(2)}) %collective-permute-start.21) | collective-permute-done | bytes 81952 | tf_op jit(solution)/shard_map/ppermute | solution.py:174
  66.3 0.6 collective-permute-start.22
  66.9 1.4 collective-permute-start.20
  68.4 2.7 %collective-permute-done.22.refs_5_ = bf16[64,640]{1,0:T(8,128)(2,1)S(1)} collective-permute-done((bf16[64,640]{1,0:T(8,128)(2,1)S(1)}, bf16[64,640]{1,0:T(8,128)(2,1)S(1)}, u32[]{:S(2)}, u32[]{:S(2)}) %collective-permute-start.22) | collective-permute-done | bytes 81952 | tf_op jit(solution)/shard_map/ppermute | solution.py:174
  71.1 0.9 collective-permute-done.20.refs_3_
  72.0 0.6 copy-done.45
  72.6 5.1 %output.2.refs_3_.current_hbm = bf16[64,640]{1,0:T(8,128)(2,1)} custom-call(bf16[64,640]{1,0:T(8,128)(2,1)} %get-tuple-element.18.current_hbm, bf16[3,16,5120]{2,1,0:T(8,128)(2,1)} %fusion.table_hbm, bf16[2,8,5120]{2,1,0:T(8,128)(2,1)} %incoming_hbm.7, bf16[320,5120]{1,0:T(8,128)(2,1)} %bitcast.24, bf16[320,5120]{1,0:T(8,128)(2,1)} %collective-permute-done.15.other_hbm, ...), custom_call_target="tpu_custom_call" | custom-call | tf_op jit(solution)/shard_map/output/pallas_call | solution.py:520
  77.7 1.4 collective-permute-start.30
  79.1 3.0 %collective-permute-start.26 = (bf16[64,640]{1,0:T(8,128)(2,1)}, bf16[64,640]{1,0:T(8,128)(2,1)S(1)}, u32[]{:S(2)}, u32[]{:S(2)}) collective-permute-start(bf16[64,640]{1,0:T(8,128)(2,1)} %output.2.refs_3_.current_hbm), channel_id=1, source_target_pairs={{0,4},{1,5},{2,6},{3,7},{4,0},{5,1},{6,2},{7,3},{8,12},{9,13},{10,... | collective-permute-start | bytes 245768 | tf_op jit(solution)/shard_map/ppermute | solution.py:174
  82.2 0.9 collective-permute-start.25
  83.0 2.1 %collective-permute-done.30.refs_9_ = bf16[64,640]{1,0:T(8,128)(2,1)S(1)} collective-permute-done((bf16[64,640]{1,0:T(8,128)(2,1)}, bf16[64,640]{1,0:T(8,128)(2,1)S(1)}, u32[]{:S(2)}, u32[]{:S(2)}) %collective-permute-start.30) | collective-permute-done | bytes 81952 | tf_op jit(solution)/shard_map/ppermute | solution.py:174
  85.1 0.9 collective-permute-start.31
  86.1 1.5 %collective-permute-done.28.refs_7_ = bf16[64,640]{1,0:T(8,128)(2,1)S(1)} collective-permute-done((bf16[64,640]{1,0:T(8,128)(2,1)}, bf16[64,640]{1,0:T(8,128)(2,1)S(1)}, u32[]{:S(2)}, u32[]{:S(2)}) %collective-permute-start.28) | collective-permute-done | bytes 81952 | tf_op jit(solution)/shard_map/ppermute | solution.py:174
  87.8 0.9 collective-permute-start.29
  88.7 1.1 collective-permute-start.27
  90.5 2.5 %collective-permute-done.29.refs_8_ = bf16[64,640]{1,0:T(8,128)(2,1)S(1)} collective-permute-done((bf16[64,640]{1,0:T(8,128)(2,1)S(1)}, bf16[64,640]{1,0:T(8,128)(2,1)S(1)}, u32[]{:S(2)}, u32[]{:S(2)}) %collective-permute-start.29) | collective-permute-done | bytes 81952 | tf_op jit(solution)/shard_map/ppermute | solution.py:174
  93.1 1.2 collective-permute-done.27.refs_6_
  94.3 1.3 collective-permute-done.35.refs_14_
  95.8 8.8 %project.3 = (bf16[64,320]{1,0:T(8,128)(2,1)}, bf16[320,320]{1,0:T(8,128)(2,1)}, f32[16,2,128]{2,1,0:T(2,128)}) custom-call(f32[2,5120]{1,0:T(2,128)} %pad_maximum_fusion.gain_hbm, bf16[3,16,5120]{2,1,0:T(8,128)(2,1)} %fusion.table_hbm, bf16[2,8,5120]{2,1,0:T(8,128)(2,1)} %incoming_hbm.7, bf16[320,5120]{1,0:T(8,128)(2,1)} %bitcast.18, ...), custom_call_target="tpu_custom_call" | custom-call | tf_op jit(solution)/shard_map/project/pallas_call | solution.py:334
  104.8 10.5 %all_to_all.31.squares_hbm = f32[16,2,128]{2,1,0:T(2,128)} all-to-all(f32[16,2,128]{2,1,0:T(2,128)} %get-tuple-element.26), channel_id=1, replica_groups=mesh['groups'=2,'queue'=16] {'queue'}, dimensions={0} | all-to-all | bytes 32768 | tf_op jit(solution)/shard_map/all_to_all | solution.py:619
  115.3 0.7 copy-done.3
  116.0 3.1 %attend.3.refs_0_ = bf16[64,640]{1,0:T(8,128)(2,1)} custom-call(bf16[64,320]{1,0:T(8,128)(2,1)} %get-tuple-element.24.own_hbm, bf16[320,320]{1,0:T(8,128)(2,1)} %get-tuple-element.25.sent_hbm, bf16[320,320]{1,0:T(8,128)(2,1)} %copy-done.3, f32[16,2,128]{2,1,0:T(2,128)} %all_to_all.31.squares_hbm, bf16[16,2,16,640]{3,2,1,0:T(8,128)(2,1)} %all-to-all-done.1.text_hbm, ...), custom_call_target="tpu_custom_call" | custom-call | tf_op jit(solution)/shard_map/attend/pallas_call | solution.py:441
  119.1 0.6 collective-permute-start.46
  119.7 1.4 collective-permute-start.44
  121.1 2.5 %collective-permute-start.42 = (bf16[64,640]{1,0:T(8,128)(2,1)}, bf16[64,640]{1,0:T(8,128)(2,1)S(1)}, u32[]{:S(2)}, u32[]{:S(2)}) collective-permute-start(bf16[64,640]{1,0:T(8,128)(2,1)} %attend.3.refs_0_), channel_id=1, source_target_pairs={{0,4},{1,5},{2,6},{3,7},{4,0},{5,1},{6,2},{7,3},{8,12},{9,13},{10,... | collective-permute-start | bytes 245768 | tf_op jit(solution)/shard_map/ppermute | solution.py:174
  123.9 2.7 %collective-permute-done.46.refs_6_ = bf16[64,640]{1,0:T(8,128)(2,1)S(1)} collective-permute-done((bf16[64,640]{1,0:T(8,128)(2,1)}, bf16[64,640]{1,0:T(8,128)(2,1)S(1)}, u32[]{:S(2)}, u32[]{:S(2)}) %collective-permute-start.46) | collective-permute-done | bytes 81952 | tf_op jit(solution)/shard_map/ppermute | solution.py:174
  126.9 2.1 %collective-permute-done.44.refs_4_ = bf16[64,640]{1,0:T(8,128)(2,1)S(1)} collective-permute-done((bf16[64,640]{1,0:T(8,128)(2,1)}, bf16[64,640]{1,0:T(8,128)(2,1)S(1)}, u32[]{:S(2)}, u32[]{:S(2)}) %collective-permute-start.44) | collective-permute-done | bytes 81952 | tf_op jit(solution)/shard_map/ppermute | solution.py:174
  129.0 0.6 collective-permute-start.45
  129.6 1.5 collective-permute-start.43
  131.1 2.7 %collective-permute-done.45.refs_5_ = bf16[64,640]{1,0:T(8,128)(2,1)S(1)} collective-permute-done((bf16[64,640]{1,0:T(8,128)(2,1)S(1)}, bf16[64,640]{1,0:T(8,128)(2,1)S(1)}, u32[]{:S(2)}, u32[]{:S(2)}) %collective-permute-start.45) | collective-permute-done | bytes 81952 | tf_op jit(solution)/shard_map/ppermute | solution.py:174
  133.8 0.9 collective-permute-done.43.refs_3_
  134.8 0.6 copy-done.46
  135.4 5.1 %output.3 = bf16[8,8,640]{2,1,0:T(8,128)(2,1)} custom-call(bf16[64,640]{1,0:T(8,128)(2,1)} %output.2.refs_3_.current_hbm, bf16[3,16,5120]{2,1,0:T(8,128)(2,1)} %fusion.table_hbm, bf16[2,8,5120]{2,1,0:T(8,128)(2,1)} %incoming_hbm.7, bf16[320,5120]{1,0:T(8,128)(2,1)} %bitcast.25, bf16[320,5120]{1,0:T(8,128)(2,1)} %collective-permute-done.15.other_hbm, ...), custom_call_target="tpu_custom_call" | custom-call | tf_op jit(solution)/shard_map/output/pallas_call | solution.py:520
  140.5 10.3 %all_to_all.32 = bf16[8,8,640]{2,1,0:T(8,128)(2,1)S(1)} all-to-all(bf16[8,8,640]{2,1,0:T(8,128)(2,1)} %output.3), channel_id=1, replica_groups={{0,2,4,6,8,10,12,14},{1,3,5,7,9,11,13,15},{16,18,20,22,24,26,28,30},{17..., dimensions={0} | all-to-all | bytes 163840 | tf_op jit(solution)/shard_map/all_to_all | solution.py:634
  150.8 0.6 copy.14
  (141 shorter events, 4.5 us)
Async XLA Ops:
  0.0 14.9 %copy-start = (bf16[96,3,5120]{2,0,1:T(8,128)(2,1)S(1)}, bf16[96,3,5120]{2,0,1:T(8,128)(2,1)}, u32[]{:S(2)}) copy-start(bf16[96,3,5120]{2,0,1:T(8,128)(2,1)} %param.15) | copy-start | bytes 8847364
  0.0 23.8 %copy-start.4 = (bf16[8,5120]{1,0:T(8,128)(2,1)S(1)}, bf16[8,5120]{1,0:T(8,128)(2,1)}, u32[]{:S(2)}) copy-start(bf16[8,5120]{1,0:T(8,128)(2,1)} %refs_3_.1) | copy-start | bytes 245764
  0.0 71.9 %collective-permute-start.15 = (bf16[320,5120]{1,0:T(8,128)(2,1)}, bf16[320,5120]{1,0:T(8,128)(2,1)}, u32[]{:S(2)}, u32[]{:S(2)}) collective-permute-start(bf16[320,5120]{1,0:T(8,128)(2,1)} %bitcast.23), channel_id=1, source_target_pairs={{0,1},{1,0},{2,3},{3,2},{4,5},{5,4},{6,7},{7,6},{8,9},{9,8},{10,11... | collective-permute-start | bytes 9830408 | tf_op jit(solution)/shard_map/ppermute | solution.py:174
  0.5 8.4 %collective-permute-start.5 = (bf16[8,5120]{1,0:T(8,128)(2,1)}, bf16[8,5120]{1,0:T(8,128)(2,1)S(1)}, u32[]{:S(2)}, u32[]{:S(2)}) collective-permute-start(bf16[8,5120]{1,0:T(8,128)(2,1)} %refs_3_.1), channel_id=1, source_target_pairs={{0,12},{1,13},{2,14},{3,15},{4,8},{5,9},{6,10},{7,11},{8,4},{9,5},... | collective-permute-start | bytes 245768 | tf_op jit(solution)/shard_map/ppermute | solution.py:174
  5.1 7.7 %collective-permute-start.3 = (bf16[8,5120]{1,0:T(8,128)(2,1)}, bf16[8,5120]{1,0:T(8,128)(2,1)S(1)}, u32[]{:S(2)}, u32[]{:S(2)}) collective-permute-start(bf16[8,5120]{1,0:T(8,128)(2,1)} %refs_3_.1), channel_id=1, source_target_pairs={{0,8},{1,9},{2,10},{3,11},{4,12},{5,13},{6,14},{7,15},{8,0},{9,1},... | collective-permute-start | bytes 245768 | tf_op jit(solution)/shard_map/ppermute | solution.py:174
  5.1 9.2 %collective-permute-start.1 = (bf16[8,5120]{1,0:T(8,128)(2,1)}, bf16[8,5120]{1,0:T(8,128)(2,1)S(1)}, u32[]{:S(2)}, u32[]{:S(2)}) collective-permute-start(bf16[8,5120]{1,0:T(8,128)(2,1)} %refs_3_.1), channel_id=1, source_target_pairs={{0,4},{1,5},{2,6},{3,7},{4,0},{5,1},{6,2},{7,3},{8,12},{9,13},{10,... | collective-permute-start | bytes 245768 | tf_op jit(solution)/shard_map/ppermute | solution.py:174
  5.8 13.1 %collective-permute-start = (bf16[8,5120]{1,0:T(8,128)(2,1)}, bf16[8,5120]{1,0:T(8,128)(2,1)S(1)}, u32[]{:S(2)}, u32[]{:S(2)}) collective-permute-start(bf16[8,5120]{1,0:T(8,128)(2,1)} %refs_3_.1), channel_id=1, source_target_pairs={{0,2},{1,3},{2,0},{3,1},{4,6},{5,7},{6,4},{7,5},{8,10},{9,11},{10,... | collective-permute-start | bytes 245768 | tf_op jit(solution)/shard_map/ppermute | solution.py:174
  8.8 18.7 %copy-start.5 = (bf16[8,5120]{1,0:T(8,128)(2,1)}, bf16[8,5120]{1,0:T(8,128)(2,1)S(1)}, u32[]{:S(2)}) copy-start(bf16[8,5120]{1,0:T(8,128)(2,1)S(1)} %collective-permute-done.5.refs_9_) | copy-start | bytes 245764
  8.8 10.0 %collective-permute-start.6 = (bf16[8,5120]{1,0:T(8,128)(2,1)S(1)}, bf16[8,5120]{1,0:T(8,128)(2,1)S(1)}, u32[]{:S(2)}, u32[]{:S(2)}) collective-permute-start(bf16[8,5120]{1,0:T(8,128)(2,1)S(1)} %collective-permute-done.5.refs_9_), channel_id=1, source_target_pairs={{0,2},{1,3},{2,0},{3,1},{4,6},{5,7},{6,4},{7,5},{8,10},{9,11},{10,... | collective-permute-start | bytes 245768 | tf_op jit(solution)/shard_map/ppermute | solution.py:174
  12.8 14.7 %copy-start.6 = (bf16[8,5120]{1,0:T(8,128)(2,1)}, bf16[8,5120]{1,0:T(8,128)(2,1)S(1)}, u32[]{:S(2)}) copy-start(bf16[8,5120]{1,0:T(8,128)(2,1)S(1)} %collective-permute-done.3.refs_7_) | copy-start | bytes 245764
  12.8 6.1 %collective-permute-start.4 = (bf16[8,5120]{1,0:T(8,128)(2,1)S(1)}, bf16[8,5120]{1,0:T(8,128)(2,1)S(1)}, u32[]{:S(2)}, u32[]{:S(2)}) collective-permute-start(bf16[8,5120]{1,0:T(8,128)(2,1)S(1)} %collective-permute-done.3.refs_7_), channel_id=1, source_target_pairs={{0,2},{1,3},{2,0},{3,1},{4,6},{5,7},{6,4},{7,5},{8,10},{9,11},{10,... | collective-permute-start | bytes 245768 | tf_op jit(solution)/shard_map/ppermute | solution.py:174
  14.3 13.2 %copy-start.7 = (bf16[8,5120]{1,0:T(8,128)(2,1)}, bf16[8,5120]{1,0:T(8,128)(2,1)S(1)}, u32[]{:S(2)}) copy-start(bf16[8,5120]{1,0:T(8,128)(2,1)S(1)} %collective-permute-done.1.refs_5_) | copy-start | bytes 245764
  14.3 4.7 %collective-permute-start.2 = (bf16[8,5120]{1,0:T(8,128)(2,1)S(1)}, bf16[8,5120]{1,0:T(8,128)(2,1)}, u32[]{:S(2)}, u32[]{:S(2)}) collective-permute-start(bf16[8,5120]{1,0:T(8,128)(2,1)S(1)} %collective-permute-done.1.refs_5_), channel_id=1, source_target_pairs={{0,2},{1,3},{2,0},{3,1},{4,6},{5,7},{6,4},{7,5},{8,10},{9,11},{10,... | collective-permute-start | bytes 245768 | tf_op jit(solution)/shard_map/ppermute | solution.py:174
  18.9 8.7 %copy-start.9 = (bf16[8,5120]{1,0:T(8,128)(2,1)}, bf16[8,5120]{1,0:T(8,128)(2,1)S(1)}, u32[]{:S(2)}) copy-start(bf16[8,5120]{1,0:T(8,128)(2,1)S(1)} %collective-permute-done.refs_4_) | copy-start | bytes 245764
  18.9 8.7 %copy-start.12 = (bf16[8,5120]{1,0:T(8,128)(2,1)}, bf16[8,5120]{1,0:T(8,128)(2,1)S(1)}, u32[]{:S(2)}) copy-start(bf16[8,5120]{1,0:T(8,128)(2,1)S(1)} %collective-permute-done.6.refs_10_) | copy-start | bytes 245764
  18.9 8.7 %copy-start.15 = (bf16[8,5120]{1,0:T(8,128)(2,1)}, bf16[8,5120]{1,0:T(8,128)(2,1)S(1)}, u32[]{:S(2)}) copy-start(bf16[8,5120]{1,0:T(8,128)(2,1)S(1)} %collective-permute-done.4.refs_8_) | copy-start | bytes 245764
  19.1 21.4 %all-to-all-start.1 = ((bf16[16,2,16,640]{3,2,1,0:T(8,128)(2,1)}), bf16[16,2,16,640]{3,2,1,0:T(8,128)(2,1)}, u32[]{:S(2)}, u32[]{:S(2)}) async-start(bf16[16,2,16,640]{3,2,1,0:T(8,128)(2,1)} %arrange.1), calls=%async_computation.1 | async-start | bytes 1310720 | tf_op jit(solution)/shard_map/all_to_all | solution.py:611
  23.8 1.3 collective-permute-start.7
  24.2 1.3 collective-permute-start.13
  24.4 1.3 collective-permute-start.11
  24.7 1.3 collective-permute-start.9
  25.2 1.3 collective-permute-start.8
  25.5 1.3 collective-permute-start.14
  25.7 1.3 collective-permute-start.12
  26.0 1.5 collective-permute-start.10
  40.5 11.9 %collective-permute-start.17 = (bf16[16,2,16,640]{3,2,1,0:T(8,128)(2,1)}, bf16[16,2,16,640]{3,2,1,0:T(8,128)(2,1)S(1)}, u32[]{:S(2)}, u32[]{:S(2)}) collective-permute-start(bf16[16,2,16,640]{3,2,1,0:T(8,128)(2,1)} %all-to-all-done.1.text_hbm), channel_id=1, source_target_pairs={{0,1},{1,0},{2,3},{3,2},{4,5},{5,4},{6,7},{7,6},{8,9},{9,8},{10,11... | collective-permute-start | bytes 1966088 | tf_op jit(solution)/shard_map/ppermute | solution.py:174
  40.5 11.8 %collective-permute-start.16 = (bf16[320,320]{1,0:T(8,128)(2,1)}, bf16[320,320]{1,0:T(8,128)(2,1)S(1)}, u32[]{:S(2)}, u32[]{:S(2)}) collective-permute-start(bf16[320,320]{1,0:T(8,128)(2,1)} %get-tuple-element.20.sent_hbm), channel_id=1, source_target_pairs={{0,1},{1,0},{2,3},{3,2},{4,5},{5,4},{6,7},{7,6},{8,9},{9,8},{10,11... | collective-permute-start | bytes 614408 | tf_op jit(solution)/shard_map/ppermute | solution.py:174
  56.4 7.4 %collective-permute-start.23 = (bf16[64,640]{1,0:T(8,128)(2,1)}, bf16[64,640]{1,0:T(8,128)(2,1)S(1)}, u32[]{:S(2)}, u32[]{:S(2)}) collective-permute-start(bf16[64,640]{1,0:T(8,128)(2,1)} %attend.2.refs_0_), channel_id=1, source_target_pairs={{0,12},{1,13},{2,14},{3,15},{4,8},{5,9},{6,10},{7,11},{8,4},{9,5},... | collective-permute-start | bytes 245768 | tf_op jit(solution)/shard_map/ppermute | solution.py:174
  57.0 9.3 %collective-permute-start.21 = (bf16[64,640]{1,0:T(8,128)(2,1)}, bf16[64,640]{1,0:T(8,128)(2,1)S(1)}, u32[]{:S(2)}, u32[]{:S(2)}) collective-permute-start(bf16[64,640]{1,0:T(8,128)(2,1)} %attend.2.refs_0_), channel_id=1, source_target_pairs={{0,8},{1,9},{2,10},{3,11},{4,12},{5,13},{6,14},{7,15},{8,0},{9,1},... | collective-permute-start | bytes 245768 | tf_op jit(solution)/shard_map/ppermute | solution.py:174
  58.4 8.5 %collective-permute-start.19 = (bf16[64,640]{1,0:T(8,128)(2,1)}, bf16[64,640]{1,0:T(8,128)(2,1)S(1)}, u32[]{:S(2)}, u32[]{:S(2)}) collective-permute-start(bf16[64,640]{1,0:T(8,128)(2,1)} %attend.2.refs_0_), channel_id=1, source_target_pairs={{0,4},{1,5},{2,6},{3,7},{4,0},{5,1},{6,2},{7,3},{8,12},{9,13},{10,... | collective-permute-start | bytes 245768 | tf_op jit(solution)/shard_map/ppermute | solution.py:174
  60.9 7.5 %collective-permute-start.18 = (bf16[64,640]{1,0:T(8,128)(2,1)}, bf16[64,640]{1,0:T(8,128)(2,1)S(1)}, u32[]{:S(2)}, u32[]{:S(2)}) collective-permute-start(bf16[64,640]{1,0:T(8,128)(2,1)} %attend.2.refs_0_), channel_id=1, source_target_pairs={{0,2},{1,3},{2,0},{3,1},{4,6},{5,7},{6,4},{7,5},{8,10},{9,11},{10,... | collective-permute-start | bytes 245768 | tf_op jit(solution)/shard_map/ppermute | solution.py:174
  63.9 8.1 %copy-start.26 = (bf16[64,640]{1,0:T(8,128)(2,1)}, bf16[64,640]{1,0:T(8,128)(2,1)S(1)}, u32[]{:S(2)}) copy-start(bf16[64,640]{1,0:T(8,128)(2,1)S(1)} %collective-permute-done.23.refs_6_) | copy-start | bytes 245764
  63.9 4.5 %collective-permute-start.24 = (bf16[64,640]{1,0:T(8,128)(2,1)S(1)}, bf16[64,640]{1,0:T(8,128)(2,1)S(1)}, u32[]{:S(2)}, u32[]{:S(2)}) collective-permute-start(bf16[64,640]{1,0:T(8,128)(2,1)S(1)} %collective-permute-done.23.refs_6_), channel_id=1, source_target_pairs={{0,2},{1,3},{2,0},{3,1},{4,6},{5,7},{6,4},{7,5},{8,10},{9,11},{10,... | collective-permute-start | bytes 245768 | tf_op jit(solution)/shard_map/ppermute | solution.py:174
  66.3 4.7 %collective-permute-start.22 = (bf16[64,640]{1,0:T(8,128)(2,1)S(1)}, bf16[64,640]{1,0:T(8,128)(2,1)S(1)}, u32[]{:S(2)}, u32[]{:S(2)}) collective-permute-start(bf16[64,640]{1,0:T(8,128)(2,1)S(1)} %collective-permute-done.21.refs_4_), channel_id=1, source_target_pairs={{0,2},{1,3},{2,0},{3,1},{4,6},{5,7},{6,4},{7,5},{8,10},{9,11},{10,... | collective-permute-start | bytes 245768 | tf_op jit(solution)/shard_map/ppermute | solution.py:174
  66.9 5.0 %collective-permute-start.20 = (bf16[64,640]{1,0:T(8,128)(2,1)S(1)}, bf16[64,640]{1,0:T(8,128)(2,1)S(1)}, u32[]{:S(2)}, u32[]{:S(2)}) collective-permute-start(bf16[64,640]{1,0:T(8,128)(2,1)S(1)} %collective-permute-done.19.refs_2_), channel_id=1, source_target_pairs={{0,2},{1,3},{2,0},{3,1},{4,6},{5,7},{6,4},{7,5},{8,10},{9,11},{10,... | collective-permute-start | bytes 245768 | tf_op jit(solution)/shard_map/ppermute | solution.py:174
  77.7 7.4 %collective-permute-start.30 = (bf16[64,640]{1,0:T(8,128)(2,1)}, bf16[64,640]{1,0:T(8,128)(2,1)S(1)}, u32[]{:S(2)}, u32[]{:S(2)}) collective-permute-start(bf16[64,640]{1,0:T(8,128)(2,1)} %output.2.refs_3_.current_hbm), channel_id=1, source_target_pairs={{0,12},{1,13},{2,14},{3,15},{4,8},{5,9},{6,10},{7,11},{8,4},{9,5},... | collective-permute-start | bytes 245768 | tf_op jit(solution)/shard_map/ppermute | solution.py:174
  79.1 6.0 %collective-permute-start.32 = (bf16[64,640]{1,0:T(8,128)(2,1)}, bf16[64,640]{1,0:T(8,128)(2,1)S(1)}, u32[]{:S(2)}, u32[]{:S(2)}) collective-permute-start(bf16[64,640]{1,0:T(8,128)(2,1)} %output.2.refs_3_.current_hbm), channel_id=1, source_target_pairs={{0,1},{1,0},{2,3},{3,2},{4,5},{5,4},{6,7},{7,6},{8,9},{9,8},{10,11... | collective-permute-start | bytes 245768 | tf_op jit(solution)/shard_map/ppermute | solution.py:174
  79.1 8.5 %collective-permute-start.28 = (bf16[64,640]{1,0:T(8,128)(2,1)}, bf16[64,640]{1,0:T(8,128)(2,1)S(1)}, u32[]{:S(2)}, u32[]{:S(2)}) collective-permute-start(bf16[64,640]{1,0:T(8,128)(2,1)} %output.2.refs_3_.current_hbm), channel_id=1, source_target_pairs={{0,8},{1,9},{2,10},{3,11},{4,12},{5,13},{6,14},{7,15},{8,0},{9,1},... | collective-permute-start | bytes 245768 | tf_op jit(solution)/shard_map/ppermute | solution.py:174
  79.1 8.7 %collective-permute-start.26 = (bf16[64,640]{1,0:T(8,128)(2,1)}, bf16[64,640]{1,0:T(8,128)(2,1)S(1)}, u32[]{:S(2)}, u32[]{:S(2)}) collective-permute-start(bf16[64,640]{1,0:T(8,128)(2,1)} %output.2.refs_3_.current_hbm), channel_id=1, source_target_pairs={{0,4},{1,5},{2,6},{3,7},{4,0},{5,1},{6,2},{7,3},{8,12},{9,13},{10,... | collective-permute-start | bytes 245768 | tf_op jit(solution)/shard_map/ppermute | solution.py:174
  82.2 6.5 %collective-permute-start.25 = (bf16[64,640]{1,0:T(8,128)(2,1)}, bf16[64,640]{1,0:T(8,128)(2,1)S(1)}, u32[]{:S(2)}, u32[]{:S(2)}) collective-permute-start(bf16[64,640]{1,0:T(8,128)(2,1)} %output.2.refs_3_.current_hbm), channel_id=1, source_target_pairs={{0,2},{1,3},{2,0},{3,1},{4,6},{5,7},{6,4},{7,5},{8,10},{9,11},{10,... | collective-permute-start | bytes 245768 | tf_op jit(solution)/shard_map/ppermute | solution.py:174
  85.1 10.5 %copy-start.8 = (bf16[64,640]{1,0:T(8,128)(2,1)}, bf16[64,640]{1,0:T(8,128)(2,1)S(1)}, u32[]{:S(2)}) copy-start(bf16[64,640]{1,0:T(8,128)(2,1)S(1)} %collective-permute-done.30.refs_9_) | copy-start | bytes 245764
  85.1 4.7 %collective-permute-start.38 = (bf16[64,640]{1,0:T(8,128)(2,1)S(1)}, bf16[64,640]{1,0:T(8,128)(2,1)S(1)}, u32[]{:S(2)}, u32[]{:S(2)}) collective-permute-start(bf16[64,640]{1,0:T(8,128)(2,1)S(1)} %collective-permute-done.30.refs_9_), channel_id=1, source_target_pairs={{0,1},{1,0},{2,3},{3,2},{4,5},{5,4},{6,7},{7,6},{8,9},{9,8},{10,11... | collective-permute-start | bytes 245768 | tf_op jit(solution)/shard_map/ppermute | solution.py:174
  85.1 10.5 %copy-start.10 = (bf16[64,640]{1,0:T(8,128)(2,1)}, bf16[64,640]{1,0:T(8,128)(2,1)S(1)}, u32[]{:S(2)}) copy-start(bf16[64,640]{1,0:T(8,128)(2,1)S(1)} %collective-permute-done.32.refs_11_) | copy-start | bytes 245764
  85.1 4.9 %collective-permute-start.31 = (bf16[64,640]{1,0:T(8,128)(2,1)S(1)}, bf16[64,640]{1,0:T(8,128)(2,1)S(1)}, u32[]{:S(2)}, u32[]{:S(2)}) collective-permute-start(bf16[64,640]{1,0:T(8,128)(2,1)S(1)} %collective-permute-done.30.refs_9_), channel_id=1, source_target_pairs={{0,2},{1,3},{2,0},{3,1},{4,6},{5,7},{6,4},{7,5},{8,10},{9,11},{10,... | collective-permute-start | bytes 245768 | tf_op jit(solution)/shard_map/ppermute | solution.py:174
  87.6 8.0 %copy-start.11 = (bf16[64,640]{1,0:T(8,128)(2,1)}, bf16[64,640]{1,0:T(8,128)(2,1)S(1)}, u32[]{:S(2)}) copy-start(bf16[64,640]{1,0:T(8,128)(2,1)S(1)} %collective-permute-done.28.refs_7_) | copy-start | bytes 245764
  87.6 2.7 %collective-permute-start.36 = (bf16[64,640]{1,0:T(8,128)(2,1)S(1)}, bf16[64,640]{1,0:T(8,128)(2,1)S(1)}, u32[]{:S(2)}, u32[]{:S(2)}) collective-permute-start(bf16[64,640]{1,0:T(8,128)(2,1)S(1)} %collective-permute-done.28.refs_7_), channel_id=1, source_target_pairs={{0,1},{1,0},{2,3},{3,2},{4,5},{5,4},{6,7},{7,6},{8,9},{9,8},{10,11... | collective-permute-start | bytes 245768 | tf_op jit(solution)/shard_map/ppermute | solution.py:174
  87.8 7.9 %copy-start.13 = (bf16[64,640]{1,0:T(8,128)(2,1)}, bf16[64,640]{1,0:T(8,128)(2,1)S(1)}, u32[]{:S(2)}) copy-start(bf16[64,640]{1,0:T(8,128)(2,1)S(1)} %collective-permute-done.26.refs_5_) | copy-start | bytes 245764
  87.8 5.3 %collective-permute-start.29 = (bf16[64,640]{1,0:T(8,128)(2,1)S(1)}, bf16[64,640]{1,0:T(8,128)(2,1)S(1)}, u32[]{:S(2)}, u32[]{:S(2)}) collective-permute-start(bf16[64,640]{1,0:T(8,128)(2,1)S(1)} %collective-permute-done.28.refs_7_), channel_id=1, source_target_pairs={{0,2},{1,3},{2,0},{3,1},{4,6},{5,7},{6,4},{7,5},{8,10},{9,11},{10,... | collective-permute-start | bytes 245768 | tf_op jit(solution)/shard_map/ppermute | solution.py:174
  88.7 7.0 %copy-start.14 = (bf16[64,640]{1,0:T(8,128)(2,1)}, bf16[64,640]{1,0:T(8,128)(2,1)S(1)}, u32[]{:S(2)}) copy-start(bf16[64,640]{1,0:T(8,128)(2,1)S(1)} %collective-permute-done.25.refs_4_) | copy-start | bytes 245764
  88.7 5.6 %collective-permute-start.27 = (bf16[64,640]{1,0:T(8,128)(2,1)S(1)}, bf16[64,640]{1,0:T(8,128)(2,1)S(1)}, u32[]{:S(2)}, u32[]{:S(2)}) collective-permute-start(bf16[64,640]{1,0:T(8,128)(2,1)S(1)} %collective-permute-done.26.refs_5_), channel_id=1, source_target_pairs={{0,2},{1,3},{2,0},{3,1},{4,6},{5,7},{6,4},{7,5},{8,10},{9,11},{10,... | collective-permute-start | bytes 245768 | tf_op jit(solution)/shard_map/ppermute | solution.py:174
  89.8 4.4 %collective-permute-start.34 = (bf16[64,640]{1,0:T(8,128)(2,1)S(1)}, bf16[64,640]{1,0:T(8,128)(2,1)S(1)}, u32[]{:S(2)}, u32[]{:S(2)}) collective-permute-start(bf16[64,640]{1,0:T(8,128)(2,1)S(1)} %collective-permute-done.26.refs_5_), channel_id=1, source_target_pairs={{0,1},{1,0},{2,3},{3,2},{4,5},{5,4},{6,7},{7,6},{8,9},{9,8},{10,11... | collective-permute-start | bytes 245768 | tf_op jit(solution)/shard_map/ppermute | solution.py:174
  90.0 4.3 %collective-permute-start.33 = (bf16[64,640]{1,0:T(8,128)(2,1)S(1)}, bf16[64,640]{1,0:T(8,128)(2,1)S(1)}, u32[]{:S(2)}, u32[]{:S(2)}) collective-permute-start(bf16[64,640]{1,0:T(8,128)(2,1)S(1)} %collective-permute-done.25.refs_4_), channel_id=1, source_target_pairs={{0,1},{1,0},{2,3},{3,2},{4,5},{5,4},{6,7},{7,6},{8,9},{9,8},{10,11... | collective-permute-start | bytes 245768 | tf_op jit(solution)/shard_map/ppermute | solution.py:174
  90.4 3.9 %collective-permute-start.39 = (bf16[64,640]{1,0:T(8,128)(2,1)S(1)}, bf16[64,640]{1,0:T(8,128)(2,1)S(1)}, u32[]{:S(2)}, u32[]{:S(2)}) collective-permute-start(bf16[64,640]{1,0:T(8,128)(2,1)S(1)} %collective-permute-done.31.refs_10_), channel_id=1, source_target_pairs={{0,1},{1,0},{2,3},{3,2},{4,5},{5,4},{6,7},{7,6},{8,9},{9,8},{10,11... | collective-permute-start | bytes 245768 | tf_op jit(solution)/shard_map/ppermute | solution.py:174
  93.1 1.3 collective-permute-start.37
  94.2 1.4 collective-permute-start.35
  104.5 10.8 %collective-permute-start.40 = (bf16[320,320]{1,0:T(8,128)(2,1)}, bf16[320,320]{1,0:T(8,128)(2,1)S(1)}, u32[]{:S(2)}, u32[]{:S(2)}) collective-permute-start(bf16[320,320]{1,0:T(8,128)(2,1)} %get-tuple-element.25.sent_hbm), channel_id=1, source_target_pairs={{0,1},{1,0},{2,3},{3,2},{4,5},{5,4},{6,7},{7,6},{8,9},{9,8},{10,11... | collective-permute-start | bytes 614408 | tf_op jit(solution)/shard_map/ppermute | solution.py:174
  119.1 7.4 %collective-permute-start.46 = (bf16[64,640]{1,0:T(8,128)(2,1)}, bf16[64,640]{1,0:T(8,128)(2,1)S(1)}, u32[]{:S(2)}, u32[]{:S(2)}) collective-permute-start(bf16[64,640]{1,0:T(8,128)(2,1)} %attend.3.refs_0_), channel_id=1, source_target_pairs={{0,12},{1,13},{2,14},{3,15},{4,8},{5,9},{6,10},{7,11},{8,4},{9,5},... | collective-permute-start | bytes 245768 | tf_op jit(solution)/shard_map/ppermute | solution.py:174
  119.7 9.3 %collective-permute-start.44 = (bf16[64,640]{1,0:T(8,128)(2,1)}, bf16[64,640]{1,0:T(8,128)(2,1)S(1)}, u32[]{:S(2)}, u32[]{:S(2)}) collective-permute-start(bf16[64,640]{1,0:T(8,128)(2,1)} %attend.3.refs_0_), channel_id=1, source_target_pairs={{0,8},{1,9},{2,10},{3,11},{4,12},{5,13},{6,14},{7,15},{8,0},{9,1},... | collective-permute-start | bytes 245768 | tf_op jit(solution)/shard_map/ppermute | solution.py:174
  121.1 8.5 %collective-permute-start.42 = (bf16[64,640]{1,0:T(8,128)(2,1)}, bf16[64,640]{1,0:T(8,128)(2,1)S(1)}, u32[]{:S(2)}, u32[]{:S(2)}) collective-permute-start(bf16[64,640]{1,0:T(8,128)(2,1)} %attend.3.refs_0_), channel_id=1, source_target_pairs={{0,4},{1,5},{2,6},{3,7},{4,0},{5,1},{6,2},{7,3},{8,12},{9,13},{10,... | collective-permute-start | bytes 245768 | tf_op jit(solution)/shard_map/ppermute | solution.py:174
  123.6 7.5 %collective-permute-start.41 = (bf16[64,640]{1,0:T(8,128)(2,1)}, bf16[64,640]{1,0:T(8,128)(2,1)S(1)}, u32[]{:S(2)}, u32[]{:S(2)}) collective-permute-start(bf16[64,640]{1,0:T(8,128)(2,1)} %attend.3.refs_0_), channel_id=1, source_target_pairs={{0,2},{1,3},{2,0},{3,1},{4,6},{5,7},{6,4},{7,5},{8,10},{9,11},{10,... | collective-permute-start | bytes 245768 | tf_op jit(solution)/shard_map/ppermute | solution.py:174
  126.6 8.2 %copy-start.28 = (bf16[64,640]{1,0:T(8,128)(2,1)}, bf16[64,640]{1,0:T(8,128)(2,1)S(1)}, u32[]{:S(2)}) copy-start(bf16[64,640]{1,0:T(8,128)(2,1)S(1)} %collective-permute-done.46.refs_6_) | copy-start | bytes 245764
  126.6 4.5 %collective-permute-start.47 = (bf16[64,640]{1,0:T(8,128)(2,1)S(1)}, bf16[64,640]{1,0:T(8,128)(2,1)S(1)}, u32[]{:S(2)}, u32[]{:S(2)}) collective-permute-start(bf16[64,640]{1,0:T(8,128)(2,1)S(1)} %collective-permute-done.46.refs_6_), channel_id=1, source_target_pairs={{0,2},{1,3},{2,0},{3,1},{4,6},{5,7},{6,4},{7,5},{8,10},{9,11},{10,... | collective-permute-start | bytes 245768 | tf_op jit(solution)/shard_map/ppermute | solution.py:174
  129.0 4.8 %collective-permute-start.45 = (bf16[64,640]{1,0:T(8,128)(2,1)S(1)}, bf16[64,640]{1,0:T(8,128)(2,1)S(1)}, u32[]{:S(2)}, u32[]{:S(2)}) collective-permute-start(bf16[64,640]{1,0:T(8,128)(2,1)S(1)} %collective-permute-done.44.refs_4_), channel_id=1, source_target_pairs={{0,2},{1,3},{2,0},{3,1},{4,6},{5,7},{6,4},{7,5},{8,10},{9,11},{10,... | collective-permute-start | bytes 245768 | tf_op jit(solution)/shard_map/ppermute | solution.py:174
  129.6 5.1 %collective-permute-start.43 = (bf16[64,640]{1,0:T(8,128)(2,1)S(1)}, bf16[64,640]{1,0:T(8,128)(2,1)S(1)}, u32[]{:S(2)}, u32[]{:S(2)}) collective-permute-start(bf16[64,640]{1,0:T(8,128)(2,1)S(1)} %collective-permute-done.42.refs_2_), channel_id=1, source_target_pairs={{0,2},{1,3},{2,0},{3,1},{4,6},{5,7},{6,4},{7,5},{8,10},{9,11},{10,... | collective-permute-start | bytes 245768 | tf_op jit(solution)/shard_map/ppermute | solution.py:174
  (32 other events, 79.5 us)

commit v7 on v6

--- a/solution.py
+++ b/solution.py
@@ -193,6 +193,8 @@
 HBM_SPEC = pl.BlockSpec(memory_space=pltpu.HBM)
 VMEM_SPEC = pl.BlockSpec(memory_space=pltpu.VMEM)
 PARAMS = pltpu.CompilerParams(vmem_limit_bytes=60 * 1024 * 1024)
+MIDDLE_PARAMS = pltpu.CompilerParams(vmem_limit_bytes=52 * 1024 * 1024)
+SMALL_PARAMS = pltpu.CompilerParams(vmem_limit_bytes=16 * 1024 * 1024)
 
 
 def span_at(position, step, spans):
@@ -228,7 +230,9 @@
     refs = refs[3:]
     if step == 0:
         current_hbm, refs = refs[0], refs[1:]
-    state, modulated, table, entering, gain, scale_ref, shift_ref, weights, own, send, current, sems = refs
+    state, modulated, table, entering, gain, scale_ref, shift_ref, own, send, current, sems = refs[:11]
+    fetched = step == 0
+    weights = refs[11] if fetched else weight_refs
     chip, core = own_place()
     tokens, width = modulated.shape
     half = tokens // 2
@@ -249,9 +253,11 @@
                 target = state.at[pl.ds(pl.multiple_of(owner * half, half), half), lanes]
             pairs.append((blocks[mask], target))
     pairs += [(table_hbm, table), (gain_hbm.at[:, own_lanes], gain), (incoming_hbm, entering)]
-    pairs += [(weight_refs[i], weights.at[i]) for i in range(3)]
+    inputs = len(pairs)
+    if fetched:
+        pairs += [(weight_refs[i], weights.at[i]) for i in range(3)]
     copies = started(pairs, sems)
-    copies, fetches = copies[:-3], copies[-3:]
+    copies, fetches = copies[:inputs], copies[inputs:]
     finished(copies)
     shift_ref[...] = table[0].astype(jnp.float32)
     scale_ref[...] = table[1].astype(jnp.float32) + 1.0
@@ -298,7 +304,7 @@
     products = []
     for fetch, weight in ((fetches[:1], 0), (fetches[1:], 1), ([], 2)):
         finished(fetch)
-        products.append(contract_last(modulated[...], weights[weight]))
+        products.append(contract_last(modulated[...], weights[weight][...]))
     shape = (tokens, tokens)
     ident = lax.broadcasted_iota(jnp.int32, shape, 0) == lax.broadcasted_iota(jnp.int32, shape, 1)
     for i in range(2):
@@ -334,7 +340,9 @@
     return pl.pallas_call(
         functools.partial(project_kernel, step, spans),
         out_shape=out_shape,
-        in_specs=[HBM_SPEC] * (6 + 2 * len(mine)),
+        in_specs=[HBM_SPEC] * 3
+        + [HBM_SPEC if step == 0 else VMEM_SPEC] * 3
+        + [HBM_SPEC] * (2 * len(mine)),
         out_specs=[HBM_SPEC, HBM_SPEC, VMEM_SPEC, HBM_SPEC][: len(out_shape)],
         scratch_shapes=[
             pltpu.VMEM(state, jnp.bfloat16),
@@ -344,13 +352,13 @@
             pltpu.VMEM((2, 2 * cols), jnp.float32),
             pltpu.VMEM((spans, width), jnp.float32),
             pltpu.VMEM((spans, width), jnp.float32),
-            pltpu.VMEM((3, cols, width), jnp.bfloat16),
             pltpu.VMEM((half, cols), jnp.bfloat16),
             pltpu.VMEM((half + 2 * tokens, cols), jnp.bfloat16),
             pltpu.VMEM((half, 2 * cols), jnp.bfloat16),
             pltpu.SemaphoreType.DMA((spans + 6,)),
-        ],
-        compiler_params=PARAMS,
+        ]
+        + ([pltpu.VMEM((3, cols, width), jnp.bfloat16)] if step == 0 else []),
+        compiler_params=PARAMS if step == 0 else SMALL_PARAMS,
         name="project",
     )(gain, table, incoming, *weights, *mine, *others)
 
@@ -533,27 +541,9 @@
             pltpu.VMEM((chips, 2, width // 2, width), jnp.bfloat16),
             pltpu.SemaphoreType.DMA((3 * chips + 3,)),
         ],
-        compiler_params=PARAMS,
+        compiler_params=PARAMS if last else MIDDLE_PARAMS,
         name="output",
     )(current, table, incoming, own, other, *blocks)
-
-
-def join_kernel(in_ref, out_ref):
-    chips, _, width = in_ref.shape
-    for source in range(chips):
-        out_ref[:, source * width : (source + 1) * width] = in_ref[source]
-
-
-def join(blocks):
-    chips, rows, width = blocks.shape
-    return pl.pallas_call(
-        join_kernel,
-        out_shape=jax.ShapeDtypeStruct((rows, width * chips), jnp.bfloat16),
-        in_specs=[VMEM_SPEC],
-        out_specs=VMEM_SPEC,
-        compiler_params=PARAMS,
-        name="join",
-    )(blocks)
 
 
 def arrange_kernel(spans, keys_ref, values_ref, out_ref):

time: 152 us -> 151 us (level)
  local copies, waits for them, and re-layouts: 4.14 us -> 8.48 us
  Pallas kernels: 36 us -> 32.2 us
    unnamed x95 -> x73, local copies, waits for them, and re-layouts: 4.14 us -> 8.48 us
    pallas_call x2, Pallas kernels: 17.5 us -> 14.1 us  [project(): pl.pallas_call(functools.partial(project_kernel, step, spans), out_shape=...]
  transfers between devices with their start and end apart: 49 -> 49, of which waited for: 23 -> 24; matrix products, arithmetic and copies ran while one was open for 2% -> 2% of each run, Pallas kernels for 9% -> 9%
where the time goes in v7:
time: 151 us
  starting transfers between devices  42.1 us (28%)
  waiting for transfers between devices  32.8 us (22%)
  Pallas kernels  32.2 us (21%)
  blocking collectives  31.4 us (21%)
  local copies, waits for them, and re-layouts  8.48 us (6%)
  matrix products  2 us (1%)
    ppermute x48, starting transfers between devices, swapped(): lax.ppermute(value, 'queue', [(source, source ^ bit) for source in range(...  37.4 us
    ppermute x48, waiting for transfers between devices, swapped(): lax.ppermute(value, 'queue', [(source, source ^ bit) for source in range(...  29.3 us
    all_to_all x2, blocking collectives, paired_device(): lax.all_to_all(squares, 'queue', split_axis=0, concat_axis=0, tiled=True)  21.1 us
    pallas_call x2, Pallas kernels, project(): pl.pallas_call(functools.partial(project_kernel, step, spans), out_shape=...  14.1 us
    all_to_all x1, blocking collectives, paired_device(): lax.all_to_all(result, 'queue', split_axis=0, concat_axis=2, tiled=True,...  10.3 us
    pallas_call x2, Pallas kernels, output(): pl.pallas_call(functools.partial(output_kernel, step, spans, last), out_s...  9.8 us
    unnamed x73, local copies, waits for them, and re-layouts  8.48 us
    pallas_call x2, Pallas kernels, attend(): pl.pallas_call(functools.partial(attend_kernel, step, spans, head_size),...  6.27 us
  transfers between devices with their start and end apart: 49, of which 24 were waited for; matrix products, arithmetic and copies ran while one was open for 2% of the time, Pallas kernels for 9%

profile of v7, /device:TPU:0, one launch (start us, length us, event | category | flops | bytes accessed | tf_op | source)
XLA Modules:
  0.0 150.7 jit_solution(8300836310076871233)
XLA Ops:
  0.0 0.5 collective-permute-start.15
  0.5 4.7 %collective-permute-start.5 = (bf16[8,5120]{1,0:T(8,128)(2,1)}, bf16[8,5120]{1,0:T(8,128)(2,1)S(1)}, u32[]{:S(2)}, u32[]{:S(2)}) collective-permute-start(bf16[8,5120]{1,0:T(8,128)(2,1)} %refs_3_.1), channel_id=1, source_target_pairs={{0,12},{1,13},{2,14},{3,15},{4,8},{5,9},{6,10},{7,11},{8,4},{9,5},... | collective-permute-start | bytes 245768 | tf_op jit(solution)/shard_map/ppermute | solution.py:174
  5.1 0.7 collective-permute-start.1
  5.8 1.6 %collective-permute-start = (bf16[8,5120]{1,0:T(8,128)(2,1)}, bf16[8,5120]{1,0:T(8,128)(2,1)S(1)}, u32[]{:S(2)}, u32[]{:S(2)}) collective-permute-start(bf16[8,5120]{1,0:T(8,128)(2,1)} %refs_3_.1), channel_id=1, source_target_pairs={{0,2},{1,3},{2,0},{3,1},{4,6},{5,7},{6,4},{7,5},{8,10},{9,11},{10,... | collective-permute-start | bytes 245768 | tf_op jit(solution)/shard_map/ppermute | solution.py:174
  7.4 1.4 pad_maximum_fusion.gain_hbm
  8.8 1.6 %collective-permute-start.6 = (bf16[8,5120]{1,0:T(8,128)(2,1)S(1)}, bf16[8,5120]{1,0:T(8,128)(2,1)S(1)}, u32[]{:S(2)}, u32[]{:S(2)}) collective-permute-start(bf16[8,5120]{1,0:T(8,128)(2,1)S(1)} %collective-permute-done.5.refs_9_), channel_id=1, source_target_pairs={{0,2},{1,3},{2,0},{3,1},{4,6},{5,7},{6,4},{7,5},{8,10},{9,11},{10,... | collective-permute-start | bytes 245768 | tf_op jit(solution)/shard_map/ppermute | solution.py:174
  10.4 2.4 %collective-permute-done.3.refs_7_ = bf16[8,5120]{1,0:T(8,128)(2,1)S(1)} collective-permute-done((bf16[8,5120]{1,0:T(8,128)(2,1)}, bf16[8,5120]{1,0:T(8,128)(2,1)S(1)}, u32[]{:S(2)}, u32[]{:S(2)}) %collective-permute-start.3) | collective-permute-done | bytes 81952 | tf_op jit(solution)/shard_map/ppermute | solution.py:174
  12.8 1.5 %collective-permute-start.4 = (bf16[8,5120]{1,0:T(8,128)(2,1)S(1)}, bf16[8,5120]{1,0:T(8,128)(2,1)S(1)}, u32[]{:S(2)}, u32[]{:S(2)}) collective-permute-start(bf16[8,5120]{1,0:T(8,128)(2,1)S(1)} %collective-permute-done.3.refs_7_), channel_id=1, source_target_pairs={{0,2},{1,3},{2,0},{3,1},{4,6},{5,7},{6,4},{7,5},{8,10},{9,11},{10,... | collective-permute-start | bytes 245768 | tf_op jit(solution)/shard_map/ppermute | solution.py:174
  14.3 0.5 collective-permute-start.2
  14.9 2.0 %fusion.table_hbm = bf16[3,16,5120]{2,1,0:T(8,128)(2,1)} fusion(bf16[96,3,5120]{2,0,1:T(8,128)(2,1)S(1)} %copy-done, s32[16]{0:T(128)} %param.14), kind=kOutput, calls=%fused_computation.1 | convolution fusion | flops 47433216 | bytes 3440704 | tf_op jit(solution)/shard_map/sl,ltd->tsd/dot_general | solution.py:593
  16.9 2.0 %arrange.1 = bf16[16,2,16,640]{3,2,1,0:T(8,128)(2,1)} custom-call(bf16[32,5120]{1,0:T(8,128)(2,1)} %keys_ref.1, bf16[32,5120]{1,0:T(8,128)(2,1)} %values_ref.1), custom_call_target="tpu_custom_call" | custom-call | tf_op jit(solution)/shard_map/arrange/pallas_call | solution.py:561
  19.1 4.7 %all-to-all-start.1 = ((bf16[16,2,16,640]{3,2,1,0:T(8,128)(2,1)}), bf16[16,2,16,640]{3,2,1,0:T(8,128)(2,1)}, u32[]{:S(2)}, u32[]{:S(2)}) async-start(bf16[16,2,16,640]{3,2,1,0:T(8,128)(2,1)} %arrange.1), calls=%async_computation.1 | async-start | bytes 1310720 | tf_op jit(solution)/shard_map/all_to_all | solution.py:601
  26.9 0.6 collective-permute-done.10.refs_14_
  27.6 0.5 copy-done.33
  28.1 8.8 %project.2 = (bf16[64,320]{1,0:T(8,128)(2,1)}, bf16[320,320]{1,0:T(8,128)(2,1)}, f32[16,2,128]{2,1,0:T(2,128)}, bf16[64,640]{1,0:T(8,128)(2,1)}) custom-call(f32[2,5120]{1,0:T(2,128)} %pad_maximum_fusion.gain_hbm, bf16[3,16,5120]{2,1,0:T(8,128)(2,1)} %fusion.table_hbm, bf16[2,8,5120]{2,1,0:T(8,128)(2,1)} %incoming_hbm.7, bf16[320,5120]{1,0:T(8,128)(2,1)} %bitcast.17, ...), custom_call_target="tpu_custom_call" | custom-call | tf_op jit(solution)/shard_map/project/pallas_call | solution.py:340
  36.9 3.5 %all-to-all-done.1.text_hbm = bf16[16,2,16,640]{3,2,1,0:T(8,128)(2,1)} async-done(((bf16[16,2,16,640]{3,2,1,0:T(8,128)(2,1)}), bf16[16,2,16,640]{3,2,1,0:T(8,128)(2,1)}, u32[]{:S(2)}, u32[]{:S(2)}) %all-to-all-start.1) | async-done | bytes 655392 | tf_op jit(solution)/shard_map/all_to_all | solution.py:601
  41.0 11.4 %all_to_all.30.squares_hbm = f32[16,2,128]{2,1,0:T(2,128)} all-to-all(f32[16,2,128]{2,1,0:T(2,128)} %get-tuple-element.21), channel_id=1, replica_groups=mesh['groups'=2,'queue'=16] {'queue'}, dimensions={0} | all-to-all | bytes 32768 | tf_op jit(solution)/shard_map/all_to_all | solution.py:609
  52.3 0.7 copy-done.12
  53.0 3.1 %attend.2.refs_0_ = bf16[64,640]{1,0:T(8,128)(2,1)} custom-call(bf16[64,320]{1,0:T(8,128)(2,1)} %get-tuple-element.19.own_hbm, bf16[320,320]{1,0:T(8,128)(2,1)} %get-tuple-element.20.sent_hbm, bf16[320,320]{1,0:T(8,128)(2,1)} %copy-done.12, f32[16,2,128]{2,1,0:T(2,128)} %all_to_all.30.squares_hbm, bf16[16,2,16,640]{3,2,1,0:T(8,128)(2,1)} %all-to-all-done.1.text_hbm, ...), custom_call_target="tpu_custom_call" | custom-call | tf_op jit(solution)/shard_map/attend/pallas_call | solution.py:449
  56.2 0.6 collective-permute-start.23
  56.7 1.4 collective-permute-start.21
  58.1 2.5 %collective-permute-start.19 = (bf16[64,640]{1,0:T(8,128)(2,1)}, bf16[64,640]{1,0:T(8,128)(2,1)S(1)}, u32[]{:S(2)}, u32[]{:S(2)}) collective-permute-start(bf16[64,640]{1,0:T(8,128)(2,1)} %attend.2.refs_0_), channel_id=1, source_target_pairs={{0,4},{1,5},{2,6},{3,7},{4,0},{5,1},{6,2},{7,3},{8,12},{9,13},{10,... | collective-permute-start | bytes 245768 | tf_op jit(solution)/shard_map/ppermute | solution.py:174
  61.1 2.5 %collective-permute-done.23.refs_6_ = bf16[64,640]{1,0:T(8,128)(2,1)S(1)} collective-permute-done((bf16[64,640]{1,0:T(8,128)(2,1)}, bf16[64,640]{1,0:T(8,128)(2,1)S(1)}, u32[]{:S(2)}, u32[]{:S(2)}) %collective-permute-start.23) | collective-permute-done | bytes 81952 | tf_op jit(solution)/shard_map/ppermute | solution.py:174
  63.6 0.5 collective-permute-start.24
  64.1 2.0 %collective-permute-done.21.refs_4_ = bf16[64,640]{1,0:T(8,128)(2,1)S(1)} collective-permute-done((bf16[64,640]{1,0:T(8,128)(2,1)}, bf16[64,640]{1,0:T(8,128)(2,1)S(1)}, u32[]{:S(2)}, u32[]{:S(2)}) %collective-permute-start.21) | collective-permute-done | bytes 81952 | tf_op jit(solution)/shard_map/ppermute | solution.py:174
  66.1 0.6 collective-permute-start.22
  66.7 1.4 collective-permute-start.20
  68.1 2.8 %collective-permute-done.22.refs_5_ = bf16[64,640]{1,0:T(8,128)(2,1)S(1)} collective-permute-done((bf16[64,640]{1,0:T(8,128)(2,1)S(1)}, bf16[64,640]{1,0:T(8,128)(2,1)S(1)}, u32[]{:S(2)}, u32[]{:S(2)}) %collective-permute-start.22) | collective-permute-done | bytes 81952 | tf_op jit(solution)/shard_map/ppermute | solution.py:174
  70.9 0.9 collective-permute-done.20.refs_3_
  71.8 0.9 copy-done.5
  72.7 0.9 copy-done.8
  73.6 0.9 copy-done.10
  74.5 4.7 %output.2.refs_3_.current_hbm = bf16[64,640]{1,0:T(8,128)(2,1)S(1)} custom-call(bf16[64,640]{1,0:T(8,128)(2,1)S(1)} %copy-done.10, bf16[3,16,5120]{2,1,0:T(8,128)(2,1)S(1)} %copy-done.4, bf16[2,8,5120]{2,1,0:T(8,128)(2,1)S(1)} %copy-done.5, bf16[320,5120]{1,0:T(8,128)(2,1)} %bitcast.24, bf16[320,5120]{1,0:T(8,128)(2,1)} %collective-permute-done.15.other_hbm, ...), custom_call_target="tpu_custom_call" | custom-call | tf_op jit(solution)/shard_map/output/pallas_call | solution.py:528
  79.2 1.3 collective-permute-start.30
  80.5 3.1 %collective-permute-start.26 = (bf16[64,640]{1,0:T(8,128)(2,1)S(1)}, bf16[64,640]{1,0:T(8,128)(2,1)S(1)}, u32[]{:S(2)}, u32[]{:S(2)}) collective-permute-start(bf16[64,640]{1,0:T(8,128)(2,1)S(1)} %output.2.refs_3_.current_hbm), channel_id=1, source_target_pairs={{0,4},{1,5},{2,6},{3,7},{4,0},{5,1},{6,2},{7,3},{8,12},{9,13},{10,... | collective-permute-start | bytes 245768 | tf_op jit(solution)/shard_map/ppermute | solution.py:174
  83.6 0.9 collective-permute-start.25
  84.5 1.9 %collective-permute-done.30.refs_9_ = bf16[64,640]{1,0:T(8,128)(2,1)S(1)} collective-permute-done((bf16[64,640]{1,0:T(8,128)(2,1)S(1)}, bf16[64,640]{1,0:T(8,128)(2,1)S(1)}, u32[]{:S(2)}, u32[]{:S(2)}) %collective-permute-start.30) | collective-permute-done | bytes 81952 | tf_op jit(solution)/shard_map/ppermute | solution.py:174
  86.4 0.9 collective-permute-start.31
  87.2 1.6 %collective-permute-done.28.refs_7_ = bf16[64,640]{1,0:T(8,128)(2,1)S(1)} collective-permute-done((bf16[64,640]{1,0:T(8,128)(2,1)S(1)}, bf16[64,640]{1,0:T(8,128)(2,1)S(1)}, u32[]{:S(2)}, u32[]{:S(2)}) %collective-permute-start.28) | collective-permute-done | bytes 81952 | tf_op jit(solution)/shard_map/ppermute | solution.py:174
  89.0 0.9 collective-permute-start.29
  89.9 1.1 collective-permute-start.27
  91.8 2.5 %collective-permute-done.29.refs_8_ = bf16[64,640]{1,0:T(8,128)(2,1)S(1)} collective-permute-done((bf16[64,640]{1,0:T(8,128)(2,1)S(1)}, bf16[64,640]{1,0:T(8,128)(2,1)S(1)}, u32[]{:S(2)}, u32[]{:S(2)}) %collective-permute-start.29) | collective-permute-done | bytes 81952 | tf_op jit(solution)/shard_map/ppermute | solution.py:174
  94.3 1.2 collective-permute-done.27.refs_6_
  95.6 1.2 collective-permute-done.35.refs_14_
  96.8 1.9 %copy-done.3 = bf16[5120,320]{0,1:T(8,128)(2,1)S(1)} copy-done((bf16[5120,320]{0,1:T(8,128)(2,1)S(1)}, bf16[5120,320]{0,1:T(8,128)(2,1)}, u32[]{:S(2)}) %copy-start.3) | copy-done | bytes 3276824
  98.7 5.3 %project.3 = (bf16[64,320]{1,0:T(8,128)(2,1)S(1)}, bf16[320,320]{1,0:T(8,128)(2,1)S(1)}, f32[16,2,128]{2,1,0:T(2,128)S(1)}) custom-call(f32[2,5120]{1,0:T(2,128)S(1)} %copy-done.7, bf16[3,16,5120]{2,1,0:T(8,128)(2,1)S(1)} %copy-done.4, bf16[2,8,5120]{2,1,0:T(8,128)(2,1)S(1)} %copy-done.5, bf16[320,5120]{1,0:T(8,128)(2,1)S(1)} %bitcast.18, ...), custom_call_target="tpu_custom_call" | custom-call | tf_op jit(solution)/shard_map/project/pallas_call | solution.py:340
  104.1 0.6 copy-done.11
  104.8 9.8 %all_to_all.31.squares_hbm = f32[16,2,128]{2,1,0:T(2,128)} all-to-all(f32[16,2,128]{2,1,0:T(2,128)S(1)} %get-tuple-element.26), channel_id=1, replica_groups=mesh['groups'=2,'queue'=16] {'queue'}, dimensions={0} | all-to-all | bytes 32768 | tf_op jit(solution)/shard_map/all_to_all | solution.py:609
  114.6 0.7 copy-done.13
  115.3 3.1 %attend.3.refs_0_ = bf16[64,640]{1,0:T(8,128)(2,1)} custom-call(bf16[64,320]{1,0:T(8,128)(2,1)} %copy-done.11, bf16[320,320]{1,0:T(8,128)(2,1)} %copy-done.9, bf16[320,320]{1,0:T(8,128)(2,1)} %copy-done.13, f32[16,2,128]{2,1,0:T(2,128)} %all_to_all.31.squares_hbm, bf16[16,2,16,640]{3,2,1,0:T(8,128)(2,1)} %all-to-all-done.1.text_hbm, ...), custom_call_target="tpu_custom_call" | custom-call | tf_op jit(solution)/shard_map/attend/pallas_call | solution.py:449
  118.4 0.6 collective-permute-start.46
  119.0 1.4 collective-permute-start.44
  120.4 2.5 %collective-permute-start.42 = (bf16[64,640]{1,0:T(8,128)(2,1)}, bf16[64,640]{1,0:T(8,128)(2,1)S(1)}, u32[]{:S(2)}, u32[]{:S(2)}) collective-permute-start(bf16[64,640]{1,0:T(8,128)(2,1)} %attend.3.refs_0_), channel_id=1, source_target_pairs={{0,4},{1,5},{2,6},{3,7},{4,0},{5,1},{6,2},{7,3},{8,12},{9,13},{10,... | collective-permute-start | bytes 245768 | tf_op jit(solution)/shard_map/ppermute | solution.py:174
  123.3 2.5 %collective-permute-done.46.refs_6_ = bf16[64,640]{1,0:T(8,128)(2,1)S(1)} collective-permute-done((bf16[64,640]{1,0:T(8,128)(2,1)}, bf16[64,640]{1,0:T(8,128)(2,1)S(1)}, u32[]{:S(2)}, u32[]{:S(2)}) %collective-permute-start.46) | collective-permute-done | bytes 81952 | tf_op jit(solution)/shard_map/ppermute | solution.py:174
  125.8 0.5 collective-permute-start.47
  126.3 2.0 %collective-permute-done.44.refs_4_ = bf16[64,640]{1,0:T(8,128)(2,1)S(1)} collective-permute-done((bf16[64,640]{1,0:T(8,128)(2,1)}, bf16[64,640]{1,0:T(8,128)(2,1)S(1)}, u32[]{:S(2)}, u32[]{:S(2)}) %collective-permute-start.44) | collective-permute-done | bytes 81952 | tf_op jit(solution)/shard_map/ppermute | solution.py:174
  128.3 0.6 collective-permute-start.45
  128.9 1.5 collective-permute-start.43
  130.4 2.7 %collective-permute-done.45.refs_5_ = bf16[64,640]{1,0:T(8,128)(2,1)S(1)} collective-permute-done((bf16[64,640]{1,0:T(8,128)(2,1)S(1)}, bf16[64,640]{1,0:T(8,128)(2,1)S(1)}, u32[]{:S(2)}, u32[]{:S(2)}) %collective-permute-start.45) | collective-permute-done | bytes 81952 | tf_op jit(solution)/shard_map/ppermute | solution.py:174
  133.1 0.9 collective-permute-done.43.refs_3_
  134.0 0.6 copy-done.35
  134.7 5.1 %output.3 = bf16[8,8,640]{2,1,0:T(8,128)(2,1)} custom-call(bf16[64,640]{1,0:T(8,128)(2,1)} %copy-done.6, bf16[3,16,5120]{2,1,0:T(8,128)(2,1)} %fusion.table_hbm, bf16[2,8,5120]{2,1,0:T(8,128)(2,1)} %incoming_hbm.7, bf16[320,5120]{1,0:T(8,128)(2,1)} %bitcast.25, bf16[320,5120]{1,0:T(8,128)(2,1)} %collective-permute-done.15.other_hbm, ...), custom_call_target="tpu_custom_call" | custom-call | tf_op jit(solution)/shard_map/output/pallas_call | solution.py:528
  139.8 10.3 %all_to_all.32 = bf16[8,8,640]{2,1,0:T(8,128)(2,1)S(1)} all-to-all(bf16[8,8,640]{2,1,0:T(8,128)(2,1)} %output.3), channel_id=1, replica_groups={{0,2,4,6,8,10,12,14},{1,3,5,7,9,11,13,15},{16,18,20,22,24,26,28,30},{17..., dimensions={0} | all-to-all | bytes 163840 | tf_op jit(solution)/shard_map/all_to_all | solution.py:624
  150.1 0.6 copy.14
  (119 shorter events, 6.0 us)
Async XLA Ops:
  0.0 14.9 %copy-start = (bf16[96,3,5120]{2,0,1:T(8,128)(2,1)S(1)}, bf16[96,3,5120]{2,0,1:T(8,128)(2,1)}, u32[]{:S(2)}) copy-start(bf16[96,3,5120]{2,0,1:T(8,128)(2,1)} %param.15) | copy-start | bytes 8847364
  0.0 23.8 %copy-start.14 = (bf16[8,5120]{1,0:T(8,128)(2,1)S(1)}, bf16[8,5120]{1,0:T(8,128)(2,1)}, u32[]{:S(2)}) copy-start(bf16[8,5120]{1,0:T(8,128)(2,1)} %refs_3_.1) | copy-start | bytes 245764
  0.0 71.7 %collective-permute-start.15 = (bf16[320,5120]{1,0:T(8,128)(2,1)}, bf16[320,5120]{1,0:T(8,128)(2,1)}, u32[]{:S(2)}, u32[]{:S(2)}) collective-permute-start(bf16[320,5120]{1,0:T(8,128)(2,1)} %bitcast.23), channel_id=1, source_target_pairs={{0,1},{1,0},{2,3},{3,2},{4,5},{5,4},{6,7},{7,6},{8,9},{9,8},{10,11... | collective-permute-start | bytes 9830408 | tf_op jit(solution)/shard_map/ppermute | solution.py:174
  0.5 8.4 %collective-permute-start.5 = (bf16[8,5120]{1,0:T(8,128)(2,1)}, bf16[8,5120]{1,0:T(8,128)(2,1)S(1)}, u32[]{:S(2)}, u32[]{:S(2)}) collective-permute-start(bf16[8,5120]{1,0:T(8,128)(2,1)} %refs_3_.1), channel_id=1, source_target_pairs={{0,12},{1,13},{2,14},{3,15},{4,8},{5,9},{6,10},{7,11},{8,4},{9,5},... | collective-permute-start | bytes 245768 | tf_op jit(solution)/shard_map/ppermute | solution.py:174
  5.1 7.7 %collective-permute-start.3 = (bf16[8,5120]{1,0:T(8,128)(2,1)}, bf16[8,5120]{1,0:T(8,128)(2,1)S(1)}, u32[]{:S(2)}, u32[]{:S(2)}) collective-permute-start(bf16[8,5120]{1,0:T(8,128)(2,1)} %refs_3_.1), channel_id=1, source_target_pairs={{0,8},{1,9},{2,10},{3,11},{4,12},{5,13},{6,14},{7,15},{8,0},{9,1},... | collective-permute-start | bytes 245768 | tf_op jit(solution)/shard_map/ppermute | solution.py:174
  5.1 9.2 %collective-permute-start.1 = (bf16[8,5120]{1,0:T(8,128)(2,1)}, bf16[8,5120]{1,0:T(8,128)(2,1)S(1)}, u32[]{:S(2)}, u32[]{:S(2)}) collective-permute-start(bf16[8,5120]{1,0:T(8,128)(2,1)} %refs_3_.1), channel_id=1, source_target_pairs={{0,4},{1,5},{2,6},{3,7},{4,0},{5,1},{6,2},{7,3},{8,12},{9,13},{10,... | collective-permute-start | bytes 245768 | tf_op jit(solution)/shard_map/ppermute | solution.py:174
  5.8 13.1 %collective-permute-start = (bf16[8,5120]{1,0:T(8,128)(2,1)}, bf16[8,5120]{1,0:T(8,128)(2,1)S(1)}, u32[]{:S(2)}, u32[]{:S(2)}) collective-permute-start(bf16[8,5120]{1,0:T(8,128)(2,1)} %refs_3_.1), channel_id=1, source_target_pairs={{0,2},{1,3},{2,0},{3,1},{4,6},{5,7},{6,4},{7,5},{8,10},{9,11},{10,... | collective-permute-start | bytes 245768 | tf_op jit(solution)/shard_map/ppermute | solution.py:174
  8.8 18.7 %copy-start.15 = (bf16[8,5120]{1,0:T(8,128)(2,1)}, bf16[8,5120]{1,0:T(8,128)(2,1)S(1)}, u32[]{:S(2)}) copy-start(bf16[8,5120]{1,0:T(8,128)(2,1)S(1)} %collective-permute-done.5.refs_9_) | copy-start | bytes 245764
  8.8 10.0 %collective-permute-start.6 = (bf16[8,5120]{1,0:T(8,128)(2,1)S(1)}, bf16[8,5120]{1,0:T(8,128)(2,1)S(1)}, u32[]{:S(2)}, u32[]{:S(2)}) collective-permute-start(bf16[8,5120]{1,0:T(8,128)(2,1)S(1)} %collective-permute-done.5.refs_9_), channel_id=1, source_target_pairs={{0,2},{1,3},{2,0},{3,1},{4,6},{5,7},{6,4},{7,5},{8,10},{9,11},{10,... | collective-permute-start | bytes 245768 | tf_op jit(solution)/shard_map/ppermute | solution.py:174
  12.8 14.7 %copy-start.16 = (bf16[8,5120]{1,0:T(8,128)(2,1)}, bf16[8,5120]{1,0:T(8,128)(2,1)S(1)}, u32[]{:S(2)}) copy-start(bf16[8,5120]{1,0:T(8,128)(2,1)S(1)} %collective-permute-done.3.refs_7_) | copy-start | bytes 245764
  12.8 6.1 %collective-permute-start.4 = (bf16[8,5120]{1,0:T(8,128)(2,1)S(1)}, bf16[8,5120]{1,0:T(8,128)(2,1)S(1)}, u32[]{:S(2)}, u32[]{:S(2)}) collective-permute-start(bf16[8,5120]{1,0:T(8,128)(2,1)S(1)} %collective-permute-done.3.refs_7_), channel_id=1, source_target_pairs={{0,2},{1,3},{2,0},{3,1},{4,6},{5,7},{6,4},{7,5},{8,10},{9,11},{10,... | collective-permute-start | bytes 245768 | tf_op jit(solution)/shard_map/ppermute | solution.py:174
  14.3 13.2 %copy-start.17 = (bf16[8,5120]{1,0:T(8,128)(2,1)}, bf16[8,5120]{1,0:T(8,128)(2,1)S(1)}, u32[]{:S(2)}) copy-start(bf16[8,5120]{1,0:T(8,128)(2,1)S(1)} %collective-permute-done.1.refs_5_) | copy-start | bytes 245764
  14.3 4.7 %collective-permute-start.2 = (bf16[8,5120]{1,0:T(8,128)(2,1)S(1)}, bf16[8,5120]{1,0:T(8,128)(2,1)}, u32[]{:S(2)}, u32[]{:S(2)}) collective-permute-start(bf16[8,5120]{1,0:T(8,128)(2,1)S(1)} %collective-permute-done.1.refs_5_), channel_id=1, source_target_pairs={{0,2},{1,3},{2,0},{3,1},{4,6},{5,7},{6,4},{7,5},{8,10},{9,11},{10,... | collective-permute-start | bytes 245768 | tf_op jit(solution)/shard_map/ppermute | solution.py:174
  18.9 8.7 %copy-start.18 = (bf16[8,5120]{1,0:T(8,128)(2,1)}, bf16[8,5120]{1,0:T(8,128)(2,1)S(1)}, u32[]{:S(2)}) copy-start(bf16[8,5120]{1,0:T(8,128)(2,1)S(1)} %collective-permute-done.refs_4_) | copy-start | bytes 245764
  18.9 8.7 %copy-start.19 = (bf16[8,5120]{1,0:T(8,128)(2,1)}, bf16[8,5120]{1,0:T(8,128)(2,1)S(1)}, u32[]{:S(2)}) copy-start(bf16[8,5120]{1,0:T(8,128)(2,1)S(1)} %collective-permute-done.6.refs_10_) | copy-start | bytes 245764
  18.9 8.7 %copy-start.20 = (bf16[8,5120]{1,0:T(8,128)(2,1)}, bf16[8,5120]{1,0:T(8,128)(2,1)S(1)}, u32[]{:S(2)}) copy-start(bf16[8,5120]{1,0:T(8,128)(2,1)S(1)} %collective-permute-done.4.refs_8_) | copy-start | bytes 245764
  19.1 21.4 %all-to-all-start.1 = ((bf16[16,2,16,640]{3,2,1,0:T(8,128)(2,1)}), bf16[16,2,16,640]{3,2,1,0:T(8,128)(2,1)}, u32[]{:S(2)}, u32[]{:S(2)}) async-start(bf16[16,2,16,640]{3,2,1,0:T(8,128)(2,1)} %arrange.1), calls=%async_computation.1 | async-start | bytes 1310720 | tf_op jit(solution)/shard_map/all_to_all | solution.py:601
  23.8 1.3 collective-permute-start.7
  24.2 1.3 collective-permute-start.13
  24.4 1.3 collective-permute-start.11
  24.7 1.3 collective-permute-start.9
  25.1 1.3 collective-permute-start.8
  25.5 1.3 collective-permute-start.14
  25.7 1.3 collective-permute-start.12
  26.0 1.5 collective-permute-start.10
  28.1 43.6 %copy-start.4 = (bf16[3,16,5120]{2,1,0:T(8,128)(2,1)S(1)}, bf16[3,16,5120]{2,1,0:T(8,128)(2,1)}, u32[]{:S(2)}) copy-start(bf16[3,16,5120]{2,1,0:T(8,128)(2,1)} %fusion.table_hbm) | copy-start | bytes 1474564
  40.4 11.9 %collective-permute-start.17 = (bf16[16,2,16,640]{3,2,1,0:T(8,128)(2,1)}, bf16[16,2,16,640]{3,2,1,0:T(8,128)(2,1)}, u32[]{:S(2)}, u32[]{:S(2)}) collective-permute-start(bf16[16,2,16,640]{3,2,1,0:T(8,128)(2,1)} %all-to-all-done.1.text_hbm), channel_id=1, source_target_pairs={{0,1},{1,0},{2,3},{3,2},{4,5},{5,4},{6,7},{7,6},{8,9},{9,8},{10,11... | collective-permute-start | bytes 1966088 | tf_op jit(solution)/shard_map/ppermute | solution.py:174
  40.5 11.8 %collective-permute-start.16 = (bf16[320,320]{1,0:T(8,128)(2,1)}, bf16[320,320]{1,0:T(8,128)(2,1)S(1)}, u32[]{:S(2)}, u32[]{:S(2)}) collective-permute-start(bf16[320,320]{1,0:T(8,128)(2,1)} %get-tuple-element.20.sent_hbm), channel_id=1, source_target_pairs={{0,1},{1,0},{2,3},{3,2},{4,5},{5,4},{6,7},{7,6},{8,9},{9,8},{10,11... | collective-permute-start | bytes 614408 | tf_op jit(solution)/shard_map/ppermute | solution.py:174
  56.2 7.4 %collective-permute-start.23 = (bf16[64,640]{1,0:T(8,128)(2,1)}, bf16[64,640]{1,0:T(8,128)(2,1)S(1)}, u32[]{:S(2)}, u32[]{:S(2)}) collective-permute-start(bf16[64,640]{1,0:T(8,128)(2,1)} %attend.2.refs_0_), channel_id=1, source_target_pairs={{0,12},{1,13},{2,14},{3,15},{4,8},{5,9},{6,10},{7,11},{8,4},{9,5},... | collective-permute-start | bytes 245768 | tf_op jit(solution)/shard_map/ppermute | solution.py:174
  56.7 9.3 %collective-permute-start.21 = (bf16[64,640]{1,0:T(8,128)(2,1)}, bf16[64,640]{1,0:T(8,128)(2,1)S(1)}, u32[]{:S(2)}, u32[]{:S(2)}) collective-permute-start(bf16[64,640]{1,0:T(8,128)(2,1)} %attend.2.refs_0_), channel_id=1, source_target_pairs={{0,8},{1,9},{2,10},{3,11},{4,12},{5,13},{6,14},{7,15},{8,0},{9,1},... | collective-permute-start | bytes 245768 | tf_op jit(solution)/shard_map/ppermute | solution.py:174
  58.1 8.5 %collective-permute-start.19 = (bf16[64,640]{1,0:T(8,128)(2,1)}, bf16[64,640]{1,0:T(8,128)(2,1)S(1)}, u32[]{:S(2)}, u32[]{:S(2)}) collective-permute-start(bf16[64,640]{1,0:T(8,128)(2,1)} %attend.2.refs_0_), channel_id=1, source_target_pairs={{0,4},{1,5},{2,6},{3,7},{4,0},{5,1},{6,2},{7,3},{8,12},{9,13},{10,... | collective-permute-start | bytes 245768 | tf_op jit(solution)/shard_map/ppermute | solution.py:174
  60.6 7.5 %collective-permute-start.18 = (bf16[64,640]{1,0:T(8,128)(2,1)}, bf16[64,640]{1,0:T(8,128)(2,1)S(1)}, u32[]{:S(2)}, u32[]{:S(2)}) collective-permute-start(bf16[64,640]{1,0:T(8,128)(2,1)} %attend.2.refs_0_), channel_id=1, source_target_pairs={{0,2},{1,3},{2,0},{3,1},{4,6},{5,7},{6,4},{7,5},{8,10},{9,11},{10,... | collective-permute-start | bytes 245768 | tf_op jit(solution)/shard_map/ppermute | solution.py:174
  63.6 4.5 %collective-permute-start.24 = (bf16[64,640]{1,0:T(8,128)(2,1)S(1)}, bf16[64,640]{1,0:T(8,128)(2,1)S(1)}, u32[]{:S(2)}, u32[]{:S(2)}) collective-permute-start(bf16[64,640]{1,0:T(8,128)(2,1)S(1)} %collective-permute-done.23.refs_6_), channel_id=1, source_target_pairs={{0,2},{1,3},{2,0},{3,1},{4,6},{5,7},{6,4},{7,5},{8,10},{9,11},{10,... | collective-permute-start | bytes 245768 | tf_op jit(solution)/shard_map/ppermute | solution.py:174
  66.1 4.8 %collective-permute-start.22 = (bf16[64,640]{1,0:T(8,128)(2,1)S(1)}, bf16[64,640]{1,0:T(8,128)(2,1)S(1)}, u32[]{:S(2)}, u32[]{:S(2)}) collective-permute-start(bf16[64,640]{1,0:T(8,128)(2,1)S(1)} %collective-permute-done.21.refs_4_), channel_id=1, source_target_pairs={{0,2},{1,3},{2,0},{3,1},{4,6},{5,7},{6,4},{7,5},{8,10},{9,11},{10,... | collective-permute-start | bytes 245768 | tf_op jit(solution)/shard_map/ppermute | solution.py:174
  66.7 5.1 %collective-permute-start.20 = (bf16[64,640]{1,0:T(8,128)(2,1)S(1)}, bf16[64,640]{1,0:T(8,128)(2,1)S(1)}, u32[]{:S(2)}, u32[]{:S(2)}) collective-permute-start(bf16[64,640]{1,0:T(8,128)(2,1)S(1)} %collective-permute-done.19.refs_2_), channel_id=1, source_target_pairs={{0,2},{1,3},{2,0},{3,1},{4,6},{5,7},{6,4},{7,5},{8,10},{9,11},{10,... | collective-permute-start | bytes 245768 | tf_op jit(solution)/shard_map/ppermute | solution.py:174
  74.4 22.3 %copy-start.1 = (bf16[5120,320]{0,1:T(8,128)(2,1)S(1)}, bf16[5120,320]{0,1:T(8,128)(2,1)}, u32[]{:S(2)}) copy-start(bf16[5120,320]{0,1:T(8,128)(2,1)} %param.16) | copy-start | bytes 9830404
  74.5 22.3 %copy-start.2 = (bf16[5120,320]{0,1:T(8,128)(2,1)S(1)}, bf16[5120,320]{0,1:T(8,128)(2,1)}, u32[]{:S(2)}) copy-start(bf16[5120,320]{0,1:T(8,128)(2,1)} %param.17) | copy-start | bytes 9830404
  74.5 22.3 %copy-start.7 = (f32[2,5120]{1,0:T(2,128)S(1)}, f32[2,5120]{1,0:T(2,128)}, u32[]{:S(2)}) copy-start(f32[2,5120]{1,0:T(2,128)} %pad_maximum_fusion.gain_hbm) | copy-start | bytes 122884
  79.1 24.9 %copy-start.6 = (bf16[64,640]{1,0:T(8,128)(2,1)}, bf16[64,640]{1,0:T(8,128)(2,1)S(1)}, u32[]{:S(2)}) copy-start(bf16[64,640]{1,0:T(8,128)(2,1)S(1)} %output.2.refs_3_.current_hbm) | copy-start | bytes 245764
  79.2 7.2 %collective-permute-start.30 = (bf16[64,640]{1,0:T(8,128)(2,1)S(1)}, bf16[64,640]{1,0:T(8,128)(2,1)S(1)}, u32[]{:S(2)}, u32[]{:S(2)}) collective-permute-start(bf16[64,640]{1,0:T(8,128)(2,1)S(1)} %output.2.refs_3_.current_hbm), channel_id=1, source_target_pairs={{0,12},{1,13},{2,14},{3,15},{4,8},{5,9},{6,10},{7,11},{8,4},{9,5},... | collective-permute-start | bytes 245768 | tf_op jit(solution)/shard_map/ppermute | solution.py:174
  80.5 5.9 %collective-permute-start.32 = (bf16[64,640]{1,0:T(8,128)(2,1)S(1)}, bf16[64,640]{1,0:T(8,128)(2,1)S(1)}, u32[]{:S(2)}, u32[]{:S(2)}) collective-permute-start(bf16[64,640]{1,0:T(8,128)(2,1)S(1)} %output.2.refs_3_.current_hbm), channel_id=1, source_target_pairs={{0,1},{1,0},{2,3},{3,2},{4,5},{5,4},{6,7},{7,6},{8,9},{9,8},{10,11... | collective-permute-start | bytes 245768 | tf_op jit(solution)/shard_map/ppermute | solution.py:174
  80.5 8.4 %collective-permute-start.28 = (bf16[64,640]{1,0:T(8,128)(2,1)S(1)}, bf16[64,640]{1,0:T(8,128)(2,1)S(1)}, u32[]{:S(2)}, u32[]{:S(2)}) collective-permute-start(bf16[64,640]{1,0:T(8,128)(2,1)S(1)} %output.2.refs_3_.current_hbm), channel_id=1, source_target_pairs={{0,8},{1,9},{2,10},{3,11},{4,12},{5,13},{6,14},{7,15},{8,0},{9,1},... | collective-permute-start | bytes 245768 | tf_op jit(solution)/shard_map/ppermute | solution.py:174
  80.5 8.5 %collective-permute-start.26 = (bf16[64,640]{1,0:T(8,128)(2,1)S(1)}, bf16[64,640]{1,0:T(8,128)(2,1)S(1)}, u32[]{:S(2)}, u32[]{:S(2)}) collective-permute-start(bf16[64,640]{1,0:T(8,128)(2,1)S(1)} %output.2.refs_3_.current_hbm), channel_id=1, source_target_pairs={{0,4},{1,5},{2,6},{3,7},{4,0},{5,1},{6,2},{7,3},{8,12},{9,13},{10,... | collective-permute-start | bytes 245768 | tf_op jit(solution)/shard_map/ppermute | solution.py:174
  83.6 6.3 %collective-permute-start.25 = (bf16[64,640]{1,0:T(8,128)(2,1)S(1)}, bf16[64,640]{1,0:T(8,128)(2,1)S(1)}, u32[]{:S(2)}, u32[]{:S(2)}) collective-permute-start(bf16[64,640]{1,0:T(8,128)(2,1)S(1)} %output.2.refs_3_.current_hbm), channel_id=1, source_target_pairs={{0,2},{1,3},{2,0},{3,1},{4,6},{5,7},{6,4},{7,5},{8,10},{9,11},{10,... | collective-permute-start | bytes 245768 | tf_op jit(solution)/shard_map/ppermute | solution.py:174
  86.4 4.7 %collective-permute-start.38 = (bf16[64,640]{1,0:T(8,128)(2,1)S(1)}, bf16[64,640]{1,0:T(8,128)(2,1)S(1)}, u32[]{:S(2)}, u32[]{:S(2)}) collective-permute-start(bf16[64,640]{1,0:T(8,128)(2,1)S(1)} %collective-permute-done.30.refs_9_), channel_id=1, source_target_pairs={{0,1},{1,0},{2,3},{3,2},{4,5},{5,4},{6,7},{7,6},{8,9},{9,8},{10,11... | collective-permute-start | bytes 245768 | tf_op jit(solution)/shard_map/ppermute | solution.py:174
  86.4 4.9 %collective-permute-start.31 = (bf16[64,640]{1,0:T(8,128)(2,1)S(1)}, bf16[64,640]{1,0:T(8,128)(2,1)S(1)}, u32[]{:S(2)}, u32[]{:S(2)}) collective-permute-start(bf16[64,640]{1,0:T(8,128)(2,1)S(1)} %collective-permute-done.30.refs_9_), channel_id=1, source_target_pairs={{0,2},{1,3},{2,0},{3,1},{4,6},{5,7},{6,4},{7,5},{8,10},{9,11},{10,... | collective-permute-start | bytes 245768 | tf_op jit(solution)/shard_map/ppermute | solution.py:174
  88.9 2.7 %collective-permute-start.36 = (bf16[64,640]{1,0:T(8,128)(2,1)S(1)}, bf16[64,640]{1,0:T(8,128)(2,1)S(1)}, u32[]{:S(2)}, u32[]{:S(2)}) collective-permute-start(bf16[64,640]{1,0:T(8,128)(2,1)S(1)} %collective-permute-done.28.refs_7_), channel_id=1, source_target_pairs={{0,1},{1,0},{2,3},{3,2},{4,5},{5,4},{6,7},{7,6},{8,9},{9,8},{10,11... | collective-permute-start | bytes 245768 | tf_op jit(solution)/shard_map/ppermute | solution.py:174
  89.0 5.3 %collective-permute-start.29 = (bf16[64,640]{1,0:T(8,128)(2,1)S(1)}, bf16[64,640]{1,0:T(8,128)(2,1)S(1)}, u32[]{:S(2)}, u32[]{:S(2)}) collective-permute-start(bf16[64,640]{1,0:T(8,128)(2,1)S(1)} %collective-permute-done.28.refs_7_), channel_id=1, source_target_pairs={{0,2},{1,3},{2,0},{3,1},{4,6},{5,7},{6,4},{7,5},{8,10},{9,11},{10,... | collective-permute-start | bytes 245768 | tf_op jit(solution)/shard_map/ppermute | solution.py:174
  89.9 5.6 %collective-permute-start.27 = (bf16[64,640]{1,0:T(8,128)(2,1)S(1)}, bf16[64,640]{1,0:T(8,128)(2,1)S(1)}, u32[]{:S(2)}, u32[]{:S(2)}) collective-permute-start(bf16[64,640]{1,0:T(8,128)(2,1)S(1)} %collective-permute-done.26.refs_5_), channel_id=1, source_target_pairs={{0,2},{1,3},{2,0},{3,1},{4,6},{5,7},{6,4},{7,5},{8,10},{9,11},{10,... | collective-permute-start | bytes 245768 | tf_op jit(solution)/shard_map/ppermute | solution.py:174
  91.1 4.4 %collective-permute-start.34 = (bf16[64,640]{1,0:T(8,128)(2,1)S(1)}, bf16[64,640]{1,0:T(8,128)(2,1)S(1)}, u32[]{:S(2)}, u32[]{:S(2)}) collective-permute-start(bf16[64,640]{1,0:T(8,128)(2,1)S(1)} %collective-permute-done.26.refs_5_), channel_id=1, source_target_pairs={{0,1},{1,0},{2,3},{3,2},{4,5},{5,4},{6,7},{7,6},{8,9},{9,8},{10,11... | collective-permute-start | bytes 245768 | tf_op jit(solution)/shard_map/ppermute | solution.py:174
  91.2 4.2 %collective-permute-start.33 = (bf16[64,640]{1,0:T(8,128)(2,1)S(1)}, bf16[64,640]{1,0:T(8,128)(2,1)S(1)}, u32[]{:S(2)}, u32[]{:S(2)}) collective-permute-start(bf16[64,640]{1,0:T(8,128)(2,1)S(1)} %collective-permute-done.25.refs_4_), channel_id=1, source_target_pairs={{0,1},{1,0},{2,3},{3,2},{4,5},{5,4},{6,7},{7,6},{8,9},{9,8},{10,11... | collective-permute-start | bytes 245768 | tf_op jit(solution)/shard_map/ppermute | solution.py:174
  91.6 3.9 %collective-permute-start.39 = (bf16[64,640]{1,0:T(8,128)(2,1)S(1)}, bf16[64,640]{1,0:T(8,128)(2,1)S(1)}, u32[]{:S(2)}, u32[]{:S(2)}) collective-permute-start(bf16[64,640]{1,0:T(8,128)(2,1)S(1)} %collective-permute-done.31.refs_10_), channel_id=1, source_target_pairs={{0,1},{1,0},{2,3},{3,2},{4,5},{5,4},{6,7},{7,6},{8,9},{9,8},{10,11... | collective-permute-start | bytes 245768 | tf_op jit(solution)/shard_map/ppermute | solution.py:174
  94.3 1.3 collective-permute-start.37
  95.5 1.3 collective-permute-start.35
  104.7 9.9 %copy-start.9 = (bf16[320,320]{1,0:T(8,128)(2,1)}, bf16[320,320]{1,0:T(8,128)(2,1)S(1)}, u32[]{:S(2)}) copy-start(bf16[320,320]{1,0:T(8,128)(2,1)S(1)} %get-tuple-element.25.sent_hbm) | copy-start | bytes 614404
  104.7 9.9 %collective-permute-start.40 = (bf16[320,320]{1,0:T(8,128)(2,1)S(1)}, bf16[320,320]{1,0:T(8,128)(2,1)S(1)}, u32[]{:S(2)}, u32[]{:S(2)}) collective-permute-start(bf16[320,320]{1,0:T(8,128)(2,1)S(1)} %get-tuple-element.25.sent_hbm), channel_id=1, source_target_pairs={{0,1},{1,0},{2,3},{3,2},{4,5},{5,4},{6,7},{7,6},{8,9},{9,8},{10,11... | collective-permute-start | bytes 614408 | tf_op jit(solution)/shard_map/ppermute | solution.py:174
  118.4 7.4 %collective-permute-start.46 = (bf16[64,640]{1,0:T(8,128)(2,1)}, bf16[64,640]{1,0:T(8,128)(2,1)S(1)}, u32[]{:S(2)}, u32[]{:S(2)}) collective-permute-start(bf16[64,640]{1,0:T(8,128)(2,1)} %attend.3.refs_0_), channel_id=1, source_target_pairs={{0,12},{1,13},{2,14},{3,15},{4,8},{5,9},{6,10},{7,11},{8,4},{9,5},... | collective-permute-start | bytes 245768 | tf_op jit(solution)/shard_map/ppermute | solution.py:174
  119.0 9.3 %collective-permute-start.44 = (bf16[64,640]{1,0:T(8,128)(2,1)}, bf16[64,640]{1,0:T(8,128)(2,1)S(1)}, u32[]{:S(2)}, u32[]{:S(2)}) collective-permute-start(bf16[64,640]{1,0:T(8,128)(2,1)} %attend.3.refs_0_), channel_id=1, source_target_pairs={{0,8},{1,9},{2,10},{3,11},{4,12},{5,13},{6,14},{7,15},{8,0},{9,1},... | collective-permute-start | bytes 245768 | tf_op jit(solution)/shard_map/ppermute | solution.py:174
  120.4 8.5 %collective-permute-start.42 = (bf16[64,640]{1,0:T(8,128)(2,1)}, bf16[64,640]{1,0:T(8,128)(2,1)S(1)}, u32[]{:S(2)}, u32[]{:S(2)}) collective-permute-start(bf16[64,640]{1,0:T(8,128)(2,1)} %attend.3.refs_0_), channel_id=1, source_target_pairs={{0,4},{1,5},{2,6},{3,7},{4,0},{5,1},{6,2},{7,3},{8,12},{9,13},{10,... | collective-permute-start | bytes 245768 | tf_op jit(solution)/shard_map/ppermute | solution.py:174
  122.9 7.5 %collective-permute-start.41 = (bf16[64,640]{1,0:T(8,128)(2,1)}, bf16[64,640]{1,0:T(8,128)(2,1)S(1)}, u32[]{:S(2)}, u32[]{:S(2)}) collective-permute-start(bf16[64,640]{1,0:T(8,128)(2,1)} %attend.3.refs_0_), channel_id=1, source_target_pairs={{0,2},{1,3},{2,0},{3,1},{4,6},{5,7},{6,4},{7,5},{8,10},{9,11},{10,... | collective-permute-start | bytes 245768 | tf_op jit(solution)/shard_map/ppermute | solution.py:174
  125.8 8.1 %copy-start.25 = (bf16[64,640]{1,0:T(8,128)(2,1)}, bf16[64,640]{1,0:T(8,128)(2,1)S(1)}, u32[]{:S(2)}) copy-start(bf16[64,640]{1,0:T(8,128)(2,1)S(1)} %collective-permute-done.46.refs_6_) | copy-start | bytes 245764
  125.8 4.5 %collective-permute-start.47 = (bf16[64,640]{1,0:T(8,128)(2,1)S(1)}, bf16[64,640]{1,0:T(8,128)(2,1)S(1)}, u32[]{:S(2)}, u32[]{:S(2)}) collective-permute-start(bf16[64,640]{1,0:T(8,128)(2,1)S(1)} %collective-permute-done.46.refs_6_), channel_id=1, source_target_pairs={{0,2},{1,3},{2,0},{3,1},{4,6},{5,7},{6,4},{7,5},{8,10},{9,11},{10,... | collective-permute-start | bytes 245768 | tf_op jit(solution)/shard_map/ppermute | solution.py:174
  128.3 4.8 %collective-permute-start.45 = (bf16[64,640]{1,0:T(8,128)(2,1)S(1)}, bf16[64,640]{1,0:T(8,128)(2,1)S(1)}, u32[]{:S(2)}, u32[]{:S(2)}) collective-permute-start(bf16[64,640]{1,0:T(8,128)(2,1)S(1)} %collective-permute-done.44.refs_4_), channel_id=1, source_target_pairs={{0,2},{1,3},{2,0},{3,1},{4,6},{5,7},{6,4},{7,5},{8,10},{9,11},{10,... | collective-permute-start | bytes 245768 | tf_op jit(solution)/shard_map/ppermute | solution.py:174
  128.9 5.1 %collective-permute-start.43 = (bf16[64,640]{1,0:T(8,128)(2,1)S(1)}, bf16[64,640]{1,0:T(8,128)(2,1)S(1)}, u32[]{:S(2)}, u32[]{:S(2)}) collective-permute-start(bf16[64,640]{1,0:T(8,128)(2,1)S(1)} %collective-permute-done.42.refs_2_), channel_id=1, source_target_pairs={{0,2},{1,3},{2,0},{3,1},{4,6},{5,7},{6,4},{7,5},{8,10},{9,11},{10,... | collective-permute-start | bytes 245768 | tf_op jit(solution)/shard_map/ppermute | solution.py:174
  (21 other events, 37.5 us)

commit v8 on v7

--- a/solution.py
+++ b/solution.py
@@ -252,7 +252,9 @@
                 lanes = pl.ds(pl.multiple_of(other_chip * 2 * cols, 2 * cols), 2 * cols)
                 target = state.at[pl.ds(pl.multiple_of(owner * half, half), half), lanes]
             pairs.append((blocks[mask], target))
-    pairs += [(table_hbm, table), (gain_hbm.at[:, own_lanes], gain), (incoming_hbm, entering)]
+    pairs += [(table_hbm.at[pl.ds(0, 2)], table.at[pl.ds(0, 2)]), (gain_hbm.at[:, own_lanes], gain)]
+    if step == 0:
+        pairs.append((incoming_hbm.at[step], entering.at[step]))
     inputs = len(pairs)
     if fetched:
         pairs += [(weight_refs[i], weights.at[i]) for i in range(3)]

time: 151 us -> 151 us (level)
  no operation moved by 1% of the time
where the time goes in v8:
time: 151 us; the launch traced here: 150 us
  starting transfers between devices  42.1 us (28%)
  waiting for transfers between devices  32.8 us (22%)
  Pallas kernels  31.7 us (21%)
  blocking collectives  31.4 us (21%)
  local copies, waits for them, and re-layouts  8.48 us (6%)
  matrix products  2 us (1%)
    ppermute x48, starting transfers between devices, swapped(): lax.ppermute(value, 'queue', [(source, source ^ bit) for source in range(...  37.4 us
    ppermute x48, waiting for transfers between devices, swapped(): lax.ppermute(value, 'queue', [(source, source ^ bit) for source in range(...  29.3 us
    all_to_all x2, blocking collectives, paired_device(): lax.all_to_all(squares, 'queue', split_axis=0, concat_axis=0, tiled=True)  21.1 us
    pallas_call x2, Pallas kernels, project(): pl.pallas_call(functools.partial(project_kernel, step, spans), out_shape=...  13.6 us
    all_to_all x1, blocking collectives, paired_device(): lax.all_to_all(result, 'queue', split_axis=0, concat_axis=2, tiled=True,...  10.3 us
    pallas_call x2, Pallas kernels, output(): pl.pallas_call(functools.partial(output_kernel, step, spans, last), out_s...  9.8 us
    unnamed x73, local copies, waits for them, and re-layouts  8.48 us
    pallas_call x2, Pallas kernels, attend(): pl.pallas_call(functools.partial(attend_kernel, step, spans, head_size),...  6.27 us
  transfers between devices with their start and end apart: 49, of which 24 were waited for; matrix products, arithmetic and copies ran while one was open for 2% of the time, Pallas kernels for 9%

profile of v8, /device:TPU:0, one launch (start us, length us, event | category | flops | bytes accessed | tf_op | source)
XLA Modules:
  0.0 150.3 jit_solution(15919224631741250194)
XLA Ops:
  0.0 0.5 collective-permute-start.15
  0.5 4.7 %collective-permute-start.5 = (bf16[8,5120]{1,0:T(8,128)(2,1)}, bf16[8,5120]{1,0:T(8,128)(2,1)S(1)}, u32[]{:S(2)}, u32[]{:S(2)}) collective-permute-start(bf16[8,5120]{1,0:T(8,128)(2,1)} %refs_3_.1), channel_id=1, source_target_pairs={{0,12},{1,13},{2,14},{3,15},{4,8},{5,9},{6,10},{7,11},{8,4},{9,5},... | collective-permute-start | bytes 245768 | tf_op jit(solution)/shard_map/ppermute | solution.py:174
  5.1 0.7 collective-permute-start.1
  5.8 1.6 %collective-permute-start = (bf16[8,5120]{1,0:T(8,128)(2,1)}, bf16[8,5120]{1,0:T(8,128)(2,1)S(1)}, u32[]{:S(2)}, u32[]{:S(2)}) collective-permute-start(bf16[8,5120]{1,0:T(8,128)(2,1)} %refs_3_.1), channel_id=1, source_target_pairs={{0,2},{1,3},{2,0},{3,1},{4,6},{5,7},{6,4},{7,5},{8,10},{9,11},{10,... | collective-permute-start | bytes 245768 | tf_op jit(solution)/shard_map/ppermute | solution.py:174
  7.4 1.4 pad_maximum_fusion.gain_hbm
  8.8 1.6 %collective-permute-start.6 = (bf16[8,5120]{1,0:T(8,128)(2,1)S(1)}, bf16[8,5120]{1,0:T(8,128)(2,1)S(1)}, u32[]{:S(2)}, u32[]{:S(2)}) collective-permute-start(bf16[8,5120]{1,0:T(8,128)(2,1)S(1)} %collective-permute-done.5.refs_9_), channel_id=1, source_target_pairs={{0,2},{1,3},{2,0},{3,1},{4,6},{5,7},{6,4},{7,5},{8,10},{9,11},{10,... | collective-permute-start | bytes 245768 | tf_op jit(solution)/shard_map/ppermute | solution.py:174
  10.4 2.4 %collective-permute-done.3.refs_7_ = bf16[8,5120]{1,0:T(8,128)(2,1)S(1)} collective-permute-done((bf16[8,5120]{1,0:T(8,128)(2,1)}, bf16[8,5120]{1,0:T(8,128)(2,1)S(1)}, u32[]{:S(2)}, u32[]{:S(2)}) %collective-permute-start.3) | collective-permute-done | bytes 81952 | tf_op jit(solution)/shard_map/ppermute | solution.py:174
  12.8 1.5 %collective-permute-start.4 = (bf16[8,5120]{1,0:T(8,128)(2,1)S(1)}, bf16[8,5120]{1,0:T(8,128)(2,1)S(1)}, u32[]{:S(2)}, u32[]{:S(2)}) collective-permute-start(bf16[8,5120]{1,0:T(8,128)(2,1)S(1)} %collective-permute-done.3.refs_7_), channel_id=1, source_target_pairs={{0,2},{1,3},{2,0},{3,1},{4,6},{5,7},{6,4},{7,5},{8,10},{9,11},{10,... | collective-permute-start | bytes 245768 | tf_op jit(solution)/shard_map/ppermute | solution.py:174
  14.3 0.5 collective-permute-start.2
  14.9 2.0 %fusion.table_hbm = bf16[3,16,5120]{2,1,0:T(8,128)(2,1)} fusion(bf16[96,3,5120]{2,0,1:T(8,128)(2,1)S(1)} %copy-done, s32[16]{0:T(128)} %param.14), kind=kOutput, calls=%fused_computation.1 | convolution fusion | flops 47433216 | bytes 3440704 | tf_op jit(solution)/shard_map/sl,ltd->tsd/dot_general | solution.py:595
  16.9 2.0 %arrange.1 = bf16[16,2,16,640]{3,2,1,0:T(8,128)(2,1)} custom-call(bf16[32,5120]{1,0:T(8,128)(2,1)} %keys_ref.1, bf16[32,5120]{1,0:T(8,128)(2,1)} %values_ref.1), custom_call_target="tpu_custom_call" | custom-call | tf_op jit(solution)/shard_map/arrange/pallas_call | solution.py:563
  19.1 4.7 %all-to-all-start.1 = ((bf16[16,2,16,640]{3,2,1,0:T(8,128)(2,1)}), bf16[16,2,16,640]{3,2,1,0:T(8,128)(2,1)}, u32[]{:S(2)}, u32[]{:S(2)}) async-start(bf16[16,2,16,640]{3,2,1,0:T(8,128)(2,1)} %arrange.1), calls=%async_computation.1 | async-start | bytes 1310720 | tf_op jit(solution)/shard_map/all_to_all | solution.py:603
  26.9 0.6 collective-permute-done.10.refs_14_
  27.6 0.5 copy-done.33
  28.1 8.7 %project.2 = (bf16[64,320]{1,0:T(8,128)(2,1)}, bf16[320,320]{1,0:T(8,128)(2,1)}, f32[16,2,128]{2,1,0:T(2,128)}, bf16[64,640]{1,0:T(8,128)(2,1)}) custom-call(f32[2,5120]{1,0:T(2,128)} %pad_maximum_fusion.gain_hbm, bf16[3,16,5120]{2,1,0:T(8,128)(2,1)} %fusion.table_hbm, bf16[2,8,5120]{2,1,0:T(8,128)(2,1)} %incoming_hbm.7, bf16[320,5120]{1,0:T(8,128)(2,1)} %bitcast.17, ...), custom_call_target="tpu_custom_call" | custom-call | tf_op jit(solution)/shard_map/project/pallas_call | solution.py:342
  36.9 3.6 %all-to-all-done.1.text_hbm = bf16[16,2,16,640]{3,2,1,0:T(8,128)(2,1)} async-done(((bf16[16,2,16,640]{3,2,1,0:T(8,128)(2,1)}), bf16[16,2,16,640]{3,2,1,0:T(8,128)(2,1)}, u32[]{:S(2)}, u32[]{:S(2)}) %all-to-all-start.1) | async-done | bytes 655392 | tf_op jit(solution)/shard_map/all_to_all | solution.py:603
  41.0 11.4 %all_to_all.30.squares_hbm = f32[16,2,128]{2,1,0:T(2,128)} all-to-all(f32[16,2,128]{2,1,0:T(2,128)} %get-tuple-element.21), channel_id=1, replica_groups=mesh['groups'=2,'queue'=16] {'queue'}, dimensions={0} | all-to-all | bytes 32768 | tf_op jit(solution)/shard_map/all_to_all | solution.py:611
  52.3 0.7 copy-done.12
  53.0 3.1 %attend.2.refs_0_ = bf16[64,640]{1,0:T(8,128)(2,1)} custom-call(bf16[64,320]{1,0:T(8,128)(2,1)} %get-tuple-element.19.own_hbm, bf16[320,320]{1,0:T(8,128)(2,1)} %get-tuple-element.20.sent_hbm, bf16[320,320]{1,0:T(8,128)(2,1)} %copy-done.12, f32[16,2,128]{2,1,0:T(2,128)} %all_to_all.30.squares_hbm, bf16[16,2,16,640]{3,2,1,0:T(8,128)(2,1)} %all-to-all-done.1.text_hbm, ...), custom_call_target="tpu_custom_call" | custom-call | tf_op jit(solution)/shard_map/attend/pallas_call | solution.py:451
  56.2 0.6 collective-permute-start.23
  56.7 1.4 collective-permute-start.21
  58.1 2.5 %collective-permute-start.19 = (bf16[64,640]{1,0:T(8,128)(2,1)}, bf16[64,640]{1,0:T(8,128)(2,1)S(1)}, u32[]{:S(2)}, u32[]{:S(2)}) collective-permute-start(bf16[64,640]{1,0:T(8,128)(2,1)} %attend.2.refs_0_), channel_id=1, source_target_pairs={{0,4},{1,5},{2,6},{3,7},{4,0},{5,1},{6,2},{7,3},{8,12},{9,13},{10,... | collective-permute-start | bytes 245768 | tf_op jit(solution)/shard_map/ppermute | solution.py:174
  61.1 2.5 %collective-permute-done.23.refs_6_ = bf16[64,640]{1,0:T(8,128)(2,1)S(1)} collective-permute-done((bf16[64,640]{1,0:T(8,128)(2,1)}, bf16[64,640]{1,0:T(8,128)(2,1)S(1)}, u32[]{:S(2)}, u32[]{:S(2)}) %collective-permute-start.23) | collective-permute-done | bytes 81952 | tf_op jit(solution)/shard_map/ppermute | solution.py:174
  63.6 0.5 collective-permute-start.24
  64.1 2.0 %collective-permute-done.21.refs_4_ = bf16[64,640]{1,0:T(8,128)(2,1)S(1)} collective-permute-done((bf16[64,640]{1,0:T(8,128)(2,1)}, bf16[64,640]{1,0:T(8,128)(2,1)S(1)}, u32[]{:S(2)}, u32[]{:S(2)}) %collective-permute-start.21) | collective-permute-done | bytes 81952 | tf_op jit(solution)/shard_map/ppermute | solution.py:174
  66.1 0.6 collective-permute-start.22
  66.7 1.4 collective-permute-start.20
  68.1 2.8 %collective-permute-done.22.refs_5_ = bf16[64,640]{1,0:T(8,128)(2,1)S(1)} collective-permute-done((bf16[64,640]{1,0:T(8,128)(2,1)S(1)}, bf16[64,640]{1,0:T(8,128)(2,1)S(1)}, u32[]{:S(2)}, u32[]{:S(2)}) %collective-permute-start.22) | collective-permute-done | bytes 81952 | tf_op jit(solution)/shard_map/ppermute | solution.py:174
  70.9 0.9 collective-permute-done.20.refs_3_
  71.8 0.9 copy-done.5
  72.7 0.9 copy-done.8
  73.6 0.9 copy-done.10
  74.5 4.7 %output.2.refs_3_.current_hbm = bf16[64,640]{1,0:T(8,128)(2,1)S(1)} custom-call(bf16[64,640]{1,0:T(8,128)(2,1)S(1)} %copy-done.10, bf16[3,16,5120]{2,1,0:T(8,128)(2,1)S(1)} %copy-done.4, bf16[2,8,5120]{2,1,0:T(8,128)(2,1)S(1)} %copy-done.5, bf16[320,5120]{1,0:T(8,128)(2,1)} %bitcast.24, bf16[320,5120]{1,0:T(8,128)(2,1)} %collective-permute-done.15.other_hbm, ...), custom_call_target="tpu_custom_call" | custom-call | tf_op jit(solution)/shard_map/output/pallas_call | solution.py:530
  79.2 1.3 collective-permute-start.30
  80.5 3.1 %collective-permute-start.26 = (bf16[64,640]{1,0:T(8,128)(2,1)S(1)}, bf16[64,640]{1,0:T(8,128)(2,1)S(1)}, u32[]{:S(2)}, u32[]{:S(2)}) collective-permute-start(bf16[64,640]{1,0:T(8,128)(2,1)S(1)} %output.2.refs_3_.current_hbm), channel_id=1, source_target_pairs={{0,4},{1,5},{2,6},{3,7},{4,0},{5,1},{6,2},{7,3},{8,12},{9,13},{10,... | collective-permute-start | bytes 245768 | tf_op jit(solution)/shard_map/ppermute | solution.py:174
  83.6 0.9 collective-permute-start.25
  84.5 1.9 %collective-permute-done.30.refs_9_ = bf16[64,640]{1,0:T(8,128)(2,1)S(1)} collective-permute-done((bf16[64,640]{1,0:T(8,128)(2,1)S(1)}, bf16[64,640]{1,0:T(8,128)(2,1)S(1)}, u32[]{:S(2)}, u32[]{:S(2)}) %collective-permute-start.30) | collective-permute-done | bytes 81952 | tf_op jit(solution)/shard_map/ppermute | solution.py:174
  86.4 0.9 collective-permute-start.31
  87.2 1.6 %collective-permute-done.28.refs_7_ = bf16[64,640]{1,0:T(8,128)(2,1)S(1)} collective-permute-done((bf16[64,640]{1,0:T(8,128)(2,1)S(1)}, bf16[64,640]{1,0:T(8,128)(2,1)S(1)}, u32[]{:S(2)}, u32[]{:S(2)}) %collective-permute-start.28) | collective-permute-done | bytes 81952 | tf_op jit(solution)/shard_map/ppermute | solution.py:174
  89.0 0.9 collective-permute-start.29
  89.9 1.1 collective-permute-start.27
  91.8 2.5 %collective-permute-done.29.refs_8_ = bf16[64,640]{1,0:T(8,128)(2,1)S(1)} collective-permute-done((bf16[64,640]{1,0:T(8,128)(2,1)S(1)}, bf16[64,640]{1,0:T(8,128)(2,1)S(1)}, u32[]{:S(2)}, u32[]{:S(2)}) %collective-permute-start.29) | collective-permute-done | bytes 81952 | tf_op jit(solution)/shard_map/ppermute | solution.py:174
  94.3 1.2 collective-permute-done.27.refs_6_
  95.6 1.2 collective-permute-done.35.refs_14_
  96.8 1.9 %copy-done.3 = bf16[5120,320]{0,1:T(8,128)(2,1)S(1)} copy-done((bf16[5120,320]{0,1:T(8,128)(2,1)S(1)}, bf16[5120,320]{0,1:T(8,128)(2,1)}, u32[]{:S(2)}) %copy-start.3) | copy-done | bytes 3276824
  98.7 4.9 %project.3 = (bf16[64,320]{1,0:T(8,128)(2,1)S(1)}, bf16[320,320]{1,0:T(8,128)(2,1)S(1)}, f32[16,2,128]{2,1,0:T(2,128)S(1)}) custom-call(f32[2,5120]{1,0:T(2,128)S(1)} %copy-done.7, bf16[3,16,5120]{2,1,0:T(8,128)(2,1)S(1)} %copy-done.4, bf16[2,8,5120]{2,1,0:T(8,128)(2,1)S(1)} %copy-done.5, bf16[320,5120]{1,0:T(8,128)(2,1)S(1)} %bitcast.18, ...), custom_call_target="tpu_custom_call" | custom-call | tf_op jit(solution)/shard_map/project/pallas_call | solution.py:342
  103.6 0.6 copy-done.11
  104.4 9.8 %all_to_all.31.squares_hbm = f32[16,2,128]{2,1,0:T(2,128)} all-to-all(f32[16,2,128]{2,1,0:T(2,128)S(1)} %get-tuple-element.26), channel_id=1, replica_groups=mesh['groups'=2,'queue'=16] {'queue'}, dimensions={0} | all-to-all | bytes 32768 | tf_op jit(solution)/shard_map/all_to_all | solution.py:611
  114.1 0.7 copy-done.13
  114.8 3.1 %attend.3.refs_0_ = bf16[64,640]{1,0:T(8,128)(2,1)} custom-call(bf16[64,320]{1,0:T(8,128)(2,1)} %copy-done.11, bf16[320,320]{1,0:T(8,128)(2,1)} %copy-done.9, bf16[320,320]{1,0:T(8,128)(2,1)} %copy-done.13, f32[16,2,128]{2,1,0:T(2,128)} %all_to_all.31.squares_hbm, bf16[16,2,16,640]{3,2,1,0:T(8,128)(2,1)} %all-to-all-done.1.text_hbm, ...), custom_call_target="tpu_custom_call" | custom-call | tf_op jit(solution)/shard_map/attend/pallas_call | solution.py:451
  118.0 0.6 collective-permute-start.46
  118.5 1.4 collective-permute-start.44
  119.9 2.5 %collective-permute-start.42 = (bf16[64,640]{1,0:T(8,128)(2,1)}, bf16[64,640]{1,0:T(8,128)(2,1)S(1)}, u32[]{:S(2)}, u32[]{:S(2)}) collective-permute-start(bf16[64,640]{1,0:T(8,128)(2,1)} %attend.3.refs_0_), channel_id=1, source_target_pairs={{0,4},{1,5},{2,6},{3,7},{4,0},{5,1},{6,2},{7,3},{8,12},{9,13},{10,... | collective-permute-start | bytes 245768 | tf_op jit(solution)/shard_map/ppermute | solution.py:174
  122.9 2.5 %collective-permute-done.46.refs_6_ = bf16[64,640]{1,0:T(8,128)(2,1)S(1)} collective-permute-done((bf16[64,640]{1,0:T(8,128)(2,1)}, bf16[64,640]{1,0:T(8,128)(2,1)S(1)}, u32[]{:S(2)}, u32[]{:S(2)}) %collective-permute-start.46) | collective-permute-done | bytes 81952 | tf_op jit(solution)/shard_map/ppermute | solution.py:174
  125.4 0.5 collective-permute-start.47
  125.9 2.0 %collective-permute-done.44.refs_4_ = bf16[64,640]{1,0:T(8,128)(2,1)S(1)} collective-permute-done((bf16[64,640]{1,0:T(8,128)(2,1)}, bf16[64,640]{1,0:T(8,128)(2,1)S(1)}, u32[]{:S(2)}, u32[]{:S(2)}) %collective-permute-start.44) | collective-permute-done | bytes 81952 | tf_op jit(solution)/shard_map/ppermute | solution.py:174
  127.9 0.6 collective-permute-start.45
  128.4 1.5 collective-permute-start.43
  129.9 2.7 %collective-permute-done.45.refs_5_ = bf16[64,640]{1,0:T(8,128)(2,1)S(1)} collective-permute-done((bf16[64,640]{1,0:T(8,128)(2,1)S(1)}, bf16[64,640]{1,0:T(8,128)(2,1)S(1)}, u32[]{:S(2)}, u32[]{:S(2)}) %collective-permute-start.45) | collective-permute-done | bytes 81952 | tf_op jit(solution)/shard_map/ppermute | solution.py:174
  132.6 0.9 collective-permute-done.43.refs_3_
  133.6 0.6 copy-done.35
  134.2 5.1 %output.3 = bf16[8,8,640]{2,1,0:T(8,128)(2,1)} custom-call(bf16[64,640]{1,0:T(8,128)(2,1)} %copy-done.6, bf16[3,16,5120]{2,1,0:T(8,128)(2,1)} %fusion.table_hbm, bf16[2,8,5120]{2,1,0:T(8,128)(2,1)} %incoming_hbm.7, bf16[320,5120]{1,0:T(8,128)(2,1)} %bitcast.25, bf16[320,5120]{1,0:T(8,128)(2,1)} %collective-permute-done.15.other_hbm, ...), custom_call_target="tpu_custom_call" | custom-call | tf_op jit(solution)/shard_map/output/pallas_call | solution.py:530
  139.3 10.3 %all_to_all.32 = bf16[8,8,640]{2,1,0:T(8,128)(2,1)S(1)} all-to-all(bf16[8,8,640]{2,1,0:T(8,128)(2,1)} %output.3), channel_id=1, replica_groups={{0,2,4,6,8,10,12,14},{1,3,5,7,9,11,13,15},{16,18,20,22,24,26,28,30},{17..., dimensions={0} | all-to-all | bytes 163840 | tf_op jit(solution)/shard_map/all_to_all | solution.py:626
  149.6 0.6 copy.14
  (119 shorter events, 6.0 us)
Async XLA Ops:
  0.0 14.9 %copy-start = (bf16[96,3,5120]{2,0,1:T(8,128)(2,1)S(1)}, bf16[96,3,5120]{2,0,1:T(8,128)(2,1)}, u32[]{:S(2)}) copy-start(bf16[96,3,5120]{2,0,1:T(8,128)(2,1)} %param.15) | copy-start | bytes 8847364
  0.0 23.8 %copy-start.14 = (bf16[8,5120]{1,0:T(8,128)(2,1)S(1)}, bf16[8,5120]{1,0:T(8,128)(2,1)}, u32[]{:S(2)}) copy-start(bf16[8,5120]{1,0:T(8,128)(2,1)} %refs_3_.1) | copy-start | bytes 245764
  0.0 71.7 %collective-permute-start.15 = (bf16[320,5120]{1,0:T(8,128)(2,1)}, bf16[320,5120]{1,0:T(8,128)(2,1)}, u32[]{:S(2)}, u32[]{:S(2)}) collective-permute-start(bf16[320,5120]{1,0:T(8,128)(2,1)} %bitcast.23), channel_id=1, source_target_pairs={{0,1},{1,0},{2,3},{3,2},{4,5},{5,4},{6,7},{7,6},{8,9},{9,8},{10,11... | collective-permute-start | bytes 9830408 | tf_op jit(solution)/shard_map/ppermute | solution.py:174
  0.5 8.4 %collective-permute-start.5 = (bf16[8,5120]{1,0:T(8,128)(2,1)}, bf16[8,5120]{1,0:T(8,128)(2,1)S(1)}, u32[]{:S(2)}, u32[]{:S(2)}) collective-permute-start(bf16[8,5120]{1,0:T(8,128)(2,1)} %refs_3_.1), channel_id=1, source_target_pairs={{0,12},{1,13},{2,14},{3,15},{4,8},{5,9},{6,10},{7,11},{8,4},{9,5},... | collective-permute-start | bytes 245768 | tf_op jit(solution)/shard_map/ppermute | solution.py:174
  5.1 7.7 %collective-permute-start.3 = (bf16[8,5120]{1,0:T(8,128)(2,1)}, bf16[8,5120]{1,0:T(8,128)(2,1)S(1)}, u32[]{:S(2)}, u32[]{:S(2)}) collective-permute-start(bf16[8,5120]{1,0:T(8,128)(2,1)} %refs_3_.1), channel_id=1, source_target_pairs={{0,8},{1,9},{2,10},{3,11},{4,12},{5,13},{6,14},{7,15},{8,0},{9,1},... | collective-permute-start | bytes 245768 | tf_op jit(solution)/shard_map/ppermute | solution.py:174
  5.1 9.2 %collective-permute-start.1 = (bf16[8,5120]{1,0:T(8,128)(2,1)}, bf16[8,5120]{1,0:T(8,128)(2,1)S(1)}, u32[]{:S(2)}, u32[]{:S(2)}) collective-permute-start(bf16[8,5120]{1,0:T(8,128)(2,1)} %refs_3_.1), channel_id=1, source_target_pairs={{0,4},{1,5},{2,6},{3,7},{4,0},{5,1},{6,2},{7,3},{8,12},{9,13},{10,... | collective-permute-start | bytes 245768 | tf_op jit(solution)/shard_map/ppermute | solution.py:174
  5.8 13.1 %collective-permute-start = (bf16[8,5120]{1,0:T(8,128)(2,1)}, bf16[8,5120]{1,0:T(8,128)(2,1)S(1)}, u32[]{:S(2)}, u32[]{:S(2)}) collective-permute-start(bf16[8,5120]{1,0:T(8,128)(2,1)} %refs_3_.1), channel_id=1, source_target_pairs={{0,2},{1,3},{2,0},{3,1},{4,6},{5,7},{6,4},{7,5},{8,10},{9,11},{10,... | collective-permute-start | bytes 245768 | tf_op jit(solution)/shard_map/ppermute | solution.py:174
  8.8 18.7 %copy-start.15 = (bf16[8,5120]{1,0:T(8,128)(2,1)}, bf16[8,5120]{1,0:T(8,128)(2,1)S(1)}, u32[]{:S(2)}) copy-start(bf16[8,5120]{1,0:T(8,128)(2,1)S(1)} %collective-permute-done.5.refs_9_) | copy-start | bytes 245764
  8.8 10.0 %collective-permute-start.6 = (bf16[8,5120]{1,0:T(8,128)(2,1)S(1)}, bf16[8,5120]{1,0:T(8,128)(2,1)S(1)}, u32[]{:S(2)}, u32[]{:S(2)}) collective-permute-start(bf16[8,5120]{1,0:T(8,128)(2,1)S(1)} %collective-permute-done.5.refs_9_), channel_id=1, source_target_pairs={{0,2},{1,3},{2,0},{3,1},{4,6},{5,7},{6,4},{7,5},{8,10},{9,11},{10,... | collective-permute-start | bytes 245768 | tf_op jit(solution)/shard_map/ppermute | solution.py:174
  12.8 14.7 %copy-start.16 = (bf16[8,5120]{1,0:T(8,128)(2,1)}, bf16[8,5120]{1,0:T(8,128)(2,1)S(1)}, u32[]{:S(2)}) copy-start(bf16[8,5120]{1,0:T(8,128)(2,1)S(1)} %collective-permute-done.3.refs_7_) | copy-start | bytes 245764
  12.8 6.1 %collective-permute-start.4 = (bf16[8,5120]{1,0:T(8,128)(2,1)S(1)}, bf16[8,5120]{1,0:T(8,128)(2,1)S(1)}, u32[]{:S(2)}, u32[]{:S(2)}) collective-permute-start(bf16[8,5120]{1,0:T(8,128)(2,1)S(1)} %collective-permute-done.3.refs_7_), channel_id=1, source_target_pairs={{0,2},{1,3},{2,0},{3,1},{4,6},{5,7},{6,4},{7,5},{8,10},{9,11},{10,... | collective-permute-start | bytes 245768 | tf_op jit(solution)/shard_map/ppermute | solution.py:174
  14.3 13.2 %copy-start.17 = (bf16[8,5120]{1,0:T(8,128)(2,1)}, bf16[8,5120]{1,0:T(8,128)(2,1)S(1)}, u32[]{:S(2)}) copy-start(bf16[8,5120]{1,0:T(8,128)(2,1)S(1)} %collective-permute-done.1.refs_5_) | copy-start | bytes 245764
  14.3 4.7 %collective-permute-start.2 = (bf16[8,5120]{1,0:T(8,128)(2,1)S(1)}, bf16[8,5120]{1,0:T(8,128)(2,1)}, u32[]{:S(2)}, u32[]{:S(2)}) collective-permute-start(bf16[8,5120]{1,0:T(8,128)(2,1)S(1)} %collective-permute-done.1.refs_5_), channel_id=1, source_target_pairs={{0,2},{1,3},{2,0},{3,1},{4,6},{5,7},{6,4},{7,5},{8,10},{9,11},{10,... | collective-permute-start | bytes 245768 | tf_op jit(solution)/shard_map/ppermute | solution.py:174
  18.9 8.7 %copy-start.18 = (bf16[8,5120]{1,0:T(8,128)(2,1)}, bf16[8,5120]{1,0:T(8,128)(2,1)S(1)}, u32[]{:S(2)}) copy-start(bf16[8,5120]{1,0:T(8,128)(2,1)S(1)} %collective-permute-done.refs_4_) | copy-start | bytes 245764
  18.9 8.7 %copy-start.19 = (bf16[8,5120]{1,0:T(8,128)(2,1)}, bf16[8,5120]{1,0:T(8,128)(2,1)S(1)}, u32[]{:S(2)}) copy-start(bf16[8,5120]{1,0:T(8,128)(2,1)S(1)} %collective-permute-done.6.refs_10_) | copy-start | bytes 245764
  18.9 8.7 %copy-start.20 = (bf16[8,5120]{1,0:T(8,128)(2,1)}, bf16[8,5120]{1,0:T(8,128)(2,1)S(1)}, u32[]{:S(2)}) copy-start(bf16[8,5120]{1,0:T(8,128)(2,1)S(1)} %collective-permute-done.4.refs_8_) | copy-start | bytes 245764
  19.1 21.4 %all-to-all-start.1 = ((bf16[16,2,16,640]{3,2,1,0:T(8,128)(2,1)}), bf16[16,2,16,640]{3,2,1,0:T(8,128)(2,1)}, u32[]{:S(2)}, u32[]{:S(2)}) async-start(bf16[16,2,16,640]{3,2,1,0:T(8,128)(2,1)} %arrange.1), calls=%async_computation.1 | async-start | bytes 1310720 | tf_op jit(solution)/shard_map/all_to_all | solution.py:603
  23.8 1.3 collective-permute-start.7
  24.2 1.3 collective-permute-start.13
  24.4 1.3 collective-permute-start.11
  24.7 1.3 collective-permute-start.9
  25.1 1.3 collective-permute-start.8
  25.5 1.3 collective-permute-start.14
  25.7 1.3 collective-permute-start.12
  26.0 1.5 collective-permute-start.10
  28.1 43.6 %copy-start.4 = (bf16[3,16,5120]{2,1,0:T(8,128)(2,1)S(1)}, bf16[3,16,5120]{2,1,0:T(8,128)(2,1)}, u32[]{:S(2)}) copy-start(bf16[3,16,5120]{2,1,0:T(8,128)(2,1)} %fusion.table_hbm) | copy-start | bytes 1474564
  40.4 11.9 %collective-permute-start.17 = (bf16[16,2,16,640]{3,2,1,0:T(8,128)(2,1)}, bf16[16,2,16,640]{3,2,1,0:T(8,128)(2,1)}, u32[]{:S(2)}, u32[]{:S(2)}) collective-permute-start(bf16[16,2,16,640]{3,2,1,0:T(8,128)(2,1)} %all-to-all-done.1.text_hbm), channel_id=1, source_target_pairs={{0,1},{1,0},{2,3},{3,2},{4,5},{5,4},{6,7},{7,6},{8,9},{9,8},{10,11... | collective-permute-start | bytes 1966088 | tf_op jit(solution)/shard_map/ppermute | solution.py:174
  40.5 11.8 %collective-permute-start.16 = (bf16[320,320]{1,0:T(8,128)(2,1)}, bf16[320,320]{1,0:T(8,128)(2,1)S(1)}, u32[]{:S(2)}, u32[]{:S(2)}) collective-permute-start(bf16[320,320]{1,0:T(8,128)(2,1)} %get-tuple-element.20.sent_hbm), channel_id=1, source_target_pairs={{0,1},{1,0},{2,3},{3,2},{4,5},{5,4},{6,7},{7,6},{8,9},{9,8},{10,11... | collective-permute-start | bytes 614408 | tf_op jit(solution)/shard_map/ppermute | solution.py:174
  56.2 7.4 %collective-permute-start.23 = (bf16[64,640]{1,0:T(8,128)(2,1)}, bf16[64,640]{1,0:T(8,128)(2,1)S(1)}, u32[]{:S(2)}, u32[]{:S(2)}) collective-permute-start(bf16[64,640]{1,0:T(8,128)(2,1)} %attend.2.refs_0_), channel_id=1, source_target_pairs={{0,12},{1,13},{2,14},{3,15},{4,8},{5,9},{6,10},{7,11},{8,4},{9,5},... | collective-permute-start | bytes 245768 | tf_op jit(solution)/shard_map/ppermute | solution.py:174
  56.7 9.3 %collective-permute-start.21 = (bf16[64,640]{1,0:T(8,128)(2,1)}, bf16[64,640]{1,0:T(8,128)(2,1)S(1)}, u32[]{:S(2)}, u32[]{:S(2)}) collective-permute-start(bf16[64,640]{1,0:T(8,128)(2,1)} %attend.2.refs_0_), channel_id=1, source_target_pairs={{0,8},{1,9},{2,10},{3,11},{4,12},{5,13},{6,14},{7,15},{8,0},{9,1},... | collective-permute-start | bytes 245768 | tf_op jit(solution)/shard_map/ppermute | solution.py:174
  58.1 8.5 %collective-permute-start.19 = (bf16[64,640]{1,0:T(8,128)(2,1)}, bf16[64,640]{1,0:T(8,128)(2,1)S(1)}, u32[]{:S(2)}, u32[]{:S(2)}) collective-permute-start(bf16[64,640]{1,0:T(8,128)(2,1)} %attend.2.refs_0_), channel_id=1, source_target_pairs={{0,4},{1,5},{2,6},{3,7},{4,0},{5,1},{6,2},{7,3},{8,12},{9,13},{10,... | collective-permute-start | bytes 245768 | tf_op jit(solution)/shard_map/ppermute | solution.py:174
  60.6 7.5 %collective-permute-start.18 = (bf16[64,640]{1,0:T(8,128)(2,1)}, bf16[64,640]{1,0:T(8,128)(2,1)S(1)}, u32[]{:S(2)}, u32[]{:S(2)}) collective-permute-start(bf16[64,640]{1,0:T(8,128)(2,1)} %attend.2.refs_0_), channel_id=1, source_target_pairs={{0,2},{1,3},{2,0},{3,1},{4,6},{5,7},{6,4},{7,5},{8,10},{9,11},{10,... | collective-permute-start | bytes 245768 | tf_op jit(solution)/shard_map/ppermute | solution.py:174
  63.6 4.5 %collective-permute-start.24 = (bf16[64,640]{1,0:T(8,128)(2,1)S(1)}, bf16[64,640]{1,0:T(8,128)(2,1)S(1)}, u32[]{:S(2)}, u32[]{:S(2)}) collective-permute-start(bf16[64,640]{1,0:T(8,128)(2,1)S(1)} %collective-permute-done.23.refs_6_), channel_id=1, source_target_pairs={{0,2},{1,3},{2,0},{3,1},{4,6},{5,7},{6,4},{7,5},{8,10},{9,11},{10,... | collective-permute-start | bytes 245768 | tf_op jit(solution)/shard_map/ppermute | solution.py:174
  66.1 4.8 %collective-permute-start.22 = (bf16[64,640]{1,0:T(8,128)(2,1)S(1)}, bf16[64,640]{1,0:T(8,128)(2,1)S(1)}, u32[]{:S(2)}, u32[]{:S(2)}) collective-permute-start(bf16[64,640]{1,0:T(8,128)(2,1)S(1)} %collective-permute-done.21.refs_4_), channel_id=1, source_target_pairs={{0,2},{1,3},{2,0},{3,1},{4,6},{5,7},{6,4},{7,5},{8,10},{9,11},{10,... | collective-permute-start | bytes 245768 | tf_op jit(solution)/shard_map/ppermute | solution.py:174
  66.7 5.1 %collective-permute-start.20 = (bf16[64,640]{1,0:T(8,128)(2,1)S(1)}, bf16[64,640]{1,0:T(8,128)(2,1)S(1)}, u32[]{:S(2)}, u32[]{:S(2)}) collective-permute-start(bf16[64,640]{1,0:T(8,128)(2,1)S(1)} %collective-permute-done.19.refs_2_), channel_id=1, source_target_pairs={{0,2},{1,3},{2,0},{3,1},{4,6},{5,7},{6,4},{7,5},{8,10},{9,11},{10,... | collective-permute-start | bytes 245768 | tf_op jit(solution)/shard_map/ppermute | solution.py:174
  74.4 22.3 %copy-start.1 = (bf16[5120,320]{0,1:T(8,128)(2,1)S(1)}, bf16[5120,320]{0,1:T(8,128)(2,1)}, u32[]{:S(2)}) copy-start(bf16[5120,320]{0,1:T(8,128)(2,1)} %param.16) | copy-start | bytes 9830404
  74.5 22.3 %copy-start.2 = (bf16[5120,320]{0,1:T(8,128)(2,1)S(1)}, bf16[5120,320]{0,1:T(8,128)(2,1)}, u32[]{:S(2)}) copy-start(bf16[5120,320]{0,1:T(8,128)(2,1)} %param.17) | copy-start | bytes 9830404
  74.5 22.3 %copy-start.7 = (f32[2,5120]{1,0:T(2,128)S(1)}, f32[2,5120]{1,0:T(2,128)}, u32[]{:S(2)}) copy-start(f32[2,5120]{1,0:T(2,128)} %pad_maximum_fusion.gain_hbm) | copy-start | bytes 122884
  79.1 24.4 %copy-start.6 = (bf16[64,640]{1,0:T(8,128)(2,1)}, bf16[64,640]{1,0:T(8,128)(2,1)S(1)}, u32[]{:S(2)}) copy-start(bf16[64,640]{1,0:T(8,128)(2,1)S(1)} %output.2.refs_3_.current_hbm) | copy-start | bytes 245764
  79.2 7.2 %collective-permute-start.30 = (bf16[64,640]{1,0:T(8,128)(2,1)S(1)}, bf16[64,640]{1,0:T(8,128)(2,1)S(1)}, u32[]{:S(2)}, u32[]{:S(2)}) collective-permute-start(bf16[64,640]{1,0:T(8,128)(2,1)S(1)} %output.2.refs_3_.current_hbm), channel_id=1, source_target_pairs={{0,12},{1,13},{2,14},{3,15},{4,8},{5,9},{6,10},{7,11},{8,4},{9,5},... | collective-permute-start | bytes 245768 | tf_op jit(solution)/shard_map/ppermute | solution.py:174
  80.5 5.9 %collective-permute-start.32 = (bf16[64,640]{1,0:T(8,128)(2,1)S(1)}, bf16[64,640]{1,0:T(8,128)(2,1)S(1)}, u32[]{:S(2)}, u32[]{:S(2)}) collective-permute-start(bf16[64,640]{1,0:T(8,128)(2,1)S(1)} %output.2.refs_3_.current_hbm), channel_id=1, source_target_pairs={{0,1},{1,0},{2,3},{3,2},{4,5},{5,4},{6,7},{7,6},{8,9},{9,8},{10,11... | collective-permute-start | bytes 245768 | tf_op jit(solution)/shard_map/ppermute | solution.py:174
  80.5 8.4 %collective-permute-start.28 = (bf16[64,640]{1,0:T(8,128)(2,1)S(1)}, bf16[64,640]{1,0:T(8,128)(2,1)S(1)}, u32[]{:S(2)}, u32[]{:S(2)}) collective-permute-start(bf16[64,640]{1,0:T(8,128)(2,1)S(1)} %output.2.refs_3_.current_hbm), channel_id=1, source_target_pairs={{0,8},{1,9},{2,10},{3,11},{4,12},{5,13},{6,14},{7,15},{8,0},{9,1},... | collective-permute-start | bytes 245768 | tf_op jit(solution)/shard_map/ppermute | solution.py:174
  80.5 8.5 %collective-permute-start.26 = (bf16[64,640]{1,0:T(8,128)(2,1)S(1)}, bf16[64,640]{1,0:T(8,128)(2,1)S(1)}, u32[]{:S(2)}, u32[]{:S(2)}) collective-permute-start(bf16[64,640]{1,0:T(8,128)(2,1)S(1)} %output.2.refs_3_.current_hbm), channel_id=1, source_target_pairs={{0,4},{1,5},{2,6},{3,7},{4,0},{5,1},{6,2},{7,3},{8,12},{9,13},{10,... | collective-permute-start | bytes 245768 | tf_op jit(solution)/shard_map/ppermute | solution.py:174
  83.6 6.3 %collective-permute-start.25 = (bf16[64,640]{1,0:T(8,128)(2,1)S(1)}, bf16[64,640]{1,0:T(8,128)(2,1)S(1)}, u32[]{:S(2)}, u32[]{:S(2)}) collective-permute-start(bf16[64,640]{1,0:T(8,128)(2,1)S(1)} %output.2.refs_3_.current_hbm), channel_id=1, source_target_pairs={{0,2},{1,3},{2,0},{3,1},{4,6},{5,7},{6,4},{7,5},{8,10},{9,11},{10,... | collective-permute-start | bytes 245768 | tf_op jit(solution)/shard_map/ppermute | solution.py:174
  86.4 4.7 %collective-permute-start.38 = (bf16[64,640]{1,0:T(8,128)(2,1)S(1)}, bf16[64,640]{1,0:T(8,128)(2,1)S(1)}, u32[]{:S(2)}, u32[]{:S(2)}) collective-permute-start(bf16[64,640]{1,0:T(8,128)(2,1)S(1)} %collective-permute-done.30.refs_9_), channel_id=1, source_target_pairs={{0,1},{1,0},{2,3},{3,2},{4,5},{5,4},{6,7},{7,6},{8,9},{9,8},{10,11... | collective-permute-start | bytes 245768 | tf_op jit(solution)/shard_map/ppermute | solution.py:174
  86.4 4.9 %collective-permute-start.31 = (bf16[64,640]{1,0:T(8,128)(2,1)S(1)}, bf16[64,640]{1,0:T(8,128)(2,1)S(1)}, u32[]{:S(2)}, u32[]{:S(2)}) collective-permute-start(bf16[64,640]{1,0:T(8,128)(2,1)S(1)} %collective-permute-done.30.refs_9_), channel_id=1, source_target_pairs={{0,2},{1,3},{2,0},{3,1},{4,6},{5,7},{6,4},{7,5},{8,10},{9,11},{10,... | collective-permute-start | bytes 245768 | tf_op jit(solution)/shard_map/ppermute | solution.py:174
  88.9 2.7 %collective-permute-start.36 = (bf16[64,640]{1,0:T(8,128)(2,1)S(1)}, bf16[64,640]{1,0:T(8,128)(2,1)S(1)}, u32[]{:S(2)}, u32[]{:S(2)}) collective-permute-start(bf16[64,640]{1,0:T(8,128)(2,1)S(1)} %collective-permute-done.28.refs_7_), channel_id=1, source_target_pairs={{0,1},{1,0},{2,3},{3,2},{4,5},{5,4},{6,7},{7,6},{8,9},{9,8},{10,11... | collective-permute-start | bytes 245768 | tf_op jit(solution)/shard_map/ppermute | solution.py:174
  89.0 5.3 %collective-permute-start.29 = (bf16[64,640]{1,0:T(8,128)(2,1)S(1)}, bf16[64,640]{1,0:T(8,128)(2,1)S(1)}, u32[]{:S(2)}, u32[]{:S(2)}) collective-permute-start(bf16[64,640]{1,0:T(8,128)(2,1)S(1)} %collective-permute-done.28.refs_7_), channel_id=1, source_target_pairs={{0,2},{1,3},{2,0},{3,1},{4,6},{5,7},{6,4},{7,5},{8,10},{9,11},{10,... | collective-permute-start | bytes 245768 | tf_op jit(solution)/shard_map/ppermute | solution.py:174
  89.9 5.6 %collective-permute-start.27 = (bf16[64,640]{1,0:T(8,128)(2,1)S(1)}, bf16[64,640]{1,0:T(8,128)(2,1)S(1)}, u32[]{:S(2)}, u32[]{:S(2)}) collective-permute-start(bf16[64,640]{1,0:T(8,128)(2,1)S(1)} %collective-permute-done.26.refs_5_), channel_id=1, source_target_pairs={{0,2},{1,3},{2,0},{3,1},{4,6},{5,7},{6,4},{7,5},{8,10},{9,11},{10,... | collective-permute-start | bytes 245768 | tf_op jit(solution)/shard_map/ppermute | solution.py:174
  91.1 4.4 %collective-permute-start.34 = (bf16[64,640]{1,0:T(8,128)(2,1)S(1)}, bf16[64,640]{1,0:T(8,128)(2,1)S(1)}, u32[]{:S(2)}, u32[]{:S(2)}) collective-permute-start(bf16[64,640]{1,0:T(8,128)(2,1)S(1)} %collective-permute-done.26.refs_5_), channel_id=1, source_target_pairs={{0,1},{1,0},{2,3},{3,2},{4,5},{5,4},{6,7},{7,6},{8,9},{9,8},{10,11... | collective-permute-start | bytes 245768 | tf_op jit(solution)/shard_map/ppermute | solution.py:174
  91.2 4.2 %collective-permute-start.33 = (bf16[64,640]{1,0:T(8,128)(2,1)S(1)}, bf16[64,640]{1,0:T(8,128)(2,1)S(1)}, u32[]{:S(2)}, u32[]{:S(2)}) collective-permute-start(bf16[64,640]{1,0:T(8,128)(2,1)S(1)} %collective-permute-done.25.refs_4_), channel_id=1, source_target_pairs={{0,1},{1,0},{2,3},{3,2},{4,5},{5,4},{6,7},{7,6},{8,9},{9,8},{10,11... | collective-permute-start | bytes 245768 | tf_op jit(solution)/shard_map/ppermute | solution.py:174
  91.6 3.9 %collective-permute-start.39 = (bf16[64,640]{1,0:T(8,128)(2,1)S(1)}, bf16[64,640]{1,0:T(8,128)(2,1)S(1)}, u32[]{:S(2)}, u32[]{:S(2)}) collective-permute-start(bf16[64,640]{1,0:T(8,128)(2,1)S(1)} %collective-permute-done.31.refs_10_), channel_id=1, source_target_pairs={{0,1},{1,0},{2,3},{3,2},{4,5},{5,4},{6,7},{7,6},{8,9},{9,8},{10,11... | collective-permute-start | bytes 245768 | tf_op jit(solution)/shard_map/ppermute | solution.py:174
  94.3 1.3 collective-permute-start.37
  95.5 1.3 collective-permute-start.35
  104.2 9.9 %copy-start.9 = (bf16[320,320]{1,0:T(8,128)(2,1)}, bf16[320,320]{1,0:T(8,128)(2,1)S(1)}, u32[]{:S(2)}) copy-start(bf16[320,320]{1,0:T(8,128)(2,1)S(1)} %get-tuple-element.25.sent_hbm) | copy-start | bytes 614404
  104.2 9.9 %collective-permute-start.40 = (bf16[320,320]{1,0:T(8,128)(2,1)S(1)}, bf16[320,320]{1,0:T(8,128)(2,1)S(1)}, u32[]{:S(2)}, u32[]{:S(2)}) collective-permute-start(bf16[320,320]{1,0:T(8,128)(2,1)S(1)} %get-tuple-element.25.sent_hbm), channel_id=1, source_target_pairs={{0,1},{1,0},{2,3},{3,2},{4,5},{5,4},{6,7},{7,6},{8,9},{9,8},{10,11... | collective-permute-start | bytes 614408 | tf_op jit(solution)/shard_map/ppermute | solution.py:174
  118.0 7.4 %collective-permute-start.46 = (bf16[64,640]{1,0:T(8,128)(2,1)}, bf16[64,640]{1,0:T(8,128)(2,1)S(1)}, u32[]{:S(2)}, u32[]{:S(2)}) collective-permute-start(bf16[64,640]{1,0:T(8,128)(2,1)} %attend.3.refs_0_), channel_id=1, source_target_pairs={{0,12},{1,13},{2,14},{3,15},{4,8},{5,9},{6,10},{7,11},{8,4},{9,5},... | collective-permute-start | bytes 245768 | tf_op jit(solution)/shard_map/ppermute | solution.py:174
  118.5 9.3 %collective-permute-start.44 = (bf16[64,640]{1,0:T(8,128)(2,1)}, bf16[64,640]{1,0:T(8,128)(2,1)S(1)}, u32[]{:S(2)}, u32[]{:S(2)}) collective-permute-start(bf16[64,640]{1,0:T(8,128)(2,1)} %attend.3.refs_0_), channel_id=1, source_target_pairs={{0,8},{1,9},{2,10},{3,11},{4,12},{5,13},{6,14},{7,15},{8,0},{9,1},... | collective-permute-start | bytes 245768 | tf_op jit(solution)/shard_map/ppermute | solution.py:174
  119.9 8.5 %collective-permute-start.42 = (bf16[64,640]{1,0:T(8,128)(2,1)}, bf16[64,640]{1,0:T(8,128)(2,1)S(1)}, u32[]{:S(2)}, u32[]{:S(2)}) collective-permute-start(bf16[64,640]{1,0:T(8,128)(2,1)} %attend.3.refs_0_), channel_id=1, source_target_pairs={{0,4},{1,5},{2,6},{3,7},{4,0},{5,1},{6,2},{7,3},{8,12},{9,13},{10,... | collective-permute-start | bytes 245768 | tf_op jit(solution)/shard_map/ppermute | solution.py:174
  122.4 7.5 %collective-permute-start.41 = (bf16[64,640]{1,0:T(8,128)(2,1)}, bf16[64,640]{1,0:T(8,128)(2,1)S(1)}, u32[]{:S(2)}, u32[]{:S(2)}) collective-permute-start(bf16[64,640]{1,0:T(8,128)(2,1)} %attend.3.refs_0_), channel_id=1, source_target_pairs={{0,2},{1,3},{2,0},{3,1},{4,6},{5,7},{6,4},{7,5},{8,10},{9,11},{10,... | collective-permute-start | bytes 245768 | tf_op jit(solution)/shard_map/ppermute | solution.py:174
  125.4 8.1 %copy-start.25 = (bf16[64,640]{1,0:T(8,128)(2,1)}, bf16[64,640]{1,0:T(8,128)(2,1)S(1)}, u32[]{:S(2)}) copy-start(bf16[64,640]{1,0:T(8,128)(2,1)S(1)} %collective-permute-done.46.refs_6_) | copy-start | bytes 245764
  125.4 4.5 %collective-permute-start.47 = (bf16[64,640]{1,0:T(8,128)(2,1)S(1)}, bf16[64,640]{1,0:T(8,128)(2,1)S(1)}, u32[]{:S(2)}, u32[]{:S(2)}) collective-permute-start(bf16[64,640]{1,0:T(8,128)(2,1)S(1)} %collective-permute-done.46.refs_6_), channel_id=1, source_target_pairs={{0,2},{1,3},{2,0},{3,1},{4,6},{5,7},{6,4},{7,5},{8,10},{9,11},{10,... | collective-permute-start | bytes 245768 | tf_op jit(solution)/shard_map/ppermute | solution.py:174
  127.9 4.8 %collective-permute-start.45 = (bf16[64,640]{1,0:T(8,128)(2,1)S(1)}, bf16[64,640]{1,0:T(8,128)(2,1)S(1)}, u32[]{:S(2)}, u32[]{:S(2)}) collective-permute-start(bf16[64,640]{1,0:T(8,128)(2,1)S(1)} %collective-permute-done.44.refs_4_), channel_id=1, source_target_pairs={{0,2},{1,3},{2,0},{3,1},{4,6},{5,7},{6,4},{7,5},{8,10},{9,11},{10,... | collective-permute-start | bytes 245768 | tf_op jit(solution)/shard_map/ppermute | solution.py:174
  128.4 5.1 %collective-permute-start.43 = (bf16[64,640]{1,0:T(8,128)(2,1)S(1)}, bf16[64,640]{1,0:T(8,128)(2,1)S(1)}, u32[]{:S(2)}, u32[]{:S(2)}) collective-permute-start(bf16[64,640]{1,0:T(8,128)(2,1)S(1)} %collective-permute-done.42.refs_2_), channel_id=1, source_target_pairs={{0,2},{1,3},{2,0},{3,1},{4,6},{5,7},{6,4},{7,5},{8,10},{9,11},{10,... | collective-permute-start | bytes 245768 | tf_op jit(solution)/shard_map/ppermute | solution.py:174
  (21 other events, 37.5 us)
